TPU v7x, 32 devices: a whole 2x2x4 slice. The times are simulated.
32 devices in a mesh: groups: 2 (over y), graph: 4 (over z), mp: 4 (over x, core).
Axes of the slice: x: 2, y: 2, z: 4, core: 2. Of those that a mesh axis runs over, the one named last changes fastest.
Arguments:
- node_state: float32 [1536, 512], P(('groups', 'graph'), 'mp'), parts along dimension 0, may hold values from -6 to 6
- edge_state: float32 [12288, 512], P(('groups', 'graph'), 'mp'), parts along dimension 0, may hold values from -6 to 6
- edge_first: bfloat16 [2, 1536, 512], P(None, None, 'mp'), may hold values from -0.15625 to 0.15625
- edge_second: bfloat16 [2, 512, 512], P(None, 'mp'), may hold values from -0.25 to 0.25
- node_first: bfloat16 [2, 1024, 512], P(None, None, 'mp'), may hold values from -0.1875 to 0.1875
- node_second: bfloat16 [2, 512, 512], P(None, 'mp'), may hold values from -0.25 to 0.25
- senders: int32 [6144], P('graph'), may hold values from 0 to 303, as said below
- receivers: int32 [6144], P('graph'), may hold values from 0 to 191, as said below
- boundary_rows: int32 [256], P('graph'), may hold values from 0 to 191, as said below
Outputs:
- node_result: float32 [1536, 512], P(('groups', 'graph'), 'mp'), parts along dimension 0
- edge_result: float32 [12288, 512], P(('groups', 'graph'), 'mp'), parts along dimension 0
There are 2 independent parts, one for each index of `groups`. A program takes and returns all parts, laid end to end along the dimension named above; an argument that names none is the same for every part. Nothing has to cross between parts.
Inputs may be any that keep to these rules, and one draw needn't show every extreme that they name: Entries index the node table of the edge's block: below 192 the block's own nodes, then 32 rows of the previous block's list for its next neighbour, then 32 rows of the next block's list for its previous neighbour (blocks taken cyclically), then the 48 coarse nodes, block by block, each block's last 12 nodes in order. In every block the last 192 edges have coarse senders and the others do not. `receivers`: receivers are nodes of the edge's own block; the last 192 edges of every block go to one of its last 12 nodes. `boundary_rows`: entry b * 2 * 32 + j is a node of block b: for j < 32 one that block b - 1 reads, else one that block b + 1 reads (cyclically).
All inputs are finite; a program needn't handle non-finite values.
Results may differ from a plain program's by a relative error of at most 0.014.
Values may be sent and summed in bfloat16 or wider, within the bound.
No kernel may reach another device: no remote copies, remote signals or barrier semaphores. Data moves between devices by JAX's collectives and lax.ppermute only.
A program may use at most 64 MiB of HBM per device.

v0:
```python
import jax
import jax.numpy as jnp
from jax import lax
from jax.sharding import PartitionSpec as P

COARSE_DEV = 12


EPS = 1e-05


def padded_2(x, sides, width):
    for axis, dim in sides:
        size, length = (lax.axis_size(axis), x.shape[dim])
        up = [(i, (i + 1) % size) for i in range(size)]
        down = [(j, i) for i, j in up]
        last = lax.slice_in_dim(x, length - width, length, axis=dim)
        initial = lax.slice_in_dim(x, 0, width, axis=dim)
        before = lax.ppermute(last, axis, up)
        after = lax.ppermute(initial, axis, down)
        x = jnp.concatenate([before, x, after], axis=dim)
    return x


def normalize_rows(summed, row_sums, squares, feature_count):
    row_mean = row_sums / feature_count
    spread = squares / feature_count - row_mean * row_mean
    return (summed - row_mean[:, None]) * lax.rsqrt(spread + EPS)[:, None]


def split_norm(partial_value, for_edges):
    feature_count = partial_value.shape[1]
    if for_edges:
        owned_share = lax.psum_scatter(
            partial_value.astype(jnp.bfloat16), "mp", scatter_dimension=1, tiled=True
        ).astype(jnp.float32)
    else:
        owned_share = lax.psum_scatter(
            partial_value.astype(jnp.bfloat16), "mp", scatter_dimension=1, tiled=True
        ).astype(jnp.float32)
    row_sums = jnp.sum(owned_share, axis=1)
    squares = jnp.sum(owned_share * owned_share, axis=1)
    if for_edges:
        row_sums, squares = lax.psum((row_sums, squares), "mp")
    else:
        row_sums, squares = lax.psum((row_sums, squares), "mp")
    return normalize_rows(owned_share, row_sums, squares, feature_count)


def aggregate(incidence_bf, edge_rows):
    upper = edge_rows.astype(jnp.bfloat16)
    lower = (edge_rows - upper.astype(jnp.float32)).astype(jnp.bfloat16)
    total = jnp.dot(incidence_bf, upper, preferred_element_type=jnp.float32)
    return total + jnp.dot(incidence_bf, lower, preferred_element_type=jnp.float32)


def prepare_rims(node_rows, boundary_rows):
    outgoing = jnp.take(node_rows, boundary_rows, axis=0)
    coarse_rows = node_rows[node_rows.shape[0] - COARSE_DEV :]
    return (outgoing, coarse_rows)


def assemble_table(node_rows, padded, coarse):
    halo_width = padded.shape[0] // 4
    return jnp.concatenate(
        [node_rows, padded[:halo_width], padded[3 * halo_width :], coarse], axis=0
    )


def edge_hidden(edge_bf, node_table, senders, receivers, first):
    feature_count = edge_bf.shape[1]
    sender_rows = jnp.take(node_table, senders, axis=0)
    receiver_rows = jnp.take(node_table, receivers, axis=0)
    preact = jnp.dot(edge_bf, first[:feature_count], preferred_element_type=jnp.float32)
    preact = preact + jnp.dot(
        sender_rows, first[feature_count : 2 * feature_count], preferred_element_type=jnp.float32
    )
    preact = preact + jnp.dot(
        receiver_rows, first[2 * feature_count :], preferred_element_type=jnp.float32
    )
    return jax.nn.silu(preact).astype(jnp.bfloat16)


def node_hidden(node_bf, incoming_bf, first):
    feature_count = node_bf.shape[1]
    preact = jnp.dot(node_bf, first[:feature_count], preferred_element_type=jnp.float32)
    preact = preact + jnp.dot(
        incoming_bf, first[feature_count:], preferred_element_type=jnp.float32
    )
    return jax.nn.silu(preact).astype(jnp.bfloat16)


def on_device(
    node_state,
    edge_state,
    edge_first,
    edge_second,
    node_first,
    node_second,
    senders,
    receivers,
    boundary_rows,
):
    node_count = node_state.shape[0]
    layer_count = edge_first.shape[0]
    halo_width = boundary_rows.shape[0] // 2
    incidence = (receivers[None, :] == jnp.arange(node_count, dtype=jnp.int32)[:, None]).astype(
        jnp.bfloat16
    )
    node_result = node_state
    edge_result = edge_state
    for layer_index in range(layer_count):
        node_split = node_result.astype(jnp.bfloat16)
        outgoing, coarse_rows = prepare_rims(node_split, boundary_rows)
        padded = padded_2(outgoing, (("graph", 0),), halo_width)
        coarse = lax.all_gather(coarse_rows, "graph", axis=0, tiled=True)
        split_table = assemble_table(node_split, padded, coarse)
        node_table, edge_bf = (
            lax.all_gather(split_table, "mp", axis=1, tiled=True),
            lax.all_gather(edge_result.astype(jnp.bfloat16), "mp", axis=1, tiled=True),
        )
        hidden = edge_hidden(edge_bf, node_table, senders, receivers, edge_first[layer_index])
        partial_value = jnp.dot(
            hidden, edge_second[layer_index], preferred_element_type=jnp.float32
        )
        edge_result = edge_result + split_norm(partial_value, True)
        incoming = aggregate(incidence, edge_result)
        incoming_bf = lax.all_gather(incoming.astype(jnp.bfloat16), "mp", axis=1, tiled=True)
        hidden = node_hidden(node_table[:node_count], incoming_bf, node_first[layer_index])
        partial_value = jnp.dot(
            hidden, node_second[layer_index], preferred_element_type=jnp.float32
        )
        node_result = node_result + split_norm(partial_value, False)
    return (node_result, edge_result)


def solution(mesh):
    in_specs = (
        P(("groups", "graph"), "mp"),
        P(("groups", "graph"), "mp"),
        P(None, None, "mp"),
        P(None, "mp", None),
        P(None, None, "mp"),
        P(None, "mp", None),
        P("graph"),
        P("graph"),
        P("graph"),
    )
    out_specs = (P(("groups", "graph"), "mp"), P(("groups", "graph"), "mp"))
    return jax.shard_map(
        on_device, mesh=mesh, in_specs=in_specs, out_specs=out_specs, check_vma=False
    )
```

profile of v0, /device:TPU:0, one launch (start us, length us, event | category | flops | bytes accessed | tf_op | source)
XLA Modules:
  0.0 263.8 jit_solution(3107420411898100058)
XLA Ops:
  10.0 5.1 %collective-permute-start.1 = (bf16[32,128]{1,0:T(8,128)(2,1)S(1)}, bf16[32,128]{1,0:T(8,128)(2,1)S(1)}, u32[]{:S(2)}, u32[]{:S(2)}) collective-permute-start(bf16[32,128]{1,0:T(8,128)(2,1)S(1)} %get-tuple-element.23), channel_id=1, source_target_pairs={{4,0},{8,4},{12,8},{0,12},{5,1},{9,5},{13,9},{1,13},{6,2},{10,6},{... | collective-permute-start | bytes 24584 | tf_op jit(solution)/shard_map/ppermute | solution.py:20
  15.3 13.1 %all-gather = bf16[4,12,128]{2,1,0:T(8,128)(2,1)S(1)} all-gather(bf16[1,12,128]{2,1,0:T(8,128)(2,1)S(1)} %slice_bitcast_fusion.1), channel_id=1, replica_groups=mesh['groups'=2,'graph'=4,'mp'=4] {'graph'}, dimensions={0}, use_global_device_ids=true | all-gather | bytes 15360 | tf_op jit(solution)/shard_map/all_gather | solution.py:116
  28.5 6.1 %all_gather.25 = bf16[304,512]{1,0:T(8,128)(2,1)S(1)} all-gather(bf16[304,128]{1,0:T(8,128)(2,1)S(1)} %pad_maximum_fusion), channel_id=1, replica_groups=mesh['groups'=2,'graph'=4,'mp'=4] {'mp'}, dimensions={1}, use_global_device_ids=true | all-gather | bytes 389120 | tf_op jit(solution)/shard_map/all_gather | solution.py:119
  34.5 5.4 %gather_fusion.1 = bf16[1536,512]{1,0:T(8,128)(2,1)} fusion(bf16[304,512]{1,0:T(8,128)(2,1)S(1)} %all_gather.25, s32[2048]{0:T(1024)S(1)} %pad_clamp_fusion.1), kind=kCustom, calls=%fused_computation.1.clone | custom fusion | bytes 3151872 | tf_op jit(solution)/shard_map/jit(_take)/gather | solution.py:72
  40.0 4.8 %gather_fusion.2 = bf16[1536,512]{1,0:T(8,128)(2,1)S(1)} fusion(bf16[304,512]{1,0:T(8,128)(2,1)S(1)} %all_gather.25, s32[2048]{0:T(1024)S(1)} %pad_clamp_fusion), kind=kCustom, calls=%fused_computation.3.clone | custom fusion | bytes 3151872 | tf_op jit(solution)/shard_map/jit(_take)/gather | solution.py:73
  49.4 3.4 %convolution_convert_fusion.1 = bf16[1536,512]{1,0:T(8,128)(2,1)} fusion(f32[1536,128]{1,0:T(8,128)} %convolution_add_fusion.3, bf16[1536,512]{1,0:T(8,128)(2,1)S(1)} %gather_fusion.2, pred[1536]{0:T(1024)(128)(4,1)S(1)} %compare_and_fusion, bf16[2,128,512]{2,1,0:T(8,128)(2,1)S(1)} %copy-done.21, bf16[2,1536,128]{2,1,0:T(8,128)(2,1)} %param.15), kind=kOutput, calls=%fused_computation.7 | convolution fusion | flops 405405696 | bytes 4196352 | tf_op jit(solution)/shard_map/dot_general | solution.py:123
  52.8 2.6 copy.11
  56.6 28.5 %reduce-scatter.13.cloned.1.call-done = bf16[128,1536]{1,0:T(8,128)(2,1)} async-done(((bf16[512,1536]{1,0:T(8,128)(2,1)}), bf16[128,1536]{1,0:T(8,128)(2,1)}) %reduce-scatter.13.cloned.1.call-update) | async-done | bytes 393232
  86.7 10.1 %all-reduce.3 = (f32[1536]{0:T(1024)S(1)}, f32[1536]{0:T(1024)S(1)}) all-reduce(f32[1536]{0:T(1024)S(1)} %get-tuple-element.7, f32[1536]{0:T(1024)S(1)} %get-tuple-element.6), channel_id=1, replica_groups=mesh['groups'=2,'graph'=4,'mp'=4] {'mp'}, use_global_device_ids=true, to_apply=%region_4.7 | all-reduce | flops 3072 | bytes 24576 | tf_op jit(solution)/shard_map/psum | solution.py:44
  98.5 5.6 %all_gather.27 = bf16[192,512]{1,0:T(8,128)(2,1)S(1)} all-gather(bf16[192,128]{1,0:T(8,128)(2,1)S(1)} %fusion.15), channel_id=1, replica_groups=mesh['groups'=2,'graph'=4,'mp'=4] {'mp'}, dimensions={1}, use_global_device_ids=true | all-gather | bytes 245760 | tf_op jit(solution)/shard_map/all_gather | solution.py:128
  105.9 20.6 %reduce-scatter.15.cloned.1.call-done = bf16[128,192]{1,0:T(8,128)(2,1)} async-done(((bf16[512,192]{1,0:T(8,128)(2,1)}), bf16[128,192]{1,0:T(8,128)(2,1)}) %reduce-scatter.15.cloned.1.call-update) | async-done | bytes 49168
  127.7 5.8 %all-reduce.2 = (f32[192]{0:T(256)S(1)}, f32[192]{0:T(256)S(1)}) all-reduce(f32[192]{0:T(256)S(1)} %get-tuple-element.11, f32[192]{0:T(256)S(1)} %get-tuple-element.10), channel_id=1, replica_groups=mesh['groups'=2,'graph'=4,'mp'=4] {'mp'}, use_global_device_ids=true, to_apply=%region_9.12 | all-reduce | flops 384 | bytes 3072 | tf_op jit(solution)/shard_map/psum | solution.py:46
  134.3 3.6 %collective-permute-start.3 = (bf16[32,128]{1,0:T(8,128)(2,1)S(1)}, bf16[32,128]{1,0:T(8,128)(2,1)S(1)}, u32[]{:S(2)}, u32[]{:S(2)}) collective-permute-start(bf16[32,128]{1,0:T(8,128)(2,1)S(1)} %get-tuple-element.21), channel_id=1, source_target_pairs={{4,0},{8,4},{12,8},{0,12},{5,1},{9,5},{13,9},{1,13},{6,2},{10,6},{... | collective-permute-start | bytes 24584 | tf_op jit(solution)/shard_map/ppermute | solution.py:20
  137.9 13.1 %all-gather.1 = bf16[4,12,128]{2,1,0:T(8,128)(2,1)S(1)} all-gather(bf16[1,12,128]{2,1,0:T(8,128)(2,1)S(1)} %slice_bitcast_fusion), channel_id=1, replica_groups=mesh['groups'=2,'graph'=4,'mp'=4] {'graph'}, dimensions={0}, use_global_device_ids=true | all-gather | bytes 15360 | tf_op jit(solution)/shard_map/all_gather | solution.py:116
  151.1 6.1 %all_gather.29 = bf16[304,512]{1,0:T(8,128)(2,1)S(1)} all-gather(bf16[304,128]{1,0:T(8,128)(2,1)S(1)} %pad_maximum_fusion.1), channel_id=1, replica_groups=mesh['groups'=2,'graph'=4,'mp'=4] {'mp'}, dimensions={1}, use_global_device_ids=true | all-gather | bytes 389120 | tf_op jit(solution)/shard_map/all_gather | solution.py:119
  157.2 5.4 %gather_fusion.4 = bf16[1536,512]{1,0:T(8,128)(2,1)} fusion(bf16[304,512]{1,0:T(8,128)(2,1)S(1)} %all_gather.29, s32[2048]{0:T(1024)S(1)} %pad_clamp_fusion.1), kind=kCustom, calls=%fused_computation.4.clone | custom fusion | bytes 3151872 | tf_op jit(solution)/shard_map/jit(_take)/gather | solution.py:72
  162.6 4.8 %gather_fusion.5 = bf16[1536,512]{1,0:T(8,128)(2,1)S(1)} fusion(bf16[304,512]{1,0:T(8,128)(2,1)S(1)} %all_gather.29, s32[2048]{0:T(1024)S(1)} %copy-done.9), kind=kCustom, calls=%fused_computation.5.clone | custom fusion | bytes 3151872 | tf_op jit(solution)/shard_map/jit(_take)/gather | solution.py:73
  172.0 3.4 %convolution_convert_fusion = bf16[1536,512]{1,0:T(8,128)(2,1)} fusion(f32[1536,128]{1,0:T(8,128)} %convolution_add_fusion.1, bf16[1536,512]{1,0:T(8,128)(2,1)S(1)} %gather_fusion.5, pred[1536]{0:T(1024)(128)(4,1)S(1)} %copy-done.16, bf16[2,128,512]{2,1,0:T(8,128)(2,1)} %param.16, bf16[2,1536,128]{2,1,0:T(8,128)(2,1)} %param.15), kind=kOutput, calls=%fused_computation.6 | convolution fusion | flops 405405696 | bytes 4195840 | tf_op jit(solution)/shard_map/dot_general | solution.py:123
  175.4 2.6 copy.15
  179.3 28.2 %reduce-scatter.17.cloned.1.call-done = bf16[128,1536]{1,0:T(8,128)(2,1)} async-done(((bf16[512,1536]{1,0:T(8,128)(2,1)}), bf16[128,1536]{1,0:T(8,128)(2,1)}) %reduce-scatter.17.cloned.1.call-update) | async-done | bytes 393232
  209.1 10.1 %all-reduce.1 = (f32[1536]{0:T(1024)S(1)}, f32[1536]{0:T(1024)S(1)}) all-reduce(f32[1536]{0:T(1024)S(1)} %get-tuple-element.5, f32[1536]{0:T(1024)S(1)} %get-tuple-element.4), channel_id=1, replica_groups=mesh['groups'=2,'graph'=4,'mp'=4] {'mp'}, use_global_device_ids=true, to_apply=%region_14.17 | all-reduce | flops 3072 | bytes 24576 | tf_op jit(solution)/shard_map/psum | solution.py:44
  221.2 5.6 %all_gather.31 = bf16[192,512]{1,0:T(8,128)(2,1)S(1)} all-gather(bf16[192,128]{1,0:T(8,128)(2,1)S(1)} %fusion.14), channel_id=1, replica_groups=mesh['groups'=2,'graph'=4,'mp'=4] {'mp'}, dimensions={1}, use_global_device_ids=true | all-gather | bytes 245760 | tf_op jit(solution)/shard_map/all_gather | solution.py:128
  228.0 21.3 %reduce-scatter.19.cloned.1.call-done = bf16[128,192]{1,0:T(8,128)(2,1)} async-done(((bf16[512,192]{1,0:T(8,128)(2,1)}), bf16[128,192]{1,0:T(8,128)(2,1)}) %reduce-scatter.19.cloned.1.call-update) | async-done | bytes 49168
  250.4 5.8 %all-reduce = (f32[192]{0:T(256)S(1)}, f32[192]{0:T(256)S(1)}) all-reduce(f32[192]{0:T(256)S(1)} %get-tuple-element.9, f32[192]{0:T(256)S(1)} %get-tuple-element.8), channel_id=1, replica_groups=mesh['groups'=2,'graph'=4,'mp'=4] {'mp'}, use_global_device_ids=true, to_apply=%region_19.22 | all-reduce | flops 384 | bytes 3072 | tf_op jit(solution)/shard_map/psum | solution.py:46
  (123 shorter events, 27.9 us)
Async XLA Ops:
  7.2 8.0 %copy-start.14 = (s32[1536]{0:T(1024)S(1)}, s32[1536]{0:T(1024)}, u32[]{:S(2)}) copy-start(s32[1536]{0:T(1024)} %param.19) | copy-start | bytes 18436
  7.2 8.0 %copy-start.6 = (s32[1536]{0:T(1024)S(1)}, s32[1536]{0:T(1024)}, u32[]{:S(2)}) copy-start(s32[1536]{0:T(1024)} %param.20) | copy-start | bytes 18436
  7.2 37.6 %all-gather.5.cloned.1.call-start = ((), (), s32[]{:S(2)}) async-start(), calls=%async_computation.4 | async-start | bytes 1966080 | tf_op jit(solution)/shard_map/all_gather | solution.py:120
  9.2 75.9 %reduce-scatter.13.cloned.1.call-start = ((), (), s32[]{:S(2)}) async-start(), calls=%async_computation.6 | async-start | bytes 1966080
  10.0 18.4 %collective-permute-start.1 = (bf16[32,128]{1,0:T(8,128)(2,1)S(1)}, bf16[32,128]{1,0:T(8,128)(2,1)S(1)}, u32[]{:S(2)}, u32[]{:S(2)}) collective-permute-start(bf16[32,128]{1,0:T(8,128)(2,1)S(1)} %get-tuple-element.23), channel_id=1, source_target_pairs={{4,0},{8,4},{12,8},{0,12},{5,1},{9,5},{13,9},{1,13},{6,2},{10,6},{... | collective-permute-start | bytes 24584 | tf_op jit(solution)/shard_map/ppermute | solution.py:20
  15.1 13.3 %collective-permute-start = (bf16[32,128]{1,0:T(8,128)(2,1)S(1)}, bf16[32,128]{1,0:T(8,128)(2,1)S(1)}, u32[]{:S(2)}, u32[]{:S(2)}) collective-permute-start(bf16[32,128]{1,0:T(8,128)(2,1)S(1)} %get-tuple-element.22), channel_id=1, source_target_pairs={{0,4},{4,8},{8,12},{12,0},{1,5},{5,9},{9,13},{13,1},{2,6},{6,10},{... | collective-permute-start | bytes 24584 | tf_op jit(solution)/shard_map/ppermute | solution.py:19
  15.2 31.7 %copy-start.17 = (pred[1536]{0:T(1024)(128)(4,1)}, pred[1536]{0:T(1024)(128)(4,1)S(1)}, u32[]{:S(2)}) copy-start(pred[1536]{0:T(1024)(128)(4,1)S(1)} %compare_and_fusion.1) | copy-start | bytes 4612
  15.2 34.2 %copy-start.15 = (pred[1536]{0:T(1024)(128)(4,1)}, pred[1536]{0:T(1024)(128)(4,1)S(1)}, u32[]{:S(2)}) copy-start(pred[1536]{0:T(1024)(128)(4,1)S(1)} %compare_and_fusion) | copy-start | bytes 4612
  15.3 24.7 %copy-start.8 = (s32[2048]{0:T(1024)}, s32[2048]{0:T(1024)S(1)}, u32[]{:S(2)}) copy-start(s32[2048]{0:T(1024)S(1)} %pad_clamp_fusion) | copy-start | bytes 24580
  55.4 41.5 %copy-start = (f32[1536,128]{1,0:T(8,128)S(1)}, f32[1536,128]{1,0:T(8,128)}, u32[]{:S(2)}) copy-start(f32[1536,128]{1,0:T(8,128)} %param.14) | copy-start | bytes 2359300
  55.4 71.1 %reduce-scatter.15.cloned.1.call-start = ((), (), s32[]{:S(2)}) async-start(), calls=%async_computation.7 | async-start | bytes 327680
  97.4 7.0 %copy-start.4 = (bf16[1536,128]{1,0:T(8,128)(2,1)}, bf16[1536,128]{1,0:T(8,128)(2,1)S(1)}, u32[]{:S(2)}) copy-start(bf16[1536,128]{1,0:T(8,128)(2,1)S(1)} %fusion.108) | copy-start | bytes 1179652
  97.4 6.7 %copy-start.22 = (bf16[2,128,512]{2,1,0:T(8,128)(2,1)S(1)}, bf16[2,128,512]{2,1,0:T(8,128)(2,1)}, u32[]{:S(2)}) copy-start(bf16[2,128,512]{2,1,0:T(8,128)(2,1)} %param.18) | copy-start | bytes 786436
  105.3 62.2 %all-gather.7.cloned.1.call-start = ((), (), s32[]{:S(2)}) async-start(), calls=%async_computation.5 | async-start | bytes 1966080 | tf_op jit(solution)/shard_map/all_gather | solution.py:120
  105.9 101.6 %reduce-scatter.17.cloned.1.call-start = ((), (), s32[]{:S(2)}) async-start(), calls=%async_computation.8 | async-start | bytes 1966080
  134.3 16.7 %collective-permute-start.3 = (bf16[32,128]{1,0:T(8,128)(2,1)S(1)}, bf16[32,128]{1,0:T(8,128)(2,1)S(1)}, u32[]{:S(2)}, u32[]{:S(2)}) collective-permute-start(bf16[32,128]{1,0:T(8,128)(2,1)S(1)} %get-tuple-element.21), channel_id=1, source_target_pairs={{4,0},{8,4},{12,8},{0,12},{5,1},{9,5},{13,9},{1,13},{6,2},{10,6},{... | collective-permute-start | bytes 24584 | tf_op jit(solution)/shard_map/ppermute | solution.py:20
  137.9 13.2 %collective-permute-start.2 = (bf16[32,128]{1,0:T(8,128)(2,1)S(1)}, bf16[32,128]{1,0:T(8,128)(2,1)S(1)}, u32[]{:S(2)}, u32[]{:S(2)}) collective-permute-start(bf16[32,128]{1,0:T(8,128)(2,1)S(1)} %get-tuple-element.20), channel_id=1, source_target_pairs={{0,4},{4,8},{8,12},{12,0},{1,5},{5,9},{9,13},{13,1},{2,6},{6,10},{... | collective-permute-start | bytes 24584 | tf_op jit(solution)/shard_map/ppermute | solution.py:19
  157.2 5.4 %copy-start.9 = (s32[2048]{0:T(1024)S(1)}, s32[2048]{0:T(1024)}, u32[]{:S(2)}) copy-start(s32[2048]{0:T(1024)} %copy-done.8) | copy-start | bytes 24580
  178.0 41.2 %copy-start.11 = (f32[1536]{0:T(1024)S(1)}, f32[1536]{0:T(1024)}, u32[]{:S(2)}) copy-start(f32[1536]{0:T(1024)} %copy-done.10) | copy-start | bytes 18436
  178.0 41.2 %copy-start.13 = (f32[1536]{0:T(1024)S(1)}, f32[1536]{0:T(1024)}, u32[]{:S(2)}) copy-start(f32[1536]{0:T(1024)} %copy-done.12) | copy-start | bytes 18436
  178.0 71.2 %reduce-scatter.19.cloned.1.call-start = ((), (), s32[]{:S(2)}) async-start(), calls=%async_computation.9 | async-start | bytes 327680
  208.7 11.8 %copy-start.7 = (s32[1536]{0:T(1024)S(1)}, s32[1536]{0:T(1024)}, u32[]{:S(2)}) copy-start(s32[1536]{0:T(1024)} %param.20) | copy-start | bytes 18436
  220.4 7.5 %copy-start.1 = (f32[1536,128]{1,0:T(8,128)}, f32[1536,128]{1,0:T(8,128)S(1)}, u32[]{:S(2)}) copy-start(f32[1536,128]{1,0:T(8,128)S(1)} %fusion.20) | copy-start | bytes 2359300
  220.5 6.3 %copy-start.23 = (bf16[2,128,512]{2,1,0:T(8,128)(2,1)S(1)}, bf16[2,128,512]{2,1,0:T(8,128)(2,1)}, u32[]{:S(2)}) copy-start(bf16[2,128,512]{2,1,0:T(8,128)(2,1)} %param.18) | copy-start | bytes 786436
  (11 other events, 20.0 us)
Sparse Core Ops, SparseCore 0:
  10.2 22.5 all-gather.4
  55.5 29.5 reduce-scatter.12
  105.4 21.0 reduce-scatter.14
  128.6 19.8 all-gather.6
  178.2 29.2 reduce-scatter.16
  228.1 21.0 reduce-scatter.18
where the time goes:
time: 264 us
  waiting for transfers between devices  99.2 us (38%)
  blocking collectives  81.5 us (31%)
  local copies, waits for them, and re-layouts  35 us (13%)
  matrix products  18.5 us (7%)
  between operations  14.7 us (6%)
  starting transfers between devices  8.93 us (3%)
  other arithmetic  5.88 us (2%)
    unnamed x10, waiting for transfers between devices  99.2 us
    psum x4, blocking collectives, split_norm(): row_sums, squares = lax.psum((row_sums, squares), 'mp')  31.8 us
    all_gather x2, blocking collectives, on_device(): coarse = lax.all_gather(coarse_rows, 'graph', axis=0, tiled=True)  26.3 us
    unnamed x62, local copies, waits for them, and re-layouts  13.3 us
    all_gather x2, blocking collectives, on_device(): lax.all_gather(split_table, 'mp', axis=1, tiled=True)  12.2 us
    all_gather x2, blocking collectives, on_device(): lax.all_gather(incoming.astype(jnp.bfloat16), 'mp', axis=1, tiled=True)  11.3 us
    gather x2, local copies, waits for them, and re-layouts, edge_hidden(): sender_rows = jnp.take(node_table, senders, axis=0)  10.9 us
    gather x2, local copies, waits for them, and re-layouts, edge_hidden(): receiver_rows = jnp.take(node_table, receivers, axis=0)  9.61 us
  transfers between devices with their start and end apart: 10, of which 4 were waited for; matrix products, arithmetic and copies ran while one was open for 9% of the time, Pallas kernels for 0%

commit v1 on v0

v1 whole, which is shorter than its diff:
```python
import functools

import jax
import jax.numpy as jnp
from jax import lax
from jax.experimental import pallas as pl
from jax.experimental.pallas import tpu as pltpu
from jax.sharding import PartitionSpec as P

COARSE_DEV = 12
COARSE_PAD = 16
EPS = 1e-05
TILE = 256
F32 = jnp.float32
BF16 = jnp.bfloat16


def silu(x):
    half = 0.5 * x
    return half + half * jnp.tanh(half)


def normalize(msg):
    width = msg.shape[1]
    mean = jnp.sum(msg, axis=1, keepdims=True) / width
    square = jnp.sum(msg * msg, axis=1, keepdims=True) / width
    return (msg - mean) * lax.rsqrt(square - mean * mean + EPS)


def dot(a, b):
    return jnp.dot(a, b, preferred_element_type=F32)


def fill_weights(spot_ref, pieces, full_ref, second_ref, first_rows):
    own, core, x_near, x_far, d_near, d_far = pieces
    rows, part = own.shape
    half = rows // 2
    near = pl.multiple_of(spot_ref[1] * half, half)
    far = pl.multiple_of((1 - spot_ref[1]) * half, half)
    full_ref[:, 0:part] = own[...]
    full_ref[:, part : 2 * part] = core[...]
    full_ref[pl.ds(near, half), 2 * part : 3 * part] = x_near[...]
    full_ref[pl.ds(far, half), 2 * part : 3 * part] = x_far[...]
    full_ref[pl.ds(near, half), 3 * part : 4 * part] = d_near[...]
    full_ref[pl.ds(far, half), 3 * part : 4 * part] = d_far[...]
    for j in range(4):
        for q in range(4):
            second_ref[j * part : (j + 1) * part, q * part : (q + 1) * part] = full_ref[
                first_rows + q * part : first_rows + (q + 1) * part, j * part : (j + 1) * part
            ]


def fill_features(spot_ref, shards, full_ref):
    part = shards[0].shape[1]
    for j, shard in enumerate(shards):
        column = pl.multiple_of((spot_ref[0] ^ j) * part, part)
        full_ref[:, pl.ds(column, part)] = shard[...]


def pick_rows(wanted_ref, node_bf):
    wanted = wanted_ref[...]
    lanes = lax.broadcasted_iota(jnp.int32, (wanted.shape[0], node_bf.shape[0]), 1)
    return dot(jnp.where(lanes == wanted, 1.0, 0.0).astype(BF16), node_bf).astype(BF16)


def send_rows(wanted_ref, node_bf, outs):
    picked = pick_rows(wanted_ref, node_bf)
    start = 0
    for out in outs:
        out[...] = picked[start : start + out.shape[0]]
        start += out.shape[0]


def start_kernel(spot_ref, own, core, far, diag, wanted_ref, node_ref, right_ref, left_ref, coarse_ref):
    fill_features(spot_ref, (own, core, far, diag), node_ref)
    send_rows(wanted_ref, node_ref[...], (right_ref, left_ref, coarse_ref))


def edge_kernel(pieces, shards, layer_last, *refs):
    refs = list(refs)
    spot_ref = refs.pop(0)
    weights = [refs.pop(0) for _ in range(6)]
    edges = [refs.pop(0) for _ in range(shards)]
    own_ref = refs.pop(0)
    tables = [refs.pop(0) for _ in range(pieces)]
    index_ref, receiver_ref = refs.pop(0), refs.pop(0)
    own_out, incoming_out = refs.pop(0), refs.pop(0)
    full_out = None if layer_last else refs.pop(0)
    w_ref, second_ref, product_ref, table_ref, norm_ref = refs[:5]
    feature_count = second_ref.shape[1]
    node_count = incoming_out.shape[0]
    first_rows = 3 * feature_count
    fill_weights(spot_ref, weights, w_ref, second_ref, first_rows)
    if shards == 1:
        edge_ref = edges[0]
    else:
        edge_ref = refs[5]
        fill_features(spot_ref, edges, edge_ref)
    start = 0
    for table in tables:
        table_ref[start : start + table.shape[0], :] = table[...]
        start += table.shape[0]
    product_ref[0:start, :] = dot(
        table_ref[...], w_ref[feature_count : 2 * feature_count, :]
    ).astype(BF16)
    product_ref[start : start + node_count, :] = dot(
        tables[0][...], w_ref[2 * feature_count : first_rows, :]
    ).astype(BF16)
    used = start + node_count
    lanes_all = product_ref.shape[0]
    if used < lanes_all:
        product_ref[used:, :] = jnp.zeros((lanes_all - used, feature_count), BF16)
    part = own_ref.shape[1]
    column = pl.multiple_of(spot_ref[0] * part, part)
    incoming = jnp.zeros((node_count, feature_count), F32)
    for at in range(0, edge_ref.shape[0], TILE):
        rows = slice(at, at + TILE)
        edge_bf = edge_ref[rows, :]
        index = index_ref[rows, :]
        lanes = lax.broadcasted_iota(jnp.int32, (TILE, lanes_all), 1)
        hot = (lanes == index[:, 0:1]) | (lanes == index[:, 1:2])
        pre = dot(edge_bf, w_ref[0:feature_count, :]) + dot(
            jnp.where(hot, 1.0, 0.0).astype(BF16), product_ref[...]
        )
        norm = normalize(dot(silu(pre).astype(BF16), second_ref[...]))
        norm_ref[rows, :] = norm
        edge_new = (edge_bf.astype(F32) + norm).astype(BF16)
        if full_out is not None:
            full_out[rows, :] = edge_new
        own_out[rows, :] = own_ref[rows, :] + norm_ref[rows, pl.ds(column, part)]
        nodes = lax.broadcasted_iota(jnp.int32, (node_count, TILE), 0)
        incidence = jnp.where(nodes == receiver_ref[:, rows], 1.0, 0.0).astype(BF16)
        incoming = incoming + dot(incidence, edge_new)
    incoming_out[...] = incoming.astype(BF16)


def node_kernel(layer_last, *refs):
    refs = list(refs)
    spot_ref = refs.pop(0)
    weights = [refs.pop(0) for _ in range(6)]
    node_ref, own_ref, incoming_ref = refs.pop(0), refs.pop(0), refs.pop(0)
    wanted_ref = None if layer_last else refs.pop(0)
    own_out = refs.pop(0)
    outs = [] if layer_last else [refs.pop(0) for _ in range(4)]
    w_ref, second_ref, norm_ref = refs
    feature_count = second_ref.shape[1]
    first_rows = 2 * feature_count
    fill_weights(spot_ref, weights, w_ref, second_ref, first_rows)
    node_bf = node_ref[...]
    pre = dot(node_bf, w_ref[0:feature_count, :]) + dot(
        incoming_ref[...], w_ref[feature_count:first_rows, :]
    )
    norm = normalize(dot(silu(pre).astype(BF16), second_ref[...]))
    norm_ref[...] = norm
    part = own_ref.shape[1]
    column = pl.multiple_of(spot_ref[0] * part, part)
    own_out[...] = own_ref[...] + norm_ref[:, pl.ds(column, part)]
    if not layer_last:
        node_new = (node_bf.astype(F32) + norm).astype(BF16)
        outs[0][...] = node_new
        send_rows(wanted_ref, node_new, outs[1:])


def call(kernel, out_shape, args, scratch, flops, name):
    in_specs = [pl.BlockSpec(memory_space=pltpu.SMEM)]
    in_specs += [pl.BlockSpec(memory_space=pltpu.VMEM)] * (len(args) - 1)
    moved = sum(a.size * a.dtype.itemsize for a in list(args) + list(out_shape))
    return pl.pallas_call(
        kernel,
        out_shape=out_shape,
        in_specs=in_specs,
        out_specs=[pl.BlockSpec(memory_space=pltpu.VMEM)] * len(out_shape),
        scratch_shapes=scratch,
        compiler_params=pltpu.CompilerParams(vmem_limit_bytes=48 * 1024 * 1024),
        cost_estimate=pl.CostEstimate(flops=flops, bytes_accessed=moved, transcendentals=0),
        name=name,
    )(*args)


def swap(x, mask):
    size = lax.axis_size("mp")
    return lax.ppermute(x, "mp", [(i, i ^ mask) for i in range(size)])


def pack(first, second):
    part = first.shape[1]
    blocks = [second[:, q : q + part] for q in range(0, second.shape[1], part)]
    return jnp.concatenate([first] + blocks, axis=0)


def gather_weights(packed):
    half = packed.shape[0] // 2
    near = lax.dynamic_slice_in_dim(packed, lax.axis_index("groups") * half, half, axis=0)
    x_near = swap(near, 2)
    x_far = lax.ppermute(x_near, "groups", [(0, 1), (1, 0)])
    return (packed, swap(packed, 1), x_near, x_far, swap(x_near, 1), swap(x_far, 1))


def shift(x, by):
    size = lax.axis_size("graph")
    return lax.ppermute(x, "graph", [(i, (i + by) % size) for i in range(size)])


def neighbour_rows(right, left, coarse, halo):
    if lax.axis_size("graph") == 4:
        return [shift(right, 1), shift(left, -1), shift(coarse, 2)]
    everyone = lax.all_gather(coarse, "graph", axis=0, tiled=True)
    return [shift(right[:halo], 1), shift(left[:halo], -1), everyone]


def table_index(senders, node_count, halo):
    size = lax.axis_size("graph")
    coarse_start = node_count + 2 * halo
    number = jnp.maximum(senders - coarse_start, 0)
    block, row = number // COARSE_DEV, number % COARSE_DEV
    if size != 4:
        return jnp.where(senders < coarse_start, senders, coarse_start + block * COARSE_PAD + row)
    wide = halo + COARSE_PAD
    away = (block - lax.axis_index("graph")) % size
    starts = (node_count - COARSE_DEV, node_count + wide + halo, node_count + 2 * wide, node_count + halo)
    base = jnp.where(
        away < 2,
        jnp.where(away == 0, starts[0], starts[1]),
        jnp.where(away == 2, starts[2], starts[3]),
    )
    fine = jnp.where(senders < node_count + halo, senders, senders + COARSE_PAD)
    return jnp.where(senders < coarse_start, fine, base + row)


def on_device(
    node_state,
    edge_state,
    edge_first,
    edge_second,
    node_first,
    node_second,
    senders,
    receivers,
    boundary_rows,
):
    node_count, part = node_state.shape
    edge_count = edge_state.shape[0]
    layer_count = edge_first.shape[0]
    feature_count = edge_second.shape[2]
    halo = boundary_rows.shape[0] // 2
    shape = jax.ShapeDtypeStruct
    spot = jnp.stack([lax.axis_index("mp"), lax.axis_index("groups")]).astype(jnp.int32)

    node_bf = node_state.astype(BF16)
    node_shards = (node_bf, swap(node_bf, 1), swap(node_bf, 2), swap(node_bf, 3))
    edge_bf = edge_state.astype(BF16)
    edge_far = swap(edge_bf, 2)
    edges = (edge_bf, swap(edge_bf, 1), edge_far, swap(edge_far, 1))

    own_coarse = jnp.arange(node_count - COARSE_DEV, node_count, dtype=jnp.int32)
    padding = jnp.full((COARSE_PAD - COARSE_DEV,), -1, jnp.int32)
    coarse_list = jnp.concatenate([own_coarse, padding])
    wanted = jnp.concatenate(
        [boundary_rows[halo:], coarse_list, boundary_rows[:halo], coarse_list, coarse_list]
    )[:, None]
    sent = [
        shape((halo + COARSE_PAD, feature_count), BF16),
        shape((halo + COARSE_PAD, feature_count), BF16),
        shape((COARSE_PAD, feature_count), BF16),
    ]
    full_node = shape((node_count, feature_count), BF16)
    picking = 2 * wanted.shape[0] * node_count * feature_count
    node_full, right, left, coarse = call(
        start_kernel, [full_node] + sent, [spot, *node_shards, wanted], [], picking, "boundary_rows"
    )

    edge_weights = [
        gather_weights(pack(edge_first[layer], edge_second[layer])) for layer in range(layer_count)
    ]
    node_weights = [
        gather_weights(pack(node_first[layer], node_second[layer])) for layer in range(layer_count)
    ]

    node_own, edge_own = node_state, edge_state
    receiver_row = receivers[None, :]
    for layer in range(layer_count):
        last = layer == layer_count - 1
        tables = [node_full] + neighbour_rows(right, left, coarse, halo)
        table_rows = sum(t.shape[0] for t in tables)
        lanes = -(-(table_rows + node_count) // 128) * 128
        index = jnp.stack(
            [table_index(senders, node_count, halo), receivers + table_rows], axis=1
        )
        outs = [shape((edge_count, part), F32), shape((node_count, feature_count), BF16)]
        if not last:
            outs.append(shape((edge_count, feature_count), BF16))
        scratch = [
            pltpu.VMEM((4 * feature_count, feature_count), BF16),
            pltpu.VMEM((feature_count, feature_count), BF16),
            pltpu.VMEM((lanes, feature_count), BF16),
            pltpu.VMEM((table_rows, feature_count), BF16),
            pltpu.VMEM((edge_count, feature_count), F32),
        ]
        if len(edges) > 1:
            scratch.append(pltpu.VMEM((edge_count, feature_count), BF16))
        done = call(
            functools.partial(edge_kernel, len(tables), len(edges), last),
            outs,
            [spot, *edge_weights[layer], *edges, edge_own, *tables, index, receiver_row],
            scratch,
            2 * edge_count * feature_count * (2 * feature_count + lanes + node_count),
            "edge_layer",
        )
        edge_own, incoming = done[0], done[1]
        edges = done[2:]
        outs = [shape((node_count, part), F32)]
        args = [spot, *node_weights[layer], node_full, node_own, incoming]
        if not last:
            outs += [full_node] + sent
            args.append(wanted)
        done = call(
            functools.partial(node_kernel, last),
            outs,
            args,
            [
                pltpu.VMEM((3 * feature_count, feature_count), BF16),
                pltpu.VMEM((feature_count, feature_count), BF16),
                pltpu.VMEM((node_count, feature_count), F32),
            ],
            2 * node_count * feature_count * 3 * feature_count,
            "node_layer",
        )
        node_own = done[0]
        if not last:
            node_full, right, left, coarse = done[1:]
    return (node_own, edge_own)


def solution(mesh):
    in_specs = (
        P(("groups", "graph"), "mp"),
        P(("groups", "graph"), "mp"),
        P(None, None, "mp"),
        P(None, "mp", None),
        P(None, None, "mp"),
        P(None, "mp", None),
        P("graph"),
        P("graph"),
        P("graph"),
    )
    out_specs = (P(("groups", "graph"), "mp"), P(("groups", "graph"), "mp"))
    return jax.shard_map(
        on_device, mesh=mesh, in_specs=in_specs, out_specs=out_specs, check_vma=False
    )
```

time: 264 us -> 91.8 us (0.35)
  blocking collectives: 81.5 us -> 0 us
  waiting for transfers between devices: 99.2 us -> 28.8 us
  local copies, waits for them, and re-layouts: 35 us -> 11.3 us
  Pallas kernels: 0 us -> 22.2 us
  matrix products: 18.5 us -> 0 us
  starting transfers between devices: 8.93 us -> 25 us
  between operations: 14.7 us -> 1.03 us
  other arithmetic: 5.88 us -> 2.95 us
    unnamed x10 -> x0, waiting for transfers between devices: 99.2 us -> none
    all_gather x6 -> x0, blocking collectives: 49.7 us -> none  [the longest x2 26.3 us: on_device(): coarse = lax.all_gather(coarse_rows, 'graph', axis=0, tiled=True)]
    psum x4 -> x0, blocking collectives: 31.8 us -> none  [split_norm(): row_sums, squares = lax.psum((row_sums, squares), 'mp')]
    ppermute x4 -> x32, waiting for transfers between devices: 0.01 us -> 28.8 us  [the longest x22 13.2 us: swap(): return lax.ppermute(x, 'mp', [(i, i ^ mask) for i in range(size)])]
    pallas_call x0 -> x5, Pallas kernels: none -> 22.2 us  [call(): pl.pallas_call(kernel, out_shape=out_shape, in_specs=in_specs, out_specs=...]
    gather x6 -> x0, local copies, waits for them, and re-layouts: 21.7 us -> none  [the longest x2 10.9 us: edge_hidden(): sender_rows = jnp.take(node_table, senders, axis=0)]
    dot_general x14 -> x0, matrix products: 18.5 us -> none  [the longest x2 6.75 us: on_device(): jnp.dot(hidden, edge_second[layer_index], preferred_element_type=jnp.floa...]
    ppermute x4 -> x32, starting transfers between devices: 8.69 us -> 25 us  [the longest x22 10.8 us: swap(): return lax.ppermute(x, 'mp', [(i, i ^ mask) for i in range(size)])]
  transfers between devices with their start and end apart: 10 -> 32, of which waited for: 4 -> 7; matrix products, arithmetic and copies ran while one was open for 9% -> 7% of each run, Pallas kernels for 0% -> 22%
where the time goes in v1:
time: 91.8 us; the launch traced here: 91.3 us
  waiting for transfers between devices  28.8 us (31%)
  starting transfers between devices  25 us (27%)
  Pallas kernels  22.2 us (24%)
  local copies, waits for them, and re-layouts  11.3 us (12%)
  other arithmetic  2.95 us (3%)
  between operations  1.03 us (1%)
    pallas_call x5, Pallas kernels, call(): pl.pallas_call(kernel, out_shape=out_shape, in_specs=in_specs, out_specs=...  22.2 us
    ppermute x22, waiting for transfers between devices, swap(): return lax.ppermute(x, 'mp', [(i, i ^ mask) for i in range(size)])  13.2 us
    ppermute x22, starting transfers between devices, swap(): return lax.ppermute(x, 'mp', [(i, i ^ mask) for i in range(size)])  10.8 us
    ppermute x6, starting transfers between devices, shift(): return lax.ppermute(x, 'graph', [(i, (i + by) % size) for i in range(size)])  8.77 us
    ppermute x6, waiting for transfers between devices, shift(): return lax.ppermute(x, 'graph', [(i, (i + by) % size) for i in range(size)])  8.22 us
    ppermute x4, waiting for transfers between devices, gather_weights(): x_far = lax.ppermute(x_near, 'groups', [(0, 1), (1, 0)])  7.37 us
    unnamed x60, local copies, waits for them, and re-layouts  7.28 us
    ppermute x4, starting transfers between devices, gather_weights(): x_far = lax.ppermute(x_near, 'groups', [(0, 1), (1, 0)])  5.45 us
  transfers between devices with their start and end apart: 32, of which 7 were waited for; matrix products, arithmetic and copies ran while one was open for 7% of the time, Pallas kernels for 22%

profile of v1, /device:TPU:0, one launch (start us, length us, event | category | flops | bytes accessed | tf_op | source)
XLA Modules:
  0.0 91.3 jit_solution(320201060798866591)
XLA Ops:
  2.1 2.6 %collective-permute-start.11 = (bf16[192,128]{1,0:T(8,128)(2,1)S(1)}, bf16[192,128]{1,0:T(8,128)(2,1)S(1)}, u32[]{:S(2)}, u32[]{:S(2)}) collective-permute-start(bf16[192,128]{1,0:T(8,128)(2,1)S(1)} %convert_element_type.6.own), channel_id=1, source_target_pairs={{0,2},{1,3},{2,0},{3,1},{4,6},{5,7},{6,4},{7,5},{8,10},{9,11},{10,... | collective-permute-start | bytes 147464 | tf_op jit(solution)/shard_map/ppermute | solution.py:182
  4.7 1.2 %convert_element_type.7.refs_7_ = bf16[1536,128]{1,0:T(8,128)(2,1)S(1)} convert(f32[1536,128]{1,0:T(8,128)} %refs_11_.1) | non-fusion elementwise | flops 196608 | bytes 1179648 | tf_op jit(solution)/shard_map/convert_element_type | solution.py:251
  5.9 1.8 %collective-permute-start.19 = (bf16[1536,128]{1,0:T(8,128)(2,1)S(1)}, bf16[1536,128]{1,0:T(8,128)(2,1)}, u32[]{:S(2)}, u32[]{:S(2)}) collective-permute-start(bf16[1536,128]{1,0:T(8,128)(2,1)S(1)} %convert_element_type.7.refs_7_), channel_id=1, source_target_pairs={{0,2},{1,3},{2,0},{3,1},{4,6},{5,7},{6,4},{7,5},{8,10},{9,11},{10,... | collective-permute-start | bytes 1179656 | tf_op jit(solution)/shard_map/ppermute | solution.py:182
  12.1 1.9 %collective-permute-start.21 = (bf16[48,512]{1,0:T(8,128)(2,1)S(1)}, bf16[48,512]{1,0:T(8,128)(2,1)S(1)}, u32[]{:S(2)}, u32[]{:S(2)}) collective-permute-start(bf16[48,512]{1,0:T(8,128)(2,1)S(1)} %get-tuple-element.17), channel_id=1, source_target_pairs={{0,4},{4,8},{8,12},{12,0},{1,5},{5,9},{9,13},{13,1},{2,6},{6,10},{... | collective-permute-start | bytes 147464 | tf_op jit(solution)/shard_map/ppermute | solution.py:201
  14.0 2.1 %collective-permute-start.22 = (bf16[48,512]{1,0:T(8,128)(2,1)S(1)}, bf16[48,512]{1,0:T(8,128)(2,1)S(1)}, u32[]{:S(2)}, u32[]{:S(2)}) collective-permute-start(bf16[48,512]{1,0:T(8,128)(2,1)S(1)} %get-tuple-element.18), channel_id=1, source_target_pairs={{0,12},{4,0},{8,4},{12,8},{1,13},{5,1},{9,5},{13,9},{2,14},{6,2},{... | collective-permute-start | bytes 147464 | tf_op jit(solution)/shard_map/ppermute | solution.py:201
  17.0 3.7 %collective-permute-done.23.refs_15_ = bf16[16,512]{1,0:T(8,128)(2,1)S(1)} collective-permute-done((bf16[16,512]{1,0:T(8,128)(2,1)S(1)}, bf16[16,512]{1,0:T(8,128)(2,1)S(1)}, u32[]{:S(2)}, u32[]{:S(2)}) %collective-permute-start.23) | collective-permute-done | bytes 16416 | tf_op jit(solution)/shard_map/ppermute | solution.py:201
  20.7 1.7 %collective-permute-start.14 = (bf16[1024,128]{1,0:T(8,128)(2,1)}, bf16[1024,128]{1,0:T(8,128)(2,1)}, u32[]{:S(2)}, u32[]{:S(2)}) collective-permute-start(bf16[1024,128]{1,0:T(8,128)(2,1)} %constant_dynamic-slice_fusion.1), channel_id=1, source_target_pairs={{0,2},{1,3},{2,0},{3,1},{4,6},{5,7},{6,4},{7,5},{8,10},{9,11},{10,... | collective-permute-start | bytes 786440 | tf_op jit(solution)/shard_map/ppermute | solution.py:182
  23.4 1.7 %collective-permute-start.25 = (bf16[1024,128]{1,0:T(8,128)(2,1)S(1)}, bf16[1024,128]{1,0:T(8,128)(2,1)S(1)}, u32[]{:S(2)}, u32[]{:S(2)}) collective-permute-start(bf16[1024,128]{1,0:T(8,128)(2,1)S(1)} %constant_dynamic-slice_fusion), channel_id=1, source_target_pairs={{0,2},{1,3},{2,0},{3,1},{4,6},{5,7},{6,4},{7,5},{8,10},{9,11},{10,... | collective-permute-start | bytes 786440 | tf_op jit(solution)/shard_map/ppermute | solution.py:182
  25.2 9.1 %collective-permute-done.1.refs_3_ = bf16[768,128]{1,0:T(8,128)(2,1)S(1)} collective-permute-done((bf16[768,128]{1,0:T(8,128)(2,1)S(1)}, bf16[768,128]{1,0:T(8,128)(2,1)S(1)}, u32[]{:S(2)}, u32[]{:S(2)}) %collective-permute-start.1) | collective-permute-done | bytes 196640 | tf_op jit(solution)/shard_map/ppermute | solution.py:182
  34.3 1.7 %collective-permute-start.7 = (bf16[768,128]{1,0:T(8,128)(2,1)}, bf16[768,128]{1,0:T(8,128)(2,1)S(1)}, u32[]{:S(2)}, u32[]{:S(2)}) collective-permute-start(bf16[768,128]{1,0:T(8,128)(2,1)} %collective-permute-done.6.refs_3_), channel_id=1, source_target_pairs={{0,16},{16,0},{1,17},{17,1},{2,18},{18,2},{3,19},{19,3},{4,20},{20... | collective-permute-start | bytes 589832 | tf_op jit(solution)/shard_map/ppermute | solution.py:195
  36.0 3.5 %collective-permute-done.25.refs_3_ = bf16[1024,128]{1,0:T(8,128)(2,1)S(1)} collective-permute-done((bf16[1024,128]{1,0:T(8,128)(2,1)S(1)}, bf16[1024,128]{1,0:T(8,128)(2,1)S(1)}, u32[]{:S(2)}, u32[]{:S(2)}) %collective-permute-start.25) | collective-permute-done | bytes 262176 | tf_op jit(solution)/shard_map/ppermute | solution.py:182
  39.5 1.7 %collective-permute-start.15 = (bf16[1024,128]{1,0:T(8,128)(2,1)}, bf16[1024,128]{1,0:T(8,128)(2,1)}, u32[]{:S(2)}, u32[]{:S(2)}) collective-permute-start(bf16[1024,128]{1,0:T(8,128)(2,1)} %collective-permute-done.14.refs_3_), channel_id=1, source_target_pairs={{0,16},{16,0},{1,17},{17,1},{2,18},{18,2},{3,19},{19,3},{4,20},{20... | collective-permute-start | bytes 786440 | tf_op jit(solution)/shard_map/ppermute | solution.py:195
  44.1 4.9 %collective-permute-done.15.refs_4_ = bf16[1024,128]{1,0:T(8,128)(2,1)} collective-permute-done((bf16[1024,128]{1,0:T(8,128)(2,1)}, bf16[1024,128]{1,0:T(8,128)(2,1)}, u32[]{:S(2)}, u32[]{:S(2)}) %collective-permute-start.15) | collective-permute-done | bytes 262176 | tf_op jit(solution)/shard_map/ppermute | solution.py:195
  50.4 1.2 %copy.18.refs_16_.refs_13_ = s32[1536,2]{1,0:T(8,128)} copy(s32[1536,2]{0,1:T(2,128)S(1)} %pad_add_fusion) | data formatting | bytes 24576 | tf_op jit(solution)/shard_map/stack | solution.py:286
  51.6 2.5 %collective-permute-done.26.refs_4_ = bf16[1024,128]{1,0:T(8,128)(2,1)} collective-permute-done((bf16[1024,128]{1,0:T(8,128)(2,1)}, bf16[1024,128]{1,0:T(8,128)(2,1)}, u32[]{:S(2)}, u32[]{:S(2)}) %collective-permute-start.26) | collective-permute-done | bytes 262176 | tf_op jit(solution)/shard_map/ppermute | solution.py:195
  54.1 1.7 %collective-permute-start.2 = (bf16[768,128]{1,0:T(8,128)(2,1)}, bf16[768,128]{1,0:T(8,128)(2,1)S(1)}, u32[]{:S(2)}, u32[]{:S(2)}) collective-permute-start(bf16[768,128]{1,0:T(8,128)(2,1)} %copy-done.3), channel_id=1, source_target_pairs={{0,16},{16,0},{1,17},{17,1},{2,18},{18,2},{3,19},{19,3},{4,20},{20... | collective-permute-start | bytes 589832 | tf_op jit(solution)/shard_map/ppermute | solution.py:195
  57.3 1.0 %copy-done.10 = bf16[1536,128]{1,0:T(8,128)(2,1)S(1)} copy-done((bf16[1536,128]{1,0:T(8,128)(2,1)S(1)}, bf16[1536,128]{1,0:T(8,128)(2,1)}, u32[]{:S(2)}) %copy-start.10) | copy-done | bytes 393240
  59.9 9.1 %edge_layer.2 = (f32[1536,128]{1,0:T(8,128)S(1)}, bf16[192,512]{1,0:T(8,128)(2,1)S(1)}, bf16[1536,512]{1,0:T(8,128)(2,1)}) custom-call(s32[2]{0:T(128)S(1)} %pad_add_fusion.1.spot_ref.refs_0_, bf16[2048,128]{1,0:T(8,128)(2,1)S(1)} %constant_dynamic-update-slice_fusion.8.refs_1_, bf16[2048,128]{1,0:T(8,128)(2,1)} %collective-permute-done.13.refs_2_, ...), custom_call_target="tpu_custom_call" | custom-call | flops 2717908992 | bytes 7342088 | tf_op jit(solution)/shard_map/edge_layer/pallas_call | solution.py:168
  69.0 2.4 %node_layer.2 = (f32[192,128]{1,0:T(8,128)S(1)}, bf16[192,512]{1,0:T(8,128)(2,1)S(1)}, bf16[48,512]{1,0:T(8,128)(2,1)S(1)}, bf16[48,512]{1,0:T(8,128)(2,1)S(1)}, bf16[16,512]{1,0:T(8,128)(2,1)S(1)}) custom-call(s32[2]{0:T(128)S(1)} %pad_add_fusion.1.spot_ref.refs_0_, bf16[1536,128]{1,0:T(8,128)(2,1)S(1)} %constant_dynamic-update-slice_fusion.4.refs_1_, ...), custom_call_target="tpu_custom_call" | custom-call | flops 301989888 | bytes 2474440 | tf_op jit(solution)/shard_map/node_layer/pallas_call | solution.py:168
  71.5 3.8 %collective-permute-start.30 = (bf16[48,512]{1,0:T(8,128)(2,1)S(1)}, bf16[48,512]{1,0:T(8,128)(2,1)S(1)}, u32[]{:S(2)}, u32[]{:S(2)}) collective-permute-start(bf16[48,512]{1,0:T(8,128)(2,1)S(1)} %get-tuple-element.26), channel_id=1, source_target_pairs={{0,12},{4,0},{8,4},{12,8},{1,13},{5,1},{9,5},{13,9},{2,14},{6,2},{... | collective-permute-start | bytes 147464 | tf_op jit(solution)/shard_map/ppermute | solution.py:201
  75.4 4.5 %collective-permute-done.31.refs_12_ = bf16[16,512]{1,0:T(8,128)(2,1)S(1)} collective-permute-done((bf16[16,512]{1,0:T(8,128)(2,1)S(1)}, bf16[16,512]{1,0:T(8,128)(2,1)S(1)}, u32[]{:S(2)}, u32[]{:S(2)}) %collective-permute-start.31) | collective-permute-done | bytes 16416 | tf_op jit(solution)/shard_map/ppermute | solution.py:201
  80.0 1.4 %copy-done.17 = bf16[1536,512]{1,0:T(8,128)(2,1)S(1)} copy-done((bf16[1536,512]{1,0:T(8,128)(2,1)S(1)}, bf16[1536,512]{1,0:T(8,128)(2,1)}, u32[]{:S(2)}) %copy-start.17) | copy-done | bytes 1572888
  81.4 7.7 %edge_layer.3 = (f32[1536,128]{1,0:T(8,128)}, bf16[192,512]{1,0:T(8,128)(2,1)S(1)}) custom-call(s32[2]{0:T(128)S(1)} %pad_add_fusion.1.spot_ref.refs_0_, bf16[2048,128]{1,0:T(8,128)(2,1)S(1)} %constant_dynamic-update-slice_fusion.12.refs_1_, bf16[2048,128]{1,0:T(8,128)(2,1)} %collective-permute-done.24.refs_2_, bf16[1024,128]{1,0:T(8,128)(2,1)S(1)} %copy-done.12, ...), custom_call_target="tpu_custom_call" | custom-call | flops 2717908992 | bytes 5769224 | tf_op jit(solution)/shard_map/edge_layer/pallas_call | solution.py:168
  89.1 2.2 %node_layer.3 = f32[192,128]{1,0:T(8,128)} custom-call(s32[2]{0:T(128)S(1)} %pad_add_fusion.1.spot_ref.refs_0_, bf16[1536,128]{1,0:T(8,128)(2,1)S(1)} %constant_dynamic-update-slice_fusion.refs_1_, bf16[1536,128]{1,0:T(8,128)(2,1)S(1)} %collective-permute-done.refs_2_, bf16[768,128]{1,0:T(8,128)(2,1)S(1)} %copy-done.4, ...), custom_call_target="tpu_custom_call" | custom-call | flops 301989888 | bytes 2162696 | tf_op jit(solution)/shard_map/node_layer/pallas_call | solution.py:168
  (130 shorter events, 15.3 us)
Async XLA Ops:
  1.6 9.7 %collective-permute-start.10 = (bf16[192,128]{1,0:T(8,128)(2,1)S(1)}, bf16[192,128]{1,0:T(8,128)(2,1)S(1)}, u32[]{:S(2)}, u32[]{:S(2)}) collective-permute-start(bf16[192,128]{1,0:T(8,128)(2,1)S(1)} %convert_element_type.6.own), channel_id=1, source_target_pairs={{0,1},{1,0},{2,3},{3,2},{4,5},{5,4},{6,7},{7,6},{8,9},{9,8},{10,11... | collective-permute-start | bytes 147464 | tf_op jit(solution)/shard_map/ppermute | solution.py:182
  2.1 9.2 %collective-permute-start.11 = (bf16[192,128]{1,0:T(8,128)(2,1)S(1)}, bf16[192,128]{1,0:T(8,128)(2,1)S(1)}, u32[]{:S(2)}, u32[]{:S(2)}) collective-permute-start(bf16[192,128]{1,0:T(8,128)(2,1)S(1)} %convert_element_type.6.own), channel_id=1, source_target_pairs={{0,2},{1,3},{2,0},{3,1},{4,6},{5,7},{6,4},{7,5},{8,10},{9,11},{10,... | collective-permute-start | bytes 147464 | tf_op jit(solution)/shard_map/ppermute | solution.py:182
  5.9 33.5 %collective-permute-start.19 = (bf16[1536,128]{1,0:T(8,128)(2,1)S(1)}, bf16[1536,128]{1,0:T(8,128)(2,1)}, u32[]{:S(2)}, u32[]{:S(2)}) collective-permute-start(bf16[1536,128]{1,0:T(8,128)(2,1)S(1)} %convert_element_type.7.refs_7_), channel_id=1, source_target_pairs={{0,2},{1,3},{2,0},{3,1},{4,6},{5,7},{6,4},{7,5},{8,10},{9,11},{10,... | collective-permute-start | bytes 1179656 | tf_op jit(solution)/shard_map/ppermute | solution.py:182
  9.6 13.9 %collective-permute-start.6 = (bf16[768,128]{1,0:T(8,128)(2,1)}, bf16[768,128]{1,0:T(8,128)(2,1)}, u32[]{:S(2)}, u32[]{:S(2)}) collective-permute-start(bf16[768,128]{1,0:T(8,128)(2,1)} %constant_dynamic-slice_fusion.2), channel_id=1, source_target_pairs={{0,2},{1,3},{2,0},{3,1},{4,6},{5,7},{6,4},{7,5},{8,10},{9,11},{10,... | collective-permute-start | bytes 589832 | tf_op jit(solution)/shard_map/ppermute | solution.py:182
  12.1 8.6 %collective-permute-start.21 = (bf16[48,512]{1,0:T(8,128)(2,1)S(1)}, bf16[48,512]{1,0:T(8,128)(2,1)S(1)}, u32[]{:S(2)}, u32[]{:S(2)}) collective-permute-start(bf16[48,512]{1,0:T(8,128)(2,1)S(1)} %get-tuple-element.17), channel_id=1, source_target_pairs={{0,4},{4,8},{8,12},{12,0},{1,5},{5,9},{9,13},{13,1},{2,6},{6,10},{... | collective-permute-start | bytes 147464 | tf_op jit(solution)/shard_map/ppermute | solution.py:201
  14.0 8.5 %collective-permute-start.22 = (bf16[48,512]{1,0:T(8,128)(2,1)S(1)}, bf16[48,512]{1,0:T(8,128)(2,1)S(1)}, u32[]{:S(2)}, u32[]{:S(2)}) collective-permute-start(bf16[48,512]{1,0:T(8,128)(2,1)S(1)} %get-tuple-element.18), channel_id=1, source_target_pairs={{0,12},{4,0},{8,4},{12,8},{1,13},{5,1},{9,5},{13,9},{2,14},{6,2},{... | collective-permute-start | bytes 147464 | tf_op jit(solution)/shard_map/ppermute | solution.py:201
  20.7 20.5 %collective-permute-start.18 = (bf16[1536,128]{1,0:T(8,128)(2,1)S(1)}, bf16[1536,128]{1,0:T(8,128)(2,1)S(1)}, u32[]{:S(2)}, u32[]{:S(2)}) collective-permute-start(bf16[1536,128]{1,0:T(8,128)(2,1)S(1)} %convert_element_type.7.refs_7_), channel_id=1, source_target_pairs={{0,1},{1,0},{2,3},{3,2},{4,5},{5,4},{6,7},{7,6},{8,9},{9,8},{10,11... | collective-permute-start | bytes 1179656 | tf_op jit(solution)/shard_map/ppermute | solution.py:182
  20.7 15.3 %collective-permute-start.14 = (bf16[1024,128]{1,0:T(8,128)(2,1)}, bf16[1024,128]{1,0:T(8,128)(2,1)}, u32[]{:S(2)}, u32[]{:S(2)}) collective-permute-start(bf16[1024,128]{1,0:T(8,128)(2,1)} %constant_dynamic-slice_fusion.1), channel_id=1, source_target_pairs={{0,2},{1,3},{2,0},{3,1},{4,6},{5,7},{6,4},{7,5},{8,10},{9,11},{10,... | collective-permute-start | bytes 786440 | tf_op jit(solution)/shard_map/ppermute | solution.py:182
  23.0 11.3 %collective-permute-start.1 = (bf16[768,128]{1,0:T(8,128)(2,1)S(1)}, bf16[768,128]{1,0:T(8,128)(2,1)S(1)}, u32[]{:S(2)}, u32[]{:S(2)}) collective-permute-start(bf16[768,128]{1,0:T(8,128)(2,1)S(1)} %constant_dynamic-slice_fusion.3), channel_id=1, source_target_pairs={{0,2},{1,3},{2,0},{3,1},{4,6},{5,7},{6,4},{7,5},{8,10},{9,11},{10,... | collective-permute-start | bytes 589832 | tf_op jit(solution)/shard_map/ppermute | solution.py:182
  23.4 16.0 %collective-permute-start.25 = (bf16[1024,128]{1,0:T(8,128)(2,1)S(1)}, bf16[1024,128]{1,0:T(8,128)(2,1)S(1)}, u32[]{:S(2)}, u32[]{:S(2)}) collective-permute-start(bf16[1024,128]{1,0:T(8,128)(2,1)S(1)} %constant_dynamic-slice_fusion), channel_id=1, source_target_pairs={{0,2},{1,3},{2,0},{3,1},{4,6},{5,7},{6,4},{7,5},{8,10},{9,11},{10,... | collective-permute-start | bytes 786440 | tf_op jit(solution)/shard_map/ppermute | solution.py:182
  36.0 8.1 %collective-permute-start.5 = (bf16[1536,128]{1,0:T(8,128)(2,1)S(1)}, bf16[1536,128]{1,0:T(8,128)(2,1)S(1)}, u32[]{:S(2)}, u32[]{:S(2)}) collective-permute-start(bf16[1536,128]{1,0:T(8,128)(2,1)S(1)} %constant_dynamic-update-slice_fusion.4.refs_1_), channel_id=1, source_target_pairs={{0,1},{1,0},{2,3},{3,2},{4,5},{5,4},{6,7},{7,6},{8,9},{9,8},{10,11... | collective-permute-start | bytes 1179656 | tf_op jit(solution)/shard_map/ppermute | solution.py:182
  39.5 10.9 %collective-permute-start.13 = (bf16[2048,128]{1,0:T(8,128)(2,1)S(1)}, bf16[2048,128]{1,0:T(8,128)(2,1)}, u32[]{:S(2)}, u32[]{:S(2)}) collective-permute-start(bf16[2048,128]{1,0:T(8,128)(2,1)S(1)} %constant_dynamic-update-slice_fusion.8.refs_1_), channel_id=1, source_target_pairs={{0,1},{1,0},{2,3},{3,2},{4,5},{5,4},{6,7},{7,6},{8,9},{9,8},{10,11... | collective-permute-start | bytes 1572872 | tf_op jit(solution)/shard_map/ppermute | solution.py:182
  39.5 9.5 %collective-permute-start.15 = (bf16[1024,128]{1,0:T(8,128)(2,1)}, bf16[1024,128]{1,0:T(8,128)(2,1)}, u32[]{:S(2)}, u32[]{:S(2)}) collective-permute-start(bf16[1024,128]{1,0:T(8,128)(2,1)} %collective-permute-done.14.refs_3_), channel_id=1, source_target_pairs={{0,16},{16,0},{1,17},{17,1},{2,18},{18,2},{3,19},{19,3},{4,20},{20... | collective-permute-start | bytes 786440 | tf_op jit(solution)/shard_map/ppermute | solution.py:195
  43.8 10.4 %collective-permute-start.26 = (bf16[1024,128]{1,0:T(8,128)(2,1)}, bf16[1024,128]{1,0:T(8,128)(2,1)}, u32[]{:S(2)}, u32[]{:S(2)}) collective-permute-start(bf16[1024,128]{1,0:T(8,128)(2,1)} %copy-done.11), channel_id=1, source_target_pairs={{0,16},{16,0},{1,17},{17,1},{2,18},{18,2},{3,19},{19,3},{4,20},{20... | collective-permute-start | bytes 786440 | tf_op jit(solution)/shard_map/ppermute | solution.py:195
  44.1 11.9 %collective-permute-start.20 = (bf16[1536,128]{1,0:T(8,128)(2,1)}, bf16[1536,128]{1,0:T(8,128)(2,1)}, u32[]{:S(2)}, u32[]{:S(2)}) collective-permute-start(bf16[1536,128]{1,0:T(8,128)(2,1)} %collective-permute-done.19.refs_9_), channel_id=1, source_target_pairs={{0,1},{1,0},{2,3},{3,2},{4,5},{5,4},{6,7},{7,6},{8,9},{9,8},{10,11... | collective-permute-start | bytes 1179656 | tf_op jit(solution)/shard_map/ppermute | solution.py:182
  49.7 25.6 %collective-permute-start.24 = (bf16[2048,128]{1,0:T(8,128)(2,1)S(1)}, bf16[2048,128]{1,0:T(8,128)(2,1)}, u32[]{:S(2)}, u32[]{:S(2)}) collective-permute-start(bf16[2048,128]{1,0:T(8,128)(2,1)S(1)} %constant_dynamic-update-slice_fusion.12.refs_1_), channel_id=1, source_target_pairs={{0,1},{1,0},{2,3},{3,2},{4,5},{5,4},{6,7},{7,6},{8,9},{9,8},{10,11... | collective-permute-start | bytes 1572872 | tf_op jit(solution)/shard_map/ppermute | solution.py:182
  54.1 35.0 %collective-permute-start = (bf16[1536,128]{1,0:T(8,128)(2,1)S(1)}, bf16[1536,128]{1,0:T(8,128)(2,1)S(1)}, u32[]{:S(2)}, u32[]{:S(2)}) collective-permute-start(bf16[1536,128]{1,0:T(8,128)(2,1)S(1)} %constant_dynamic-update-slice_fusion.refs_1_), channel_id=1, source_target_pairs={{0,1},{1,0},{2,3},{3,2},{4,5},{5,4},{6,7},{7,6},{8,9},{9,8},{10,11... | collective-permute-start | bytes 1179656 | tf_op jit(solution)/shard_map/ppermute | solution.py:182
  54.1 17.3 %collective-permute-start.2 = (bf16[768,128]{1,0:T(8,128)(2,1)}, bf16[768,128]{1,0:T(8,128)(2,1)S(1)}, u32[]{:S(2)}, u32[]{:S(2)}) collective-permute-start(bf16[768,128]{1,0:T(8,128)(2,1)} %copy-done.3), channel_id=1, source_target_pairs={{0,16},{16,0},{1,17},{17,1},{2,18},{18,2},{3,19},{19,3},{4,20},{20... | collective-permute-start | bytes 589832 | tf_op jit(solution)/shard_map/ppermute | solution.py:195
  55.8 15.7 %collective-permute-start.27 = (bf16[1024,128]{1,0:T(8,128)(2,1)}, bf16[1024,128]{1,0:T(8,128)(2,1)S(1)}, u32[]{:S(2)}, u32[]{:S(2)}) collective-permute-start(bf16[1024,128]{1,0:T(8,128)(2,1)} %copy-done.11), channel_id=1, source_target_pairs={{0,1},{1,0},{2,3},{3,2},{4,5},{5,4},{6,7},{7,6},{8,9},{9,8},{10,11... | collective-permute-start | bytes 786440 | tf_op jit(solution)/shard_map/ppermute | solution.py:182
  56.0 19.3 %collective-permute-start.28 = (bf16[1024,128]{1,0:T(8,128)(2,1)}, bf16[1024,128]{1,0:T(8,128)(2,1)S(1)}, u32[]{:S(2)}, u32[]{:S(2)}) collective-permute-start(bf16[1024,128]{1,0:T(8,128)(2,1)} %collective-permute-done.26.refs_4_), channel_id=1, source_target_pairs={{0,1},{1,0},{2,3},{3,2},{4,5},{5,4},{6,7},{7,6},{8,9},{9,8},{10,11... | collective-permute-start | bytes 786440 | tf_op jit(solution)/shard_map/ppermute | solution.py:182
  71.4 8.5 %collective-permute-start.29 = (bf16[48,512]{1,0:T(8,128)(2,1)S(1)}, bf16[48,512]{1,0:T(8,128)(2,1)S(1)}, u32[]{:S(2)}, u32[]{:S(2)}) collective-permute-start(bf16[48,512]{1,0:T(8,128)(2,1)S(1)} %get-tuple-element.25), channel_id=1, source_target_pairs={{0,4},{4,8},{8,12},{12,0},{1,5},{5,9},{9,13},{13,1},{2,6},{6,10},{... | collective-permute-start | bytes 147464 | tf_op jit(solution)/shard_map/ppermute | solution.py:201
  71.5 8.5 %collective-permute-start.30 = (bf16[48,512]{1,0:T(8,128)(2,1)S(1)}, bf16[48,512]{1,0:T(8,128)(2,1)S(1)}, u32[]{:S(2)}, u32[]{:S(2)}) collective-permute-start(bf16[48,512]{1,0:T(8,128)(2,1)S(1)} %get-tuple-element.26), channel_id=1, source_target_pairs={{0,12},{4,0},{8,4},{12,8},{1,13},{5,1},{9,5},{13,9},{2,14},{6,2},{... | collective-permute-start | bytes 147464 | tf_op jit(solution)/shard_map/ppermute | solution.py:201
  75.3 13.8 %collective-permute-start.3 = (bf16[768,128]{1,0:T(8,128)(2,1)S(1)}, bf16[768,128]{1,0:T(8,128)(2,1)S(1)}, u32[]{:S(2)}, u32[]{:S(2)}) collective-permute-start(bf16[768,128]{1,0:T(8,128)(2,1)S(1)} %copy-done.4), channel_id=1, source_target_pairs={{0,1},{1,0},{2,3},{3,2},{4,5},{5,4},{6,7},{7,6},{8,9},{9,8},{10,11... | collective-permute-start | bytes 589832 | tf_op jit(solution)/shard_map/ppermute | solution.py:182
  79.9 9.2 %collective-permute-start.4 = (bf16[768,128]{1,0:T(8,128)(2,1)S(1)}, bf16[768,128]{1,0:T(8,128)(2,1)S(1)}, u32[]{:S(2)}, u32[]{:S(2)}) collective-permute-start(bf16[768,128]{1,0:T(8,128)(2,1)S(1)} %collective-permute-done.2.refs_4_), channel_id=1, source_target_pairs={{0,1},{1,0},{2,3},{3,2},{4,5},{5,4},{6,7},{7,6},{8,9},{9,8},{10,11... | collective-permute-start | bytes 589832 | tf_op jit(solution)/shard_map/ppermute | solution.py:182
  (31 other events, 266.6 us)

commit v2 on v0

v2 whole, which is shorter than its diff:
```python
import functools

import jax
import jax.numpy as jnp
from jax import lax
from jax.experimental import pallas as pl
from jax.experimental.pallas import tpu as pltpu
from jax.sharding import PartitionSpec as P

COARSE_DEV = 12
COARSE_PAD = 16
EPS = 1e-05
TILE = 256
F32 = jnp.float32
BF16 = jnp.bfloat16


def silu(x):
    half = 0.5 * x
    return half + half * jnp.tanh(half)


def normalize(msg):
    width = msg.shape[1]
    mean = jnp.sum(msg, axis=1, keepdims=True) * (1.0 / width)
    square = jnp.sum(msg * msg, axis=1, keepdims=True) * (1.0 / width)
    return (msg - mean) * lax.rsqrt(square - mean * mean + EPS)


def dot(a, b):
    return jnp.dot(a, b, preferred_element_type=F32)


def own_columns(full, spot_ref, part):
    mine = spot_ref[0]
    out = full[:, 0:part]
    for j in range(1, full.shape[1] // part):
        out = jnp.where(mine == j, full[:, j * part : (j + 1) * part], out)
    return out


class Copies:
    def __init__(self, sems):
        self.sems, self.started = sems, []

    def start(self, source, target):
        copy = pltpu.make_async_copy(source, target, self.sems.at[len(self.started)])
        copy.start()
        self.started.append(copy)

    def wait(self):
        for copy in self.started:
            copy.wait()


def load_weights(copies, shards, base, first_ref, second_ref, y):
    first_rows = first_ref.shape[0]
    hidden, features = second_ref.shape
    part = hidden // 4
    for j, shard in enumerate(shards):
        columns = pl.ds(j * part, part)
        if len(shard) == 1:
            copies.start(shard[0].at[pl.ds(base, first_rows)], first_ref.at[:, columns])
        for q in range(features // part):
            target = second_ref.at[pl.ds(j * part, part), pl.ds(q * part, part)]
            at = first_rows + q * part
            if len(shard) == 1:
                copies.start(shard[0].at[pl.ds(base + at, part)], target)


def pack_kernel(spot_ref, ef, es, nf, ns, edge_out, node_out, late_out, ride_out, big, sems):
    features = es.shape[2]
    part = es.shape[1]
    copies = Copies(sems)
    at = 0
    for layer in range(ef.shape[0]):
        for first, second in ((ef, es), (nf, ns)):
            rows = first.shape[1]
            copies.start(first.at[layer], big.at[pl.ds(at, rows)])
            at += rows
            for q in range(features // part):
                copies.start(second.at[layer, :, pl.ds(q * part, part)], big.at[pl.ds(at, part)])
                at += part
    copies.wait()
    copies = Copies(sems)
    at = 0
    for out in (edge_out, node_out, late_out):
        copies.start(big.at[pl.ds(at, out.shape[0])], out)
        at += out.shape[0]
    if ride_out is not None:
        y, eighth = spot_ref[1], spot_ref[2]
        half = edge_out.shape[0] // 2
        copies.start(big.at[pl.ds(pl.multiple_of(y * half, half), half)], ride_out.at[pl.ds(0, half)])
        to, at = half, edge_out.shape[0]
        for out in (node_out, late_out):
            size = out.shape[0] // 8
            start = pl.multiple_of(at + eighth * size, 16)
            copies.start(big.at[pl.ds(start, size)], ride_out.at[pl.ds(to, size)])
            to += size
            at += out.shape[0]
    copies.wait()


def pack_kernel_plain(spot_ref, ef, es, nf, ns, edge_out, node_out, late_out, big, sems):
    pack_kernel(spot_ref, ef, es, nf, ns, edge_out, node_out, late_out, None, big, sems)


def pick_rows(wanted_ref, node_bf, outs):
    wanted = wanted_ref[...]
    lanes = lax.broadcasted_iota(jnp.int32, (wanted.shape[0], node_bf.shape[0]), 1)
    picked = dot(jnp.where(lanes == wanted, 1.0, 0.0).astype(BF16), node_bf).astype(BF16)
    start = 0
    for out in outs:
        out[...] = picked[start : start + out.shape[0]]
        start += out.shape[0]


def start_kernel(edge_ref, node_ref, wanted_ref, edge_out, node_out, right, left, coarse):
    edge_out[...] = edge_ref[...].astype(BF16)
    node_bf = node_ref[...].astype(BF16)
    node_out[...] = node_bf
    pick_rows(wanted_ref, node_bf, (right, left, coarse))


def load_first_weights(copies, spot_ref, own, core, x_pair, d_pair, w_ref, blocks_ref):
    rows = own.shape[0]
    part = own.shape[1]
    copies.start(own, w_ref.at[:, pl.ds(0, part)])
    copies.start(core, w_ref.at[:, pl.ds(part, part)])
    for j, pair in ((2, x_pair), (3, d_pair)):
        columns = pl.ds(j * part, part)
        if len(pair) == 1:
            copies.start(pair[0], w_ref.at[:, columns])
            continue
        half = rows // 2
        near = pl.multiple_of(spot_ref[1] * half, half)
        far = pl.multiple_of((1 - spot_ref[1]) * half, half)
        copies.start(pair[0], w_ref.at[pl.ds(near, half), columns])
        copies.start(pair[1], w_ref.at[pl.ds(far, half), columns])


def edge_rows(spot_ref, edge_ref, table, nodes, own_ref, index_ref, receiver_ref, first_ref, second_ref, product_ref, own_out, full_out):
    features = second_ref.shape[1]
    node_count = nodes.shape[0]
    table_rows = table.shape[0]
    lanes_all = product_ref.shape[0]
    used = table_rows + node_count
    part = own_ref.shape[1]
    product_ref[0:table_rows, :] = dot(table, first_ref[features : 2 * features, :]).astype(BF16)
    product_ref[table_rows:used, :] = dot(
        nodes, first_ref[2 * features : 3 * features, :]
    ).astype(BF16)
    if used < lanes_all:
        product_ref[used:, :] = jnp.zeros((lanes_all - used, features), BF16)
    incoming = jnp.zeros((node_count, features), F32)
    for at in range(0, own_ref.shape[0], TILE):
        rows = slice(at, at + TILE)
        edge_bf = edge_ref[rows, :]
        index = index_ref[rows, :]
        lanes = lax.broadcasted_iota(jnp.int32, (TILE, lanes_all), 1)
        hot = (lanes == index[:, 0:1]) | (lanes == index[:, 1:2])
        pre = dot(edge_bf, first_ref[0:features, :]) + dot(
            jnp.where(hot, 1.0, 0.0).astype(BF16), product_ref[...]
        )
        norm = normalize(dot(silu(pre).astype(BF16), second_ref[...]))
        edge_new = (edge_bf.astype(F32) + norm).astype(BF16)
        if full_out is not None:
            full_out[rows, :] = edge_new
        own_out[rows, :] = own_ref[rows, :] + own_columns(norm, spot_ref, part)
        node_ids = lax.broadcasted_iota(jnp.int32, (node_count, TILE), 0)
        incidence = jnp.where(node_ids == receiver_ref[:, rows], 1.0, 0.0).astype(BF16)
        incoming = incoming + dot(incidence, edge_new)
    return incoming.astype(BF16)


def first_edge_kernel(halves, spot_ref, *refs):
    refs = list(refs)
    own_w, core_w = refs.pop(0), refs.pop(0)
    x_pair = [refs.pop(0) for _ in range(halves)]
    d_pair = [refs.pop(0) for _ in range(halves)]
    shards = [refs.pop(0) for _ in range(4)]
    own_ref, index_ref, receiver_ref = [refs.pop(0) for _ in range(3)]
    own_out, incoming_out, full_out, node_out = [refs.pop(0) for _ in range(4)]
    w_ref, second_ref, product_ref, x_ref, sems = refs
    hidden, features = second_ref.shape
    part = own_ref.shape[1]
    edge_count = own_ref.shape[0]
    node_count = node_out.shape[0]
    copies = Copies(sems)
    load_first_weights(copies, spot_ref, own_w, core_w, x_pair, d_pair, w_ref, second_ref)
    for j, shard in enumerate(shards):
        column = pl.multiple_of((spot_ref[0] ^ j) * part, part)
        copies.start(shard, x_ref.at[:, pl.ds(column, part)])
    copies.wait()
    first_rows = 3 * features
    for j in range(4):
        for q in range(features // part):
            second_ref[j * part : (j + 1) * part, q * part : (q + 1) * part] = w_ref[
                first_rows + q * part : first_rows + (q + 1) * part, j * part : (j + 1) * part
            ]
    nodes = x_ref[edge_count : edge_count + node_count, :]
    node_out[...] = nodes
    incoming_out[...] = edge_rows(
        spot_ref, x_ref, x_ref[edge_count:, :], nodes, own_ref, index_ref, receiver_ref,
        w_ref, second_ref, product_ref, own_out, full_out,
    )


def late_edge_kernel(last, pieces, base, spot_ref, *refs):
    refs = list(refs)
    shards = [(refs.pop(0),) for _ in range(4)]
    edge_ref, own_ref = refs.pop(0), refs.pop(0)
    tables = [refs.pop(0) for _ in range(pieces)]
    index_ref, receiver_ref = refs.pop(0), refs.pop(0)
    own_out, incoming_out = refs.pop(0), refs.pop(0)
    full_out = None if last else refs.pop(0)
    first_ref, second_ref, product_ref, table_ref, sems = refs
    copies = Copies(sems)
    load_weights(copies, shards, base, first_ref, second_ref, None)
    start = 0
    for table in tables:
        table_ref[start : start + table.shape[0], :] = table[...]
        start += table.shape[0]
    copies.wait()
    incoming_out[...] = edge_rows(
        spot_ref, edge_ref, table_ref[...], tables[0][...], own_ref, index_ref, receiver_ref,
        first_ref, second_ref, product_ref, own_out, full_out,
    )


def node_kernel(last, base, spot_ref, *refs):
    refs = list(refs)
    shards = [(refs.pop(0),) for _ in range(4)]
    node_ref, own_ref, incoming_ref = [refs.pop(0) for _ in range(3)]
    wanted_ref = None if last else refs.pop(0)
    own_out = refs.pop(0)
    outs = [] if last else [refs.pop(0) for _ in range(4)]
    first_ref, second_ref, sems = refs
    features = second_ref.shape[1]
    copies = Copies(sems)
    load_weights(copies, shards, base, first_ref, second_ref, None)
    copies.wait()
    node_bf = node_ref[...]
    pre = dot(node_bf, first_ref[0:features, :]) + dot(incoming_ref[...], first_ref[features:, :])
    norm = normalize(dot(silu(pre).astype(BF16), second_ref[...]))
    own_out[...] = own_ref[...] + own_columns(norm, spot_ref, own_ref.shape[1])
    if not last:
        node_new = (node_bf.astype(F32) + norm).astype(BF16)
        outs[0][...] = node_new
        pick_rows(wanted_ref, node_new, outs[1:])


SMEM, VMEM, ANY = "smem", "vmem", "any"
SPACES = {SMEM: pltpu.SMEM, VMEM: pltpu.VMEM, ANY: pl.ANY}


def call(kernel, out_shape, args, scratch, flops, name, out_space=VMEM):
    arrays = [a for _, a in args]
    moved = sum(a.size * a.dtype.itemsize for a in arrays + list(out_shape))
    return pl.pallas_call(
        kernel,
        out_shape=out_shape,
        in_specs=[pl.BlockSpec(memory_space=SPACES[s]) for s, _ in args],
        out_specs=[pl.BlockSpec(memory_space=SPACES[out_space])] * len(out_shape),
        scratch_shapes=scratch,
        compiler_params=pltpu.CompilerParams(vmem_limit_bytes=40 * 1024 * 1024),
        cost_estimate=pl.CostEstimate(flops=flops, bytes_accessed=moved, transcendentals=0),
        name=name,
    )(*arrays)


def swap(x, mask):
    size = lax.axis_size("mp")
    return lax.ppermute(x, "mp", [(i, i ^ mask) for i in range(size)])


def shift(x, by):
    size = lax.axis_size("graph")
    return lax.ppermute(x, "graph", [(i, (i + by) % size) for i in range(size)])


def after(x, *others):
    return lax.optimization_barrier((x, *others))[0]


def neighbour_rows(right, left, coarse, halo):
    if lax.axis_size("graph") == 4:
        return [shift(right, 1), shift(left, -1), shift(coarse, 2)]
    everyone = lax.all_gather(coarse, "graph", axis=0, tiled=True)
    return [shift(right[:halo], 1), shift(left[:halo], -1), everyone]


def table_index(senders, node_count, halo):
    size = lax.axis_size("graph")
    coarse_start = node_count + 2 * halo
    number = jnp.maximum(senders - coarse_start, 0)
    block, row = number // COARSE_DEV, number % COARSE_DEV
    if size != 4:
        return jnp.where(senders < coarse_start, senders, coarse_start + block * COARSE_PAD + row)
    wide = halo + COARSE_PAD
    away = (block - lax.axis_index("graph")) % size
    starts = (node_count - COARSE_DEV, node_count + wide + halo, node_count + 2 * wide, node_count + halo)
    base = jnp.where(
        away < 2,
        jnp.where(away == 0, starts[0], starts[1]),
        jnp.where(away == 2, starts[2], starts[3]),
    )
    fine = jnp.where(senders < node_count + halo, senders, senders + COARSE_PAD)
    return jnp.where(senders < coarse_start, fine, base + row)


def on_device(
    node_state,
    edge_state,
    edge_first,
    edge_second,
    node_first,
    node_second,
    senders,
    receivers,
    boundary_rows,
):
    node_count, part = node_state.shape
    edge_count = edge_state.shape[0]
    features = edge_second.shape[2]
    hidden = 4 * part
    halo = boundary_rows.shape[0] // 2
    blocks = lax.axis_size("graph")
    split = blocks == 4
    shape = jax.ShapeDtypeStruct
    dma = pltpu.SemaphoreType.DMA
    block = lax.axis_index("graph")
    group = lax.axis_index("groups")
    spot = jnp.stack([lax.axis_index("mp"), group, group * blocks + block]).astype(jnp.int32)

    own_coarse = jnp.arange(node_count - COARSE_DEV, node_count, dtype=jnp.int32)
    padding = jnp.full((COARSE_PAD - COARSE_DEV,), -1, jnp.int32)
    coarse_list = jnp.concatenate([own_coarse, padding])
    wanted = jnp.concatenate(
        [boundary_rows[halo:], coarse_list, boundary_rows[:halo], coarse_list, coarse_list]
    )[:, None]
    wide = halo + COARSE_PAD

    def sent(width):
        return [shape((n, width), BF16) for n in (wide, wide, COARSE_PAD)]

    edge_bf, node_bf, right, left, coarse = call(
        start_kernel,
        [shape((edge_count, part), BF16), shape((node_count, part), BF16)] + sent(part),
        [(VMEM, edge_state), (VMEM, node_state), (VMEM, wanted)],
        [],
        2 * wanted.shape[0] * node_count * part,
        "boundary_rows",
    )

    edge_pack = edge_first.shape[1] + features
    node_pack = node_first.shape[1] + features
    late_pack = edge_pack + node_pack
    pack_shapes = [shape((n, part), BF16) for n in (edge_pack, node_pack, late_pack)]
    ride_rows = (edge_pack // 2, node_pack // 8, late_pack // 8)
    if split:
        pack_shapes.append(shape((sum(ride_rows), part), BF16))
    packs = call(
        pack_kernel if split else pack_kernel_plain,
        pack_shapes,
        [(SMEM, spot), (ANY, edge_first), (ANY, edge_second), (ANY, node_first), (ANY, node_second)],
        [pltpu.VMEM((edge_pack + node_pack + late_pack, part), BF16), dma((24,))],
        0,
        "packed_weights",
        ANY,
    )
    edge_w, node_w, late_w = packs[:3]
    if split:
        came = swap(packs[3], 2)
        near = came[: ride_rows[0]]
        node_eighth = came[ride_rows[0] : ride_rows[0] + ride_rows[1]]
        late_eighth = came[ride_rows[0] + ride_rows[1] :]
    halo_rows = neighbour_rows(right, left, coarse, halo)
    latents = jnp.concatenate([edge_bf, node_bf] + halo_rows, axis=0)
    table_rows = latents.shape[0] - edge_count
    if split:
        far_latents = swap(after(latents, came), 2)
        far = lax.ppermute(near, "groups", [(0, 1), (1, 0)])
        x_pair, d_pair = [near, far], [swap(near, 1), swap(far, 1)]
        node_x = lax.all_gather(node_eighth, ("groups", "graph"), axis=0, tiled=True)
        late_x = lax.all_gather(late_eighth, ("groups", "graph"), axis=0, tiled=True)
    else:
        far_latents = swap(latents, 2)
        x_pair = [swap(edge_w, 2)]
        d_pair = [swap(x_pair[0], 1)]
        node_x, late_x = swap(node_w, 2), swap(late_w, 2)
    shards = [latents, swap(latents, 1), far_latents, swap(far_latents, 1)]
    node_ws = [node_w, swap(node_w, 1), node_x, swap(node_x, 1)]
    late_ws = [late_w, swap(late_w, 1), late_x, swap(late_x, 1)]

    index = jnp.stack([table_index(senders, node_count, halo), receivers + table_rows], axis=1)
    receiver_row = receivers[None, :]
    lanes = -(-(table_rows + node_count) // 128) * 128
    edge_flops = 2 * edge_count * features * (2 * features + lanes + node_count)
    node_flops = 2 * node_count * features * 3 * features
    full_edge = shape((edge_count, features), BF16)
    full_node = shape((node_count, features), BF16)
    own_edge = shape((edge_count, part), F32)
    own_node = shape((node_count, part), F32)

    edge_own, incoming, edge_full, node_full = call(
        functools.partial(first_edge_kernel, len(x_pair)),
        [own_edge, full_node, full_edge, full_node],
        [(SMEM, spot), (ANY, edge_w), (ANY, swap(edge_w, 1))]
        + [(ANY, w) for w in x_pair + d_pair]
        + [(ANY, s) for s in shards]
        + [(VMEM, edge_state), (VMEM, index), (VMEM, receiver_row)],
        [
            pltpu.VMEM((edge_pack, hidden), BF16),
            pltpu.VMEM((hidden, features), BF16),
            pltpu.VMEM((lanes, hidden), BF16),
            pltpu.VMEM((edge_count + table_rows, features), BF16),
            dma((10,)),
        ],
        edge_flops,
        "edge_layer",
    )
    node_scratch = [
        pltpu.VMEM((node_first.shape[1], hidden), BF16),
        pltpu.VMEM((hidden, features), BF16),
        dma((20,)),
    ]
    node_own, node_full, right, left, coarse = call(
        functools.partial(node_kernel, False, 0),
        [own_node, full_node] + sent(features),
        [(SMEM, spot)]
        + [(ANY, w) for w in node_ws]
        + [(VMEM, node_full), (VMEM, node_state), (VMEM, incoming), (VMEM, wanted)],
        node_scratch,
        node_flops,
        "node_layer",
    )
    tables = [node_full] + neighbour_rows(right, left, coarse, halo)
    edge_own, incoming = call(
        functools.partial(late_edge_kernel, True, len(tables), 0),
        [own_edge, full_node],
        [(SMEM, spot)]
        + [(ANY, w) for w in late_ws]
        + [(VMEM, edge_full), (VMEM, edge_own)]
        + [(VMEM, t) for t in tables]
        + [(VMEM, index), (VMEM, receiver_row)],
        [
            pltpu.VMEM((edge_first.shape[1], hidden), BF16),
            pltpu.VMEM((hidden, features), BF16),
            pltpu.VMEM((lanes, hidden), BF16),
            pltpu.VMEM((table_rows, features), BF16),
            dma((20,)),
        ],
        edge_flops,
        "edge_layer",
    )
    (node_own,) = call(
        functools.partial(node_kernel, True, edge_pack),
        [own_node],
        [(SMEM, spot)]
        + [(ANY, w) for w in late_ws]
        + [(VMEM, node_full), (VMEM, node_own), (VMEM, incoming)],
        node_scratch,
        node_flops,
        "node_layer",
    )
    return (node_own, edge_own)


def solution(mesh):
    in_specs = (
        P(("groups", "graph"), "mp"),
        P(("groups", "graph"), "mp"),
        P(None, None, "mp"),
        P(None, "mp", None),
        P(None, None, "mp"),
        P(None, "mp", None),
        P("graph"),
        P("graph"),
        P("graph"),
    )
    out_specs = (P(("groups", "graph"), "mp"), P(("groups", "graph"), "mp"))
    return jax.shard_map(
        on_device, mesh=mesh, in_specs=in_specs, out_specs=out_specs, check_vma=False
    )
```

time: 264 us -> 141 us (0.53)
  waiting for transfers between devices: 99.2 us -> 13.1 us
  Pallas kernels: 0 us -> 24.2 us
  matrix products: 18.5 us -> 0 us
  blocking collectives: 81.5 us -> 65.7 us
  local copies, waits for them, and re-layouts: 35 us -> 19.5 us
  between operations: 14.7 us -> 1.05 us
  starting transfers between devices: 8.93 us -> 16.8 us
  other arithmetic: 5.88 us -> 0.12 us
    unnamed x10 -> x0, waiting for transfers between devices: 99.2 us -> none
    psum x4 -> x0, blocking collectives: 31.8 us -> none  [split_norm(): row_sums, squares = lax.psum((row_sums, squares), 'mp')]
    pallas_call x0 -> x6, Pallas kernels: none -> 24.2 us  [call(): pl.pallas_call(kernel, out_shape=out_shape, in_specs=[pl.BlockSpec(memory...]
    gather x6 -> x0, local copies, waits for them, and re-layouts: 21.7 us -> none  [the longest x2 10.9 us: edge_hidden(): sender_rows = jnp.take(node_table, senders, axis=0)]
    dot_general x14 -> x0, matrix products: 18.5 us -> none  [the longest x2 6.75 us: on_device(): jnp.dot(hidden, edge_second[layer_index], preferred_element_type=jnp.floa...]
    all_gather x6 -> x2, blocking collectives: 49.7 us -> 65.7 us  [the longest x1 33.9 us: on_device(): lax.all_gather(late_eighth, ('groups', 'graph'), axis=0, tiled=True)]
    ppermute x4 -> x18, waiting for transfers between devices: 0.01 us -> 13.1 us  [the longest x11 8.47 us: swap(): return lax.ppermute(x, 'mp', [(i, i ^ mask) for i in range(size)])]
    ppermute x4 -> x18, starting transfers between devices: 8.69 us -> 16.8 us  [the longest x6 9.99 us: shift(): return lax.ppermute(x, 'graph', [(i, (i + by) % size) for i in range(size)])]
  transfers between devices with their start and end apart: 10 -> 18, of which waited for: 4 -> 2; matrix products, arithmetic and copies ran while one was open for 9% -> 1% of each run, Pallas kernels for 0% -> 9%
where the time goes in v2:
time: 141 us; the launch traced here: 140 us
  blocking collectives  65.7 us (47%)
  Pallas kernels  24.2 us (17%)
  local copies, waits for them, and re-layouts  19.5 us (14%)
  starting transfers between devices  16.8 us (12%)
  waiting for transfers between devices  13.1 us (9%)
    all_gather x1, blocking collectives, on_device(): lax.all_gather(late_eighth, ('groups', 'graph'), axis=0, tiled=True)  33.9 us
    all_gather x1, blocking collectives, on_device(): lax.all_gather(node_eighth, ('groups', 'graph'), axis=0, tiled=True)  31.7 us
    pallas_call x6, Pallas kernels, call(): pl.pallas_call(kernel, out_shape=out_shape, in_specs=[pl.BlockSpec(memory...  24.2 us
    unnamed x54, local copies, waits for them, and re-layouts  17.2 us
    ppermute x6, starting transfers between devices, shift(): return lax.ppermute(x, 'graph', [(i, (i + by) % size) for i in range(size)])  9.99 us
    ppermute x11, waiting for transfers between devices, swap(): return lax.ppermute(x, 'mp', [(i, i ^ mask) for i in range(size)])  8.47 us
    ppermute x11, starting transfers between devices, swap(): return lax.ppermute(x, 'mp', [(i, i ^ mask) for i in range(size)])  5.24 us
    ppermute x6, waiting for transfers between devices, shift(): return lax.ppermute(x, 'graph', [(i, (i + by) % size) for i in range(size)])  4.64 us
  transfers between devices with their start and end apart: 18, of which 2 were waited for; matrix products, arithmetic and copies ran while one was open for 1% of the time, Pallas kernels for 9%

profile of v2, /device:TPU:0, one launch (start us, length us, event | category | flops | bytes accessed | tf_op | source)
XLA Modules:
  0.0 140.4 jit_solution(13346561219167557297)
XLA Ops:
  1.7 1.1 copy-done.1
  3.9 3.1 %collective-permute-start.9 = (bf16[48,128]{1,0:T(8,128)(2,1)S(1)}, bf16[48,128]{1,0:T(8,128)(2,1)S(1)}, u32[]{:S(2)}, u32[]{:S(2)}) collective-permute-start(bf16[48,128]{1,0:T(8,128)(2,1)S(1)} %get-tuple-element.29), channel_id=1, source_target_pairs={{0,4},{4,8},{8,12},{12,0},{1,5},{5,9},{9,13},{13,1},{2,6},{6,10},{... | collective-permute-start | bytes 36872 | tf_op jit(solution)/shard_map/ppermute | solution.py:279
  7.0 2.1 %collective-permute-start.10 = (bf16[48,128]{1,0:T(8,128)(2,1)S(1)}, bf16[48,128]{1,0:T(8,128)(2,1)S(1)}, u32[]{:S(2)}, u32[]{:S(2)}) collective-permute-start(bf16[48,128]{1,0:T(8,128)(2,1)S(1)} %get-tuple-element.30), channel_id=1, source_target_pairs={{0,12},{4,0},{8,4},{12,8},{1,13},{5,1},{9,5},{13,9},{2,14},{6,2},{... | collective-permute-start | bytes 36872 | tf_op jit(solution)/shard_map/ppermute | solution.py:279
  10.1 1.0 copy-done.4
  13.0 2.1 %packed_weights.1 = (bf16[2048,128]{1,0:T(8,128)(2,1)S(1)}, bf16[1536,128]{1,0:T(8,128)(2,1)}, bf16[3584,128]{1,0:T(8,128)(2,1)S(1)}, bf16[1664,128]{1,0:T(8,128)(2,1)S(1)}) custom-call(s32[3]{0:T(128)S(1)} %pad_add_fusion.1.spot_ref, bf16[2,1536,128]{2,1,0:T(8,128)(2,1)S(1)} %copy-done, bf16[2,128,512]{2,1,0:T(8,128)(2,1)S(1)} %copy-done.9, ...), custom_call_target="tpu_custom_call" | custom-call | bytes 4096012 | tf_op jit(solution)/shard_map/packed_weights/pallas_call | solution.py:260
  15.2 1.6 %collective-permute-start.1 = (bf16[1664,128]{1,0:T(8,128)(2,1)S(1)}, bf16[1664,128]{1,0:T(8,128)(2,1)S(1)}, u32[]{:S(2)}, u32[]{:S(2)}) collective-permute-start(bf16[1664,128]{1,0:T(8,128)(2,1)S(1)} %get-tuple-element.24), channel_id=1, source_target_pairs={{0,2},{1,3},{2,0},{3,1},{4,6},{5,7},{6,4},{7,5},{8,10},{9,11},{10,... | collective-permute-start | bytes 1277960 | tf_op jit(solution)/shard_map/ppermute | solution.py:274
  17.5 8.4 %collective-permute-done.1 = bf16[1664,128]{1,0:T(8,128)(2,1)S(1)} collective-permute-done((bf16[1664,128]{1,0:T(8,128)(2,1)S(1)}, bf16[1664,128]{1,0:T(8,128)(2,1)S(1)}, u32[]{:S(2)}, u32[]{:S(2)}) %collective-permute-start.1) | collective-permute-done | bytes 426016 | tf_op jit(solution)/shard_map/ppermute | solution.py:274
  26.0 1.5 %collective-permute-start.13 = (bf16[1840,128]{1,0:T(8,128)(2,1)S(1)}, bf16[1840,128]{1,0:T(8,128)(2,1)}, u32[]{:S(2)}, u32[]{:S(2)}) collective-permute-start(bf16[1840,128]{1,0:T(8,128)(2,1)S(1)} %constant_dynamic-update-slice_fusion.refs_6_), channel_id=1, source_target_pairs={{0,2},{1,3},{2,0},{3,1},{4,6},{5,7},{6,4},{7,5},{8,10},{9,11},{10,... | collective-permute-start | bytes 1413128 | tf_op jit(solution)/shard_map/ppermute | solution.py:274
  27.5 1.6 %collective-permute-start.6 = (bf16[1024,128]{1,0:T(8,128)(2,1)S(1)}, bf16[1024,128]{1,0:T(8,128)(2,1)S(1)}, u32[]{:S(2)}, u32[]{:S(2)}) collective-permute-start(bf16[1024,128]{1,0:T(8,128)(2,1)S(1)} %slice.22.refs_2_), channel_id=1, source_target_pairs={{0,16},{16,0},{1,17},{17,1},{2,18},{18,2},{3,19},{19,3},{4,20},{20... | collective-permute-start | bytes 786440 | tf_op jit(solution)/shard_map/ppermute | solution.py:383
  29.1 33.9 %all_gather.6.refs_2_ = bf16[3584,128]{1,0:T(8,128)(2,1)S(1)} all-gather(bf16[448,128]{1,0:T(8,128)(2,1)S(1)} %slice.20), channel_id=1, replica_groups=mesh['groups'=2,'graph'=4,'mp'=4] {'groups','graph'}, dimensions={0}, use_global_device_ids=true | all-gather | bytes 1032192 | tf_op jit(solution)/shard_map/all_gather | solution.py:386
  65.6 31.7 %all_gather.7.refs_2_ = bf16[1536,128]{1,0:T(8,128)(2,1)S(1)} all-gather(bf16[192,128]{1,0:T(8,128)(2,1)S(1)} %slice.21), channel_id=1, replica_groups=mesh['groups'=2,'graph'=4,'mp'=4] {'groups','graph'}, dimensions={0}, use_global_device_ids=true | all-gather | bytes 442368 | tf_op jit(solution)/shard_map/all_gather | solution.py:385
  99.3 1.2 copy.18.refs_11_.refs_10_
  100.5 1.1 copy-done.2
  101.6 1.1 copy-done.3
  102.8 1.0 copy-done.8
  103.8 1.0 copy-done.12
  104.8 1.0 copy-done.14
  105.9 1.0 copy-done.16
  109.8 7.7 %edge_layer.2 = (f32[1536,128]{1,0:T(8,128)S(1)}, bf16[192,512]{1,0:T(8,128)(2,1)S(1)}, bf16[1536,512]{1,0:T(8,128)(2,1)S(1)}, bf16[192,512]{1,0:T(8,128)(2,1)S(1)}) custom-call(s32[3]{0:T(128)S(1)} %pad_add_fusion.1.spot_ref, bf16[2048,128]{1,0:T(8,128)(2,1)S(1)} %copy-done.12, bf16[2048,128]{1,0:T(8,128)(2,1)S(1)} %copy-done.14, ...), custom_call_target="tpu_custom_call" | custom-call | flops 2717908992 | bytes 7538700 | tf_op jit(solution)/shard_map/edge_layer/pallas_call | solution.py:260
  117.5 2.9 %node_layer.2 = (f32[192,128]{1,0:T(8,128)S(1)}, bf16[192,512]{1,0:T(8,128)(2,1)S(1)}, bf16[48,512]{1,0:T(8,128)(2,1)S(1)}, bf16[48,512]{1,0:T(8,128)(2,1)S(1)}, bf16[16,512]{1,0:T(8,128)(2,1)S(1)}) custom-call(s32[3]{0:T(128)S(1)} %pad_add_fusion.1.spot_ref, bf16[1536,128]{1,0:T(8,128)(2,1)} %get-tuple-element.25.refs_0_, ...), custom_call_target="tpu_custom_call" | custom-call | flops 301989888 | bytes 2474444 | tf_op jit(solution)/shard_map/node_layer/pallas_call | solution.py:260
  120.5 3.8 %collective-permute-start.16 = (bf16[48,512]{1,0:T(8,128)(2,1)S(1)}, bf16[48,512]{1,0:T(8,128)(2,1)S(1)}, u32[]{:S(2)}, u32[]{:S(2)}) collective-permute-start(bf16[48,512]{1,0:T(8,128)(2,1)S(1)} %get-tuple-element.40), channel_id=1, source_target_pairs={{0,12},{4,0},{8,4},{12,8},{1,13},{5,1},{9,5},{13,9},{2,14},{6,2},{... | collective-permute-start | bytes 147464 | tf_op jit(solution)/shard_map/ppermute | solution.py:279
  124.3 4.6 %collective-permute-done.17.refs_9_ = bf16[16,512]{1,0:T(8,128)(2,1)S(1)} collective-permute-done((bf16[16,512]{1,0:T(8,128)(2,1)S(1)}, bf16[16,512]{1,0:T(8,128)(2,1)S(1)}, u32[]{:S(2)}, u32[]{:S(2)}) %collective-permute-start.17) | collective-permute-done | bytes 16416 | tf_op jit(solution)/shard_map/ppermute | solution.py:279
  128.9 8.1 %edge_layer.3 = (f32[1536,128]{1,0:T(8,128)}, bf16[192,512]{1,0:T(8,128)(2,1)S(1)}) custom-call(s32[3]{0:T(128)S(1)} %pad_add_fusion.1.spot_ref, bf16[3584,128]{1,0:T(8,128)(2,1)S(1)} %get-tuple-element.23.refs_0_, bf16[3584,128]{1,0:T(8,128)(2,1)S(1)} %collective-permute-done.refs_1_, bf16[3584,128]{1,0:T(8,128)(2,1)S(1)} %all_gather.6.refs_2_, ...), custom_call_target="tpu_custom_call" | custom-call | flops 2717908992 | bytes 7342092 | tf_op jit(solution)/shard_map/edge_layer/pallas_call | solution.py:260
  137.0 3.2 %node_layer.3 = f32[192,128]{1,0:T(8,128)} custom-call(s32[3]{0:T(128)S(1)} %pad_add_fusion.1.spot_ref, bf16[3584,128]{1,0:T(8,128)(2,1)S(1)} %get-tuple-element.23.refs_0_, bf16[3584,128]{1,0:T(8,128)(2,1)S(1)} %collective-permute-done.refs_1_, bf16[3584,128]{1,0:T(8,128)(2,1)S(1)} %all_gather.6.refs_2_, bf16[3584,128]{1,0:T(8,128)(2,1)} %collective-permute-done.2.refs_3_, ...), custom_call_target="tpu_custom_call" | custom-call | flops 301989888 | bytes 4259852 | tf_op jit(solution)/shard_map/node_layer/pallas_call | solution.py:260
  (91 shorter events, 13.3 us)
Async XLA Ops:
  0.6 9.5 %copy-start = (bf16[2,1536,128]{2,1,0:T(8,128)(2,1)S(1)}, bf16[2,1536,128]{2,1,0:T(8,128)(2,1)}, u32[]{:S(2)}) copy-start(bf16[2,1536,128]{2,1,0:T(8,128)(2,1)} %ef.1) | copy-start | bytes 2359300
  3.9 23.6 %copy-start.24 = (s32[1536]{0:T(1024)S(1)}, s32[1536]{0:T(1024)}, u32[]{:S(2)}) copy-start(s32[1536]{0:T(1024)} %param.15) | copy-start | bytes 18436
  3.9 12.9 %collective-permute-start.9 = (bf16[48,128]{1,0:T(8,128)(2,1)S(1)}, bf16[48,128]{1,0:T(8,128)(2,1)S(1)}, u32[]{:S(2)}, u32[]{:S(2)}) collective-permute-start(bf16[48,128]{1,0:T(8,128)(2,1)S(1)} %get-tuple-element.29), channel_id=1, source_target_pairs={{0,4},{4,8},{8,12},{12,0},{1,5},{5,9},{9,13},{13,1},{2,6},{6,10},{... | collective-permute-start | bytes 36872 | tf_op jit(solution)/shard_map/ppermute | solution.py:279
  7.0 10.4 %collective-permute-start.10 = (bf16[48,128]{1,0:T(8,128)(2,1)S(1)}, bf16[48,128]{1,0:T(8,128)(2,1)S(1)}, u32[]{:S(2)}, u32[]{:S(2)}) collective-permute-start(bf16[48,128]{1,0:T(8,128)(2,1)S(1)} %get-tuple-element.30), channel_id=1, source_target_pairs={{0,12},{4,0},{8,4},{12,8},{1,13},{5,1},{9,5},{13,9},{2,14},{6,2},{... | collective-permute-start | bytes 36872 | tf_op jit(solution)/shard_map/ppermute | solution.py:279
  9.1 8.3 %collective-permute-start.11 = (bf16[16,128]{1,0:T(8,128)(2,1)S(1)}, bf16[16,128]{1,0:T(8,128)(2,1)S(1)}, u32[]{:S(2)}, u32[]{:S(2)}) collective-permute-start(bf16[16,128]{1,0:T(8,128)(2,1)S(1)} %get-tuple-element.31), channel_id=1, source_target_pairs={{0,8},{4,12},{8,0},{12,4},{1,9},{5,13},{9,1},{13,5},{2,10},{6,14},... | collective-permute-start | bytes 12296 | tf_op jit(solution)/shard_map/ppermute | solution.py:279
  15.2 82.2 %copy-start.11 = (bf16[2048,128]{1,0:T(8,128)(2,1)}, bf16[2048,128]{1,0:T(8,128)(2,1)S(1)}, u32[]{:S(2)}) copy-start(bf16[2048,128]{1,0:T(8,128)(2,1)S(1)} %get-tuple-element.26.refs_0_) | copy-start | bytes 1572868
  15.2 50.4 %copy-start.23 = (s32[1536]{0:T(1024)S(1)}, s32[1536]{0:T(1024)}, u32[]{:S(2)}) copy-start(s32[1536]{0:T(1024)} %param.16) | copy-start | bytes 18436
  15.2 10.8 %collective-permute-start.1 = (bf16[1664,128]{1,0:T(8,128)(2,1)S(1)}, bf16[1664,128]{1,0:T(8,128)(2,1)S(1)}, u32[]{:S(2)}, u32[]{:S(2)}) collective-permute-start(bf16[1664,128]{1,0:T(8,128)(2,1)S(1)} %get-tuple-element.24), channel_id=1, source_target_pairs={{0,2},{1,3},{2,0},{3,1},{4,6},{5,7},{6,4},{7,5},{8,10},{9,11},{10,... | collective-permute-start | bytes 1277960 | tf_op jit(solution)/shard_map/ppermute | solution.py:274
  16.7 47.1 %collective-permute-start.5 = (bf16[2048,128]{1,0:T(8,128)(2,1)S(1)}, bf16[2048,128]{1,0:T(8,128)(2,1)S(1)}, u32[]{:S(2)}, u32[]{:S(2)}) collective-permute-start(bf16[2048,128]{1,0:T(8,128)(2,1)S(1)} %get-tuple-element.26.refs_0_), channel_id=1, source_target_pairs={{0,1},{1,0},{2,3},{3,2},{4,5},{5,4},{6,7},{7,6},{8,9},{9,8},{10,11... | collective-permute-start | bytes 1572872 | tf_op jit(solution)/shard_map/ppermute | solution.py:274
  16.8 107.5 %collective-permute-start = (bf16[3584,128]{1,0:T(8,128)(2,1)S(1)}, bf16[3584,128]{1,0:T(8,128)(2,1)S(1)}, u32[]{:S(2)}, u32[]{:S(2)}) collective-permute-start(bf16[3584,128]{1,0:T(8,128)(2,1)S(1)} %get-tuple-element.23.refs_0_), channel_id=1, source_target_pairs={{0,1},{1,0},{2,3},{3,2},{4,5},{5,4},{6,7},{7,6},{8,9},{9,8},{10,11... | collective-permute-start | bytes 2752520 | tf_op jit(solution)/shard_map/ppermute | solution.py:274
  17.4 80.7 %copy-start.7 = (bf16[1840,128]{1,0:T(8,128)(2,1)}, bf16[1840,128]{1,0:T(8,128)(2,1)S(1)}, u32[]{:S(2)}) copy-start(bf16[1840,128]{1,0:T(8,128)(2,1)S(1)} %constant_dynamic-update-slice_fusion.refs_6_) | copy-start | bytes 1413124
  17.4 45.6 %collective-permute-start.12 = (bf16[1840,128]{1,0:T(8,128)(2,1)S(1)}, bf16[1840,128]{1,0:T(8,128)(2,1)S(1)}, u32[]{:S(2)}, u32[]{:S(2)}) collective-permute-start(bf16[1840,128]{1,0:T(8,128)(2,1)S(1)} %constant_dynamic-update-slice_fusion.refs_6_), channel_id=1, source_target_pairs={{0,1},{1,0},{2,3},{3,2},{4,5},{5,4},{6,7},{7,6},{8,9},{9,8},{10,11... | collective-permute-start | bytes 1413128 | tf_op jit(solution)/shard_map/ppermute | solution.py:274
  26.0 39.2 %collective-permute-start.13 = (bf16[1840,128]{1,0:T(8,128)(2,1)S(1)}, bf16[1840,128]{1,0:T(8,128)(2,1)}, u32[]{:S(2)}, u32[]{:S(2)}) collective-permute-start(bf16[1840,128]{1,0:T(8,128)(2,1)S(1)} %constant_dynamic-update-slice_fusion.refs_6_), channel_id=1, source_target_pairs={{0,2},{1,3},{2,0},{3,1},{4,6},{5,7},{6,4},{7,5},{8,10},{9,11},{10,... | collective-permute-start | bytes 1413128 | tf_op jit(solution)/shard_map/ppermute | solution.py:274
  27.5 36.8 %collective-permute-start.6 = (bf16[1024,128]{1,0:T(8,128)(2,1)S(1)}, bf16[1024,128]{1,0:T(8,128)(2,1)S(1)}, u32[]{:S(2)}, u32[]{:S(2)}) collective-permute-start(bf16[1024,128]{1,0:T(8,128)(2,1)S(1)} %slice.22.refs_2_), channel_id=1, source_target_pairs={{0,16},{16,0},{1,17},{17,1},{2,18},{18,2},{3,19},{19,3},{4,20},{20... | collective-permute-start | bytes 786440 | tf_op jit(solution)/shard_map/ppermute | solution.py:383
  63.8 33.5 %collective-permute-start.7 = (bf16[1024,128]{1,0:T(8,128)(2,1)S(1)}, bf16[1024,128]{1,0:T(8,128)(2,1)S(1)}, u32[]{:S(2)}, u32[]{:S(2)}) collective-permute-start(bf16[1024,128]{1,0:T(8,128)(2,1)S(1)} %slice.22.refs_2_), channel_id=1, source_target_pairs={{0,1},{1,0},{2,3},{3,2},{4,5},{5,4},{6,7},{7,6},{8,9},{9,8},{10,11... | collective-permute-start | bytes 786440 | tf_op jit(solution)/shard_map/ppermute | solution.py:274
  63.8 34.3 %copy-start.13 = (bf16[2048,128]{1,0:T(8,128)(2,1)}, bf16[2048,128]{1,0:T(8,128)(2,1)S(1)}, u32[]{:S(2)}) copy-start(bf16[2048,128]{1,0:T(8,128)(2,1)S(1)} %collective-permute-done.5.refs_1_) | copy-start | bytes 1572868
  63.8 60.5 %collective-permute-start.2 = (bf16[3584,128]{1,0:T(8,128)(2,1)S(1)}, bf16[3584,128]{1,0:T(8,128)(2,1)}, u32[]{:S(2)}, u32[]{:S(2)}) collective-permute-start(bf16[3584,128]{1,0:T(8,128)(2,1)S(1)} %all_gather.6.refs_2_), channel_id=1, source_target_pairs={{0,1},{1,0},{2,3},{3,2},{4,5},{5,4},{6,7},{7,6},{8,9},{9,8},{10,11... | collective-permute-start | bytes 2752520 | tf_op jit(solution)/shard_map/ppermute | solution.py:274
  64.3 33.7 %collective-permute-start.8 = (bf16[1024,128]{1,0:T(8,128)(2,1)S(1)}, bf16[1024,128]{1,0:T(8,128)(2,1)S(1)}, u32[]{:S(2)}, u32[]{:S(2)}) collective-permute-start(bf16[1024,128]{1,0:T(8,128)(2,1)S(1)} %collective-permute-done.6.refs_3_), channel_id=1, source_target_pairs={{0,1},{1,0},{2,3},{3,2},{4,5},{5,4},{6,7},{7,6},{8,9},{9,8},{10,11... | collective-permute-start | bytes 786440 | tf_op jit(solution)/shard_map/ppermute | solution.py:274
  65.1 35.4 %collective-permute-start.14 = (bf16[1840,128]{1,0:T(8,128)(2,1)}, bf16[1840,128]{1,0:T(8,128)(2,1)}, u32[]{:S(2)}, u32[]{:S(2)}) collective-permute-start(bf16[1840,128]{1,0:T(8,128)(2,1)} %collective-permute-done.13.refs_8_), channel_id=1, source_target_pairs={{0,1},{1,0},{2,3},{3,2},{4,5},{5,4},{6,7},{7,6},{8,9},{9,8},{10,11... | collective-permute-start | bytes 1413128 | tf_op jit(solution)/shard_map/ppermute | solution.py:274
  98.1 19.4 %collective-permute-start.3 = (bf16[1536,128]{1,0:T(8,128)(2,1)}, bf16[1536,128]{1,0:T(8,128)(2,1)}, u32[]{:S(2)}, u32[]{:S(2)}) collective-permute-start(bf16[1536,128]{1,0:T(8,128)(2,1)} %get-tuple-element.25.refs_0_), channel_id=1, source_target_pairs={{0,1},{1,0},{2,3},{3,2},{4,5},{5,4},{6,7},{7,6},{8,9},{9,8},{10,11... | collective-permute-start | bytes 1179656 | tf_op jit(solution)/shard_map/ppermute | solution.py:274
  98.8 18.7 %collective-permute-start.4 = (bf16[1536,128]{1,0:T(8,128)(2,1)S(1)}, bf16[1536,128]{1,0:T(8,128)(2,1)}, u32[]{:S(2)}, u32[]{:S(2)}) collective-permute-start(bf16[1536,128]{1,0:T(8,128)(2,1)S(1)} %all_gather.7.refs_2_), channel_id=1, source_target_pairs={{0,1},{1,0},{2,3},{3,2},{4,5},{5,4},{6,7},{7,6},{8,9},{9,8},{10,11... | collective-permute-start | bytes 1179656 | tf_op jit(solution)/shard_map/ppermute | solution.py:274
  120.4 8.5 %collective-permute-start.15 = (bf16[48,512]{1,0:T(8,128)(2,1)S(1)}, bf16[48,512]{1,0:T(8,128)(2,1)S(1)}, u32[]{:S(2)}, u32[]{:S(2)}) collective-permute-start(bf16[48,512]{1,0:T(8,128)(2,1)S(1)} %get-tuple-element.39), channel_id=1, source_target_pairs={{0,4},{4,8},{8,12},{12,0},{1,5},{5,9},{9,13},{13,1},{2,6},{6,10},{... | collective-permute-start | bytes 147464 | tf_op jit(solution)/shard_map/ppermute | solution.py:279
  120.5 8.5 %collective-permute-start.16 = (bf16[48,512]{1,0:T(8,128)(2,1)S(1)}, bf16[48,512]{1,0:T(8,128)(2,1)S(1)}, u32[]{:S(2)}, u32[]{:S(2)}) collective-permute-start(bf16[48,512]{1,0:T(8,128)(2,1)S(1)} %get-tuple-element.40), channel_id=1, source_target_pairs={{0,12},{4,0},{8,4},{12,8},{1,13},{5,1},{9,5},{13,9},{2,14},{6,2},{... | collective-permute-start | bytes 147464 | tf_op jit(solution)/shard_map/ppermute | solution.py:279
  124.3 4.6 %collective-permute-start.17 = (bf16[16,512]{1,0:T(8,128)(2,1)S(1)}, bf16[16,512]{1,0:T(8,128)(2,1)S(1)}, u32[]{:S(2)}, u32[]{:S(2)}) collective-permute-start(bf16[16,512]{1,0:T(8,128)(2,1)S(1)} %get-tuple-element.41), channel_id=1, source_target_pairs={{0,8},{4,12},{8,0},{12,4},{1,9},{5,13},{9,1},{13,5},{2,10},{6,14},... | collective-permute-start | bytes 49160 | tf_op jit(solution)/shard_map/ppermute | solution.py:279
  (19 other events, 24.9 us)

commit v3 on v2

v3 whole, which is shorter than its diff:
```python
import functools

import jax
import jax.numpy as jnp
from jax import lax
from jax.experimental import pallas as pl
from jax.experimental.pallas import tpu as pltpu
from jax.sharding import PartitionSpec as P

COARSE_DEV = 12
COARSE_PAD = 16
EPS = 1e-05
TILE = 256
F32 = jnp.float32
BF16 = jnp.bfloat16


def silu(x):
    half = 0.5 * x
    return half + half * jnp.tanh(half)


def normalize(msg):
    width = msg.shape[1]
    mean = jnp.sum(msg, axis=1, keepdims=True) * (1.0 / width)
    square = jnp.sum(msg * msg, axis=1, keepdims=True) * (1.0 / width)
    return (msg - mean) * lax.rsqrt(square - mean * mean + EPS)


def dot(a, b):
    return jnp.dot(a, b, preferred_element_type=F32)


def own_columns(full, spot_ref, part):
    mine = spot_ref[0]
    out = full[:, 0:part]
    for j in range(1, full.shape[1] // part):
        out = jnp.where(mine == j, full[:, j * part : (j + 1) * part], out)
    return out


class Copies:
    def __init__(self, sems):
        self.sems, self.started = sems, []

    def start(self, source, target):
        copy = pltpu.make_async_copy(source, target, self.sems.at[len(self.started)])
        copy.start()
        self.started.append(copy)

    def wait(self):
        for copy in self.started:
            copy.wait()


def load_shard(copies, layer, first, second, j, first_ref, second_ref):
    part = second.shape[1]
    copies.start(first.at[layer], first_ref.at[:, pl.ds(j * part, part)])
    copies.start(second.at[layer], second_ref.at[pl.ds(j * part, part)])


def load_packed(copies, packed, j, first_ref, second_ref):
    rows = first_ref.shape[0]
    hidden, features = second_ref.shape
    part = hidden // 4
    copies.start(packed.at[pl.ds(0, rows)], first_ref.at[:, pl.ds(j * part, part)])
    for q in range(features // part):
        copies.start(
            packed.at[pl.ds(rows + q * part, part)],
            second_ref.at[pl.ds(j * part, part), pl.ds(q * part, part)],
        )


def load_half(copies, packed, base, half, j, first_ref, second_ref):
    rows = first_ref.shape[0] // 2
    hidden, features = second_ref.shape
    part = hidden // 4
    deep = part // 2
    at = pl.multiple_of(half * rows, rows)
    copies.start(packed.at[pl.ds(base, rows)], first_ref.at[pl.ds(at, rows), pl.ds(j * part, part)])
    at = pl.multiple_of(j * part + half * deep, deep)
    for q in range(features // part):
        copies.start(
            packed.at[pl.ds(base + rows + q * deep, deep)],
            second_ref.at[pl.ds(at, deep), pl.ds(q * part, part)],
        )
    return base + rows + features // part * deep


def ride_kernel(spot_ref, ef, es, nf, ns, ride_out, sems):
    y = spot_ref[1]
    part, features = es.shape[1:]
    copies = Copies(sems)
    at = 0
    for first, second in ((ef, es), (nf, ns)):
        rows = first.shape[1] // 2
        source = first.at[0, pl.ds(pl.multiple_of(y * rows, rows), rows)]
        copies.start(source, ride_out.at[pl.ds(at, rows)])
        at += rows
        deep = part // 2
        for q in range(features // part):
            source = second.at[0, pl.ds(pl.multiple_of(y * deep, deep), deep), pl.ds(q * part, part)]
            copies.start(source, ride_out.at[pl.ds(at, deep)])
            at += deep
    copies.wait()


def pack_kernel(ef, es, nf, ns, edge_out, node_out, sems):
    part, features = es.shape[1:]
    copies = Copies(sems)
    for first, second, out in ((ef, es, edge_out), (nf, ns, node_out)):
        rows = first.shape[1]
        copies.start(first.at[1], out.at[pl.ds(0, rows)])
        for q in range(features // part):
            copies.start(second.at[1, :, pl.ds(q * part, part)], out.at[pl.ds(rows + q * part, part)])
    copies.wait()


def pick_rows(wanted_ref, node_bf, outs):
    wanted = wanted_ref[...]
    lanes = lax.broadcasted_iota(jnp.int32, (wanted.shape[0], node_bf.shape[0]), 1)
    picked = dot(jnp.where(lanes == wanted, 1.0, 0.0).astype(BF16), node_bf).astype(BF16)
    start = 0
    for out in outs:
        out[...] = picked[start : start + out.shape[0]]
        start += out.shape[0]


def start_kernel(node_ref, wanted_ref, node_out, right, left, coarse):
    node_bf = node_ref[...].astype(BF16)
    node_out[...] = node_bf
    pick_rows(wanted_ref, node_bf, (right, left, coarse))


def latent_kernel(edge_ref, *refs):
    rows, out = refs[:-1], refs[-1]
    at = edge_ref.shape[0]
    out[0:at, :] = edge_ref[...].astype(BF16)
    for piece in rows:
        out[at : at + piece.shape[0], :] = piece[...]
        at += piece.shape[0]


def edge_rows(spot_ref, edge_ref, table, nodes, own_ref, index_ref, receiver_ref, first_ref, second_ref, product_ref, own_out, full_out):
    features = second_ref.shape[1]
    node_count = nodes.shape[0]
    table_rows = table.shape[0]
    lanes_all = product_ref.shape[0]
    used = table_rows + node_count
    part = own_ref.shape[1]
    product_ref[0:table_rows, :] = dot(table, first_ref[features : 2 * features, :]).astype(BF16)
    product_ref[table_rows:used, :] = dot(
        nodes, first_ref[2 * features : 3 * features, :]
    ).astype(BF16)
    if used < lanes_all:
        product_ref[used:, :] = jnp.zeros((lanes_all - used, features), BF16)
    incoming = jnp.zeros((node_count, features), F32)
    for at in range(0, own_ref.shape[0], TILE):
        rows = slice(at, at + TILE)
        edge_bf = edge_ref[rows, :]
        index = index_ref[rows, :]
        lanes = lax.broadcasted_iota(jnp.int32, (TILE, lanes_all), 1)
        hot = (lanes == index[:, 0:1]) | (lanes == index[:, 1:2])
        pre = dot(edge_bf, first_ref[0:features, :]) + dot(
            jnp.where(hot, 1.0, 0.0).astype(BF16), product_ref[...]
        )
        norm = normalize(dot(silu(pre).astype(BF16), second_ref[...]))
        edge_new = (edge_bf.astype(F32) + norm).astype(BF16)
        if full_out is not None:
            full_out[rows, :] = edge_new
        own_out[rows, :] = own_ref[rows, :] + own_columns(norm, spot_ref, part)
        node_ids = lax.broadcasted_iota(jnp.int32, (node_count, TILE), 0)
        incidence = jnp.where(node_ids == receiver_ref[:, rows], 1.0, 0.0).astype(BF16)
        incoming = incoming + dot(incidence, edge_new)
    return incoming.astype(BF16)


def node_rows(spot_ref, node_bf, incoming, own_ref, first_ref, second_ref, own_out):
    features = second_ref.shape[1]
    pre = dot(node_bf, first_ref[0:features, :]) + dot(incoming, first_ref[features:, :])
    norm = normalize(dot(silu(pre).astype(BF16), second_ref[...]))
    own_out[...] = own_ref[...] + own_columns(norm, spot_ref, own_ref.shape[1])
    return (node_bf.astype(F32) + norm).astype(BF16)


def first_kernel(spot_ref, *refs):
    refs = list(refs)
    own_w = [refs.pop(0) for _ in range(4)]
    core_w = [refs.pop(0) for _ in range(4)]
    halves = [[refs.pop(0) for _ in range(2)] for _ in range(2)]
    shards = [refs.pop(0) for _ in range(4)]
    edge_own, node_own, index_ref, receiver_ref, wanted_ref = [refs.pop(0) for _ in range(5)]
    edge_out, full_out, node_out, node_full = [refs.pop(0) for _ in range(4)]
    sends = [refs.pop(0) for _ in range(3)]
    edge_w, edge_w2, node_w, node_w2, product_ref, x_ref, edge_sems, node_sems = refs
    part = edge_own.shape[1]
    edge_count = edge_own.shape[0]
    node_count = node_own.shape[0]
    edge_copies, node_copies = Copies(edge_sems), Copies(node_sems)
    for j, shard in enumerate(shards):
        column = pl.multiple_of((spot_ref[0] ^ j) * part, part)
        edge_copies.start(shard, x_ref.at[:, pl.ds(column, part)])
    y = spot_ref[1]
    starts = [0, 0]
    for base, copies, (first, second), at in (
        (0, edge_copies, (edge_w, edge_w2), 0),
        (1, node_copies, (node_w, node_w2), 2),
    ):
        load_shard(copies, 0, own_w[at], own_w[at + 1], 0, first, second)
        load_shard(copies, 0, core_w[at], core_w[at + 1], 1, first, second)
        for j, pair in enumerate(halves):
            for k, piece in enumerate(pair):
                half = y if k == 0 else 1 - y
                end = load_half(copies, piece, starts[base], half, 2 + j, first, second)
        starts[1] = end
    edge_copies.wait()
    nodes = x_ref[edge_count : edge_count + node_count, :]
    incoming = edge_rows(
        spot_ref, x_ref, x_ref[edge_count:, :], nodes, edge_own, index_ref, receiver_ref,
        edge_w, edge_w2, product_ref, edge_out, full_out,
    )
    node_copies.wait()
    node_new = node_rows(spot_ref, nodes, incoming, node_own, node_w, node_w2, node_out)
    node_full[...] = node_new
    pick_rows(wanted_ref, node_new, sends)


def late_weights(copies, refs, first, second):
    load_shard(copies, 1, refs[0], refs[1], 0, first, second)
    load_shard(copies, 1, refs[2], refs[3], 1, first, second)
    load_packed(copies, refs[4], 2, first, second)
    load_packed(copies, refs[5], 3, first, second)


def late_edge_kernel(pieces, spot_ref, *refs):
    refs = list(refs)
    weights = [refs.pop(0) for _ in range(6)]
    edge_ref, own_ref = refs.pop(0), refs.pop(0)
    tables = [refs.pop(0) for _ in range(pieces)]
    index_ref, receiver_ref = refs.pop(0), refs.pop(0)
    own_out, incoming_out = refs.pop(0), refs.pop(0)
    first_ref, second_ref, product_ref, table_ref, sems = refs
    copies = Copies(sems)
    late_weights(copies, weights, first_ref, second_ref)
    start = 0
    for table in tables:
        table_ref[start : start + table.shape[0], :] = table[...]
        start += table.shape[0]
    copies.wait()
    incoming_out[...] = edge_rows(
        spot_ref, edge_ref, table_ref[...], tables[0][...], own_ref, index_ref, receiver_ref,
        first_ref, second_ref, product_ref, own_out, None,
    )


def late_node_kernel(spot_ref, *refs):
    refs = list(refs)
    weights = [refs.pop(0) for _ in range(6)]
    node_ref, own_ref, incoming_ref, own_out, first_ref, second_ref, sems = refs
    copies = Copies(sems)
    late_weights(copies, weights, first_ref, second_ref)
    copies.wait()
    node_rows(spot_ref, node_ref[...], incoming_ref[...], own_ref, first_ref, second_ref, own_out)


SMEM, VMEM, HBM = pltpu.SMEM, pltpu.VMEM, pltpu.HBM


def call(kernel, out_shape, args, scratch, flops, name, out_space=VMEM):
    arrays = [a for _, a in args]
    moved = sum(a.size * a.dtype.itemsize for a in arrays + list(out_shape))
    return pl.pallas_call(
        kernel,
        out_shape=out_shape,
        in_specs=[pl.BlockSpec(memory_space=s) for s, _ in args],
        out_specs=[pl.BlockSpec(memory_space=out_space)] * len(out_shape),
        scratch_shapes=scratch,
        compiler_params=pltpu.CompilerParams(vmem_limit_bytes=40 * 1024 * 1024),
        cost_estimate=pl.CostEstimate(flops=flops, bytes_accessed=moved, transcendentals=0),
        name=name,
    )(*arrays)


def swap(x, mask):
    size = lax.axis_size("mp")
    return lax.ppermute(x, "mp", [(i, i ^ mask) for i in range(size)])


def shift(x, by):
    size = lax.axis_size("graph")
    return lax.ppermute(x, "graph", [(i, (i + by) % size) for i in range(size)])


def after(x, *others):
    return lax.optimization_barrier((x, *others))[0]


def neighbour_rows(right, left, coarse, halo):
    if lax.axis_size("graph") == 4:
        return [shift(right, 1), shift(left, -1), shift(coarse, 2)]
    everyone = lax.all_gather(coarse, "graph", axis=0, tiled=True)
    return [shift(right[:halo], 1), shift(left[:halo], -1), everyone]


def table_index(senders, node_count, halo):
    size = lax.axis_size("graph")
    coarse_start = node_count + 2 * halo
    number = jnp.maximum(senders - coarse_start, 0)
    block, row = number // COARSE_DEV, number % COARSE_DEV
    if size != 4:
        return jnp.where(senders < coarse_start, senders, coarse_start + block * COARSE_PAD + row)
    wide = halo + COARSE_PAD
    away = (block - lax.axis_index("graph")) % size
    starts = (node_count - COARSE_DEV, node_count + wide + halo, node_count + 2 * wide, node_count + halo)
    base = jnp.where(
        away < 2,
        jnp.where(away == 0, starts[0], starts[1]),
        jnp.where(away == 2, starts[2], starts[3]),
    )
    fine = jnp.where(senders < node_count + halo, senders, senders + COARSE_PAD)
    return jnp.where(senders < coarse_start, fine, base + row)


def on_device(
    node_state,
    edge_state,
    edge_first,
    edge_second,
    node_first,
    node_second,
    senders,
    receivers,
    boundary_rows,
):
    node_count, part = node_state.shape
    edge_count = edge_state.shape[0]
    features = edge_second.shape[2]
    hidden = 4 * part
    halo = boundary_rows.shape[0] // 2
    blocks = lax.axis_size("graph")
    shape = jax.ShapeDtypeStruct
    dma = pltpu.SemaphoreType.DMA
    block = lax.axis_index("graph")
    group = lax.axis_index("groups")
    spot = jnp.stack([lax.axis_index("mp"), group, group * blocks + block]).astype(jnp.int32)

    own_coarse = jnp.arange(node_count - COARSE_DEV, node_count, dtype=jnp.int32)
    padding = jnp.full((COARSE_PAD - COARSE_DEV,), -1, jnp.int32)
    coarse_list = jnp.concatenate([own_coarse, padding])
    wanted = jnp.concatenate(
        [boundary_rows[halo:], coarse_list, boundary_rows[:halo], coarse_list, coarse_list]
    )[:, None]
    wide = halo + COARSE_PAD

    def sent(width):
        return [shape((n, width), BF16) for n in (wide, wide, COARSE_PAD)]

    weights = (edge_first, edge_second, node_first, node_second)
    edge_pack = edge_first.shape[1] + features
    node_pack = node_first.shape[1] + features
    (ride,) = call(
        ride_kernel,
        [shape(((edge_pack + node_pack) // 2, part), BF16)],
        [(SMEM, spot)] + [(HBM, w) for w in weights],
        [dma((10,))],
        0,
        "layer_0_half",
        HBM,
    )
    near = swap(ride, 2)
    node_bf, right, left, coarse = call(
        start_kernel,
        [shape((node_count, part), BF16)] + sent(part),
        [(VMEM, after(node_state, ride)), (VMEM, wanted)],
        [],
        2 * wanted.shape[0] * node_count * part,
        "boundary_rows",
    )
    halo_rows = neighbour_rows(right, left, coarse, halo)
    edge_late, node_late = call(
        pack_kernel,
        [shape((edge_pack, part), BF16), shape((node_pack, part), BF16)],
        [(HBM, after(weights[0], right))] + [(HBM, w) for w in weights[1:]],
        [dma((10,))],
        0,
        "layer_1_packed",
        HBM,
    )
    core_w = [swap(after(w, right), 1) for w in weights]
    table_rows = node_count + sum(r.shape[0] for r in halo_rows)
    (latents,) = call(
        latent_kernel,
        [shape((edge_count + table_rows, part), BF16)],
        [(VMEM, edge_state), (VMEM, node_bf)] + [(VMEM, r) for r in halo_rows],
        [],
        0,
        "latents",
    )
    far_latents = swap(after(latents, near), 2)
    shards = [latents, swap(latents, 1), far_latents, swap(far_latents, 1)]
    far = lax.ppermute(near, "groups", [(0, 1), (1, 0)])
    pairs = [near, far, swap(near, 1), swap(far, 1)]
    edge_late_x = swap(after(edge_late, far_latents), 2)

    index = jnp.stack([table_index(senders, node_count, halo), receivers + table_rows], axis=1)
    receiver_row = receivers[None, :]
    lanes = -(-(table_rows + node_count) // 128) * 128
    edge_flops = 2 * edge_count * features * (2 * features + lanes + node_count)
    node_flops = 2 * node_count * features * 3 * features
    full_edge = shape((edge_count, features), BF16)
    full_node = shape((node_count, features), BF16)
    own_edge = shape((edge_count, part), F32)
    own_node = shape((node_count, part), F32)
    second_shape = pltpu.VMEM((hidden, features), BF16)
    edge_shape = pltpu.VMEM((edge_first.shape[1], hidden), BF16)
    node_shape = pltpu.VMEM((node_first.shape[1], hidden), BF16)

    edge_own, edge_full, node_own, node_full, right, left, coarse = call(
        first_kernel,
        [own_edge, full_edge, own_node, full_node] + sent(features),
        [(SMEM, spot)]
        + [(HBM, w) for w in list(weights) + core_w + pairs + shards]
        + [(VMEM, a) for a in (edge_state, node_state, index, receiver_row, wanted)],
        [
            edge_shape,
            second_shape,
            node_shape,
            second_shape,
            pltpu.VMEM((lanes, hidden), BF16),
            pltpu.VMEM((edge_count + table_rows, features), BF16),
            dma((28,)),
            dma((24,)),
        ],
        edge_flops + node_flops,
        "layer_0",
    )
    edge_late_d = swap(after(edge_late_x, right), 1)
    node_late_x = swap(after(node_late, edge_late_x, right), 2)
    node_late_d = swap(node_late_x, 1)
    tables = [node_full] + neighbour_rows(right, left, coarse, halo)
    edge_own, incoming = call(
        functools.partial(late_edge_kernel, len(tables)),
        [own_edge, full_node],
        [(SMEM, spot)]
        + [(HBM, w) for w in (*weights[:2], *core_w[:2], edge_late_x, edge_late_d)]
        + [(VMEM, edge_full), (VMEM, edge_own)]
        + [(VMEM, t) for t in tables]
        + [(VMEM, index), (VMEM, receiver_row)],
        [
            edge_shape,
            second_shape,
            pltpu.VMEM((lanes, hidden), BF16),
            pltpu.VMEM((table_rows, features), BF16),
            dma((14,)),
        ],
        edge_flops,
        "layer_1_edges",
    )
    (node_own,) = call(
        late_node_kernel,
        [own_node],
        [(SMEM, spot)]
        + [(HBM, w) for w in (*weights[2:], *core_w[2:], node_late_x, node_late_d)]
        + [(VMEM, node_full), (VMEM, node_own), (VMEM, incoming)],
        [node_shape, second_shape, dma((14,))],
        node_flops,
        "layer_1_nodes",
    )
    return (node_own, edge_own)


def solution(mesh):
    in_specs = (
        P(("groups", "graph"), "mp"),
        P(("groups", "graph"), "mp"),
        P(None, None, "mp"),
        P(None, "mp", None),
        P(None, None, "mp"),
        P(None, "mp", None),
        P("graph"),
        P("graph"),
        P("graph"),
    )
    out_specs = (P(("groups", "graph"), "mp"), P(("groups", "graph"), "mp"))
    return jax.shard_map(
        on_device, mesh=mesh, in_specs=in_specs, out_specs=out_specs, check_vma=False
    )
```

time: 141 us -> 84.7 us (0.60)
  blocking collectives: 65.7 us -> 0 us
  waiting for transfers between devices: 13.1 us -> 28.2 us
  local copies, waits for them, and re-layouts: 19.5 us -> 14.7 us
  Pallas kernels: 24.2 us -> 22.3 us
    all_gather x2 -> x0, blocking collectives: 65.7 us -> none  [the longest x1 33.9 us: on_device(): lax.all_gather(late_eighth, ('groups', 'graph'), axis=0, tiled=True)]
    ppermute x1, waiting for transfers between devices: 0.01 us -> 7.86 us  [on_device(): far = lax.ppermute(near, 'groups', [(0, 1), (1, 0)])]
    ppermute x6, waiting for transfers between devices: 4.64 us -> 9.8 us  [shift(): return lax.ppermute(x, 'graph', [(i, (i + by) % size) for i in range(size)])]
    unnamed x54 -> x60, local copies, waits for them, and re-layouts: 17.2 us -> 14.1 us
    ppermute x11 -> x14, starting transfers between devices: 5.24 us -> 8.11 us  [swap(): return lax.ppermute(x, 'mp', [(i, i ^ mask) for i in range(size)])]
    ppermute x11 -> x14, waiting for transfers between devices: 8.47 us -> 10.6 us  [swap(): return lax.ppermute(x, 'mp', [(i, i ^ mask) for i in range(size)])]
    pallas_call x6 -> x7, Pallas kernels: 24.2 us -> 22.3 us  [call(): pl.pallas_call(kernel, out_shape=out_shape, in_specs=[pl.BlockSpec(memory...]
    ppermute x6, starting transfers between devices: 9.99 us -> 8.07 us  [shift(): return lax.ppermute(x, 'graph', [(i, (i + by) % size) for i in range(size)])]
  transfers between devices with their start and end apart: 18 -> 21, of which waited for: 2 -> 7; matrix products, arithmetic and copies ran while one was open for 1% -> 1% of each run, Pallas kernels for 9% -> 22%
where the time goes in v3:
time: 84.7 us; the launch traced here: 84.2 us
  waiting for transfers between devices  28.2 us (33%)
  Pallas kernels  22.3 us (26%)
  starting transfers between devices  17.7 us (21%)
  local copies, waits for them, and re-layouts  14.7 us (17%)
  between operations  1.13 us (1%)
    pallas_call x7, Pallas kernels, call(): pl.pallas_call(kernel, out_shape=out_shape, in_specs=[pl.BlockSpec(memory...  22.3 us
    unnamed x60, local copies, waits for them, and re-layouts  14.1 us
    ppermute x14, waiting for transfers between devices, swap(): return lax.ppermute(x, 'mp', [(i, i ^ mask) for i in range(size)])  10.6 us
    ppermute x6, waiting for transfers between devices, shift(): return lax.ppermute(x, 'graph', [(i, (i + by) % size) for i in range(size)])  9.8 us
    ppermute x14, starting transfers between devices, swap(): return lax.ppermute(x, 'mp', [(i, i ^ mask) for i in range(size)])  8.11 us
    ppermute x6, starting transfers between devices, shift(): return lax.ppermute(x, 'graph', [(i, (i + by) % size) for i in range(size)])  8.07 us
    ppermute x1, waiting for transfers between devices, on_device(): far = lax.ppermute(near, 'groups', [(0, 1), (1, 0)])  7.86 us
  transfers between devices with their start and end apart: 21, of which 7 were waited for; matrix products, arithmetic and copies ran while one was open for 1% of the time, Pallas kernels for 22%

profile of v3, /device:TPU:0, one launch (start us, length us, event | category | flops | bytes accessed | tf_op | source)
XLA Modules:
  0.0 84.2 jit_solution(496554958979139861)
XLA Ops:
  0.7 1.0 %copy-done = bf16[2,1024,128]{2,1,0:T(8,128)(2,1)S(1)} copy-done((bf16[2,1024,128]{2,1,0:T(8,128)(2,1)S(1)}, bf16[2,1024,128]{2,1,0:T(8,128)(2,1)}, u32[]{:S(2)}) %copy-start) | copy-done | bytes 524312
  1.8 1.1 %copy-done.2 = bf16[2,1536,128]{2,1,0:T(8,128)(2,1)S(1)} copy-done((bf16[2,1536,128]{2,1,0:T(8,128)(2,1)S(1)}, bf16[2,1536,128]{2,1,0:T(8,128)(2,1)}, u32[]{:S(2)}) %copy-start.2) | copy-done | bytes 786456
  2.9 0.9 %copy-done.4 = bf16[2,128,512]{2,1,0:T(8,128)(2,1)S(1)} copy-done((bf16[2,128,512]{2,1,0:T(8,128)(2,1)S(1)}, bf16[2,128,512]{2,1,0:T(8,128)(2,1)}, u32[]{:S(2)}) %copy-start.4) | copy-done | bytes 262168
  4.8 1.1 %layer_0_half.1 = bf16[1792,128]{1,0:T(8,128)(2,1)S(1)} custom-call(s32[3]{0:T(128)S(1)} %pad_add_fusion.1.spot_ref, bf16[2,1536,128]{2,1,0:T(8,128)(2,1)S(1)} %copy-done.2, bf16[2,128,512]{2,1,0:T(8,128)(2,1)S(1)} %copy-done.6, bf16[2,1024,128]{2,1,0:T(8,128)(2,1)S(1)} %copy-done, bf16[2,128,512]{2,1,0:T(8,128)(2,1)S(1)} %copy-done.4), custom_call_target="tpu_custom_call" | custom-call | bytes 2293772 | tf_op jit(solution)/shard_map/layer_0_half/pallas_call | solution.py:272
  5.9 3.0 %collective-permute-start.5 = (bf16[1792,128]{1,0:T(8,128)(2,1)S(1)}, bf16[1792,128]{1,0:T(8,128)(2,1)}, u32[]{:S(2)}, u32[]{:S(2)}) collective-permute-start(bf16[1792,128]{1,0:T(8,128)(2,1)S(1)} %layer_0_half.1), channel_id=1, source_target_pairs={{0,2},{1,3},{2,0},{3,1},{4,6},{5,7},{6,4},{7,5},{8,10},{9,11},{10,... | collective-permute-start | bytes 1376264 | tf_op jit(solution)/shard_map/ppermute | solution.py:286
  9.5 3.7 %collective-permute-start.3 = (bf16[48,128]{1,0:T(8,128)(2,1)S(1)}, bf16[48,128]{1,0:T(8,128)(2,1)S(1)}, u32[]{:S(2)}, u32[]{:S(2)}) collective-permute-start(bf16[48,128]{1,0:T(8,128)(2,1)S(1)} %get-tuple-element.34), channel_id=1, source_target_pairs={{0,12},{4,0},{8,4},{12,8},{1,13},{5,1},{9,5},{13,9},{2,14},{6,2},{... | collective-permute-start | bytes 36872 | tf_op jit(solution)/shard_map/ppermute | solution.py:291
  13.2 1.0 %collective-permute-start.4 = (bf16[16,128]{1,0:T(8,128)(2,1)S(1)}, bf16[16,128]{1,0:T(8,128)(2,1)S(1)}, u32[]{:S(2)}, u32[]{:S(2)}) collective-permute-start(bf16[16,128]{1,0:T(8,128)(2,1)S(1)} %get-tuple-element.35), channel_id=1, source_target_pairs={{0,8},{4,12},{8,0},{12,4},{1,9},{5,13},{9,1},{13,5},{2,10},{6,14},... | collective-permute-start | bytes 12296 | tf_op jit(solution)/shard_map/ppermute | solution.py:291
  14.2 3.5 %collective-permute-done.4.refs_3_ = bf16[16,128]{1,0:T(8,128)(2,1)S(1)} collective-permute-done((bf16[16,128]{1,0:T(8,128)(2,1)S(1)}, bf16[16,128]{1,0:T(8,128)(2,1)S(1)}, u32[]{:S(2)}, u32[]{:S(2)}) %collective-permute-start.4) | collective-permute-done | bytes 4128 | tf_op jit(solution)/shard_map/ppermute | solution.py:291
  17.7 1.0 %collective-permute-done.2.refs_1_ = bf16[48,128]{1,0:T(8,128)(2,1)S(1)} collective-permute-done((bf16[48,128]{1,0:T(8,128)(2,1)S(1)}, bf16[48,128]{1,0:T(8,128)(2,1)S(1)}, u32[]{:S(2)}, u32[]{:S(2)}) %collective-permute-start.2) | collective-permute-done | bytes 12320 | tf_op jit(solution)/shard_map/ppermute | solution.py:291
  18.7 1.1 %copy-done.8 = f32[1536,128]{1,0:T(8,128)S(1)} copy-done((f32[1536,128]{1,0:T(8,128)S(1)}, f32[1536,128]{1,0:T(8,128)}, u32[]{:S(2)}) %copy-start.8) | copy-done | bytes 786456
  20.0 1.3 %collective-permute-start.6 = (bf16[1840,128]{1,0:T(8,128)(2,1)S(1)}, bf16[1840,128]{1,0:T(8,128)(2,1)}, u32[]{:S(2)}, u32[]{:S(2)}) collective-permute-start(bf16[1840,128]{1,0:T(8,128)(2,1)S(1)} %latents.1.refs_12_), channel_id=1, source_target_pairs={{0,2},{1,3},{2,0},{3,1},{4,6},{5,7},{6,4},{7,5},{8,10},{9,11},{10,... | collective-permute-start | bytes 1413128 | tf_op jit(solution)/shard_map/ppermute | solution.py:286
  21.3 1.5 %collective-permute-start.10 = (bf16[1792,128]{1,0:T(8,128)(2,1)}, bf16[1792,128]{1,0:T(8,128)(2,1)}, u32[]{:S(2)}, u32[]{:S(2)}) collective-permute-start(bf16[1792,128]{1,0:T(8,128)(2,1)} %collective-permute-done.5.refs_8_), channel_id=1, source_target_pairs={{0,16},{16,0},{1,17},{17,1},{2,18},{18,2},{3,19},{19,3},{4,20},{20... | collective-permute-start | bytes 1376264 | tf_op jit(solution)/shard_map/ppermute | solution.py:401
  25.6 7.9 %collective-permute-done.10.refs_9_ = bf16[1792,128]{1,0:T(8,128)(2,1)} collective-permute-done((bf16[1792,128]{1,0:T(8,128)(2,1)}, bf16[1792,128]{1,0:T(8,128)(2,1)}, u32[]{:S(2)}, u32[]{:S(2)}) %collective-permute-start.10) | collective-permute-done | bytes 458784 | tf_op jit(solution)/shard_map/ppermute | solution.py:401
  36.5 1.5 %collective-permute-start.7 = (bf16[2048,128]{1,0:T(8,128)(2,1)}, bf16[2048,128]{1,0:T(8,128)(2,1)}, u32[]{:S(2)}, u32[]{:S(2)}) collective-permute-start(bf16[2048,128]{1,0:T(8,128)(2,1)} %get-tuple-element.37), channel_id=1, source_target_pairs={{0,2},{1,3},{2,0},{3,1},{4,6},{5,7},{6,4},{7,5},{8,10},{9,11},{10,... | collective-permute-start | bytes 1572872 | tf_op jit(solution)/shard_map/ppermute | solution.py:286
  38.4 1.0 %copy-done.11 = bf16[2,1024,128]{2,1,0:T(8,128)(2,1)S(1)} copy-done((bf16[2,1024,128]{2,1,0:T(8,128)(2,1)S(1)}, bf16[2,1024,128]{2,1,0:T(8,128)(2,1)}, u32[]{:S(2)}) %copy-start.11) | copy-done | bytes 524312
  39.5 1.0 %copy-done.14 = bf16[1840,128]{1,0:T(8,128)(2,1)S(1)} copy-done((bf16[1840,128]{1,0:T(8,128)(2,1)S(1)}, bf16[1840,128]{1,0:T(8,128)(2,1)}, u32[]{:S(2)}) %copy-start.14) | copy-done | bytes 471064
  42.3 1.0 %copy-done.21 = bf16[1840,128]{1,0:T(8,128)(2,1)S(1)} copy-done((bf16[1840,128]{1,0:T(8,128)(2,1)S(1)}, bf16[1840,128]{1,0:T(8,128)(2,1)}, u32[]{:S(2)}) %copy-start.21) | copy-done | bytes 471064
  44.3 9.3 %layer_0.1 = (f32[1536,128]{1,0:T(8,128)S(1)}, bf16[1536,512]{1,0:T(8,128)(2,1)S(1)}, f32[192,128]{1,0:T(8,128)S(1)}, bf16[192,512]{1,0:T(8,128)(2,1)S(1)}, bf16...) custom-call(s32[3]{0:T(128)S(1)} %pad_add_fusion.1.spot_ref, ...), custom_call_target="tpu_custom_call" | custom-call | flops 3019898880 | bytes 11061708 | tf_op jit(solution)/shard_map/layer_0/pallas_call | solution.py:272
  54.2 10.2 %collective-permute-done.15.refs_4_ = bf16[1536,128]{1,0:T(8,128)(2,1)S(1)} collective-permute-done((bf16[1536,128]{1,0:T(8,128)(2,1)S(1)}, bf16[1536,128]{1,0:T(8,128)(2,1)S(1)}, u32[]{:S(2)}, u32[]{:S(2)}) %collective-permute-start.15) | collective-permute-done | bytes 393248 | tf_op jit(solution)/shard_map/ppermute | solution.py:286
  64.4 2.8 %collective-permute-start.19 = (bf16[48,512]{1,0:T(8,128)(2,1)S(1)}, bf16[48,512]{1,0:T(8,128)(2,1)S(1)}, u32[]{:S(2)}, u32[]{:S(2)}) collective-permute-start(bf16[48,512]{1,0:T(8,128)(2,1)S(1)} %get-tuple-element.46), channel_id=1, source_target_pairs={{0,12},{4,0},{8,4},{12,8},{1,13},{5,1},{9,5},{13,9},{2,14},{6,2},{... | collective-permute-start | bytes 147464 | tf_op jit(solution)/shard_map/ppermute | solution.py:291
  67.8 4.1 %collective-permute-done.20.refs_11_ = bf16[16,512]{1,0:T(8,128)(2,1)S(1)} collective-permute-done((bf16[16,512]{1,0:T(8,128)(2,1)S(1)}, bf16[16,512]{1,0:T(8,128)(2,1)S(1)}, u32[]{:S(2)}, u32[]{:S(2)}) %collective-permute-start.20) | collective-permute-done | bytes 16416 | tf_op jit(solution)/shard_map/ppermute | solution.py:291
  71.9 1.2 %collective-permute-done.18.refs_9_ = bf16[48,512]{1,0:T(8,128)(2,1)S(1)} collective-permute-done((bf16[48,512]{1,0:T(8,128)(2,1)S(1)}, bf16[48,512]{1,0:T(8,128)(2,1)S(1)}, u32[]{:S(2)}, u32[]{:S(2)}) %collective-permute-start.18) | collective-permute-done | bytes 49184 | tf_op jit(solution)/shard_map/ppermute | solution.py:291
  73.2 8.2 %layer_1_edges.1 = (f32[1536,128]{1,0:T(8,128)}, bf16[192,512]{1,0:T(8,128)(2,1)S(1)}) custom-call(s32[3]{0:T(128)S(1)} %pad_add_fusion.1.spot_ref, bf16[2,1536,128]{2,1,0:T(8,128)(2,1)S(1)} %copy-done.3, bf16[2,128,512]{2,1,0:T(8,128)(2,1)S(1)} %copy-done.7, bf16[2,1536,128]{2,1,0:T(8,128)(2,1)} %collective-permute-done.8.refs_4_.refs_2_, ...), custom_call_target="tpu_custom_call" | custom-call | flops 2717908992 | bytes 6817804 | tf_op jit(solution)/shard_map/layer_1_edges/pallas_call | solution.py:272
  81.4 2.6 %layer_1_nodes.1 = f32[192,128]{1,0:T(8,128)} custom-call(s32[3]{0:T(128)S(1)} %pad_add_fusion.1.spot_ref, bf16[2,1024,128]{2,1,0:T(8,128)(2,1)S(1)} %copy-done.1, bf16[2,128,512]{2,1,0:T(8,128)(2,1)S(1)} %copy-done.5, bf16[2,1024,128]{2,1,0:T(8,128)(2,1)S(1)} %copy-done.12, bf16[2,128,512]{2,1,0:T(8,128)(2,1)S(1)} %copy-done.17, ...), custom_call_target="tpu_custom_call" | custom-call | flops 301989888 | bytes 2949132 | tf_op jit(solution)/shard_map/layer_1_nodes/pallas_call | solution.py:272
  (98 shorter events, 11.8 us)
Async XLA Ops:
  4.8 20.3 %copy-start.3 = (bf16[2,1536,128]{2,1,0:T(8,128)(2,1)S(1)}, bf16[2,1536,128]{2,1,0:T(8,128)(2,1)}, u32[]{:S(2)}) copy-start(bf16[2,1536,128]{2,1,0:T(8,128)(2,1)} %refs_0_.4) | copy-start | bytes 2359300
  4.8 29.2 %copy-start.28 = (s32[1536]{0:T(1024)S(1)}, s32[1536]{0:T(1024)}, u32[]{:S(2)}) copy-start(s32[1536]{0:T(1024)} %param.15) | copy-start | bytes 18436
  5.9 14.0 %collective-permute-start.5 = (bf16[1792,128]{1,0:T(8,128)(2,1)S(1)}, bf16[1792,128]{1,0:T(8,128)(2,1)}, u32[]{:S(2)}, u32[]{:S(2)}) collective-permute-start(bf16[1792,128]{1,0:T(8,128)(2,1)S(1)} %layer_0_half.1), channel_id=1, source_target_pairs={{0,2},{1,3},{2,0},{3,1},{4,6},{5,7},{6,4},{7,5},{8,10},{9,11},{10,... | collective-permute-start | bytes 1376264 | tf_op jit(solution)/shard_map/ppermute | solution.py:286
  9.4 13.4 %collective-permute-start.1 = (bf16[2,128,512]{2,1,0:T(8,128)(2,1)S(1)}, bf16[2,128,512]{2,1,0:T(8,128)(2,1)S(1)}, u32[]{:S(2)}, u32[]{:S(2)}) collective-permute-start(bf16[2,128,512]{2,1,0:T(8,128)(2,1)S(1)} %copy-done.5), channel_id=1, source_target_pairs={{0,1},{1,0},{2,3},{3,2},{4,5},{5,4},{6,7},{7,6},{8,9},{9,8},{10,11... | collective-permute-start | bytes 786440 | tf_op jit(solution)/shard_map/ppermute | solution.py:286
  9.5 8.2 %collective-permute-start.3 = (bf16[48,128]{1,0:T(8,128)(2,1)S(1)}, bf16[48,128]{1,0:T(8,128)(2,1)S(1)}, u32[]{:S(2)}, u32[]{:S(2)}) collective-permute-start(bf16[48,128]{1,0:T(8,128)(2,1)S(1)} %get-tuple-element.34), channel_id=1, source_target_pairs={{0,12},{4,0},{8,4},{12,8},{1,13},{5,1},{9,5},{13,9},{2,14},{6,2},{... | collective-permute-start | bytes 36872 | tf_op jit(solution)/shard_map/ppermute | solution.py:291
  13.2 5.5 %collective-permute-start.2 = (bf16[48,128]{1,0:T(8,128)(2,1)S(1)}, bf16[48,128]{1,0:T(8,128)(2,1)S(1)}, u32[]{:S(2)}, u32[]{:S(2)}) collective-permute-start(bf16[48,128]{1,0:T(8,128)(2,1)S(1)} %get-tuple-element.27), channel_id=1, source_target_pairs={{0,4},{4,8},{8,12},{12,0},{1,5},{5,9},{9,13},{13,1},{2,6},{6,10},{... | collective-permute-start | bytes 36872 | tf_op jit(solution)/shard_map/ppermute | solution.py:291
  13.2 4.5 %collective-permute-start.4 = (bf16[16,128]{1,0:T(8,128)(2,1)S(1)}, bf16[16,128]{1,0:T(8,128)(2,1)S(1)}, u32[]{:S(2)}, u32[]{:S(2)}) collective-permute-start(bf16[16,128]{1,0:T(8,128)(2,1)S(1)} %get-tuple-element.35), channel_id=1, source_target_pairs={{0,8},{4,12},{8,0},{12,4},{1,9},{5,13},{9,1},{13,5},{2,10},{6,14},... | collective-permute-start | bytes 12296 | tf_op jit(solution)/shard_map/ppermute | solution.py:291
  19.9 5.3 %collective-permute-start.13 = (bf16[1840,128]{1,0:T(8,128)(2,1)S(1)}, bf16[1840,128]{1,0:T(8,128)(2,1)S(1)}, u32[]{:S(2)}, u32[]{:S(2)}) collective-permute-start(bf16[1840,128]{1,0:T(8,128)(2,1)S(1)} %latents.1.refs_12_), channel_id=1, source_target_pairs={{0,1},{1,0},{2,3},{3,2},{4,5},{5,4},{6,7},{7,6},{8,9},{9,8},{10,11... | collective-permute-start | bytes 1413128 | tf_op jit(solution)/shard_map/ppermute | solution.py:286
  20.0 13.5 %collective-permute-start.6 = (bf16[1840,128]{1,0:T(8,128)(2,1)S(1)}, bf16[1840,128]{1,0:T(8,128)(2,1)}, u32[]{:S(2)}, u32[]{:S(2)}) collective-permute-start(bf16[1840,128]{1,0:T(8,128)(2,1)S(1)} %latents.1.refs_12_), channel_id=1, source_target_pairs={{0,2},{1,3},{2,0},{3,1},{4,6},{5,7},{6,4},{7,5},{8,10},{9,11},{10,... | collective-permute-start | bytes 1413128 | tf_op jit(solution)/shard_map/ppermute | solution.py:286
  21.3 12.1 %collective-permute-start.10 = (bf16[1792,128]{1,0:T(8,128)(2,1)}, bf16[1792,128]{1,0:T(8,128)(2,1)}, u32[]{:S(2)}, u32[]{:S(2)}) collective-permute-start(bf16[1792,128]{1,0:T(8,128)(2,1)} %collective-permute-done.5.refs_8_), channel_id=1, source_target_pairs={{0,16},{16,0},{1,17},{17,1},{2,18},{18,2},{3,19},{19,3},{4,20},{20... | collective-permute-start | bytes 1376264 | tf_op jit(solution)/shard_map/ppermute | solution.py:401
  22.8 1.5 %collective-permute-start.9 = (bf16[2,128,512]{2,1,0:T(8,128)(2,1)S(1)}, bf16[2,128,512]{2,1,0:T(8,128)(2,1)S(1)}, u32[]{:S(2)}, u32[]{:S(2)}) collective-permute-start(bf16[2,128,512]{2,1,0:T(8,128)(2,1)S(1)} %copy-done.7), channel_id=1, source_target_pairs={{0,1},{1,0},{2,3},{3,2},{4,5},{5,4},{6,7},{7,6},{8,9},{9,8},{10,11... | collective-permute-start | bytes 786440 | tf_op jit(solution)/shard_map/ppermute | solution.py:286
  23.5 12.1 %collective-permute-start = (bf16[2,1024,128]{2,1,0:T(8,128)(2,1)S(1)}, bf16[2,1024,128]{2,1,0:T(8,128)(2,1)S(1)}, u32[]{:S(2)}, u32[]{:S(2)}) collective-permute-start(bf16[2,1024,128]{2,1,0:T(8,128)(2,1)S(1)} %copy-done.1), channel_id=1, source_target_pairs={{0,1},{1,0},{2,3},{3,2},{4,5},{5,4},{6,7},{7,6},{8,9},{9,8},{10,11... | collective-permute-start | bytes 1572872 | tf_op jit(solution)/shard_map/ppermute | solution.py:286
  25.1 13.3 %collective-permute-start.8 = (bf16[2,1536,128]{2,1,0:T(8,128)(2,1)S(1)}, bf16[2,1536,128]{2,1,0:T(8,128)(2,1)}, u32[]{:S(2)}, u32[]{:S(2)}) collective-permute-start(bf16[2,1536,128]{2,1,0:T(8,128)(2,1)S(1)} %copy-done.3), channel_id=1, source_target_pairs={{0,1},{1,0},{2,3},{3,2},{4,5},{5,4},{6,7},{7,6},{8,9},{9,8},{10,11... | collective-permute-start | bytes 2359304 | tf_op jit(solution)/shard_map/ppermute | solution.py:286
  25.2 13.2 %collective-permute-start.11 = (bf16[1792,128]{1,0:T(8,128)(2,1)}, bf16[1792,128]{1,0:T(8,128)(2,1)}, u32[]{:S(2)}, u32[]{:S(2)}) collective-permute-start(bf16[1792,128]{1,0:T(8,128)(2,1)} %collective-permute-done.5.refs_8_), channel_id=1, source_target_pairs={{0,1},{1,0},{2,3},{3,2},{4,5},{5,4},{6,7},{7,6},{8,9},{9,8},{10,11... | collective-permute-start | bytes 1376264 | tf_op jit(solution)/shard_map/ppermute | solution.py:286
  33.5 4.9 %collective-permute-start.12 = (bf16[1792,128]{1,0:T(8,128)(2,1)}, bf16[1792,128]{1,0:T(8,128)(2,1)}, u32[]{:S(2)}, u32[]{:S(2)}) collective-permute-start(bf16[1792,128]{1,0:T(8,128)(2,1)} %collective-permute-done.10.refs_9_), channel_id=1, source_target_pairs={{0,1},{1,0},{2,3},{3,2},{4,5},{5,4},{6,7},{7,6},{8,9},{9,8},{10,11... | collective-permute-start | bytes 1376264 | tf_op jit(solution)/shard_map/ppermute | solution.py:286
  33.5 4.9 %collective-permute-start.14 = (bf16[1840,128]{1,0:T(8,128)(2,1)}, bf16[1840,128]{1,0:T(8,128)(2,1)}, u32[]{:S(2)}, u32[]{:S(2)}) collective-permute-start(bf16[1840,128]{1,0:T(8,128)(2,1)} %collective-permute-done.6.refs_14_), channel_id=1, source_target_pairs={{0,1},{1,0},{2,3},{3,2},{4,5},{5,4},{6,7},{7,6},{8,9},{9,8},{10,11... | collective-permute-start | bytes 1413128 | tf_op jit(solution)/shard_map/ppermute | solution.py:286
  36.5 17.1 %collective-permute-start.7 = (bf16[2048,128]{1,0:T(8,128)(2,1)}, bf16[2048,128]{1,0:T(8,128)(2,1)}, u32[]{:S(2)}, u32[]{:S(2)}) collective-permute-start(bf16[2048,128]{1,0:T(8,128)(2,1)} %get-tuple-element.37), channel_id=1, source_target_pairs={{0,2},{1,3},{2,0},{3,1},{4,6},{5,7},{6,4},{7,5},{8,10},{9,11},{10,... | collective-permute-start | bytes 1572872 | tf_op jit(solution)/shard_map/ppermute | solution.py:286
  44.3 28.8 %copy-start.26 = (bf16[2,128,512]{2,1,0:T(8,128)(2,1)S(1)}, bf16[2,128,512]{2,1,0:T(8,128)(2,1)}, u32[]{:S(2)}) copy-start(bf16[2,128,512]{2,1,0:T(8,128)(2,1)} %copy-done.24) | copy-start | bytes 786436
  53.6 10.8 %collective-permute-start.15 = (bf16[1536,128]{1,0:T(8,128)(2,1)S(1)}, bf16[1536,128]{1,0:T(8,128)(2,1)S(1)}, u32[]{:S(2)}, u32[]{:S(2)}) collective-permute-start(bf16[1536,128]{1,0:T(8,128)(2,1)S(1)} %copy-done.23), channel_id=1, source_target_pairs={{0,2},{1,3},{2,0},{3,1},{4,6},{5,7},{6,4},{7,5},{8,10},{9,11},{10,... | collective-permute-start | bytes 1179656 | tf_op jit(solution)/shard_map/ppermute | solution.py:286
  54.2 19.0 %collective-permute-start.17 = (bf16[2048,128]{1,0:T(8,128)(2,1)}, bf16[2048,128]{1,0:T(8,128)(2,1)S(1)}, u32[]{:S(2)}, u32[]{:S(2)}) collective-permute-start(bf16[2048,128]{1,0:T(8,128)(2,1)} %collective-permute-done.7.refs_4_), channel_id=1, source_target_pairs={{0,1},{1,0},{2,3},{3,2},{4,5},{5,4},{6,7},{7,6},{8,9},{9,8},{10,11... | collective-permute-start | bytes 1572872 | tf_op jit(solution)/shard_map/ppermute | solution.py:286
  64.4 16.9 %collective-permute-start.16 = (bf16[1536,128]{1,0:T(8,128)(2,1)S(1)}, bf16[1536,128]{1,0:T(8,128)(2,1)S(1)}, u32[]{:S(2)}, u32[]{:S(2)}) collective-permute-start(bf16[1536,128]{1,0:T(8,128)(2,1)S(1)} %collective-permute-done.15.refs_4_), channel_id=1, source_target_pairs={{0,1},{1,0},{2,3},{3,2},{4,5},{5,4},{6,7},{7,6},{8,9},{9,8},{10,11... | collective-permute-start | bytes 1179656 | tf_op jit(solution)/shard_map/ppermute | solution.py:286
  64.4 7.5 %collective-permute-start.19 = (bf16[48,512]{1,0:T(8,128)(2,1)S(1)}, bf16[48,512]{1,0:T(8,128)(2,1)S(1)}, u32[]{:S(2)}, u32[]{:S(2)}) collective-permute-start(bf16[48,512]{1,0:T(8,128)(2,1)S(1)} %get-tuple-element.46), channel_id=1, source_target_pairs={{0,12},{4,0},{8,4},{12,8},{1,13},{5,1},{9,5},{13,9},{2,14},{6,2},{... | collective-permute-start | bytes 147464 | tf_op jit(solution)/shard_map/ppermute | solution.py:291
  67.3 5.9 %collective-permute-start.18 = (bf16[48,512]{1,0:T(8,128)(2,1)S(1)}, bf16[48,512]{1,0:T(8,128)(2,1)S(1)}, u32[]{:S(2)}, u32[]{:S(2)}) collective-permute-start(bf16[48,512]{1,0:T(8,128)(2,1)S(1)} %get-tuple-element.39), channel_id=1, source_target_pairs={{0,4},{4,8},{8,12},{12,0},{1,5},{5,9},{9,13},{13,1},{2,6},{6,10},{... | collective-permute-start | bytes 147464 | tf_op jit(solution)/shard_map/ppermute | solution.py:291
  67.3 4.6 %collective-permute-start.20 = (bf16[16,512]{1,0:T(8,128)(2,1)S(1)}, bf16[16,512]{1,0:T(8,128)(2,1)S(1)}, u32[]{:S(2)}, u32[]{:S(2)}) collective-permute-start(bf16[16,512]{1,0:T(8,128)(2,1)S(1)} %get-tuple-element.47), channel_id=1, source_target_pairs={{0,8},{4,12},{8,0},{12,4},{1,9},{5,13},{9,1},{13,5},{2,10},{6,14},... | collective-permute-start | bytes 49160 | tf_op jit(solution)/shard_map/ppermute | solution.py:291
  (27 other events, 161.6 us)

commit v4 on v3

--- a/solution.py
+++ b/solution.py
@@ -59,14 +59,14 @@
     copies.start(second.at[layer], second_ref.at[pl.ds(j * part, part)])
 
 
-def load_packed(copies, packed, j, first_ref, second_ref):
+def load_packed(copies, packed, base, j, first_ref, second_ref):
     rows = first_ref.shape[0]
     hidden, features = second_ref.shape
     part = hidden // 4
-    copies.start(packed.at[pl.ds(0, rows)], first_ref.at[:, pl.ds(j * part, part)])
+    copies.start(packed.at[pl.ds(base, rows)], first_ref.at[:, pl.ds(j * part, part)])
     for q in range(features // part):
         copies.start(
-            packed.at[pl.ds(rows + q * part, part)],
+            packed.at[pl.ds(base + rows + q * part, part)],
             second_ref.at[pl.ds(j * part, part), pl.ds(q * part, part)],
         )
 
@@ -105,14 +105,26 @@
     copies.wait()
 
 
-def pack_kernel(ef, es, nf, ns, edge_out, node_out, sems):
+def prepare_kernel(index_ref, receiver_ref, ef, es, nf, ns, hot_out, incidence_out, late_out, sems):
     part, features = es.shape[1:]
     copies = Copies(sems)
-    for first, second, out in ((ef, es, edge_out), (nf, ns, node_out)):
+    at = 0
+    for first, second in ((ef, es), (nf, ns)):
         rows = first.shape[1]
-        copies.start(first.at[1], out.at[pl.ds(0, rows)])
+        copies.start(first.at[1], late_out.at[pl.ds(at, rows)])
+        at += rows
         for q in range(features // part):
-            copies.start(second.at[1, :, pl.ds(q * part, part)], out.at[pl.ds(rows + q * part, part)])
+            copies.start(second.at[1, :, pl.ds(q * part, part)], late_out.at[pl.ds(at, part)])
+            at += part
+    for at in range(0, hot_out.shape[0], TILE):
+        rows = slice(at, at + TILE)
+        index = index_ref[rows, :]
+        lanes = lax.broadcasted_iota(jnp.int32, (TILE, hot_out.shape[1]), 1)
+        hot = (lanes == index[:, 0:1]) | (lanes == index[:, 1:2])
+        hot_out[rows, :] = jnp.where(hot, 1.0, 0.0).astype(BF16)
+        node_ids = lax.broadcasted_iota(jnp.int32, (incidence_out.shape[0], TILE), 0)
+        hit = node_ids == receiver_ref[:, rows]
+        incidence_out[:, rows] = jnp.where(hit, 1.0, 0.0).astype(BF16)
     copies.wait()
 
 
@@ -141,7 +153,7 @@
         at += piece.shape[0]
 
 
-def edge_rows(spot_ref, edge_ref, table, nodes, own_ref, index_ref, receiver_ref, first_ref, second_ref, product_ref, own_out, full_out):
+def edge_rows(spot_ref, edge_ref, table, nodes, own_ref, hot_ref, incidence_ref, first_ref, second_ref, product_ref, own_out, full_out):
     features = second_ref.shape[1]
     node_count = nodes.shape[0]
     table_rows = table.shape[0]
@@ -158,20 +170,13 @@
     for at in range(0, own_ref.shape[0], TILE):
         rows = slice(at, at + TILE)
         edge_bf = edge_ref[rows, :]
-        index = index_ref[rows, :]
-        lanes = lax.broadcasted_iota(jnp.int32, (TILE, lanes_all), 1)
-        hot = (lanes == index[:, 0:1]) | (lanes == index[:, 1:2])
-        pre = dot(edge_bf, first_ref[0:features, :]) + dot(
-            jnp.where(hot, 1.0, 0.0).astype(BF16), product_ref[...]
-        )
+        pre = dot(edge_bf, first_ref[0:features, :]) + dot(hot_ref[rows, :], product_ref[...])
         norm = normalize(dot(silu(pre).astype(BF16), second_ref[...]))
         edge_new = (edge_bf.astype(F32) + norm).astype(BF16)
         if full_out is not None:
             full_out[rows, :] = edge_new
         own_out[rows, :] = own_ref[rows, :] + own_columns(norm, spot_ref, part)
-        node_ids = lax.broadcasted_iota(jnp.int32, (node_count, TILE), 0)
-        incidence = jnp.where(node_ids == receiver_ref[:, rows], 1.0, 0.0).astype(BF16)
-        incoming = incoming + dot(incidence, edge_new)
+        incoming = incoming + dot(incidence_ref[:, rows], edge_new)
     return incoming.astype(BF16)
 
 
@@ -189,7 +194,7 @@
     core_w = [refs.pop(0) for _ in range(4)]
     halves = [[refs.pop(0) for _ in range(2)] for _ in range(2)]
     shards = [refs.pop(0) for _ in range(4)]
-    edge_own, node_own, index_ref, receiver_ref, wanted_ref = [refs.pop(0) for _ in range(5)]
+    edge_own, node_own, hot_ref, incidence_ref, wanted_ref = [refs.pop(0) for _ in range(5)]
     edge_out, full_out, node_out, node_full = [refs.pop(0) for _ in range(4)]
     sends = [refs.pop(0) for _ in range(3)]
     edge_w, edge_w2, node_w, node_w2, product_ref, x_ref, edge_sems, node_sems = refs
@@ -216,7 +221,7 @@
     edge_copies.wait()
     nodes = x_ref[edge_count : edge_count + node_count, :]
     incoming = edge_rows(
-        spot_ref, x_ref, x_ref[edge_count:, :], nodes, edge_own, index_ref, receiver_ref,
+        spot_ref, x_ref, x_ref[edge_count:, :], nodes, edge_own, hot_ref, incidence_ref,
         edge_w, edge_w2, product_ref, edge_out, full_out,
     )
     node_copies.wait()
@@ -225,42 +230,38 @@
     pick_rows(wanted_ref, node_new, sends)
 
 
-def late_weights(copies, refs, first, second):
-    load_shard(copies, 1, refs[0], refs[1], 0, first, second)
-    load_shard(copies, 1, refs[2], refs[3], 1, first, second)
-    load_packed(copies, refs[4], 2, first, second)
-    load_packed(copies, refs[5], 3, first, second)
-
-
-def late_edge_kernel(pieces, spot_ref, *refs):
+def late_kernel(pieces, spot_ref, *refs):
     refs = list(refs)
-    weights = [refs.pop(0) for _ in range(6)]
-    edge_ref, own_ref = refs.pop(0), refs.pop(0)
+    own_w = [refs.pop(0) for _ in range(4)]
+    core_w = [refs.pop(0) for _ in range(4)]
+    packed = [refs.pop(0) for _ in range(2)]
+    edge_ref, edge_own, node_own = [refs.pop(0) for _ in range(3)]
     tables = [refs.pop(0) for _ in range(pieces)]
-    index_ref, receiver_ref = refs.pop(0), refs.pop(0)
-    own_out, incoming_out = refs.pop(0), refs.pop(0)
-    first_ref, second_ref, product_ref, table_ref, sems = refs
-    copies = Copies(sems)
-    late_weights(copies, weights, first_ref, second_ref)
+    hot_ref, incidence_ref, edge_out, node_out = [refs.pop(0) for _ in range(4)]
+    edge_w, edge_w2, node_w, node_w2, product_ref, table_ref, edge_sems, node_sems = refs
+    edge_copies, node_copies = Copies(edge_sems), Copies(node_sems)
+    base = 0
+    for copies, first, second, at in (
+        (edge_copies, edge_w, edge_w2, 0),
+        (node_copies, node_w, node_w2, 2),
+    ):
+        load_shard(copies, 1, own_w[at], own_w[at + 1], 0, first, second)
+        load_shard(copies, 1, core_w[at], core_w[at + 1], 1, first, second)
+        for j, pack in enumerate(packed):
+            load_packed(copies, pack, base, 2 + j, first, second)
+        base = edge_w.shape[0] + edge_w2.shape[1]
     start = 0
     for table in tables:
         table_ref[start : start + table.shape[0], :] = table[...]
         start += table.shape[0]
-    copies.wait()
-    incoming_out[...] = edge_rows(
-        spot_ref, edge_ref, table_ref[...], tables[0][...], own_ref, index_ref, receiver_ref,
-        first_ref, second_ref, product_ref, own_out, None,
-    )
-
-
-def late_node_kernel(spot_ref, *refs):
-    refs = list(refs)
-    weights = [refs.pop(0) for _ in range(6)]
-    node_ref, own_ref, incoming_ref, own_out, first_ref, second_ref, sems = refs
-    copies = Copies(sems)
-    late_weights(copies, weights, first_ref, second_ref)
-    copies.wait()
-    node_rows(spot_ref, node_ref[...], incoming_ref[...], own_ref, first_ref, second_ref, own_out)
+    edge_copies.wait()
+    nodes = tables[0][...]
+    incoming = edge_rows(
+        spot_ref, edge_ref, table_ref[...], nodes, edge_own, hot_ref, incidence_ref,
+        edge_w, edge_w2, product_ref, edge_out, None,
+    )
+    node_copies.wait()
+    node_rows(spot_ref, nodes, incoming, node_own, node_w, node_w2, node_out)
 
 
 SMEM, VMEM, HBM = pltpu.SMEM, pltpu.VMEM, pltpu.HBM
@@ -268,14 +269,15 @@
 
 def call(kernel, out_shape, args, scratch, flops, name, out_space=VMEM):
     arrays = [a for _, a in args]
+    out_spaces = out_space if isinstance(out_space, list) else [out_space] * len(out_shape)
     moved = sum(a.size * a.dtype.itemsize for a in arrays + list(out_shape))
     return pl.pallas_call(
         kernel,
         out_shape=out_shape,
         in_specs=[pl.BlockSpec(memory_space=s) for s, _ in args],
-        out_specs=[pl.BlockSpec(memory_space=out_space)] * len(out_shape),
+        out_specs=[pl.BlockSpec(memory_space=s) for s in out_spaces],
         scratch_shapes=scratch,
-        compiler_params=pltpu.CompilerParams(vmem_limit_bytes=40 * 1024 * 1024),
+        compiler_params=pltpu.CompilerParams(vmem_limit_bytes=60 * 1024 * 1024),
         cost_estimate=pl.CostEstimate(flops=flops, bytes_accessed=moved, transcendentals=0),
         name=name,
     )(*arrays)
@@ -377,34 +379,37 @@
         "boundary_rows",
     )
     halo_rows = neighbour_rows(right, left, coarse, halo)
-    edge_late, node_late = call(
-        pack_kernel,
-        [shape((edge_pack, part), BF16), shape((node_pack, part), BF16)],
-        [(HBM, after(weights[0], right))] + [(HBM, w) for w in weights[1:]],
+    table_rows = node_count + sum(r.shape[0] for r in halo_rows)
+    lanes = -(-(table_rows + node_count) // 128) * 128
+    index = jnp.stack([table_index(senders, node_count, halo), receivers + table_rows], axis=1)
+    hot, incidence, late_w = call(
+        prepare_kernel,
+        [
+            shape((edge_count, lanes), BF16),
+            shape((node_count, edge_count), BF16),
+            shape((edge_pack + node_pack, part), BF16),
+        ],
+        [(VMEM, after(index, right)), (VMEM, receivers[None, :])] + [(HBM, w) for w in weights],
         [dma((10,))],
         0,
-        "layer_1_packed",
-        HBM,
+        "one_hot",
+        [VMEM, VMEM, HBM],
     )
     core_w = [swap(after(w, right), 1) for w in weights]
-    table_rows = node_count + sum(r.shape[0] for r in halo_rows)
     (latents,) = call(
         latent_kernel,
         [shape((edge_count + table_rows, part), BF16)],
-        [(VMEM, edge_state), (VMEM, node_bf)] + [(VMEM, r) for r in halo_rows],
+        [(VMEM, after(edge_state, late_w)), (VMEM, node_bf)] + [(VMEM, r) for r in halo_rows],
         [],
         0,
         "latents",
     )
-    far_latents = swap(after(latents, near), 2)
+    far_latents = swap(after(latents, near, *core_w), 2)
     shards = [latents, swap(latents, 1), far_latents, swap(far_latents, 1)]
     far = lax.ppermute(near, "groups", [(0, 1), (1, 0)])
     pairs = [near, far, swap(near, 1), swap(far, 1)]
-    edge_late_x = swap(after(edge_late, far_latents), 2)
-
-    index = jnp.stack([table_index(senders, node_count, halo), receivers + table_rows], axis=1)
-    receiver_row = receivers[None, :]
-    lanes = -(-(table_rows + node_count) // 128) * 128
+    late_x = swap(after(late_w, far_latents), 2)
+
     edge_flops = 2 * edge_count * features * (2 * features + lanes + node_count)
     node_flops = 2 * node_count * features * 3 * features
     full_edge = shape((edge_count, features), BF16)
@@ -420,7 +425,7 @@
         [own_edge, full_edge, own_node, full_node] + sent(features),
         [(SMEM, spot)]
         + [(HBM, w) for w in list(weights) + core_w + pairs + shards]
-        + [(VMEM, a) for a in (edge_state, node_state, index, receiver_row, wanted)],
+        + [(VMEM, a) for a in (edge_state, node_state, hot, incidence, wanted)],
         [
             edge_shape,
             second_shape,
@@ -434,37 +439,28 @@
         edge_flops + node_flops,
         "layer_0",
     )
-    edge_late_d = swap(after(edge_late_x, right), 1)
-    node_late_x = swap(after(node_late, edge_late_x, right), 2)
-    node_late_d = swap(node_late_x, 1)
     tables = [node_full] + neighbour_rows(right, left, coarse, halo)
-    edge_own, incoming = call(
-        functools.partial(late_edge_kernel, len(tables)),
-        [own_edge, full_node],
+    late_d = swap(after(late_x, tables[1]), 1)
+    edge_own, node_own = call(
+        functools.partial(late_kernel, len(tables)),
+        [own_edge, own_node],
         [(SMEM, spot)]
-        + [(HBM, w) for w in (*weights[:2], *core_w[:2], edge_late_x, edge_late_d)]
-        + [(VMEM, edge_full), (VMEM, edge_own)]
+        + [(HBM, w) for w in list(weights) + core_w + [late_x, late_d]]
+        + [(VMEM, a) for a in (edge_full, edge_own, node_own)]
         + [(VMEM, t) for t in tables]
-        + [(VMEM, index), (VMEM, receiver_row)],
+        + [(VMEM, hot), (VMEM, incidence)],
         [
             edge_shape,
+            second_shape,
+            node_shape,
             second_shape,
             pltpu.VMEM((lanes, hidden), BF16),
             pltpu.VMEM((table_rows, features), BF16),
             dma((14,)),
+            dma((14,)),
         ],
-        edge_flops,
-        "layer_1_edges",
-    )
-    (node_own,) = call(
-        late_node_kernel,
-        [own_node],
-        [(SMEM, spot)]
-        + [(HBM, w) for w in (*weights[2:], *core_w[2:], node_late_x, node_late_d)]
-        + [(VMEM, node_full), (VMEM, node_own), (VMEM, incoming)],
-        [node_shape, second_shape, dma((14,))],
-        node_flops,
-        "layer_1_nodes",
+        edge_flops + node_flops,
+        "layer_1",
     )
     return (node_own, edge_own)
 

time: 84.7 us -> 124 us (1.46)
  Pallas kernels: 22.3 us -> 74.2 us
  local copies, waits for them, and re-layouts: 14.7 us -> 5.55 us
  starting transfers between devices: 17.7 us -> 16.1 us
  waiting for transfers between devices: 28.2 us -> 26.6 us
    pallas_call x7 -> x6, Pallas kernels: 22.3 us -> 74.2 us  [call(): pl.pallas_call(kernel, out_shape=out_shape, in_specs=[pl.BlockSpec(memory...]
    unnamed x60 -> x46, local copies, waits for them, and re-layouts: 14.1 us -> 2.08 us
    ppermute x1, waiting for transfers between devices: 7.86 us -> 0.01 us  [on_device(): far = lax.ppermute(near, 'groups', [(0, 1), (1, 0)])]
    ppermute x14 -> x12, starting transfers between devices: 8.11 us -> 4.78 us  [swap(): return lax.ppermute(x, 'mp', [(i, i ^ mask) for i in range(size)])]
    ppermute x14 -> x12, waiting for transfers between devices: 10.6 us -> 13.9 us  [swap(): return lax.ppermute(x, 'mp', [(i, i ^ mask) for i in range(size)])]
    ppermute x6, waiting for transfers between devices: 9.8 us -> 12.7 us  [shift(): return lax.ppermute(x, 'graph', [(i, (i + by) % size) for i in range(size)])]
    ppermute x6, starting transfers between devices: 8.07 us -> 9.79 us  [shift(): return lax.ppermute(x, 'graph', [(i, (i + by) % size) for i in range(size)])]
  transfers between devices with their start and end apart: 21 -> 19, of which waited for: 7 -> 6; matrix products, arithmetic and copies ran while one was open for 1% -> 1% of each run, Pallas kernels for 22% -> 37%
where the time goes in v4:
time: 124 us
  Pallas kernels  74.2 us (60%)
  waiting for transfers between devices  26.6 us (21%)
  starting transfers between devices  16.1 us (13%)
  local copies, waits for them, and re-layouts  5.55 us (4%)
    pallas_call x6, Pallas kernels, call(): pl.pallas_call(kernel, out_shape=out_shape, in_specs=[pl.BlockSpec(memory...  74.2 us
    ppermute x12, waiting for transfers between devices, swap(): return lax.ppermute(x, 'mp', [(i, i ^ mask) for i in range(size)])  13.9 us
    ppermute x6, waiting for transfers between devices, shift(): return lax.ppermute(x, 'graph', [(i, (i + by) % size) for i in range(size)])  12.7 us
    ppermute x6, starting transfers between devices, shift(): return lax.ppermute(x, 'graph', [(i, (i + by) % size) for i in range(size)])  9.79 us
    ppermute x12, starting transfers between devices, swap(): return lax.ppermute(x, 'mp', [(i, i ^ mask) for i in range(size)])  4.78 us
  transfers between devices with their start and end apart: 19, of which 6 were waited for; matrix products, arithmetic and copies ran while one was open for 1% of the time, Pallas kernels for 37%

profile of v4, /device:TPU:0, one launch (start us, length us, event | category | flops | bytes accessed | tf_op | source)
XLA Modules:
  0.0 124.1 jit_solution(4562956934882722750)
XLA Ops:
  0.7 0.9 fusion.5
  1.7 0.7 copy.17.wanted_ref.refs_20_
  3.0 15.8 %layer_0_half.1 = bf16[1792,128]{1,0:T(8,128)(2,1)} custom-call(s32[3]{0:T(128)} %pad_add_fusion.1.spot_ref, bf16[2,1536,128]{2,1,0:T(8,128)(2,1)} %refs_0_.3, bf16[2,128,512]{2,1,0:T(8,128)(2,1)} %refs_1_.3, bf16[2,1024,128]{2,1,0:T(8,128)(2,1)} %refs_2_.3, bf16[2,128,512]{2,1,0:T(8,128)(2,1)} %refs_3_.3), custom_call_target="tpu_custom_call" | custom-call | bytes 2293772 | tf_op jit(solution)/shard_map/layer_0_half/pallas_call | solution.py:274
  18.7 1.7 %boundary_rows.1 = (bf16[192,128]{1,0:T(8,128)(2,1)}, bf16[48,128]{1,0:T(8,128)(2,1)}, bf16[48,128]{1,0:T(8,128)(2,1)}, bf16[16,128]{1,0:T(8,128)(2,1)}) custom-call(f32[192,128]{1,0:T(8,128)} %refs_17_.1, s32[112,1]{1,0:T(8,128)} %copy.17.wanted_ref.refs_20_), custom_call_target="tpu_custom_call" | custom-call | flops 5505024 | bytes 176576 | tf_op jit(solution)/shard_map/boundary_rows/pallas_call | solution.py:274
  20.9 3.7 %collective-permute-start.6 = (bf16[16,128]{1,0:T(8,128)(2,1)}, bf16[16,128]{1,0:T(8,128)(2,1)S(1)}, u32[]{:S(2)}, u32[]{:S(2)}) collective-permute-start(bf16[16,128]{1,0:T(8,128)(2,1)} %get-tuple-element.39), channel_id=1, source_target_pairs={{0,8},{4,12},{8,0},{12,4},{1,9},{5,13},{9,1},{13,5},{2,10},{6,14},... | collective-permute-start | bytes 12296 | tf_op jit(solution)/shard_map/ppermute | solution.py:293
  24.5 1.6 %collective-permute-start.4 = (bf16[48,128]{1,0:T(8,128)(2,1)}, bf16[48,128]{1,0:T(8,128)(2,1)S(1)}, u32[]{:S(2)}, u32[]{:S(2)}) collective-permute-start(bf16[48,128]{1,0:T(8,128)(2,1)} %get-tuple-element.29), channel_id=1, source_target_pairs={{0,4},{4,8},{8,12},{12,0},{1,5},{5,9},{9,13},{13,1},{2,6},{6,10},{... | collective-permute-start | bytes 36872 | tf_op jit(solution)/shard_map/ppermute | solution.py:293
  26.1 1.5 %collective-permute-start.7 = (bf16[1792,128]{1,0:T(8,128)(2,1)}, bf16[1792,128]{1,0:T(8,128)(2,1)}, u32[]{:S(2)}, u32[]{:S(2)}) collective-permute-start(bf16[1792,128]{1,0:T(8,128)(2,1)} %layer_0_half.1), channel_id=1, source_target_pairs={{0,2},{1,3},{2,0},{3,1},{4,6},{5,7},{6,4},{7,5},{8,10},{9,11},{10,... | collective-permute-start | bytes 1376264 | tf_op jit(solution)/shard_map/ppermute | solution.py:288
  27.6 2.2 %collective-permute-start.5 = (bf16[48,128]{1,0:T(8,128)(2,1)}, bf16[48,128]{1,0:T(8,128)(2,1)S(1)}, u32[]{:S(2)}, u32[]{:S(2)}) collective-permute-start(bf16[48,128]{1,0:T(8,128)(2,1)} %get-tuple-element.38), channel_id=1, source_target_pairs={{0,12},{4,0},{8,4},{12,8},{1,13},{5,1},{9,5},{13,9},{2,14},{6,2},{... | collective-permute-start | bytes 36872 | tf_op jit(solution)/shard_map/ppermute | solution.py:293
  30.0 1.5 %collective-permute-done.5.refs_2_ = bf16[48,128]{1,0:T(8,128)(2,1)S(1)} collective-permute-done((bf16[48,128]{1,0:T(8,128)(2,1)}, bf16[48,128]{1,0:T(8,128)(2,1)S(1)}, u32[]{:S(2)}, u32[]{:S(2)}) %collective-permute-start.5) | collective-permute-done | bytes 12320 | tf_op jit(solution)/shard_map/ppermute | solution.py:293
  32.1 0.6 broadcast_in_dim.22.receiver_ref
  32.7 1.2 copy.18.index_ref
  33.9 31.5 %one_hot.1 = (bf16[1536,512]{1,0:T(8,128)(2,1)}, bf16[192,1536]{1,0:T(8,128)(2,1)}, bf16[3584,128]{1,0:T(8,128)(2,1)}) custom-call(s32[1536,2]{1,0:T(8,128)} %copy.18.index_ref, s32[1,1536]{1,0:T(1,128)} %broadcast_in_dim.22.receiver_ref, bf16[2,1536,128]{2,1,0:T(8,128)(2,1)} %refs_0_.3, bf16[2,128,512]{2,1,0:T(8,128)(2,1)} %refs_1_.3, ...), custom_call_target="tpu_custom_call" | custom-call | bytes 4933632 | tf_op jit(solution)/shard_map/one_hot/pallas_call | solution.py:274
  65.4 2.0 %latents.1.refs_12_ = bf16[1840,128]{1,0:T(8,128)(2,1)} custom-call(f32[1536,128]{1,0:T(8,128)} %refs_16_.1, bf16[192,128]{1,0:T(8,128)(2,1)} %get-tuple-element.37.refs_0_, bf16[48,128]{1,0:T(8,128)(2,1)} %copy-done.5, bf16[48,128]{1,0:T(8,128)(2,1)} %copy-done.6, bf16[16,128]{1,0:T(8,128)(2,1)} %copy-done.8), custom_call_target="tpu_custom_call" | custom-call | bytes 1335296 | tf_op jit(solution)/shard_map/latents/pallas_call | solution.py:274
  67.5 0.6 collective-permute-start.8
  68.1 1.5 %collective-permute-start.10 = (bf16[1792,128]{1,0:T(8,128)(2,1)}, bf16[1792,128]{1,0:T(8,128)(2,1)S(1)}, u32[]{:S(2)}, u32[]{:S(2)}) collective-permute-start(bf16[1792,128]{1,0:T(8,128)(2,1)} %collective-permute-done.7.refs_8_), channel_id=1, source_target_pairs={{0,16},{16,0},{1,17},{17,1},{2,18},{18,2},{3,19},{19,3},{4,20},{20... | collective-permute-start | bytes 1376264 | tf_op jit(solution)/shard_map/ppermute | solution.py:409
  69.6 10.9 %collective-permute-done.8.refs_14_ = bf16[1840,128]{1,0:T(8,128)(2,1)S(1)} collective-permute-done((bf16[1840,128]{1,0:T(8,128)(2,1)}, bf16[1840,128]{1,0:T(8,128)(2,1)S(1)}, u32[]{:S(2)}, u32[]{:S(2)}) %collective-permute-start.8) | collective-permute-done | bytes 471072 | tf_op jit(solution)/shard_map/ppermute | solution.py:288
  82.0 1.7 %collective-permute-done.13.refs_13_ = bf16[1840,128]{1,0:T(8,128)(2,1)S(1)} collective-permute-done((bf16[1840,128]{1,0:T(8,128)(2,1)}, bf16[1840,128]{1,0:T(8,128)(2,1)S(1)}, u32[]{:S(2)}, u32[]{:S(2)}) %collective-permute-start.13) | collective-permute-done | bytes 471072 | tf_op jit(solution)/shard_map/ppermute | solution.py:288
  83.7 1.3 %collective-permute-done.11.refs_10_ = bf16[1792,128]{1,0:T(8,128)(2,1)S(1)} collective-permute-done((bf16[1792,128]{1,0:T(8,128)(2,1)}, bf16[1792,128]{1,0:T(8,128)(2,1)S(1)}, u32[]{:S(2)}, u32[]{:S(2)}) %collective-permute-start.11) | collective-permute-done | bytes 458784 | tf_op jit(solution)/shard_map/ppermute | solution.py:288
  85.0 0.8 copy-done.17
  86.1 11.9 %layer_0.1 = (f32[1536,128]{1,0:T(8,128)}, bf16[1536,512]{1,0:T(8,128)(2,1)}, f32[192,128]{1,0:T(8,128)}, bf16[192,512]{1,0:T(8,128)(2,1)}, bf16[48,512]{1,0:T(8...) custom-call(s32[3]{0:T(128)} %pad_add_fusion.1.spot_ref, bf16[2,1536,128]{2,1,0:T(8,128)(2,1)} %refs_0_.3, ...), custom_call_target="tpu_custom_call" | custom-call | flops 3019898880 | bytes 13205964 | tf_op jit(solution)/shard_map/layer_0/pallas_call | solution.py:274
  98.1 6.3 %collective-permute-done.15.refs_14_ = bf16[48,512]{1,0:T(8,128)(2,1)S(1)} collective-permute-done((bf16[48,512]{1,0:T(8,128)(2,1)}, bf16[48,512]{1,0:T(8,128)(2,1)S(1)}, u32[]{:S(2)}, u32[]{:S(2)}) %collective-permute-start.15) | collective-permute-done | bytes 49184 | tf_op jit(solution)/shard_map/ppermute | solution.py:293
  104.5 2.3 %collective-permute-start.17 = (bf16[48,512]{1,0:T(8,128)(2,1)}, bf16[48,512]{1,0:T(8,128)(2,1)S(1)}, u32[]{:S(2)}, u32[]{:S(2)}) collective-permute-start(bf16[48,512]{1,0:T(8,128)(2,1)} %get-tuple-element.50), channel_id=1, source_target_pairs={{0,12},{4,0},{8,4},{12,8},{1,13},{5,1},{9,5},{13,9},{2,14},{6,2},{... | collective-permute-start | bytes 147464 | tf_op jit(solution)/shard_map/ppermute | solution.py:293
  106.8 4.8 %collective-permute-done.18.refs_16_ = bf16[16,512]{1,0:T(8,128)(2,1)S(1)} collective-permute-done((bf16[16,512]{1,0:T(8,128)(2,1)}, bf16[16,512]{1,0:T(8,128)(2,1)S(1)}, u32[]{:S(2)}, u32[]{:S(2)}) %collective-permute-start.18) | collective-permute-done | bytes 16416 | tf_op jit(solution)/shard_map/ppermute | solution.py:293
  112.7 11.3 %layer_1.1 = (f32[1536,128]{1,0:T(8,128)}, f32[192,128]{1,0:T(8,128)}) custom-call(s32[3]{0:T(128)} %pad_add_fusion.1.spot_ref, bf16[2,1536,128]{2,1,0:T(8,128)(2,1)} %refs_0_.3, bf16[2,128,512]{2,1,0:T(8,128)(2,1)} %refs_1_.3, bf16[2,1024,128]{2,1,0:T(8,128)(2,1)} %refs_2_.3, bf16[2,128,512]{2,1,0:T(8,128)(2,1)} %refs_3_.3, ...), custom_call_target="tpu_custom_call" | custom-call | flops 3019898880 | bytes 11321356 | tf_op jit(solution)/shard_map/layer_1/pallas_call | solution.py:274
  (79 shorter events, 4.8 us)
Async XLA Ops:
  0.6 30.9 %copy-start.3 = (bf16[2,128,512]{2,1,0:T(8,128)(2,1)S(1)}, bf16[2,128,512]{2,1,0:T(8,128)(2,1)}, u32[]{:S(2)}) copy-start(bf16[2,128,512]{2,1,0:T(8,128)(2,1)} %refs_3_.3) | copy-start | bytes 786436
  0.7 31.4 %copy-start.4 = (s32[1536]{0:T(1024)S(1)}, s32[1536]{0:T(1024)}, u32[]{:S(2)}) copy-start(s32[1536]{0:T(1024)} %param.16) | copy-start | bytes 18436
  20.4 47.0 %collective-permute-start = (bf16[2,1536,128]{2,1,0:T(8,128)(2,1)S(1)}, bf16[2,1536,128]{2,1,0:T(8,128)(2,1)S(1)}, u32[]{:S(2)}, u32[]{:S(2)}) collective-permute-start(bf16[2,1536,128]{2,1,0:T(8,128)(2,1)S(1)} %copy-done), channel_id=1, source_target_pairs={{0,1},{1,0},{2,3},{3,2},{4,5},{5,4},{6,7},{7,6},{8,9},{9,8},{10,11... | collective-permute-start | bytes 2359304 | tf_op jit(solution)/shard_map/ppermute | solution.py:288
  20.9 9.0 %collective-permute-start.6 = (bf16[16,128]{1,0:T(8,128)(2,1)}, bf16[16,128]{1,0:T(8,128)(2,1)S(1)}, u32[]{:S(2)}, u32[]{:S(2)}) collective-permute-start(bf16[16,128]{1,0:T(8,128)(2,1)} %get-tuple-element.39), channel_id=1, source_target_pairs={{0,8},{4,12},{8,0},{12,4},{1,9},{5,13},{9,1},{13,5},{2,10},{6,14},... | collective-permute-start | bytes 12296 | tf_op jit(solution)/shard_map/ppermute | solution.py:293
  24.5 7.0 %collective-permute-start.4 = (bf16[48,128]{1,0:T(8,128)(2,1)}, bf16[48,128]{1,0:T(8,128)(2,1)S(1)}, u32[]{:S(2)}, u32[]{:S(2)}) collective-permute-start(bf16[48,128]{1,0:T(8,128)(2,1)} %get-tuple-element.29), channel_id=1, source_target_pairs={{0,4},{4,8},{8,12},{12,0},{1,5},{5,9},{9,13},{13,1},{2,6},{6,10},{... | collective-permute-start | bytes 36872 | tf_op jit(solution)/shard_map/ppermute | solution.py:293
  26.1 41.3 %collective-permute-start.7 = (bf16[1792,128]{1,0:T(8,128)(2,1)}, bf16[1792,128]{1,0:T(8,128)(2,1)}, u32[]{:S(2)}, u32[]{:S(2)}) collective-permute-start(bf16[1792,128]{1,0:T(8,128)(2,1)} %layer_0_half.1), channel_id=1, source_target_pairs={{0,2},{1,3},{2,0},{3,1},{4,6},{5,7},{6,4},{7,5},{8,10},{9,11},{10,... | collective-permute-start | bytes 1376264 | tf_op jit(solution)/shard_map/ppermute | solution.py:288
  27.6 3.9 %collective-permute-start.5 = (bf16[48,128]{1,0:T(8,128)(2,1)}, bf16[48,128]{1,0:T(8,128)(2,1)S(1)}, u32[]{:S(2)}, u32[]{:S(2)}) collective-permute-start(bf16[48,128]{1,0:T(8,128)(2,1)} %get-tuple-element.38), channel_id=1, source_target_pairs={{0,12},{4,0},{8,4},{12,8},{1,13},{5,1},{9,5},{13,9},{2,14},{6,2},{... | collective-permute-start | bytes 36872 | tf_op jit(solution)/shard_map/ppermute | solution.py:293
  29.9 35.5 %copy-start.8 = (bf16[16,128]{1,0:T(8,128)(2,1)}, bf16[16,128]{1,0:T(8,128)(2,1)S(1)}, u32[]{:S(2)}) copy-start(bf16[16,128]{1,0:T(8,128)(2,1)S(1)} %collective-permute-done.6.refs_3_) | copy-start | bytes 12292
  29.9 37.6 %collective-permute-start.2 = (bf16[2,1024,128]{2,1,0:T(8,128)(2,1)S(1)}, bf16[2,1024,128]{2,1,0:T(8,128)(2,1)S(1)}, u32[]{:S(2)}, u32[]{:S(2)}) collective-permute-start(bf16[2,1024,128]{2,1,0:T(8,128)(2,1)S(1)} %copy-done.1), channel_id=1, source_target_pairs={{0,1},{1,0},{2,3},{3,2},{4,5},{5,4},{6,7},{7,6},{8,9},{9,8},{10,11... | collective-permute-start | bytes 1572872 | tf_op jit(solution)/shard_map/ppermute | solution.py:288
  31.5 33.9 %copy-start.6 = (bf16[48,128]{1,0:T(8,128)(2,1)}, bf16[48,128]{1,0:T(8,128)(2,1)S(1)}, u32[]{:S(2)}) copy-start(bf16[48,128]{1,0:T(8,128)(2,1)S(1)} %collective-permute-done.5.refs_2_) | copy-start | bytes 36868
  31.5 35.9 %collective-permute-start.1 = (bf16[2,128,512]{2,1,0:T(8,128)(2,1)S(1)}, bf16[2,128,512]{2,1,0:T(8,128)(2,1)S(1)}, u32[]{:S(2)}, u32[]{:S(2)}) collective-permute-start(bf16[2,128,512]{2,1,0:T(8,128)(2,1)S(1)} %copy-done.2), channel_id=1, source_target_pairs={{0,1},{1,0},{2,3},{3,2},{4,5},{5,4},{6,7},{7,6},{8,9},{9,8},{10,11... | collective-permute-start | bytes 786440 | tf_op jit(solution)/shard_map/ppermute | solution.py:288
  31.5 33.9 %copy-start.5 = (bf16[48,128]{1,0:T(8,128)(2,1)}, bf16[48,128]{1,0:T(8,128)(2,1)S(1)}, u32[]{:S(2)}) copy-start(bf16[48,128]{1,0:T(8,128)(2,1)S(1)} %collective-permute-done.4.refs_1_) | copy-start | bytes 36868
  31.5 35.9 %collective-permute-start.3 = (bf16[2,128,512]{2,1,0:T(8,128)(2,1)S(1)}, bf16[2,128,512]{2,1,0:T(8,128)(2,1)}, u32[]{:S(2)}, u32[]{:S(2)}) collective-permute-start(bf16[2,128,512]{2,1,0:T(8,128)(2,1)S(1)} %copy-done.3), channel_id=1, source_target_pairs={{0,1},{1,0},{2,3},{3,2},{4,5},{5,4},{6,7},{7,6},{8,9},{9,8},{10,11... | collective-permute-start | bytes 786440 | tf_op jit(solution)/shard_map/ppermute | solution.py:288
  67.5 13.0 %collective-permute-start.8 = (bf16[1840,128]{1,0:T(8,128)(2,1)}, bf16[1840,128]{1,0:T(8,128)(2,1)S(1)}, u32[]{:S(2)}, u32[]{:S(2)}) collective-permute-start(bf16[1840,128]{1,0:T(8,128)(2,1)} %latents.1.refs_12_), channel_id=1, source_target_pairs={{0,2},{1,3},{2,0},{3,1},{4,6},{5,7},{6,4},{7,5},{8,10},{9,11},{10,... | collective-permute-start | bytes 1413128 | tf_op jit(solution)/shard_map/ppermute | solution.py:288
  68.1 13.4 %collective-permute-start.10 = (bf16[1792,128]{1,0:T(8,128)(2,1)}, bf16[1792,128]{1,0:T(8,128)(2,1)S(1)}, u32[]{:S(2)}, u32[]{:S(2)}) collective-permute-start(bf16[1792,128]{1,0:T(8,128)(2,1)} %collective-permute-done.7.refs_8_), channel_id=1, source_target_pairs={{0,16},{16,0},{1,17},{17,1},{2,18},{18,2},{3,19},{19,3},{4,20},{20... | collective-permute-start | bytes 1376264 | tf_op jit(solution)/shard_map/ppermute | solution.py:409
  80.5 24.0 %collective-permute-start.9 = (bf16[3584,128]{1,0:T(8,128)(2,1)}, bf16[3584,128]{1,0:T(8,128)(2,1)S(1)}, u32[]{:S(2)}, u32[]{:S(2)}) collective-permute-start(bf16[3584,128]{1,0:T(8,128)(2,1)} %get-tuple-element.41), channel_id=1, source_target_pairs={{0,2},{1,3},{2,0},{3,1},{4,6},{5,7},{6,4},{7,5},{8,10},{9,11},{10,... | collective-permute-start | bytes 2752520 | tf_op jit(solution)/shard_map/ppermute | solution.py:288
  81.0 2.7 %collective-permute-start.13 = (bf16[1840,128]{1,0:T(8,128)(2,1)}, bf16[1840,128]{1,0:T(8,128)(2,1)S(1)}, u32[]{:S(2)}, u32[]{:S(2)}) collective-permute-start(bf16[1840,128]{1,0:T(8,128)(2,1)} %latents.1.refs_12_), channel_id=1, source_target_pairs={{0,1},{1,0},{2,3},{3,2},{4,5},{5,4},{6,7},{7,6},{8,9},{9,8},{10,11... | collective-permute-start | bytes 1413128 | tf_op jit(solution)/shard_map/ppermute | solution.py:288
  81.0 4.0 %collective-permute-start.14 = (bf16[1840,128]{1,0:T(8,128)(2,1)S(1)}, bf16[1840,128]{1,0:T(8,128)(2,1)S(1)}, u32[]{:S(2)}, u32[]{:S(2)}) collective-permute-start(bf16[1840,128]{1,0:T(8,128)(2,1)S(1)} %collective-permute-done.8.refs_14_), channel_id=1, source_target_pairs={{0,1},{1,0},{2,3},{3,2},{4,5},{5,4},{6,7},{7,6},{8,9},{9,8},{10,11... | collective-permute-start | bytes 1413128 | tf_op jit(solution)/shard_map/ppermute | solution.py:288
  81.5 3.5 %collective-permute-start.11 = (bf16[1792,128]{1,0:T(8,128)(2,1)}, bf16[1792,128]{1,0:T(8,128)(2,1)S(1)}, u32[]{:S(2)}, u32[]{:S(2)}) collective-permute-start(bf16[1792,128]{1,0:T(8,128)(2,1)} %collective-permute-done.7.refs_8_), channel_id=1, source_target_pairs={{0,1},{1,0},{2,3},{3,2},{4,5},{5,4},{6,7},{7,6},{8,9},{9,8},{10,11... | collective-permute-start | bytes 1376264 | tf_op jit(solution)/shard_map/ppermute | solution.py:288
  81.5 3.5 %collective-permute-start.12 = (bf16[1792,128]{1,0:T(8,128)(2,1)S(1)}, bf16[1792,128]{1,0:T(8,128)(2,1)S(1)}, u32[]{:S(2)}, u32[]{:S(2)}) collective-permute-start(bf16[1792,128]{1,0:T(8,128)(2,1)S(1)} %collective-permute-done.10.refs_9_), channel_id=1, source_target_pairs={{0,1},{1,0},{2,3},{3,2},{4,5},{5,4},{6,7},{7,6},{8,9},{9,8},{10,11... | collective-permute-start | bytes 1376264 | tf_op jit(solution)/shard_map/ppermute | solution.py:288
  98.0 6.4 %collective-permute-start.15 = (bf16[48,512]{1,0:T(8,128)(2,1)}, bf16[48,512]{1,0:T(8,128)(2,1)S(1)}, u32[]{:S(2)}, u32[]{:S(2)}) collective-permute-start(bf16[48,512]{1,0:T(8,128)(2,1)} %get-tuple-element.44), channel_id=1, source_target_pairs={{0,4},{4,8},{8,12},{12,0},{1,5},{5,9},{9,13},{13,1},{2,6},{6,10},{... | collective-permute-start | bytes 147464 | tf_op jit(solution)/shard_map/ppermute | solution.py:293
  104.5 7.2 %collective-permute-start.16 = (bf16[3584,128]{1,0:T(8,128)(2,1)S(1)}, bf16[3584,128]{1,0:T(8,128)(2,1)S(1)}, u32[]{:S(2)}, u32[]{:S(2)}) collective-permute-start(bf16[3584,128]{1,0:T(8,128)(2,1)S(1)} %collective-permute-done.9.refs_8_), channel_id=1, source_target_pairs={{0,1},{1,0},{2,3},{3,2},{4,5},{5,4},{6,7},{7,6},{8,9},{9,8},{10,11... | collective-permute-start | bytes 2752520 | tf_op jit(solution)/shard_map/ppermute | solution.py:288
  104.5 7.1 %collective-permute-start.17 = (bf16[48,512]{1,0:T(8,128)(2,1)}, bf16[48,512]{1,0:T(8,128)(2,1)S(1)}, u32[]{:S(2)}, u32[]{:S(2)}) collective-permute-start(bf16[48,512]{1,0:T(8,128)(2,1)} %get-tuple-element.50), channel_id=1, source_target_pairs={{0,12},{4,0},{8,4},{12,8},{1,13},{5,1},{9,5},{13,9},{2,14},{6,2},{... | collective-permute-start | bytes 147464 | tf_op jit(solution)/shard_map/ppermute | solution.py:293
  106.8 4.8 %collective-permute-start.18 = (bf16[16,512]{1,0:T(8,128)(2,1)}, bf16[16,512]{1,0:T(8,128)(2,1)S(1)}, u32[]{:S(2)}, u32[]{:S(2)}) collective-permute-start(bf16[16,512]{1,0:T(8,128)(2,1)} %get-tuple-element.51), channel_id=1, source_target_pairs={{0,8},{4,12},{8,0},{12,4},{1,9},{5,13},{9,1},{13,5},{2,10},{6,14},... | collective-permute-start | bytes 49160 | tf_op jit(solution)/shard_map/ppermute | solution.py:293
  (18 other events, 195.3 us)

commit v5 on v4

--- a/solution.py
+++ b/solution.py
@@ -264,20 +264,19 @@
     node_rows(spot_ref, nodes, incoming, node_own, node_w, node_w2, node_out)
 
 
-SMEM, VMEM, HBM = pltpu.SMEM, pltpu.VMEM, pltpu.HBM
-
-
-def call(kernel, out_shape, args, scratch, flops, name, out_space=VMEM):
+SMEM, VMEM, ANY = pltpu.SMEM, pltpu.VMEM, pl.ANY
+
+
+def call(kernel, out_shape, args, scratch, flops, name, vmem_mib=24):
     arrays = [a for _, a in args]
-    out_spaces = out_space if isinstance(out_space, list) else [out_space] * len(out_shape)
     moved = sum(a.size * a.dtype.itemsize for a in arrays + list(out_shape))
     return pl.pallas_call(
         kernel,
         out_shape=out_shape,
         in_specs=[pl.BlockSpec(memory_space=s) for s, _ in args],
-        out_specs=[pl.BlockSpec(memory_space=s) for s in out_spaces],
+        out_specs=[pl.BlockSpec(memory_space=VMEM)] * len(out_shape),
         scratch_shapes=scratch,
-        compiler_params=pltpu.CompilerParams(vmem_limit_bytes=60 * 1024 * 1024),
+        compiler_params=pltpu.CompilerParams(vmem_limit_bytes=vmem_mib * 1024 * 1024),
         cost_estimate=pl.CostEstimate(flops=flops, bytes_accessed=moved, transcendentals=0),
         name=name,
     )(*arrays)
@@ -346,30 +345,31 @@
     group = lax.axis_index("groups")
     spot = jnp.stack([lax.axis_index("mp"), group, group * blocks + block]).astype(jnp.int32)
 
+    wide = halo + COARSE_PAD
+
+    def sent(width):
+        return [shape((n, width), BF16) for n in (wide, wide, COARSE_PAD)]
+
+    weights = (edge_first, edge_second, node_first, node_second)
+    edge_pack = edge_first.shape[1] + features
+    node_pack = node_first.shape[1] + features
+    (ride,) = call(
+        ride_kernel,
+        [shape(((edge_pack + node_pack) // 2, part), BF16)],
+        [(SMEM, spot)] + [(ANY, w) for w in weights],
+        [dma((10,))],
+        0,
+        "layer_0_half",
+        60,
+    )
+    near = swap(ride, 2)
+    boundary_rows = after(boundary_rows, ride)
     own_coarse = jnp.arange(node_count - COARSE_DEV, node_count, dtype=jnp.int32)
     padding = jnp.full((COARSE_PAD - COARSE_DEV,), -1, jnp.int32)
     coarse_list = jnp.concatenate([own_coarse, padding])
     wanted = jnp.concatenate(
         [boundary_rows[halo:], coarse_list, boundary_rows[:halo], coarse_list, coarse_list]
     )[:, None]
-    wide = halo + COARSE_PAD
-
-    def sent(width):
-        return [shape((n, width), BF16) for n in (wide, wide, COARSE_PAD)]
-
-    weights = (edge_first, edge_second, node_first, node_second)
-    edge_pack = edge_first.shape[1] + features
-    node_pack = node_first.shape[1] + features
-    (ride,) = call(
-        ride_kernel,
-        [shape(((edge_pack + node_pack) // 2, part), BF16)],
-        [(SMEM, spot)] + [(HBM, w) for w in weights],
-        [dma((10,))],
-        0,
-        "layer_0_half",
-        HBM,
-    )
-    near = swap(ride, 2)
     node_bf, right, left, coarse = call(
         start_kernel,
         [shape((node_count, part), BF16)] + sent(part),
@@ -381,6 +381,7 @@
     halo_rows = neighbour_rows(right, left, coarse, halo)
     table_rows = node_count + sum(r.shape[0] for r in halo_rows)
     lanes = -(-(table_rows + node_count) // 128) * 128
+    senders, receivers = lax.optimization_barrier((senders, receivers, right))[:2]
     index = jnp.stack([table_index(senders, node_count, halo), receivers + table_rows], axis=1)
     hot, incidence, late_w = call(
         prepare_kernel,
@@ -389,11 +390,10 @@
             shape((node_count, edge_count), BF16),
             shape((edge_pack + node_pack, part), BF16),
         ],
-        [(VMEM, after(index, right)), (VMEM, receivers[None, :])] + [(HBM, w) for w in weights],
+        [(VMEM, index), (VMEM, receivers[None, :])] + [(ANY, w) for w in weights],
         [dma((10,))],
         0,
         "one_hot",
-        [VMEM, VMEM, HBM],
     )
     core_w = [swap(after(w, right), 1) for w in weights]
     (latents,) = call(
@@ -424,7 +424,7 @@
         first_kernel,
         [own_edge, full_edge, own_node, full_node] + sent(features),
         [(SMEM, spot)]
-        + [(HBM, w) for w in list(weights) + core_w + pairs + shards]
+        + [(ANY, w) for w in list(weights) + core_w + pairs + shards]
         + [(VMEM, a) for a in (edge_state, node_state, hot, incidence, wanted)],
         [
             edge_shape,
@@ -445,7 +445,7 @@
         functools.partial(late_kernel, len(tables)),
         [own_edge, own_node],
         [(SMEM, spot)]
-        + [(HBM, w) for w in list(weights) + core_w + [late_x, late_d]]
+        + [(ANY, w) for w in list(weights) + core_w + [late_x, late_d]]
         + [(VMEM, a) for a in (edge_full, edge_own, node_own)]
         + [(VMEM, t) for t in tables]
         + [(VMEM, hot), (VMEM, incidence)],

time: 124 us -> 70.8 us (0.57)
  Pallas kernels: 74.2 us -> 22.2 us
  local copies, waits for them, and re-layouts: 5.55 us -> 1.41 us
  starting transfers between devices: 16.1 us -> 17.7 us
    pallas_call x6, Pallas kernels: 74.2 us -> 22.2 us  [call(): pl.pallas_call(kernel, out_shape=out_shape, in_specs=[pl.BlockSpec(memory...]
    unnamed x46 -> x22, local copies, waits for them, and re-layouts: 2.08 us -> 0.06 us
    ppermute x12, starting transfers between devices: 4.78 us -> 6.11 us  [swap(): return lax.ppermute(x, 'mp', [(i, i ^ mask) for i in range(size)])]
  transfers between devices with their start and end apart: 19 -> 19, of which waited for: 6 -> 9; matrix products, arithmetic and copies ran while one was open for 1% -> 2% of each run, Pallas kernels for 37% -> 15%
where the time goes in v5:
time: 70.8 us; the launch traced here: 70.5 us
  waiting for transfers between devices  26.9 us (38%)
  Pallas kernels  22.2 us (31%)
  starting transfers between devices  17.7 us (25%)
  local copies, waits for them, and re-layouts  1.41 us (2%)
  other arithmetic  1.3 us (2%)
  between operations  1.05 us (1%)
    pallas_call x6, Pallas kernels, call(): pl.pallas_call(kernel, out_shape=out_shape, in_specs=[pl.BlockSpec(memory...  22.2 us
    ppermute x12, waiting for transfers between devices, swap(): return lax.ppermute(x, 'mp', [(i, i ^ mask) for i in range(size)])  14.8 us
    ppermute x6, waiting for transfers between devices, shift(): return lax.ppermute(x, 'graph', [(i, (i + by) % size) for i in range(size)])  12.1 us
    ppermute x6, starting transfers between devices, shift(): return lax.ppermute(x, 'graph', [(i, (i + by) % size) for i in range(size)])  10 us
    ppermute x12, starting transfers between devices, swap(): return lax.ppermute(x, 'mp', [(i, i ^ mask) for i in range(size)])  6.11 us
    ppermute x1, starting transfers between devices, on_device(): far = lax.ppermute(near, 'groups', [(0, 1), (1, 0)])  1.52 us
  transfers between devices with their start and end apart: 19, of which 9 were waited for; matrix products, arithmetic and copies ran while one was open for 2% of the time, Pallas kernels for 15%

profile of v5, /device:TPU:0, one launch (start us, length us, event | category | flops | bytes accessed | tf_op | source)
XLA Modules:
  0.0 70.5 jit_solution(4770338859894154282)
XLA Ops:
  0.7 0.7 pad_add_fusion.1.spot_ref
  1.4 2.7 %layer_0_half.1 = bf16[1792,128]{1,0:T(8,128)(2,1)} custom-call(s32[3]{0:T(128)} %pad_add_fusion.1.spot_ref, bf16[2,1536,128]{2,1,0:T(8,128)(2,1)} %refs_0_.3, bf16[2,128,512]{2,1,0:T(8,128)(2,1)} %refs_1_.3, bf16[2,1024,128]{2,1,0:T(8,128)(2,1)} %refs_2_.3, bf16[2,128,512]{2,1,0:T(8,128)(2,1)} %refs_3_.3), custom_call_target="tpu_custom_call" | custom-call | bytes 2293772 | tf_op jit(solution)/shard_map/layer_0_half/pallas_call | solution.py:273
  4.6 0.5 collective-permute-start
  5.2 4.0 %collective-permute-start.6 = (bf16[16,128]{1,0:T(8,128)(2,1)S(1)}, bf16[16,128]{1,0:T(8,128)(2,1)S(1)}, u32[]{:S(2)}, u32[]{:S(2)}) collective-permute-start(bf16[16,128]{1,0:T(8,128)(2,1)S(1)} %get-tuple-element.43), channel_id=1, source_target_pairs={{0,8},{4,12},{8,0},{12,4},{1,9},{5,13},{9,1},{13,5},{2,10},{6,14},... | collective-permute-start | bytes 12296 | tf_op jit(solution)/shard_map/ppermute | solution.py:292
  9.2 1.3 %collective-permute-start.5 = (bf16[48,128]{1,0:T(8,128)(2,1)S(1)}, bf16[48,128]{1,0:T(8,128)(2,1)S(1)}, u32[]{:S(2)}, u32[]{:S(2)}) collective-permute-start(bf16[48,128]{1,0:T(8,128)(2,1)S(1)} %get-tuple-element.42), channel_id=1, source_target_pairs={{0,12},{4,0},{8,4},{12,8},{1,13},{5,1},{9,5},{13,9},{2,14},{6,2},{... | collective-permute-start | bytes 36872 | tf_op jit(solution)/shard_map/ppermute | solution.py:292
  10.6 0.7 collective-permute-start.4
  11.3 1.5 %collective-permute-start.7 = (bf16[1792,128]{1,0:T(8,128)(2,1)}, bf16[1792,128]{1,0:T(8,128)(2,1)}, u32[]{:S(2)}, u32[]{:S(2)}) collective-permute-start(bf16[1792,128]{1,0:T(8,128)(2,1)} %layer_0_half.1), channel_id=1, source_target_pairs={{0,2},{1,3},{2,0},{3,1},{4,6},{5,7},{6,4},{7,5},{8,10},{9,11},{10,... | collective-permute-start | bytes 1376264 | tf_op jit(solution)/shard_map/ppermute | solution.py:287
  13.0 3.1 %collective-permute-done.4.refs_1_ = bf16[48,128]{1,0:T(8,128)(2,1)S(1)} collective-permute-done((bf16[48,128]{1,0:T(8,128)(2,1)S(1)}, bf16[48,128]{1,0:T(8,128)(2,1)S(1)}, u32[]{:S(2)}, u32[]{:S(2)}) %collective-permute-start.4) | collective-permute-done | bytes 12320 | tf_op jit(solution)/shard_map/ppermute | solution.py:292
  16.2 0.6 pad_add_fusion
  16.8 1.1 %copy.18.index_ref = s32[1536,2]{1,0:T(8,128)S(1)} copy(s32[1536,2]{0,1:T(2,128)} %pad_add_fusion) | data formatting | bytes 24576 | tf_op jit(solution)/shard_map/stack | solution.py:385
  17.9 1.3 %one_hot.1 = (bf16[1536,512]{1,0:T(8,128)(2,1)S(1)}, bf16[192,1536]{1,0:T(8,128)(2,1)S(1)}, bf16[3584,128]{1,0:T(8,128)(2,1)S(1)}) custom-call(s32[1536,2]{1,0:T(8,128)S(1)} %copy.18.index_ref, s32[1,1536]{1,0:T(1,128)S(1)} %broadcast_in_dim.22.receiver_ref, bf16[2,1536,128]{2,1,0:T(8,128)(2,1)S(1)} %copy-done, bf16[2,128,512]{2,1,0:T(8,128)(2,1)S(1)} %copy-done.2, ...), custom_call_target="tpu_custom_call" | custom-call | bytes 4933632 | tf_op jit(solution)/shard_map/one_hot/pallas_call | solution.py:273
  19.3 4.0 %collective-permute-done.7.refs_8_ = bf16[1792,128]{1,0:T(8,128)(2,1)} collective-permute-done((bf16[1792,128]{1,0:T(8,128)(2,1)}, bf16[1792,128]{1,0:T(8,128)(2,1)}, u32[]{:S(2)}, u32[]{:S(2)}) %collective-permute-start.7) | collective-permute-done | bytes 458784 | tf_op jit(solution)/shard_map/ppermute | solution.py:287
  23.3 1.5 %collective-permute-start.8 = (bf16[1840,128]{1,0:T(8,128)(2,1)S(1)}, bf16[1840,128]{1,0:T(8,128)(2,1)S(1)}, u32[]{:S(2)}, u32[]{:S(2)}) collective-permute-start(bf16[1840,128]{1,0:T(8,128)(2,1)S(1)} %latents.1.refs_12_), channel_id=1, source_target_pairs={{0,2},{1,3},{2,0},{3,1},{4,6},{5,7},{6,4},{7,5},{8,10},{9,11},{10,... | collective-permute-start | bytes 1413128 | tf_op jit(solution)/shard_map/ppermute | solution.py:287
  24.8 1.5 %collective-permute-start.10 = (bf16[1792,128]{1,0:T(8,128)(2,1)}, bf16[1792,128]{1,0:T(8,128)(2,1)S(1)}, u32[]{:S(2)}, u32[]{:S(2)}) collective-permute-start(bf16[1792,128]{1,0:T(8,128)(2,1)} %collective-permute-done.7.refs_8_), channel_id=1, source_target_pairs={{0,16},{16,0},{1,17},{17,1},{2,18},{18,2},{3,19},{19,3},{4,20},{20... | collective-permute-start | bytes 1376264 | tf_op jit(solution)/shard_map/ppermute | solution.py:409
  26.3 8.0 %collective-permute-done.8.refs_14_ = bf16[1840,128]{1,0:T(8,128)(2,1)S(1)} collective-permute-done((bf16[1840,128]{1,0:T(8,128)(2,1)S(1)}, bf16[1840,128]{1,0:T(8,128)(2,1)S(1)}, u32[]{:S(2)}, u32[]{:S(2)}) %collective-permute-start.8) | collective-permute-done | bytes 471072 | tf_op jit(solution)/shard_map/ppermute | solution.py:287
  34.3 1.5 %collective-permute-start.9 = (bf16[3584,128]{1,0:T(8,128)(2,1)S(1)}, bf16[3584,128]{1,0:T(8,128)(2,1)S(1)}, u32[]{:S(2)}, u32[]{:S(2)}) collective-permute-start(bf16[3584,128]{1,0:T(8,128)(2,1)S(1)} %get-tuple-element.45), channel_id=1, source_target_pairs={{0,2},{1,3},{2,0},{3,1},{4,6},{5,7},{6,4},{7,5},{8,10},{9,11},{10,... | collective-permute-start | bytes 2752520 | tf_op jit(solution)/shard_map/ppermute | solution.py:287
  36.8 0.8 %collective-permute-done.13.refs_13_ = bf16[1840,128]{1,0:T(8,128)(2,1)S(1)} collective-permute-done((bf16[1840,128]{1,0:T(8,128)(2,1)S(1)}, bf16[1840,128]{1,0:T(8,128)(2,1)S(1)}, u32[]{:S(2)}, u32[]{:S(2)}) %collective-permute-start.13) | collective-permute-done | bytes 471072 | tf_op jit(solution)/shard_map/ppermute | solution.py:287
  37.6 1.5 %collective-permute-done.11.refs_10_ = bf16[1792,128]{1,0:T(8,128)(2,1)S(1)} collective-permute-done((bf16[1792,128]{1,0:T(8,128)(2,1)}, bf16[1792,128]{1,0:T(8,128)(2,1)S(1)}, u32[]{:S(2)}, u32[]{:S(2)}) %collective-permute-start.11) | collective-permute-done | bytes 458784 | tf_op jit(solution)/shard_map/ppermute | solution.py:287
  39.6 9.1 %layer_0.1 = (f32[1536,128]{1,0:T(8,128)S(1)}, bf16[1536,512]{1,0:T(8,128)(2,1)S(1)}, f32[192,128]{1,0:T(8,128)S(1)}, bf16[192,512]{1,0:T(8,128)(2,1)S(1)}, bf16...) custom-call(s32[3]{0:T(128)S(1)} %copy-done.7, ...), custom_call_target="tpu_custom_call" | custom-call | flops 3019898880 | bytes 13205964 | tf_op jit(solution)/shard_map/layer_0/pallas_call | solution.py:273
  48.7 1.6 %collective-permute-start.15 = (bf16[48,512]{1,0:T(8,128)(2,1)S(1)}, bf16[48,512]{1,0:T(8,128)(2,1)S(1)}, u32[]{:S(2)}, u32[]{:S(2)}) collective-permute-start(bf16[48,512]{1,0:T(8,128)(2,1)S(1)} %get-tuple-element.48), channel_id=1, source_target_pairs={{0,4},{4,8},{8,12},{12,0},{1,5},{5,9},{9,13},{13,1},{2,6},{6,10},{... | collective-permute-start | bytes 147464 | tf_op jit(solution)/shard_map/ppermute | solution.py:292
  50.3 4.3 %collective-permute-done.15.refs_14_ = bf16[48,512]{1,0:T(8,128)(2,1)S(1)} collective-permute-done((bf16[48,512]{1,0:T(8,128)(2,1)S(1)}, bf16[48,512]{1,0:T(8,128)(2,1)S(1)}, u32[]{:S(2)}, u32[]{:S(2)}) %collective-permute-start.15) | collective-permute-done | bytes 49184 | tf_op jit(solution)/shard_map/ppermute | solution.py:292
  54.6 2.2 %collective-permute-start.17 = (bf16[48,512]{1,0:T(8,128)(2,1)S(1)}, bf16[48,512]{1,0:T(8,128)(2,1)S(1)}, u32[]{:S(2)}, u32[]{:S(2)}) collective-permute-start(bf16[48,512]{1,0:T(8,128)(2,1)S(1)} %get-tuple-element.54), channel_id=1, source_target_pairs={{0,12},{4,0},{8,4},{12,8},{1,13},{5,1},{9,5},{13,9},{2,14},{6,2},{... | collective-permute-start | bytes 147464 | tf_op jit(solution)/shard_map/ppermute | solution.py:292
  57.0 4.5 %collective-permute-done.18.refs_16_ = bf16[16,512]{1,0:T(8,128)(2,1)S(1)} collective-permute-done((bf16[16,512]{1,0:T(8,128)(2,1)S(1)}, bf16[16,512]{1,0:T(8,128)(2,1)S(1)}, u32[]{:S(2)}, u32[]{:S(2)}) %collective-permute-start.18) | collective-permute-done | bytes 16416 | tf_op jit(solution)/shard_map/ppermute | solution.py:292
  61.5 8.9 %layer_1.1 = (f32[1536,128]{1,0:T(8,128)}, f32[192,128]{1,0:T(8,128)}) custom-call(s32[3]{0:T(128)S(1)} %copy-done.7, bf16[2,1536,128]{2,1,0:T(8,128)(2,1)S(1)} %copy-done, bf16[2,128,512]{2,1,0:T(8,128)(2,1)S(1)} %copy-done.2, bf16[2,1024,128]{2,1,0:T(8,128)(2,1)S(1)} %copy-done.1, bf16[2,128,512]{2,1,0:T(8,128)(2,1)S(1)} %copy-done.3, ...), custom_call_target="tpu_custom_call" | custom-call | flops 3019898880 | bytes 11321356 | tf_op jit(solution)/shard_map/layer_1/pallas_call | solution.py:273
  (54 shorter events, 2.6 us)
Async XLA Ops:
  0.6 15.5 %copy-start.3 = (bf16[2,128,512]{2,1,0:T(8,128)(2,1)S(1)}, bf16[2,128,512]{2,1,0:T(8,128)(2,1)}, u32[]{:S(2)}) copy-start(bf16[2,128,512]{2,1,0:T(8,128)(2,1)} %refs_3_.3) | copy-start | bytes 786436
  0.7 15.4 %copy-start.8 = (s32[1536]{0:T(1024)S(1)}, s32[1536]{0:T(1024)}, u32[]{:S(2)}) copy-start(s32[1536]{0:T(1024)} %param.16) | copy-start | bytes 18436
  0.7 15.4 %copy-start.9 = (s32[1536]{0:T(1024)S(1)}, s32[1536]{0:T(1024)}, u32[]{:S(2)}) copy-start(s32[1536]{0:T(1024)} %param.15) | copy-start | bytes 18436
  4.6 18.6 %collective-permute-start = (bf16[2,1536,128]{2,1,0:T(8,128)(2,1)S(1)}, bf16[2,1536,128]{2,1,0:T(8,128)(2,1)}, u32[]{:S(2)}, u32[]{:S(2)}) collective-permute-start(bf16[2,1536,128]{2,1,0:T(8,128)(2,1)S(1)} %copy-done), channel_id=1, source_target_pairs={{0,1},{1,0},{2,3},{3,2},{4,5},{5,4},{6,7},{7,6},{8,9},{9,8},{10,11... | collective-permute-start | bytes 2359304 | tf_op jit(solution)/shard_map/ppermute | solution.py:287
  5.2 18.1 %collective-permute-start.2 = (bf16[2,1024,128]{2,1,0:T(8,128)(2,1)S(1)}, bf16[2,1024,128]{2,1,0:T(8,128)(2,1)}, u32[]{:S(2)}, u32[]{:S(2)}) collective-permute-start(bf16[2,1024,128]{2,1,0:T(8,128)(2,1)S(1)} %copy-done.1), channel_id=1, source_target_pairs={{0,1},{1,0},{2,3},{3,2},{4,5},{5,4},{6,7},{7,6},{8,9},{9,8},{10,11... | collective-permute-start | bytes 1572872 | tf_op jit(solution)/shard_map/ppermute | solution.py:287
  5.2 6.0 %collective-permute-start.6 = (bf16[16,128]{1,0:T(8,128)(2,1)S(1)}, bf16[16,128]{1,0:T(8,128)(2,1)S(1)}, u32[]{:S(2)}, u32[]{:S(2)}) collective-permute-start(bf16[16,128]{1,0:T(8,128)(2,1)S(1)} %get-tuple-element.43), channel_id=1, source_target_pairs={{0,8},{4,12},{8,0},{12,4},{1,9},{5,13},{9,1},{13,5},{2,10},{6,14},... | collective-permute-start | bytes 12296 | tf_op jit(solution)/shard_map/ppermute | solution.py:292
  9.2 3.7 %collective-permute-start.5 = (bf16[48,128]{1,0:T(8,128)(2,1)S(1)}, bf16[48,128]{1,0:T(8,128)(2,1)S(1)}, u32[]{:S(2)}, u32[]{:S(2)}) collective-permute-start(bf16[48,128]{1,0:T(8,128)(2,1)S(1)} %get-tuple-element.42), channel_id=1, source_target_pairs={{0,12},{4,0},{8,4},{12,8},{1,13},{5,1},{9,5},{13,9},{2,14},{6,2},{... | collective-permute-start | bytes 36872 | tf_op jit(solution)/shard_map/ppermute | solution.py:292
  10.6 5.5 %collective-permute-start.4 = (bf16[48,128]{1,0:T(8,128)(2,1)S(1)}, bf16[48,128]{1,0:T(8,128)(2,1)S(1)}, u32[]{:S(2)}, u32[]{:S(2)}) collective-permute-start(bf16[48,128]{1,0:T(8,128)(2,1)S(1)} %get-tuple-element.32), channel_id=1, source_target_pairs={{0,4},{4,8},{8,12},{12,0},{1,5},{5,9},{9,13},{13,1},{2,6},{6,10},{... | collective-permute-start | bytes 36872 | tf_op jit(solution)/shard_map/ppermute | solution.py:292
  11.3 12.0 %collective-permute-start.7 = (bf16[1792,128]{1,0:T(8,128)(2,1)}, bf16[1792,128]{1,0:T(8,128)(2,1)}, u32[]{:S(2)}, u32[]{:S(2)}) collective-permute-start(bf16[1792,128]{1,0:T(8,128)(2,1)} %layer_0_half.1), channel_id=1, source_target_pairs={{0,2},{1,3},{2,0},{3,1},{4,6},{5,7},{6,4},{7,5},{8,10},{9,11},{10,... | collective-permute-start | bytes 1376264 | tf_op jit(solution)/shard_map/ppermute | solution.py:287
  12.9 6.3 %collective-permute-start.1 = (bf16[2,128,512]{2,1,0:T(8,128)(2,1)S(1)}, bf16[2,128,512]{2,1,0:T(8,128)(2,1)}, u32[]{:S(2)}, u32[]{:S(2)}) collective-permute-start(bf16[2,128,512]{2,1,0:T(8,128)(2,1)S(1)} %copy-done.2), channel_id=1, source_target_pairs={{0,1},{1,0},{2,3},{3,2},{4,5},{5,4},{6,7},{7,6},{8,9},{9,8},{10,11... | collective-permute-start | bytes 786440 | tf_op jit(solution)/shard_map/ppermute | solution.py:287
  16.1 3.2 %collective-permute-start.3 = (bf16[2,128,512]{2,1,0:T(8,128)(2,1)S(1)}, bf16[2,128,512]{2,1,0:T(8,128)(2,1)}, u32[]{:S(2)}, u32[]{:S(2)}) collective-permute-start(bf16[2,128,512]{2,1,0:T(8,128)(2,1)S(1)} %copy-done.3), channel_id=1, source_target_pairs={{0,1},{1,0},{2,3},{3,2},{4,5},{5,4},{6,7},{7,6},{8,9},{9,8},{10,11... | collective-permute-start | bytes 786440 | tf_op jit(solution)/shard_map/ppermute | solution.py:287
  17.9 21.7 %copy-start.6 = (f32[192,128]{1,0:T(8,128)S(1)}, f32[192,128]{1,0:T(8,128)}, u32[]{:S(2)}) copy-start(f32[192,128]{1,0:T(8,128)} %refs_17_.1) | copy-start | bytes 294916
  17.9 21.7 %copy-start.7 = (s32[3]{0:T(128)S(1)}, s32[3]{0:T(128)}, u32[]{:S(2)}) copy-start(s32[3]{0:T(128)} %pad_add_fusion.1.spot_ref) | copy-start | bytes 40
  23.3 11.0 %collective-permute-start.8 = (bf16[1840,128]{1,0:T(8,128)(2,1)S(1)}, bf16[1840,128]{1,0:T(8,128)(2,1)S(1)}, u32[]{:S(2)}, u32[]{:S(2)}) collective-permute-start(bf16[1840,128]{1,0:T(8,128)(2,1)S(1)} %latents.1.refs_12_), channel_id=1, source_target_pairs={{0,2},{1,3},{2,0},{3,1},{4,6},{5,7},{6,4},{7,5},{8,10},{9,11},{10,... | collective-permute-start | bytes 1413128 | tf_op jit(solution)/shard_map/ppermute | solution.py:287
  24.8 11.5 %collective-permute-start.10 = (bf16[1792,128]{1,0:T(8,128)(2,1)}, bf16[1792,128]{1,0:T(8,128)(2,1)S(1)}, u32[]{:S(2)}, u32[]{:S(2)}) collective-permute-start(bf16[1792,128]{1,0:T(8,128)(2,1)} %collective-permute-done.7.refs_8_), channel_id=1, source_target_pairs={{0,16},{16,0},{1,17},{17,1},{2,18},{18,2},{3,19},{19,3},{4,20},{20... | collective-permute-start | bytes 1376264 | tf_op jit(solution)/shard_map/ppermute | solution.py:409
  34.3 20.4 %collective-permute-start.9 = (bf16[3584,128]{1,0:T(8,128)(2,1)S(1)}, bf16[3584,128]{1,0:T(8,128)(2,1)S(1)}, u32[]{:S(2)}, u32[]{:S(2)}) collective-permute-start(bf16[3584,128]{1,0:T(8,128)(2,1)S(1)} %get-tuple-element.45), channel_id=1, source_target_pairs={{0,2},{1,3},{2,0},{3,1},{4,6},{5,7},{6,4},{7,5},{8,10},{9,11},{10,... | collective-permute-start | bytes 2752520 | tf_op jit(solution)/shard_map/ppermute | solution.py:287
  35.8 1.8 %collective-permute-start.13 = (bf16[1840,128]{1,0:T(8,128)(2,1)S(1)}, bf16[1840,128]{1,0:T(8,128)(2,1)S(1)}, u32[]{:S(2)}, u32[]{:S(2)}) collective-permute-start(bf16[1840,128]{1,0:T(8,128)(2,1)S(1)} %latents.1.refs_12_), channel_id=1, source_target_pairs={{0,1},{1,0},{2,3},{3,2},{4,5},{5,4},{6,7},{7,6},{8,9},{9,8},{10,11... | collective-permute-start | bytes 1413128 | tf_op jit(solution)/shard_map/ppermute | solution.py:287
  35.8 3.8 %collective-permute-start.14 = (bf16[1840,128]{1,0:T(8,128)(2,1)S(1)}, bf16[1840,128]{1,0:T(8,128)(2,1)S(1)}, u32[]{:S(2)}, u32[]{:S(2)}) collective-permute-start(bf16[1840,128]{1,0:T(8,128)(2,1)S(1)} %collective-permute-done.8.refs_14_), channel_id=1, source_target_pairs={{0,1},{1,0},{2,3},{3,2},{4,5},{5,4},{6,7},{7,6},{8,9},{9,8},{10,11... | collective-permute-start | bytes 1413128 | tf_op jit(solution)/shard_map/ppermute | solution.py:287
  36.3 2.8 %collective-permute-start.11 = (bf16[1792,128]{1,0:T(8,128)(2,1)}, bf16[1792,128]{1,0:T(8,128)(2,1)S(1)}, u32[]{:S(2)}, u32[]{:S(2)}) collective-permute-start(bf16[1792,128]{1,0:T(8,128)(2,1)} %collective-permute-done.7.refs_8_), channel_id=1, source_target_pairs={{0,1},{1,0},{2,3},{3,2},{4,5},{5,4},{6,7},{7,6},{8,9},{9,8},{10,11... | collective-permute-start | bytes 1376264 | tf_op jit(solution)/shard_map/ppermute | solution.py:287
  36.3 3.3 %collective-permute-start.12 = (bf16[1792,128]{1,0:T(8,128)(2,1)S(1)}, bf16[1792,128]{1,0:T(8,128)(2,1)S(1)}, u32[]{:S(2)}, u32[]{:S(2)}) collective-permute-start(bf16[1792,128]{1,0:T(8,128)(2,1)S(1)} %collective-permute-done.10.refs_9_), channel_id=1, source_target_pairs={{0,1},{1,0},{2,3},{3,2},{4,5},{5,4},{6,7},{7,6},{8,9},{9,8},{10,11... | collective-permute-start | bytes 1376264 | tf_op jit(solution)/shard_map/ppermute | solution.py:287
  48.7 5.9 %collective-permute-start.15 = (bf16[48,512]{1,0:T(8,128)(2,1)S(1)}, bf16[48,512]{1,0:T(8,128)(2,1)S(1)}, u32[]{:S(2)}, u32[]{:S(2)}) collective-permute-start(bf16[48,512]{1,0:T(8,128)(2,1)S(1)} %get-tuple-element.48), channel_id=1, source_target_pairs={{0,4},{4,8},{8,12},{12,0},{1,5},{5,9},{9,13},{13,1},{2,6},{6,10},{... | collective-permute-start | bytes 147464 | tf_op jit(solution)/shard_map/ppermute | solution.py:292
  54.6 6.8 %collective-permute-start.16 = (bf16[3584,128]{1,0:T(8,128)(2,1)S(1)}, bf16[3584,128]{1,0:T(8,128)(2,1)S(1)}, u32[]{:S(2)}, u32[]{:S(2)}) collective-permute-start(bf16[3584,128]{1,0:T(8,128)(2,1)S(1)} %collective-permute-done.9.refs_8_), channel_id=1, source_target_pairs={{0,1},{1,0},{2,3},{3,2},{4,5},{5,4},{6,7},{7,6},{8,9},{9,8},{10,11... | collective-permute-start | bytes 2752520 | tf_op jit(solution)/shard_map/ppermute | solution.py:287
  54.6 6.8 %collective-permute-start.17 = (bf16[48,512]{1,0:T(8,128)(2,1)S(1)}, bf16[48,512]{1,0:T(8,128)(2,1)S(1)}, u32[]{:S(2)}, u32[]{:S(2)}) collective-permute-start(bf16[48,512]{1,0:T(8,128)(2,1)S(1)} %get-tuple-element.54), channel_id=1, source_target_pairs={{0,12},{4,0},{8,4},{12,8},{1,13},{5,1},{9,5},{13,9},{2,14},{6,2},{... | collective-permute-start | bytes 147464 | tf_op jit(solution)/shard_map/ppermute | solution.py:292
  56.8 4.6 %collective-permute-start.18 = (bf16[16,512]{1,0:T(8,128)(2,1)S(1)}, bf16[16,512]{1,0:T(8,128)(2,1)S(1)}, u32[]{:S(2)}, u32[]{:S(2)}) collective-permute-start(bf16[16,512]{1,0:T(8,128)(2,1)S(1)} %get-tuple-element.55), channel_id=1, source_target_pairs={{0,8},{4,12},{8,0},{12,4},{1,9},{5,13},{9,1},{13,5},{2,10},{6,14},... | collective-permute-start | bytes 49160 | tf_op jit(solution)/shard_map/ppermute | solution.py:292
  (6 other events, 30.3 us)

commit v6 on v5

--- a/solution.py
+++ b/solution.py
@@ -138,19 +138,14 @@
         start += out.shape[0]
 
 
-def start_kernel(node_ref, wanted_ref, node_out, right, left, coarse):
-    node_bf = node_ref[...].astype(BF16)
-    node_out[...] = node_bf
-    pick_rows(wanted_ref, node_bf, (right, left, coarse))
-
-
-def latent_kernel(edge_ref, *refs):
-    rows, out = refs[:-1], refs[-1]
+def start_kernel(node_ref, wanted_ref, right, left, coarse):
+    pick_rows(wanted_ref, node_ref[...].astype(BF16), (right, left, coarse))
+
+
+def latent_kernel(edge_ref, node_ref, out):
     at = edge_ref.shape[0]
     out[0:at, :] = edge_ref[...].astype(BF16)
-    for piece in rows:
-        out[at : at + piece.shape[0], :] = piece[...]
-        at += piece.shape[0]
+    out[at:, :] = node_ref[...].astype(BF16)
 
 
 def edge_rows(spot_ref, edge_ref, table, nodes, own_ref, hot_ref, incidence_ref, first_ref, second_ref, product_ref, own_out, full_out):
@@ -194,6 +189,7 @@
     core_w = [refs.pop(0) for _ in range(4)]
     halves = [[refs.pop(0) for _ in range(2)] for _ in range(2)]
     shards = [refs.pop(0) for _ in range(4)]
+    rims = [refs.pop(0) for _ in range(4)]
     edge_own, node_own, hot_ref, incidence_ref, wanted_ref = [refs.pop(0) for _ in range(5)]
     edge_out, full_out, node_out, node_full = [refs.pop(0) for _ in range(4)]
     sends = [refs.pop(0) for _ in range(3)]
@@ -202,9 +198,11 @@
     edge_count = edge_own.shape[0]
     node_count = node_own.shape[0]
     edge_copies, node_copies = Copies(edge_sems), Copies(node_sems)
-    for j, shard in enumerate(shards):
-        column = pl.multiple_of((spot_ref[0] ^ j) * part, part)
-        edge_copies.start(shard, x_ref.at[:, pl.ds(column, part)])
+    for pieces, at in ((shards, 0), (rims, edge_count + node_count)):
+        rows = pl.ds(at, pieces[0].shape[0])
+        for j, shard in enumerate(pieces):
+            column = pl.multiple_of((spot_ref[0] ^ j) * part, part)
+            edge_copies.start(shard, x_ref.at[rows, pl.ds(column, part)])
     y = spot_ref[1]
     starts = [0, 0]
     for base, copies, (first, second), at in (
@@ -363,25 +361,18 @@
         60,
     )
     near = swap(ride, 2)
-    boundary_rows = after(boundary_rows, ride)
     own_coarse = jnp.arange(node_count - COARSE_DEV, node_count, dtype=jnp.int32)
     padding = jnp.full((COARSE_PAD - COARSE_DEV,), -1, jnp.int32)
     coarse_list = jnp.concatenate([own_coarse, padding])
+    boundary_rows, senders, receivers = lax.optimization_barrier(
+        (boundary_rows, senders, receivers, ride)
+    )[:3]
     wanted = jnp.concatenate(
         [boundary_rows[halo:], coarse_list, boundary_rows[:halo], coarse_list, coarse_list]
     )[:, None]
-    node_bf, right, left, coarse = call(
-        start_kernel,
-        [shape((node_count, part), BF16)] + sent(part),
-        [(VMEM, after(node_state, ride)), (VMEM, wanted)],
-        [],
-        2 * wanted.shape[0] * node_count * part,
-        "boundary_rows",
-    )
-    halo_rows = neighbour_rows(right, left, coarse, halo)
-    table_rows = node_count + sum(r.shape[0] for r in halo_rows)
+    far_rows = 2 * wide + COARSE_PAD if blocks == 4 else 2 * halo + blocks * COARSE_PAD
+    table_rows = node_count + far_rows
     lanes = -(-(table_rows + node_count) // 128) * 128
-    senders, receivers = lax.optimization_barrier((senders, receivers, right))[:2]
     index = jnp.stack([table_index(senders, node_count, halo), receivers + table_rows], axis=1)
     hot, incidence, late_w = call(
         prepare_kernel,
@@ -395,20 +386,34 @@
         0,
         "one_hot",
     )
-    core_w = [swap(after(w, right), 1) for w in weights]
+    core_w = [swap(after(w, ride), 1) for w in weights]
     (latents,) = call(
         latent_kernel,
-        [shape((edge_count + table_rows, part), BF16)],
-        [(VMEM, after(edge_state, late_w)), (VMEM, node_bf)] + [(VMEM, r) for r in halo_rows],
+        [shape((edge_count + node_count, part), BF16)],
+        [(VMEM, after(edge_state, late_w)), (VMEM, node_state)],
         [],
         0,
         "latents",
     )
-    far_latents = swap(after(latents, near, *core_w), 2)
+    right, left, coarse = call(
+        start_kernel,
+        sent(part),
+        [(VMEM, node_state), (VMEM, after(wanted, latents))],
+        [],
+        2 * wanted.shape[0] * node_count * part,
+        "boundary_rows",
+    )
+    latents_sent, right, left, coarse = lax.optimization_barrier(
+        (latents, right, left, coarse, near, *core_w)
+    )[:4]
+    far_latents = swap(latents_sent, 2)
     shards = [latents, swap(latents, 1), far_latents, swap(far_latents, 1)]
+    rim = jnp.concatenate(neighbour_rows(right, left, coarse, halo), axis=0)
+    far_rim = swap(rim, 2)
+    rims = [rim, swap(rim, 1), far_rim, swap(far_rim, 1)]
     far = lax.ppermute(near, "groups", [(0, 1), (1, 0)])
     pairs = [near, far, swap(near, 1), swap(far, 1)]
-    late_x = swap(after(late_w, far_latents), 2)
+    late_x = swap(after(late_w, far_latents, far_rim), 2)
 
     edge_flops = 2 * edge_count * features * (2 * features + lanes + node_count)
     node_flops = 2 * node_count * features * 3 * features
@@ -424,7 +429,7 @@
         first_kernel,
         [own_edge, full_edge, own_node, full_node] + sent(features),
         [(SMEM, spot)]
-        + [(ANY, w) for w in list(weights) + core_w + pairs + shards]
+        + [(ANY, w) for w in list(weights) + core_w + pairs + shards + rims]
         + [(VMEM, a) for a in (edge_state, node_state, hot, incidence, wanted)],
         [
             edge_shape,
@@ -433,14 +438,14 @@
             second_shape,
             pltpu.VMEM((lanes, hidden), BF16),
             pltpu.VMEM((edge_count + table_rows, features), BF16),
-            dma((28,)),
+            dma((32,)),
             dma((24,)),
         ],
         edge_flops + node_flops,
         "layer_0",
     )
     tables = [node_full] + neighbour_rows(right, left, coarse, halo)
-    late_d = swap(after(late_x, tables[1]), 1)
+    late_d = swap(after(late_x, *tables[1:]), 1)
     edge_own, node_own = call(
         functools.partial(late_kernel, len(tables)),
         [own_edge, own_node],

time: 70.8 us -> 72.9 us (1.030)
  local copies, waits for them, and re-layouts: 1.41 us -> 7.96 us
  waiting for transfers between devices: 26.9 us -> 21.3 us
  starting transfers between devices: 17.7 us -> 19.2 us
    unnamed x22 -> x38, local copies, waits for them, and re-layouts: 0.06 us -> 7.27 us
    ppermute x6, waiting for transfers between devices: 12.1 us -> 6.99 us  [shift(): return lax.ppermute(x, 'graph', [(i, (i + by) % size) for i in range(size)])]
    ppermute x12 -> x15, starting transfers between devices: 6.11 us -> 8.28 us  [swap(): return lax.ppermute(x, 'mp', [(i, i ^ mask) for i in range(size)])]
    another operation x3, local copies, waits for them, and re-layouts: 1.08 us -> 0.3 us  [on_device(): jnp.stack([table_index(senders, node_count, halo), receivers + table_rows...]
    ppermute x12 -> x15, waiting for transfers between devices: 14.8 us -> 14.3 us  [swap(): return lax.ppermute(x, 'mp', [(i, i ^ mask) for i in range(size)])]
  transfers between devices with their start and end apart: 19 -> 22, of which waited for: 9 -> 8; matrix products, arithmetic and copies ran while one was open for 2% -> 1% of each run, Pallas kernels for 15% -> 15%
where the time goes in v6:
time: 72.9 us; the launch traced here: 72.6 us
  Pallas kernels  22.5 us (31%)
  waiting for transfers between devices  21.3 us (29%)
  starting transfers between devices  19.2 us (26%)
  local copies, waits for them, and re-layouts  7.96 us (11%)
  between operations  1.07 us (1%)
    pallas_call x6, Pallas kernels, call(): pl.pallas_call(kernel, out_shape=out_shape, in_specs=[pl.BlockSpec(memory...  22.5 us
    ppermute x15, waiting for transfers between devices, swap(): return lax.ppermute(x, 'mp', [(i, i ^ mask) for i in range(size)])  14.3 us
    ppermute x6, starting transfers between devices, shift(): return lax.ppermute(x, 'graph', [(i, (i + by) % size) for i in range(size)])  9.39 us
    ppermute x15, starting transfers between devices, swap(): return lax.ppermute(x, 'mp', [(i, i ^ mask) for i in range(size)])  8.28 us
    unnamed x38, local copies, waits for them, and re-layouts  7.27 us
    ppermute x6, waiting for transfers between devices, shift(): return lax.ppermute(x, 'graph', [(i, (i + by) % size) for i in range(size)])  6.99 us
    ppermute x1, starting transfers between devices, on_device(): far = lax.ppermute(near, 'groups', [(0, 1), (1, 0)])  1.52 us
  transfers between devices with their start and end apart: 22, of which 8 were waited for; matrix products, arithmetic and copies ran while one was open for 1% of the time, Pallas kernels for 15%

profile of v6, /device:TPU:0, one launch (start us, length us, event | category | flops | bytes accessed | tf_op | source)
XLA Modules:
  0.0 72.6 jit_solution(16524471087380617398)
XLA Ops:
  1.3 2.6 %layer_0_half.1 = bf16[1792,128]{1,0:T(8,128)(2,1)} custom-call(s32[3]{0:T(128)} %pad_add_fusion.1.spot_ref, bf16[2,1536,128]{2,1,0:T(8,128)(2,1)} %refs_0_.3, bf16[2,128,512]{2,1,0:T(8,128)(2,1)} %refs_1_.3, bf16[2,1024,128]{2,1,0:T(8,128)(2,1)} %refs_2_.3, bf16[2,128,512]{2,1,0:T(8,128)(2,1)} %refs_3_.3), custom_call_target="tpu_custom_call" | custom-call | bytes 2293772 | tf_op jit(solution)/shard_map/layer_0_half/pallas_call | solution.py:271
  3.9 3.0 %collective-permute-start.4 = (bf16[1792,128]{1,0:T(8,128)(2,1)}, bf16[1792,128]{1,0:T(8,128)(2,1)}, u32[]{:S(2)}, u32[]{:S(2)}) collective-permute-start(bf16[1792,128]{1,0:T(8,128)(2,1)} %layer_0_half.1), channel_id=1, source_target_pairs={{0,2},{1,3},{2,0},{3,1},{4,6},{5,7},{6,4},{7,5},{8,10},{9,11},{10,... | collective-permute-start | bytes 1376264 | tf_op jit(solution)/shard_map/ppermute | solution.py:285
  8.4 1.3 %one_hot.1 = (bf16[1536,512]{1,0:T(8,128)(2,1)S(1)}, bf16[192,1536]{1,0:T(8,128)(2,1)S(1)}, bf16[3584,128]{1,0:T(8,128)(2,1)S(1)}) custom-call(s32[1536,2]{1,0:T(8,128)S(1)} %copy.17.index_ref, s32[1,1536]{1,0:T(1,128)S(1)} %broadcast_in_dim.21.receiver_ref, bf16[2,1536,128]{2,1,0:T(8,128)(2,1)S(1)} %copy-done, bf16[2,128,512]{2,1,0:T(8,128)(2,1)S(1)} %copy-done.2, ...), custom_call_target="tpu_custom_call" | custom-call | bytes 4933632 | tf_op jit(solution)/shard_map/one_hot/pallas_call | solution.py:271
  9.7 1.2 %copy-done.7 = bf16[1536,512]{1,0:T(8,128)(2,1)} copy-done((bf16[1536,512]{1,0:T(8,128)(2,1)}, bf16[1536,512]{1,0:T(8,128)(2,1)S(1)}, u32[]{:S(2)}) %copy-start.7) | copy-done | bytes 1572888
  10.9 0.9 %copy-done.9 = bf16[3584,128]{1,0:T(8,128)(2,1)} copy-done((bf16[3584,128]{1,0:T(8,128)(2,1)}, bf16[3584,128]{1,0:T(8,128)(2,1)S(1)}, u32[]{:S(2)}) %copy-start.9) | copy-done | bytes 917528
  13.2 4.6 %collective-permute-done.4.refs_8_ = bf16[1792,128]{1,0:T(8,128)(2,1)} collective-permute-done((bf16[1792,128]{1,0:T(8,128)(2,1)}, bf16[1792,128]{1,0:T(8,128)(2,1)}, u32[]{:S(2)}, u32[]{:S(2)}) %collective-permute-start.4) | collective-permute-done | bytes 458784 | tf_op jit(solution)/shard_map/ppermute | solution.py:285
  17.8 1.7 %collective-permute-start.5 = (bf16[1728,128]{1,0:T(8,128)(2,1)S(1)}, bf16[1728,128]{1,0:T(8,128)(2,1)}, u32[]{:S(2)}, u32[]{:S(2)}) collective-permute-start(bf16[1728,128]{1,0:T(8,128)(2,1)S(1)} %latents.1.refs_12_), channel_id=1, source_target_pairs={{0,2},{1,3},{2,0},{3,1},{4,6},{5,7},{6,4},{7,5},{8,10},{9,11},{10,... | collective-permute-start | bytes 1327112 | tf_op jit(solution)/shard_map/ppermute | solution.py:285
  19.5 1.6 %collective-permute-start.6 = (bf16[48,128]{1,0:T(8,128)(2,1)S(1)}, bf16[48,128]{1,0:T(8,128)(2,1)S(1)}, u32[]{:S(2)}, u32[]{:S(2)}) collective-permute-start(bf16[48,128]{1,0:T(8,128)(2,1)S(1)} %get-tuple-element.46), channel_id=1, source_target_pairs={{0,4},{4,8},{8,12},{12,0},{1,5},{5,9},{9,13},{13,1},{2,6},{6,10},{... | collective-permute-start | bytes 36872 | tf_op jit(solution)/shard_map/ppermute | solution.py:290
  21.1 1.5 %collective-permute-start.11 = (bf16[1792,128]{1,0:T(8,128)(2,1)}, bf16[1792,128]{1,0:T(8,128)(2,1)}, u32[]{:S(2)}, u32[]{:S(2)}) collective-permute-start(bf16[1792,128]{1,0:T(8,128)(2,1)} %collective-permute-done.4.refs_8_), channel_id=1, source_target_pairs={{0,16},{16,0},{1,17},{17,1},{2,18},{18,2},{3,19},{19,3},{4,20},{20... | collective-permute-start | bytes 1376264 | tf_op jit(solution)/shard_map/ppermute | solution.py:414
  22.6 2.6 %collective-permute-start.8 = (bf16[16,128]{1,0:T(8,128)(2,1)S(1)}, bf16[16,128]{1,0:T(8,128)(2,1)S(1)}, u32[]{:S(2)}, u32[]{:S(2)}) collective-permute-start(bf16[16,128]{1,0:T(8,128)(2,1)S(1)} %get-tuple-element.48), channel_id=1, source_target_pairs={{0,8},{4,12},{8,0},{12,4},{1,9},{5,13},{9,1},{13,5},{2,10},{6,14},... | collective-permute-start | bytes 12296 | tf_op jit(solution)/shard_map/ppermute | solution.py:290
  25.2 1.3 %collective-permute-start.7 = (bf16[48,128]{1,0:T(8,128)(2,1)S(1)}, bf16[48,128]{1,0:T(8,128)(2,1)S(1)}, u32[]{:S(2)}, u32[]{:S(2)}) collective-permute-start(bf16[48,128]{1,0:T(8,128)(2,1)S(1)} %get-tuple-element.47), channel_id=1, source_target_pairs={{0,12},{4,0},{8,4},{12,8},{1,13},{5,1},{9,5},{13,9},{2,14},{6,2},{... | collective-permute-start | bytes 36872 | tf_op jit(solution)/shard_map/ppermute | solution.py:290
  26.5 2.3 %collective-permute-done.7 = bf16[48,128]{1,0:T(8,128)(2,1)S(1)} collective-permute-done((bf16[48,128]{1,0:T(8,128)(2,1)S(1)}, bf16[48,128]{1,0:T(8,128)(2,1)S(1)}, u32[]{:S(2)}, u32[]{:S(2)}) %collective-permute-start.7) | collective-permute-done | bytes 12320 | tf_op jit(solution)/shard_map/ppermute | solution.py:290
  29.5 3.6 %collective-permute-done.9.refs_18_ = bf16[112,128]{1,0:T(8,128)(2,1)S(1)} collective-permute-done((bf16[112,128]{1,0:T(8,128)(2,1)S(1)}, bf16[112,128]{1,0:T(8,128)(2,1)S(1)}, u32[]{:S(2)}, u32[]{:S(2)}) %collective-permute-start.9) | collective-permute-done | bytes 28704 | tf_op jit(solution)/shard_map/ppermute | solution.py:285
  34.7 1.4 %collective-permute-done.14.refs_13_ = bf16[1728,128]{1,0:T(8,128)(2,1)S(1)} collective-permute-done((bf16[1728,128]{1,0:T(8,128)(2,1)S(1)}, bf16[1728,128]{1,0:T(8,128)(2,1)S(1)}, u32[]{:S(2)}, u32[]{:S(2)}) %collective-permute-start.14) | collective-permute-done | bytes 442400 | tf_op jit(solution)/shard_map/ppermute | solution.py:285
  37.0 1.1 %collective-permute-done.16.refs_17_ = bf16[112,128]{1,0:T(8,128)(2,1)S(1)} collective-permute-done((bf16[112,128]{1,0:T(8,128)(2,1)S(1)}, bf16[112,128]{1,0:T(8,128)(2,1)S(1)}, u32[]{:S(2)}, u32[]{:S(2)}) %collective-permute-start.16) | collective-permute-done | bytes 28704 | tf_op jit(solution)/shard_map/ppermute | solution.py:285
  38.3 0.9 %collective-permute-done.17.refs_19_ = bf16[112,128]{1,0:T(8,128)(2,1)S(1)} collective-permute-done((bf16[112,128]{1,0:T(8,128)(2,1)S(1)}, bf16[112,128]{1,0:T(8,128)(2,1)S(1)}, u32[]{:S(2)}, u32[]{:S(2)}) %collective-permute-start.17) | collective-permute-done | bytes 28704 | tf_op jit(solution)/shard_map/ppermute | solution.py:285
  39.3 1.4 %copy-done.8 = bf16[1536,512]{1,0:T(8,128)(2,1)S(1)} copy-done((bf16[1536,512]{1,0:T(8,128)(2,1)S(1)}, bf16[1536,512]{1,0:T(8,128)(2,1)}, u32[]{:S(2)}) %copy-start.8) | copy-done | bytes 1572888
  40.7 1.1 %copy-done.11 = bf16[192,1536]{1,0:T(8,128)(2,1)S(1)} copy-done((bf16[192,1536]{1,0:T(8,128)(2,1)S(1)}, bf16[192,1536]{1,0:T(8,128)(2,1)}, u32[]{:S(2)}) %copy-start.11) | copy-done | bytes 589848
  41.8 1.0 %copy-done.14 = bf16[1728,128]{1,0:T(8,128)(2,1)S(1)} copy-done((bf16[1728,128]{1,0:T(8,128)(2,1)S(1)}, bf16[1728,128]{1,0:T(8,128)(2,1)}, u32[]{:S(2)}) %copy-start.14) | copy-done | bytes 442392
  42.8 9.3 %layer_0.1 = (f32[1536,128]{1,0:T(8,128)S(1)}, bf16[1536,512]{1,0:T(8,128)(2,1)S(1)}, f32[192,128]{1,0:T(8,128)S(1)}, bf16[192,512]{1,0:T(8,128)(2,1)S(1)}, bf16...) custom-call(s32[3]{0:T(128)S(1)} %copy-done.6, ...), custom_call_target="tpu_custom_call" | custom-call | flops 3019898880 | bytes 13205964 | tf_op jit(solution)/shard_map/layer_0/pallas_call | solution.py:271
  52.1 3.8 %collective-permute-start.19 = (bf16[48,512]{1,0:T(8,128)(2,1)S(1)}, bf16[48,512]{1,0:T(8,128)(2,1)S(1)}, u32[]{:S(2)}, u32[]{:S(2)}) collective-permute-start(bf16[48,512]{1,0:T(8,128)(2,1)S(1)} %get-tuple-element.53), channel_id=1, source_target_pairs={{0,12},{4,0},{8,4},{12,8},{1,13},{5,1},{9,5},{13,9},{2,14},{6,2},{... | collective-permute-start | bytes 147464 | tf_op jit(solution)/shard_map/ppermute | solution.py:290
  56.0 4.6 %collective-permute-done.20.refs_16_ = bf16[16,512]{1,0:T(8,128)(2,1)S(1)} collective-permute-done((bf16[16,512]{1,0:T(8,128)(2,1)S(1)}, bf16[16,512]{1,0:T(8,128)(2,1)S(1)}, u32[]{:S(2)}, u32[]{:S(2)}) %collective-permute-start.20) | collective-permute-done | bytes 16416 | tf_op jit(solution)/shard_map/ppermute | solution.py:290
  60.7 2.7 %collective-permute-done.21.refs_9_ = bf16[3584,128]{1,0:T(8,128)(2,1)S(1)} collective-permute-done((bf16[3584,128]{1,0:T(8,128)(2,1)}, bf16[3584,128]{1,0:T(8,128)(2,1)S(1)}, u32[]{:S(2)}, u32[]{:S(2)}) %collective-permute-start.21) | collective-permute-done | bytes 917536 | tf_op jit(solution)/shard_map/ppermute | solution.py:285
  63.4 9.1 %layer_1.1 = (f32[1536,128]{1,0:T(8,128)}, f32[192,128]{1,0:T(8,128)}) custom-call(s32[3]{0:T(128)S(1)} %copy-done.6, bf16[2,1536,128]{2,1,0:T(8,128)(2,1)S(1)} %copy-done, bf16[2,128,512]{2,1,0:T(8,128)(2,1)S(1)} %copy-done.2, bf16[2,1024,128]{2,1,0:T(8,128)(2,1)S(1)} %copy-done.1, bf16[2,128,512]{2,1,0:T(8,128)(2,1)S(1)} %copy-done.3, ...), custom_call_target="tpu_custom_call" | custom-call | flops 3019898880 | bytes 11321356 | tf_op jit(solution)/shard_map/layer_1/pallas_call | solution.py:271
  (78 shorter events, 6.9 us)
Async XLA Ops:
  3.9 13.8 %collective-permute-start.4 = (bf16[1792,128]{1,0:T(8,128)(2,1)}, bf16[1792,128]{1,0:T(8,128)(2,1)}, u32[]{:S(2)}, u32[]{:S(2)}) collective-permute-start(bf16[1792,128]{1,0:T(8,128)(2,1)} %layer_0_half.1), channel_id=1, source_target_pairs={{0,2},{1,3},{2,0},{3,1},{4,6},{5,7},{6,4},{7,5},{8,10},{9,11},{10,... | collective-permute-start | bytes 1376264 | tf_op jit(solution)/shard_map/ppermute | solution.py:285
  6.9 6.2 %collective-permute-start.1 = (bf16[2,128,512]{2,1,0:T(8,128)(2,1)S(1)}, bf16[2,128,512]{2,1,0:T(8,128)(2,1)}, u32[]{:S(2)}, u32[]{:S(2)}) collective-permute-start(bf16[2,128,512]{2,1,0:T(8,128)(2,1)S(1)} %copy-done.2), channel_id=1, source_target_pairs={{0,1},{1,0},{2,3},{3,2},{4,5},{5,4},{6,7},{7,6},{8,9},{9,8},{10,11... | collective-permute-start | bytes 786440 | tf_op jit(solution)/shard_map/ppermute | solution.py:285
  6.9 6.2 %collective-permute-start.3 = (bf16[2,128,512]{2,1,0:T(8,128)(2,1)S(1)}, bf16[2,128,512]{2,1,0:T(8,128)(2,1)}, u32[]{:S(2)}, u32[]{:S(2)}) collective-permute-start(bf16[2,128,512]{2,1,0:T(8,128)(2,1)S(1)} %copy-done.3), channel_id=1, source_target_pairs={{0,1},{1,0},{2,3},{3,2},{4,5},{5,4},{6,7},{7,6},{8,9},{9,8},{10,11... | collective-permute-start | bytes 786440 | tf_op jit(solution)/shard_map/ppermute | solution.py:285
  7.4 10.3 %collective-permute-start.2 = (bf16[2,1024,128]{2,1,0:T(8,128)(2,1)S(1)}, bf16[2,1024,128]{2,1,0:T(8,128)(2,1)}, u32[]{:S(2)}, u32[]{:S(2)}) collective-permute-start(bf16[2,1024,128]{2,1,0:T(8,128)(2,1)S(1)} %copy-done.1), channel_id=1, source_target_pairs={{0,1},{1,0},{2,3},{3,2},{4,5},{5,4},{6,7},{7,6},{8,9},{9,8},{10,11... | collective-permute-start | bytes 1572872 | tf_op jit(solution)/shard_map/ppermute | solution.py:285
  7.5 10.2 %collective-permute-start = (bf16[2,1536,128]{2,1,0:T(8,128)(2,1)S(1)}, bf16[2,1536,128]{2,1,0:T(8,128)(2,1)}, u32[]{:S(2)}, u32[]{:S(2)}) collective-permute-start(bf16[2,1536,128]{2,1,0:T(8,128)(2,1)S(1)} %copy-done), channel_id=1, source_target_pairs={{0,1},{1,0},{2,3},{3,2},{4,5},{5,4},{6,7},{7,6},{8,9},{9,8},{10,11... | collective-permute-start | bytes 2359304 | tf_op jit(solution)/shard_map/ppermute | solution.py:285
  8.4 30.9 %copy-start.6 = (s32[3]{0:T(128)S(1)}, s32[3]{0:T(128)}, u32[]{:S(2)}) copy-start(s32[3]{0:T(128)} %pad_add_fusion.1.spot_ref) | copy-start | bytes 40
  17.8 15.4 %collective-permute-start.5 = (bf16[1728,128]{1,0:T(8,128)(2,1)S(1)}, bf16[1728,128]{1,0:T(8,128)(2,1)}, u32[]{:S(2)}, u32[]{:S(2)}) collective-permute-start(bf16[1728,128]{1,0:T(8,128)(2,1)S(1)} %latents.1.refs_12_), channel_id=1, source_target_pairs={{0,2},{1,3},{2,0},{3,1},{4,6},{5,7},{6,4},{7,5},{8,10},{9,11},{10,... | collective-permute-start | bytes 1327112 | tf_op jit(solution)/shard_map/ppermute | solution.py:285
  19.5 7.0 %collective-permute-start.6 = (bf16[48,128]{1,0:T(8,128)(2,1)S(1)}, bf16[48,128]{1,0:T(8,128)(2,1)S(1)}, u32[]{:S(2)}, u32[]{:S(2)}) collective-permute-start(bf16[48,128]{1,0:T(8,128)(2,1)S(1)} %get-tuple-element.46), channel_id=1, source_target_pairs={{0,4},{4,8},{8,12},{12,0},{1,5},{5,9},{9,13},{13,1},{2,6},{6,10},{... | collective-permute-start | bytes 36872 | tf_op jit(solution)/shard_map/ppermute | solution.py:290
  21.1 13.1 %collective-permute-start.11 = (bf16[1792,128]{1,0:T(8,128)(2,1)}, bf16[1792,128]{1,0:T(8,128)(2,1)}, u32[]{:S(2)}, u32[]{:S(2)}) collective-permute-start(bf16[1792,128]{1,0:T(8,128)(2,1)} %collective-permute-done.4.refs_8_), channel_id=1, source_target_pairs={{0,16},{16,0},{1,17},{17,1},{2,18},{18,2},{3,19},{19,3},{4,20},{20... | collective-permute-start | bytes 1376264 | tf_op jit(solution)/shard_map/ppermute | solution.py:414
  22.6 6.3 %collective-permute-start.8 = (bf16[16,128]{1,0:T(8,128)(2,1)S(1)}, bf16[16,128]{1,0:T(8,128)(2,1)S(1)}, u32[]{:S(2)}, u32[]{:S(2)}) collective-permute-start(bf16[16,128]{1,0:T(8,128)(2,1)S(1)} %get-tuple-element.48), channel_id=1, source_target_pairs={{0,8},{4,12},{8,0},{12,4},{1,9},{5,13},{9,1},{13,5},{2,10},{6,14},... | collective-permute-start | bytes 12296 | tf_op jit(solution)/shard_map/ppermute | solution.py:290
  25.2 3.7 %collective-permute-start.7 = (bf16[48,128]{1,0:T(8,128)(2,1)S(1)}, bf16[48,128]{1,0:T(8,128)(2,1)S(1)}, u32[]{:S(2)}, u32[]{:S(2)}) collective-permute-start(bf16[48,128]{1,0:T(8,128)(2,1)S(1)} %get-tuple-element.47), channel_id=1, source_target_pairs={{0,12},{4,0},{8,4},{12,8},{1,13},{5,1},{9,5},{13,9},{2,14},{6,2},{... | collective-permute-start | bytes 36872 | tf_op jit(solution)/shard_map/ppermute | solution.py:290
  28.9 4.2 %collective-permute-start.9 = (bf16[112,128]{1,0:T(8,128)(2,1)S(1)}, bf16[112,128]{1,0:T(8,128)(2,1)S(1)}, u32[]{:S(2)}, u32[]{:S(2)}) collective-permute-start(bf16[112,128]{1,0:T(8,128)(2,1)S(1)} %constant_dynamic-update-slice_fusion.refs_16_), channel_id=1, source_target_pairs={{0,2},{1,3},{2,0},{3,1},{4,6},{5,7},{6,4},{7,5},{8,10},{9,11},{10,... | collective-permute-start | bytes 86024 | tf_op jit(solution)/shard_map/ppermute | solution.py:285
  33.1 27.5 %collective-permute-start.10 = (bf16[3584,128]{1,0:T(8,128)(2,1)}, bf16[3584,128]{1,0:T(8,128)(2,1)}, u32[]{:S(2)}, u32[]{:S(2)}) collective-permute-start(bf16[3584,128]{1,0:T(8,128)(2,1)} %copy-done.9), channel_id=1, source_target_pairs={{0,2},{1,3},{2,0},{3,1},{4,6},{5,7},{6,4},{7,5},{8,10},{9,11},{10,... | collective-permute-start | bytes 2752520 | tf_op jit(solution)/shard_map/ppermute | solution.py:285
  33.7 2.4 %collective-permute-start.14 = (bf16[1728,128]{1,0:T(8,128)(2,1)S(1)}, bf16[1728,128]{1,0:T(8,128)(2,1)S(1)}, u32[]{:S(2)}, u32[]{:S(2)}) collective-permute-start(bf16[1728,128]{1,0:T(8,128)(2,1)S(1)} %latents.1.refs_12_), channel_id=1, source_target_pairs={{0,1},{1,0},{2,3},{3,2},{4,5},{5,4},{6,7},{7,6},{8,9},{9,8},{10,11... | collective-permute-start | bytes 1327112 | tf_op jit(solution)/shard_map/ppermute | solution.py:285
  33.7 5.6 %collective-permute-start.12 = (bf16[1792,128]{1,0:T(8,128)(2,1)}, bf16[1792,128]{1,0:T(8,128)(2,1)}, u32[]{:S(2)}, u32[]{:S(2)}) collective-permute-start(bf16[1792,128]{1,0:T(8,128)(2,1)} %collective-permute-done.4.refs_8_), channel_id=1, source_target_pairs={{0,1},{1,0},{2,3},{3,2},{4,5},{5,4},{6,7},{7,6},{8,9},{9,8},{10,11... | collective-permute-start | bytes 1376264 | tf_op jit(solution)/shard_map/ppermute | solution.py:285
  34.2 5.1 %collective-permute-start.13 = (bf16[1792,128]{1,0:T(8,128)(2,1)}, bf16[1792,128]{1,0:T(8,128)(2,1)}, u32[]{:S(2)}, u32[]{:S(2)}) collective-permute-start(bf16[1792,128]{1,0:T(8,128)(2,1)} %collective-permute-done.11.refs_9_), channel_id=1, source_target_pairs={{0,1},{1,0},{2,3},{3,2},{4,5},{5,4},{6,7},{7,6},{8,9},{9,8},{10,11... | collective-permute-start | bytes 1376264 | tf_op jit(solution)/shard_map/ppermute | solution.py:285
  34.2 5.1 %collective-permute-start.15 = (bf16[1728,128]{1,0:T(8,128)(2,1)}, bf16[1728,128]{1,0:T(8,128)(2,1)}, u32[]{:S(2)}, u32[]{:S(2)}) collective-permute-start(bf16[1728,128]{1,0:T(8,128)(2,1)} %collective-permute-done.5.refs_14_), channel_id=1, source_target_pairs={{0,1},{1,0},{2,3},{3,2},{4,5},{5,4},{6,7},{7,6},{8,9},{9,8},{10,11... | collective-permute-start | bytes 1327112 | tf_op jit(solution)/shard_map/ppermute | solution.py:285
  36.9 1.2 %collective-permute-start.16 = (bf16[112,128]{1,0:T(8,128)(2,1)S(1)}, bf16[112,128]{1,0:T(8,128)(2,1)S(1)}, u32[]{:S(2)}, u32[]{:S(2)}) collective-permute-start(bf16[112,128]{1,0:T(8,128)(2,1)S(1)} %constant_dynamic-update-slice_fusion.refs_16_), channel_id=1, source_target_pairs={{0,1},{1,0},{2,3},{3,2},{4,5},{5,4},{6,7},{7,6},{8,9},{9,8},{10,11... | collective-permute-start | bytes 86024 | tf_op jit(solution)/shard_map/ppermute | solution.py:285
  38.1 1.2 %collective-permute-start.17 = (bf16[112,128]{1,0:T(8,128)(2,1)S(1)}, bf16[112,128]{1,0:T(8,128)(2,1)S(1)}, u32[]{:S(2)}, u32[]{:S(2)}) collective-permute-start(bf16[112,128]{1,0:T(8,128)(2,1)S(1)} %collective-permute-done.9.refs_18_), channel_id=1, source_target_pairs={{0,1},{1,0},{2,3},{3,2},{4,5},{5,4},{6,7},{7,6},{8,9},{9,8},{10,11... | collective-permute-start | bytes 86024 | tf_op jit(solution)/shard_map/ppermute | solution.py:285
  42.8 20.6 %copy-start.12 = (bf16[192,1536]{1,0:T(8,128)(2,1)S(1)}, bf16[192,1536]{1,0:T(8,128)(2,1)}, u32[]{:S(2)}) copy-start(bf16[192,1536]{1,0:T(8,128)(2,1)} %copy-done.10) | copy-start | bytes 1769476
  52.1 8.5 %collective-permute-start.18 = (bf16[48,512]{1,0:T(8,128)(2,1)S(1)}, bf16[48,512]{1,0:T(8,128)(2,1)S(1)}, u32[]{:S(2)}, u32[]{:S(2)}) collective-permute-start(bf16[48,512]{1,0:T(8,128)(2,1)S(1)} %get-tuple-element.52), channel_id=1, source_target_pairs={{0,4},{4,8},{8,12},{12,0},{1,5},{5,9},{9,13},{13,1},{2,6},{6,10},{... | collective-permute-start | bytes 147464 | tf_op jit(solution)/shard_map/ppermute | solution.py:290
  52.1 8.5 %collective-permute-start.19 = (bf16[48,512]{1,0:T(8,128)(2,1)S(1)}, bf16[48,512]{1,0:T(8,128)(2,1)S(1)}, u32[]{:S(2)}, u32[]{:S(2)}) collective-permute-start(bf16[48,512]{1,0:T(8,128)(2,1)S(1)} %get-tuple-element.53), channel_id=1, source_target_pairs={{0,12},{4,0},{8,4},{12,8},{1,13},{5,1},{9,5},{13,9},{2,14},{6,2},{... | collective-permute-start | bytes 147464 | tf_op jit(solution)/shard_map/ppermute | solution.py:290
  55.9 4.6 %collective-permute-start.20 = (bf16[16,512]{1,0:T(8,128)(2,1)S(1)}, bf16[16,512]{1,0:T(8,128)(2,1)S(1)}, u32[]{:S(2)}, u32[]{:S(2)}) collective-permute-start(bf16[16,512]{1,0:T(8,128)(2,1)S(1)} %get-tuple-element.54), channel_id=1, source_target_pairs={{0,8},{4,12},{8,0},{12,4},{1,9},{5,13},{9,1},{13,5},{2,10},{6,14},... | collective-permute-start | bytes 49160 | tf_op jit(solution)/shard_map/ppermute | solution.py:290
  60.6 2.7 %collective-permute-start.21 = (bf16[3584,128]{1,0:T(8,128)(2,1)}, bf16[3584,128]{1,0:T(8,128)(2,1)S(1)}, u32[]{:S(2)}, u32[]{:S(2)}) collective-permute-start(bf16[3584,128]{1,0:T(8,128)(2,1)} %collective-permute-done.10.refs_8_), channel_id=1, source_target_pairs={{0,1},{1,0},{2,3},{3,2},{4,5},{5,4},{6,7},{7,6},{8,9},{9,8},{10,11... | collective-permute-start | bytes 2752520 | tf_op jit(solution)/shard_map/ppermute | solution.py:285
  (16 other events, 61.3 us)

commit v7 on v6

--- a/solution.py
+++ b/solution.py
@@ -265,7 +265,7 @@
 SMEM, VMEM, ANY = pltpu.SMEM, pltpu.VMEM, pl.ANY
 
 
-def call(kernel, out_shape, args, scratch, flops, name, vmem_mib=24):
+def call(kernel, out_shape, args, scratch, flops, name, vmem_mib=8):
     arrays = [a for _, a in args]
     moved = sum(a.size * a.dtype.itemsize for a in arrays + list(out_shape))
     return pl.pallas_call(
@@ -403,17 +403,14 @@
         2 * wanted.shape[0] * node_count * part,
         "boundary_rows",
     )
-    latents_sent, right, left, coarse = lax.optimization_barrier(
-        (latents, right, left, coarse, near, *core_w)
-    )[:4]
-    far_latents = swap(latents_sent, 2)
+    far_latents = swap(after(latents, near), 2)
     shards = [latents, swap(latents, 1), far_latents, swap(far_latents, 1)]
     rim = jnp.concatenate(neighbour_rows(right, left, coarse, halo), axis=0)
     far_rim = swap(rim, 2)
     rims = [rim, swap(rim, 1), far_rim, swap(far_rim, 1)]
     far = lax.ppermute(near, "groups", [(0, 1), (1, 0)])
     pairs = [near, far, swap(near, 1), swap(far, 1)]
-    late_x = swap(after(late_w, far_latents, far_rim), 2)
+    late_x = swap(after(late_w, far_latents), 2)
 
     edge_flops = 2 * edge_count * features * (2 * features + lanes + node_count)
     node_flops = 2 * node_count * features * 3 * features
@@ -443,6 +440,7 @@
         ],
         edge_flops + node_flops,
         "layer_0",
+        16,
     )
     tables = [node_full] + neighbour_rows(right, left, coarse, halo)
     late_d = swap(after(late_x, *tables[1:]), 1)
@@ -466,6 +464,7 @@
         ],
         edge_flops + node_flops,
         "layer_1",
+        16,
     )
     return (node_own, edge_own)
 

time: 72.9 us -> 87.4 us (1.20)
  local copies, waits for them, and re-layouts: 7.96 us -> 14.1 us
  waiting for transfers between devices: 21.3 us -> 25.6 us
  starting transfers between devices: 19.2 us -> 22.7 us
    unnamed x38 -> x56, local copies, waits for them, and re-layouts: 7.27 us -> 13.4 us
    ppermute x1, waiting for transfers between devices: 0.01 us -> 5.57 us  [on_device(): far = lax.ppermute(near, 'groups', [(0, 1), (1, 0)])]
    ppermute x6, starting transfers between devices: 9.39 us -> 12 us  [shift(): return lax.ppermute(x, 'graph', [(i, (i + by) % size) for i in range(size)])]
    ppermute x6, waiting for transfers between devices: 6.99 us -> 4.65 us  [shift(): return lax.ppermute(x, 'graph', [(i, (i + by) % size) for i in range(size)])]
    ppermute x15, waiting for transfers between devices: 14.3 us -> 15.4 us  [swap(): return lax.ppermute(x, 'mp', [(i, i ^ mask) for i in range(size)])]
    ppermute x15, starting transfers between devices: 8.28 us -> 9.27 us  [swap(): return lax.ppermute(x, 'mp', [(i, i ^ mask) for i in range(size)])]
  transfers between devices with their start and end apart: 22 -> 22, of which waited for: 8 -> 7; matrix products, arithmetic and copies ran while one was open for 1% -> 1% of each run, Pallas kernels for 15% -> 12%
where the time goes in v7:
time: 87.4 us; the launch traced here: 86.9 us
  waiting for transfers between devices  25.6 us (29%)
  Pallas kernels  22.7 us (26%)
  starting transfers between devices  22.7 us (26%)
  local copies, waits for them, and re-layouts  14.1 us (16%)
  between operations  1.07 us (1%)
    pallas_call x6, Pallas kernels, call(): pl.pallas_call(kernel, out_shape=out_shape, in_specs=[pl.BlockSpec(memory...  22.7 us
    ppermute x15, waiting for transfers between devices, swap(): return lax.ppermute(x, 'mp', [(i, i ^ mask) for i in range(size)])  15.4 us
    unnamed x56, local copies, waits for them, and re-layouts  13.4 us
    ppermute x6, starting transfers between devices, shift(): return lax.ppermute(x, 'graph', [(i, (i + by) % size) for i in range(size)])  12 us
    ppermute x15, starting transfers between devices, swap(): return lax.ppermute(x, 'mp', [(i, i ^ mask) for i in range(size)])  9.27 us
    ppermute x1, waiting for transfers between devices, on_device(): far = lax.ppermute(near, 'groups', [(0, 1), (1, 0)])  5.57 us
    ppermute x6, waiting for transfers between devices, shift(): return lax.ppermute(x, 'graph', [(i, (i + by) % size) for i in range(size)])  4.65 us
  transfers between devices with their start and end apart: 22, of which 7 were waited for; matrix products, arithmetic and copies ran while one was open for 1% of the time, Pallas kernels for 12%

profile of v7, /device:TPU:0, one launch (start us, length us, event | category | flops | bytes accessed | tf_op | source)
XLA Modules:
  0.0 86.9 jit_solution(13182047283069751862)
XLA Ops:
  1.2 2.7 %layer_0_half.1 = bf16[1792,128]{1,0:T(8,128)(2,1)} custom-call(s32[3]{0:T(128)} %pad_add_fusion.1.spot_ref, bf16[2,1536,128]{2,1,0:T(8,128)(2,1)} %refs_0_.3, bf16[2,128,512]{2,1,0:T(8,128)(2,1)} %refs_1_.3, bf16[2,1024,128]{2,1,0:T(8,128)(2,1)} %refs_2_.3, bf16[2,128,512]{2,1,0:T(8,128)(2,1)} %refs_3_.3), custom_call_target="tpu_custom_call" | custom-call | bytes 2293772 | tf_op jit(solution)/shard_map/layer_0_half/pallas_call | solution.py:271
  4.0 3.0 %collective-permute-start.4 = (bf16[1792,128]{1,0:T(8,128)(2,1)}, bf16[1792,128]{1,0:T(8,128)(2,1)}, u32[]{:S(2)}, u32[]{:S(2)}) collective-permute-start(bf16[1792,128]{1,0:T(8,128)(2,1)} %layer_0_half.1), channel_id=1, source_target_pairs={{0,2},{1,3},{2,0},{3,1},{4,6},{5,7},{6,4},{7,5},{8,10},{9,11},{10,... | collective-permute-start | bytes 1376264 | tf_op jit(solution)/shard_map/ppermute | solution.py:285
  7.5 1.3 %one_hot.1 = (bf16[1536,512]{1,0:T(8,128)(2,1)S(1)}, bf16[192,1536]{1,0:T(8,128)(2,1)S(1)}, bf16[3584,128]{1,0:T(8,128)(2,1)S(1)}) custom-call(s32[1536,2]{1,0:T(8,128)S(1)} %copy.17.index_ref, s32[1,1536]{1,0:T(1,128)S(1)} %broadcast_in_dim.21.receiver_ref, bf16[2,1536,128]{2,1,0:T(8,128)(2,1)S(1)} %copy-done, bf16[2,128,512]{2,1,0:T(8,128)(2,1)S(1)} %copy-done.2, ...), custom_call_target="tpu_custom_call" | custom-call | bytes 4933632 | tf_op jit(solution)/shard_map/one_hot/pallas_call | solution.py:271
  8.8 1.2 %copy-done.7 = bf16[1536,512]{1,0:T(8,128)(2,1)} copy-done((bf16[1536,512]{1,0:T(8,128)(2,1)}, bf16[1536,512]{1,0:T(8,128)(2,1)S(1)}, u32[]{:S(2)}) %copy-start.7) | copy-done | bytes 1572888
  12.2 1.6 %collective-permute-start.12 = (bf16[48,128]{1,0:T(8,128)(2,1)S(1)}, bf16[48,128]{1,0:T(8,128)(2,1)S(1)}, u32[]{:S(2)}, u32[]{:S(2)}) collective-permute-start(bf16[48,128]{1,0:T(8,128)(2,1)S(1)} %get-tuple-element.41), channel_id=1, source_target_pairs={{0,4},{4,8},{8,12},{12,0},{1,5},{5,9},{9,13},{13,1},{2,6},{6,10},{... | collective-permute-start | bytes 36872 | tf_op jit(solution)/shard_map/ppermute | solution.py:290
  14.4 2.6 %collective-permute-start.14 = (bf16[16,128]{1,0:T(8,128)(2,1)S(1)}, bf16[16,128]{1,0:T(8,128)(2,1)S(1)}, u32[]{:S(2)}, u32[]{:S(2)}) collective-permute-start(bf16[16,128]{1,0:T(8,128)(2,1)S(1)} %get-tuple-element.43), channel_id=1, source_target_pairs={{0,8},{4,12},{8,0},{12,4},{1,9},{5,13},{9,1},{13,5},{2,10},{6,14},... | collective-permute-start | bytes 12296 | tf_op jit(solution)/shard_map/ppermute | solution.py:290
  17.8 3.8 %collective-permute-start.13 = (bf16[48,128]{1,0:T(8,128)(2,1)S(1)}, bf16[48,128]{1,0:T(8,128)(2,1)S(1)}, u32[]{:S(2)}, u32[]{:S(2)}) collective-permute-start(bf16[48,128]{1,0:T(8,128)(2,1)S(1)} %get-tuple-element.42), channel_id=1, source_target_pairs={{0,12},{4,0},{8,4},{12,8},{1,13},{5,1},{9,5},{13,9},{2,14},{6,2},{... | collective-permute-start | bytes 36872 | tf_op jit(solution)/shard_map/ppermute | solution.py:290
  21.7 1.5 %collective-permute-start.5 = (bf16[1728,128]{1,0:T(8,128)(2,1)S(1)}, bf16[1728,128]{1,0:T(8,128)(2,1)}, u32[]{:S(2)}, u32[]{:S(2)}) collective-permute-start(bf16[1728,128]{1,0:T(8,128)(2,1)S(1)} %latents.1.refs_12_), channel_id=1, source_target_pairs={{0,2},{1,3},{2,0},{3,1},{4,6},{5,7},{6,4},{7,5},{8,10},{9,11},{10,... | collective-permute-start | bytes 1327112 | tf_op jit(solution)/shard_map/ppermute | solution.py:285
  23.2 1.4 %collective-permute-start.16 = (bf16[112,128]{1,0:T(8,128)(2,1)S(1)}, bf16[112,128]{1,0:T(8,128)(2,1)S(1)}, u32[]{:S(2)}, u32[]{:S(2)}) collective-permute-start(bf16[112,128]{1,0:T(8,128)(2,1)S(1)} %constant_dynamic-update-slice_fusion.refs_16_), channel_id=1, source_target_pairs={{0,2},{1,3},{2,0},{3,1},{4,6},{5,7},{6,4},{7,5},{8,10},{9,11},{10,... | collective-permute-start | bytes 86024 | tf_op jit(solution)/shard_map/ppermute | solution.py:285
  24.7 8.4 %collective-permute-done.16.refs_18_ = bf16[112,128]{1,0:T(8,128)(2,1)S(1)} collective-permute-done((bf16[112,128]{1,0:T(8,128)(2,1)S(1)}, bf16[112,128]{1,0:T(8,128)(2,1)S(1)}, u32[]{:S(2)}, u32[]{:S(2)}) %collective-permute-start.16) | collective-permute-done | bytes 28704 | tf_op jit(solution)/shard_map/ppermute | solution.py:285
  33.7 1.5 %collective-permute-start.7 = (bf16[1792,128]{1,0:T(8,128)(2,1)}, bf16[1792,128]{1,0:T(8,128)(2,1)}, u32[]{:S(2)}, u32[]{:S(2)}) collective-permute-start(bf16[1792,128]{1,0:T(8,128)(2,1)} %collective-permute-done.4.refs_8_), channel_id=1, source_target_pairs={{0,16},{16,0},{1,17},{17,1},{2,18},{18,2},{3,19},{19,3},{4,20},{20... | collective-permute-start | bytes 1376264 | tf_op jit(solution)/shard_map/ppermute | solution.py:411
  36.5 1.8 %collective-permute-done.3.refs_7_ = bf16[2,128,512]{2,1,0:T(8,128)(2,1)S(1)} collective-permute-done((bf16[2,128,512]{2,1,0:T(8,128)(2,1)S(1)}, bf16[2,128,512]{2,1,0:T(8,128)(2,1)S(1)}, u32[]{:S(2)}, u32[]{:S(2)}) %collective-permute-start.3) | collective-permute-done | bytes 262176 | tf_op jit(solution)/shard_map/ppermute | solution.py:285
  39.0 1.5 %collective-permute-start.6 = (bf16[3584,128]{1,0:T(8,128)(2,1)}, bf16[3584,128]{1,0:T(8,128)(2,1)}, u32[]{:S(2)}, u32[]{:S(2)}) collective-permute-start(bf16[3584,128]{1,0:T(8,128)(2,1)} %copy-done.9), channel_id=1, source_target_pairs={{0,2},{1,3},{2,0},{3,1},{4,6},{5,7},{6,4},{7,5},{8,10},{9,11},{10,... | collective-permute-start | bytes 2752520 | tf_op jit(solution)/shard_map/ppermute | solution.py:285
  41.3 5.6 %collective-permute-done.7.refs_9_ = bf16[1792,128]{1,0:T(8,128)(2,1)} collective-permute-done((bf16[1792,128]{1,0:T(8,128)(2,1)}, bf16[1792,128]{1,0:T(8,128)(2,1)}, u32[]{:S(2)}, u32[]{:S(2)}) %collective-permute-start.7) | collective-permute-done | bytes 458784 | tf_op jit(solution)/shard_map/ppermute | solution.py:411
  48.3 1.6 %collective-permute-done.11.refs_15_ = bf16[1728,128]{1,0:T(8,128)(2,1)} collective-permute-done((bf16[1728,128]{1,0:T(8,128)(2,1)}, bf16[1728,128]{1,0:T(8,128)(2,1)}, u32[]{:S(2)}, u32[]{:S(2)}) %collective-permute-start.11) | collective-permute-done | bytes 442400 | tf_op jit(solution)/shard_map/ppermute | solution.py:285
  50.0 1.4 %copy-done.8 = bf16[1536,512]{1,0:T(8,128)(2,1)S(1)} copy-done((bf16[1536,512]{1,0:T(8,128)(2,1)S(1)}, bf16[1536,512]{1,0:T(8,128)(2,1)}, u32[]{:S(2)}) %copy-start.8) | copy-done | bytes 1572888
  51.4 1.1 %copy-done.11 = bf16[192,1536]{1,0:T(8,128)(2,1)S(1)} copy-done((bf16[192,1536]{1,0:T(8,128)(2,1)S(1)}, bf16[192,1536]{1,0:T(8,128)(2,1)}, u32[]{:S(2)}) %copy-start.11) | copy-done | bytes 589848
  52.5 1.0 %copy-done.14 = bf16[2,1024,128]{2,1,0:T(8,128)(2,1)S(1)} copy-done((bf16[2,1024,128]{2,1,0:T(8,128)(2,1)S(1)}, bf16[2,1024,128]{2,1,0:T(8,128)(2,1)}, u32[]{:S(2)}) %copy-start.14) | copy-done | bytes 524312
  53.5 1.0 %copy-done.17 = bf16[1728,128]{1,0:T(8,128)(2,1)S(1)} copy-done((bf16[1728,128]{1,0:T(8,128)(2,1)S(1)}, bf16[1728,128]{1,0:T(8,128)(2,1)}, u32[]{:S(2)}) %copy-start.17) | copy-done | bytes 442392
  57.0 9.3 %layer_0.1 = (f32[1536,128]{1,0:T(8,128)S(1)}, bf16[1536,512]{1,0:T(8,128)(2,1)S(1)}, f32[192,128]{1,0:T(8,128)S(1)}, bf16[192,512]{1,0:T(8,128)(2,1)S(1)}, bf16...) custom-call(s32[3]{0:T(128)S(1)} %copy-done.6, ...), custom_call_target="tpu_custom_call" | custom-call | flops 3019898880 | bytes 13205964 | tf_op jit(solution)/shard_map/layer_0/pallas_call | solution.py:271
  66.4 3.8 %collective-permute-start.19 = (bf16[48,512]{1,0:T(8,128)(2,1)S(1)}, bf16[48,512]{1,0:T(8,128)(2,1)S(1)}, u32[]{:S(2)}, u32[]{:S(2)}) collective-permute-start(bf16[48,512]{1,0:T(8,128)(2,1)S(1)} %get-tuple-element.47), channel_id=1, source_target_pairs={{0,12},{4,0},{8,4},{12,8},{1,13},{5,1},{9,5},{13,9},{2,14},{6,2},{... | collective-permute-start | bytes 147464 | tf_op jit(solution)/shard_map/ppermute | solution.py:290
  70.2 4.6 %collective-permute-done.20.refs_16_ = bf16[16,512]{1,0:T(8,128)(2,1)S(1)} collective-permute-done((bf16[16,512]{1,0:T(8,128)(2,1)S(1)}, bf16[16,512]{1,0:T(8,128)(2,1)S(1)}, u32[]{:S(2)}, u32[]{:S(2)}) %collective-permute-start.20) | collective-permute-done | bytes 16416 | tf_op jit(solution)/shard_map/ppermute | solution.py:290
  74.9 2.7 %collective-permute-done.21.refs_9_ = bf16[3584,128]{1,0:T(8,128)(2,1)S(1)} collective-permute-done((bf16[3584,128]{1,0:T(8,128)(2,1)}, bf16[3584,128]{1,0:T(8,128)(2,1)S(1)}, u32[]{:S(2)}, u32[]{:S(2)}) %collective-permute-start.21) | collective-permute-done | bytes 917536 | tf_op jit(solution)/shard_map/ppermute | solution.py:285
  77.6 9.1 %layer_1.1 = (f32[1536,128]{1,0:T(8,128)}, f32[192,128]{1,0:T(8,128)}) custom-call(s32[3]{0:T(128)S(1)} %copy-done.6, bf16[2,1536,128]{2,1,0:T(8,128)(2,1)S(1)} %copy-done, bf16[2,128,512]{2,1,0:T(8,128)(2,1)S(1)} %copy-done.2, bf16[2,1024,128]{2,1,0:T(8,128)(2,1)S(1)} %copy-done.1, bf16[2,128,512]{2,1,0:T(8,128)(2,1)S(1)} %copy-done.3, ...), custom_call_target="tpu_custom_call" | custom-call | flops 3019898880 | bytes 11321356 | tf_op jit(solution)/shard_map/layer_1/pallas_call | solution.py:271
  (96 shorter events, 12.1 us)
Async XLA Ops:
  4.0 13.8 %collective-permute-start.4 = (bf16[1792,128]{1,0:T(8,128)(2,1)}, bf16[1792,128]{1,0:T(8,128)(2,1)}, u32[]{:S(2)}, u32[]{:S(2)}) collective-permute-start(bf16[1792,128]{1,0:T(8,128)(2,1)} %layer_0_half.1), channel_id=1, source_target_pairs={{0,2},{1,3},{2,0},{3,1},{4,6},{5,7},{6,4},{7,5},{8,10},{9,11},{10,... | collective-permute-start | bytes 1376264 | tf_op jit(solution)/shard_map/ppermute | solution.py:285
  7.5 42.5 %copy-start.6 = (s32[3]{0:T(128)S(1)}, s32[3]{0:T(128)}, u32[]{:S(2)}) copy-start(s32[3]{0:T(128)} %pad_add_fusion.1.spot_ref) | copy-start | bytes 40
  12.2 9.5 %collective-permute-start.12 = (bf16[48,128]{1,0:T(8,128)(2,1)S(1)}, bf16[48,128]{1,0:T(8,128)(2,1)S(1)}, u32[]{:S(2)}, u32[]{:S(2)}) collective-permute-start(bf16[48,128]{1,0:T(8,128)(2,1)S(1)} %get-tuple-element.41), channel_id=1, source_target_pairs={{0,4},{4,8},{8,12},{12,0},{1,5},{5,9},{9,13},{13,1},{2,6},{6,10},{... | collective-permute-start | bytes 36872 | tf_op jit(solution)/shard_map/ppermute | solution.py:290
  13.8 22.2 %collective-permute-start.1 = (bf16[2,128,512]{2,1,0:T(8,128)(2,1)S(1)}, bf16[2,128,512]{2,1,0:T(8,128)(2,1)S(1)}, u32[]{:S(2)}, u32[]{:S(2)}) collective-permute-start(bf16[2,128,512]{2,1,0:T(8,128)(2,1)S(1)} %copy-done.2), channel_id=1, source_target_pairs={{0,1},{1,0},{2,3},{3,2},{4,5},{5,4},{6,7},{7,6},{8,9},{9,8},{10,11... | collective-permute-start | bytes 786440 | tf_op jit(solution)/shard_map/ppermute | solution.py:285
  13.8 33.1 %collective-permute-start.2 = (bf16[2,1024,128]{2,1,0:T(8,128)(2,1)S(1)}, bf16[2,1024,128]{2,1,0:T(8,128)(2,1)S(1)}, u32[]{:S(2)}, u32[]{:S(2)}) collective-permute-start(bf16[2,1024,128]{2,1,0:T(8,128)(2,1)S(1)} %copy-done.1), channel_id=1, source_target_pairs={{0,1},{1,0},{2,3},{3,2},{4,5},{5,4},{6,7},{7,6},{8,9},{9,8},{10,11... | collective-permute-start | bytes 1572872 | tf_op jit(solution)/shard_map/ppermute | solution.py:285
  14.4 8.8 %collective-permute-start.14 = (bf16[16,128]{1,0:T(8,128)(2,1)S(1)}, bf16[16,128]{1,0:T(8,128)(2,1)S(1)}, u32[]{:S(2)}, u32[]{:S(2)}) collective-permute-start(bf16[16,128]{1,0:T(8,128)(2,1)S(1)} %get-tuple-element.43), channel_id=1, source_target_pairs={{0,8},{4,12},{8,0},{12,4},{1,9},{5,13},{9,1},{13,5},{2,10},{6,14},... | collective-permute-start | bytes 12296 | tf_op jit(solution)/shard_map/ppermute | solution.py:290
  17.8 5.4 %collective-permute-start.13 = (bf16[48,128]{1,0:T(8,128)(2,1)S(1)}, bf16[48,128]{1,0:T(8,128)(2,1)S(1)}, u32[]{:S(2)}, u32[]{:S(2)}) collective-permute-start(bf16[48,128]{1,0:T(8,128)(2,1)S(1)} %get-tuple-element.42), channel_id=1, source_target_pairs={{0,12},{4,0},{8,4},{12,8},{1,13},{5,1},{9,5},{13,9},{2,14},{6,2},{... | collective-permute-start | bytes 36872 | tf_op jit(solution)/shard_map/ppermute | solution.py:290
  21.7 14.6 %collective-permute-start.5 = (bf16[1728,128]{1,0:T(8,128)(2,1)S(1)}, bf16[1728,128]{1,0:T(8,128)(2,1)}, u32[]{:S(2)}, u32[]{:S(2)}) collective-permute-start(bf16[1728,128]{1,0:T(8,128)(2,1)S(1)} %latents.1.refs_12_), channel_id=1, source_target_pairs={{0,2},{1,3},{2,0},{3,1},{4,6},{5,7},{6,4},{7,5},{8,10},{9,11},{10,... | collective-permute-start | bytes 1327112 | tf_op jit(solution)/shard_map/ppermute | solution.py:285
  23.2 9.8 %collective-permute-start.16 = (bf16[112,128]{1,0:T(8,128)(2,1)S(1)}, bf16[112,128]{1,0:T(8,128)(2,1)S(1)}, u32[]{:S(2)}, u32[]{:S(2)}) collective-permute-start(bf16[112,128]{1,0:T(8,128)(2,1)S(1)} %constant_dynamic-update-slice_fusion.refs_16_), channel_id=1, source_target_pairs={{0,2},{1,3},{2,0},{3,1},{4,6},{5,7},{6,4},{7,5},{8,10},{9,11},{10,... | collective-permute-start | bytes 86024 | tf_op jit(solution)/shard_map/ppermute | solution.py:285
  24.7 8.4 %collective-permute-start.15 = (bf16[112,128]{1,0:T(8,128)(2,1)S(1)}, bf16[112,128]{1,0:T(8,128)(2,1)S(1)}, u32[]{:S(2)}, u32[]{:S(2)}) collective-permute-start(bf16[112,128]{1,0:T(8,128)(2,1)S(1)} %constant_dynamic-update-slice_fusion.refs_16_), channel_id=1, source_target_pairs={{0,1},{1,0},{2,3},{3,2},{4,5},{5,4},{6,7},{7,6},{8,9},{9,8},{10,11... | collective-permute-start | bytes 86024 | tf_op jit(solution)/shard_map/ppermute | solution.py:285
  33.1 2.1 %collective-permute-start.17 = (bf16[112,128]{1,0:T(8,128)(2,1)S(1)}, bf16[112,128]{1,0:T(8,128)(2,1)S(1)}, u32[]{:S(2)}, u32[]{:S(2)}) collective-permute-start(bf16[112,128]{1,0:T(8,128)(2,1)S(1)} %collective-permute-done.16.refs_18_), channel_id=1, source_target_pairs={{0,1},{1,0},{2,3},{3,2},{4,5},{5,4},{6,7},{7,6},{8,9},{9,8},{10,11... | collective-permute-start | bytes 86024 | tf_op jit(solution)/shard_map/ppermute | solution.py:285
  33.7 13.2 %collective-permute-start.7 = (bf16[1792,128]{1,0:T(8,128)(2,1)}, bf16[1792,128]{1,0:T(8,128)(2,1)}, u32[]{:S(2)}, u32[]{:S(2)}) collective-permute-start(bf16[1792,128]{1,0:T(8,128)(2,1)} %collective-permute-done.4.refs_8_), channel_id=1, source_target_pairs={{0,16},{16,0},{1,17},{17,1},{2,18},{18,2},{3,19},{19,3},{4,20},{20... | collective-permute-start | bytes 1376264 | tf_op jit(solution)/shard_map/ppermute | solution.py:411
  35.8 4.7 %collective-permute-start.10 = (bf16[1728,128]{1,0:T(8,128)(2,1)S(1)}, bf16[1728,128]{1,0:T(8,128)(2,1)S(1)}, u32[]{:S(2)}, u32[]{:S(2)}) collective-permute-start(bf16[1728,128]{1,0:T(8,128)(2,1)S(1)} %latents.1.refs_12_), channel_id=1, source_target_pairs={{0,1},{1,0},{2,3},{3,2},{4,5},{5,4},{6,7},{7,6},{8,9},{9,8},{10,11... | collective-permute-start | bytes 1327112 | tf_op jit(solution)/shard_map/ppermute | solution.py:285
  36.0 2.3 %collective-permute-start.3 = (bf16[2,128,512]{2,1,0:T(8,128)(2,1)S(1)}, bf16[2,128,512]{2,1,0:T(8,128)(2,1)S(1)}, u32[]{:S(2)}, u32[]{:S(2)}) collective-permute-start(bf16[2,128,512]{2,1,0:T(8,128)(2,1)S(1)} %copy-done.3), channel_id=1, source_target_pairs={{0,1},{1,0},{2,3},{3,2},{4,5},{5,4},{6,7},{7,6},{8,9},{9,8},{10,11... | collective-permute-start | bytes 786440 | tf_op jit(solution)/shard_map/ppermute | solution.py:285
  36.3 12.0 %collective-permute-start = (bf16[2,1536,128]{2,1,0:T(8,128)(2,1)S(1)}, bf16[2,1536,128]{2,1,0:T(8,128)(2,1)}, u32[]{:S(2)}, u32[]{:S(2)}) collective-permute-start(bf16[2,1536,128]{2,1,0:T(8,128)(2,1)S(1)} %copy-done), channel_id=1, source_target_pairs={{0,1},{1,0},{2,3},{3,2},{4,5},{5,4},{6,7},{7,6},{8,9},{9,8},{10,11... | collective-permute-start | bytes 2359304 | tf_op jit(solution)/shard_map/ppermute | solution.py:285
  39.0 35.8 %collective-permute-start.6 = (bf16[3584,128]{1,0:T(8,128)(2,1)}, bf16[3584,128]{1,0:T(8,128)(2,1)}, u32[]{:S(2)}, u32[]{:S(2)}) collective-permute-start(bf16[3584,128]{1,0:T(8,128)(2,1)} %copy-done.9), channel_id=1, source_target_pairs={{0,2},{1,3},{2,0},{3,1},{4,6},{5,7},{6,4},{7,5},{8,10},{9,11},{10,... | collective-permute-start | bytes 2752520 | tf_op jit(solution)/shard_map/ppermute | solution.py:285
  41.3 7.0 %collective-permute-start.8 = (bf16[1792,128]{1,0:T(8,128)(2,1)}, bf16[1792,128]{1,0:T(8,128)(2,1)}, u32[]{:S(2)}, u32[]{:S(2)}) collective-permute-start(bf16[1792,128]{1,0:T(8,128)(2,1)} %collective-permute-done.4.refs_8_), channel_id=1, source_target_pairs={{0,1},{1,0},{2,3},{3,2},{4,5},{5,4},{6,7},{7,6},{8,9},{9,8},{10,11... | collective-permute-start | bytes 1376264 | tf_op jit(solution)/shard_map/ppermute | solution.py:285
  46.9 3.1 %collective-permute-start.9 = (bf16[1792,128]{1,0:T(8,128)(2,1)}, bf16[1792,128]{1,0:T(8,128)(2,1)}, u32[]{:S(2)}, u32[]{:S(2)}) collective-permute-start(bf16[1792,128]{1,0:T(8,128)(2,1)} %collective-permute-done.7.refs_9_), channel_id=1, source_target_pairs={{0,1},{1,0},{2,3},{3,2},{4,5},{5,4},{6,7},{7,6},{8,9},{9,8},{10,11... | collective-permute-start | bytes 1376264 | tf_op jit(solution)/shard_map/ppermute | solution.py:285
  47.7 2.3 %collective-permute-start.11 = (bf16[1728,128]{1,0:T(8,128)(2,1)}, bf16[1728,128]{1,0:T(8,128)(2,1)}, u32[]{:S(2)}, u32[]{:S(2)}) collective-permute-start(bf16[1728,128]{1,0:T(8,128)(2,1)} %collective-permute-done.5.refs_14_), channel_id=1, source_target_pairs={{0,1},{1,0},{2,3},{3,2},{4,5},{5,4},{6,7},{7,6},{8,9},{9,8},{10,11... | collective-permute-start | bytes 1327112 | tf_op jit(solution)/shard_map/ppermute | solution.py:285
  57.0 20.7 %copy-start.15 = (bf16[2,1024,128]{2,1,0:T(8,128)(2,1)S(1)}, bf16[2,1024,128]{2,1,0:T(8,128)(2,1)}, u32[]{:S(2)}) copy-start(bf16[2,1024,128]{2,1,0:T(8,128)(2,1)} %copy-done.13) | copy-start | bytes 1572868
  66.3 8.5 %collective-permute-start.18 = (bf16[48,512]{1,0:T(8,128)(2,1)S(1)}, bf16[48,512]{1,0:T(8,128)(2,1)S(1)}, u32[]{:S(2)}, u32[]{:S(2)}) collective-permute-start(bf16[48,512]{1,0:T(8,128)(2,1)S(1)} %get-tuple-element.46), channel_id=1, source_target_pairs={{0,4},{4,8},{8,12},{12,0},{1,5},{5,9},{9,13},{13,1},{2,6},{6,10},{... | collective-permute-start | bytes 147464 | tf_op jit(solution)/shard_map/ppermute | solution.py:290
  66.4 8.5 %collective-permute-start.19 = (bf16[48,512]{1,0:T(8,128)(2,1)S(1)}, bf16[48,512]{1,0:T(8,128)(2,1)S(1)}, u32[]{:S(2)}, u32[]{:S(2)}) collective-permute-start(bf16[48,512]{1,0:T(8,128)(2,1)S(1)} %get-tuple-element.47), channel_id=1, source_target_pairs={{0,12},{4,0},{8,4},{12,8},{1,13},{5,1},{9,5},{13,9},{2,14},{6,2},{... | collective-permute-start | bytes 147464 | tf_op jit(solution)/shard_map/ppermute | solution.py:290
  70.2 4.6 %collective-permute-start.20 = (bf16[16,512]{1,0:T(8,128)(2,1)S(1)}, bf16[16,512]{1,0:T(8,128)(2,1)S(1)}, u32[]{:S(2)}, u32[]{:S(2)}) collective-permute-start(bf16[16,512]{1,0:T(8,128)(2,1)S(1)} %get-tuple-element.48), channel_id=1, source_target_pairs={{0,8},{4,12},{8,0},{12,4},{1,9},{5,13},{9,1},{13,5},{2,10},{6,14},... | collective-permute-start | bytes 49160 | tf_op jit(solution)/shard_map/ppermute | solution.py:290
  74.9 2.7 %collective-permute-start.21 = (bf16[3584,128]{1,0:T(8,128)(2,1)}, bf16[3584,128]{1,0:T(8,128)(2,1)S(1)}, u32[]{:S(2)}, u32[]{:S(2)}) collective-permute-start(bf16[3584,128]{1,0:T(8,128)(2,1)} %collective-permute-done.6.refs_8_), channel_id=1, source_target_pairs={{0,1},{1,0},{2,3},{3,2},{4,5},{5,4},{6,7},{7,6},{8,9},{9,8},{10,11... | collective-permute-start | bytes 2752520 | tf_op jit(solution)/shard_map/ppermute | solution.py:285
  (25 other events, 85.0 us)

commit v8 on v7

--- a/solution.py
+++ b/solution.py
@@ -31,8 +31,8 @@
     return jnp.dot(a, b, preferred_element_type=F32)
 
 
-def own_columns(full, spot_ref, part):
-    mine = spot_ref[0]
+def own_columns(full, part):
+    mine = lax.axis_index("mp")
     out = full[:, 0:part]
     for j in range(1, full.shape[1] // part):
         out = jnp.where(mine == j, full[:, j * part : (j + 1) * part], out)
@@ -87,8 +87,8 @@
     return base + rows + features // part * deep
 
 
-def ride_kernel(spot_ref, ef, es, nf, ns, ride_out, sems):
-    y = spot_ref[1]
+def ride_kernel(ef, es, nf, ns, ride_out, sems):
+    y = lax.axis_index("groups")
     part, features = es.shape[1:]
     copies = Copies(sems)
     at = 0
@@ -105,8 +105,18 @@
     copies.wait()
 
 
-def prepare_kernel(index_ref, receiver_ref, ef, es, nf, ns, hot_out, incidence_out, late_out, sems):
+def one_hot(hit):
+    return jnp.where(hit, 1.0, 0.0).astype(BF16)
+
+
+def column(row):
+    return jnp.broadcast_to(row, (8, row.shape[1])).T[:, 0:1]
+
+
+def prepare_kernel(blocks, halo, table_rows, list_ref, ef, es, nf, ns, hot_out, incidence_out, pick_out, late_out, sems):
     part, features = es.shape[1:]
+    edge_count, lanes_all = hot_out.shape
+    node_count = incidence_out.shape[0]
     copies = Copies(sems)
     at = 0
     for first, second in ((ef, es), (nf, ns)):
@@ -116,30 +126,44 @@
         for q in range(features // part):
             copies.start(second.at[1, :, pl.ds(q * part, part)], late_out.at[pl.ds(at, part)])
             at += part
-    for at in range(0, hot_out.shape[0], TILE):
-        rows = slice(at, at + TILE)
-        index = index_ref[rows, :]
-        lanes = lax.broadcasted_iota(jnp.int32, (TILE, hot_out.shape[1]), 1)
-        hot = (lanes == index[:, 0:1]) | (lanes == index[:, 1:2])
-        hot_out[rows, :] = jnp.where(hot, 1.0, 0.0).astype(BF16)
-        node_ids = lax.broadcasted_iota(jnp.int32, (incidence_out.shape[0], TILE), 0)
-        hit = node_ids == receiver_ref[:, rows]
-        incidence_out[:, rows] = jnp.where(hit, 1.0, 0.0).astype(BF16)
+    for at in range(0, edge_count, TILE):
+        senders = table_index(list_ref[:, at : at + TILE], blocks, node_count, halo)
+        receivers = list_ref[:, edge_count + at : edge_count + at + TILE]
+        lanes = lax.broadcasted_iota(jnp.int32, (TILE, lanes_all), 1)
+        hit = (lanes == column(senders)) | (lanes == column(receivers) + table_rows)
+        hot_out[at : at + TILE, :] = one_hot(hit)
+        node_ids = lax.broadcasted_iota(jnp.int32, (node_count, TILE), 0)
+        incidence_out[:, at : at + TILE] = one_hot(node_ids == receivers)
+    wanted = column(list_ref[:, 2 * edge_count : 2 * edge_count + 2 * halo])
+    lanes = lax.broadcasted_iota(jnp.int32, (halo, node_count), 1)
+    number = lax.broadcasted_iota(jnp.int32, (COARSE_PAD, node_count), 0)
+    ids = lax.broadcasted_iota(jnp.int32, (COARSE_PAD, node_count), 1)
+    coarse = one_hot((ids == number + (node_count - COARSE_DEV)) & (number < COARSE_DEV))
+    wide = halo + COARSE_PAD
+    pick_out[0:halo, :] = one_hot(lanes == wanted[halo:])
+    pick_out[wide : wide + halo, :] = one_hot(lanes == wanted[:halo])
+    for at in (halo, wide + halo, 2 * wide):
+        pick_out[at : at + COARSE_PAD, :] = coarse
     copies.wait()
 
 
-def pick_rows(wanted_ref, node_bf, outs):
-    wanted = wanted_ref[...]
-    lanes = lax.broadcasted_iota(jnp.int32, (wanted.shape[0], node_bf.shape[0]), 1)
-    picked = dot(jnp.where(lanes == wanted, 1.0, 0.0).astype(BF16), node_bf).astype(BF16)
+def pick_rows(pick_ref, node_bf, outs):
+    picked = dot(pick_ref[...], node_bf).astype(BF16)
     start = 0
     for out in outs:
         out[...] = picked[start : start + out.shape[0]]
         start += out.shape[0]
 
 
-def start_kernel(node_ref, wanted_ref, right, left, coarse):
-    pick_rows(wanted_ref, node_ref[...].astype(BF16), (right, left, coarse))
+def join_kernel(*refs):
+    at = 0
+    for piece in refs[:-1]:
+        refs[-1][at : at + piece.shape[0], :] = piece[...]
+        at += piece.shape[0]
+
+
+def start_kernel(node_ref, pick_ref, right, left, coarse):
+    pick_rows(pick_ref, node_ref[...].astype(BF16), (right, left, coarse))
 
 
 def latent_kernel(edge_ref, node_ref, out):
@@ -148,7 +172,7 @@
     out[at:, :] = node_ref[...].astype(BF16)
 
 
-def edge_rows(spot_ref, edge_ref, table, nodes, own_ref, hot_ref, incidence_ref, first_ref, second_ref, product_ref, own_out, full_out):
+def edge_rows(edge_ref, table, nodes, own_ref, hot_ref, incidence_ref, first_ref, second_ref, product_ref, own_out, full_out):
     features = second_ref.shape[1]
     node_count = nodes.shape[0]
     table_rows = table.shape[0]
@@ -170,27 +194,27 @@
         edge_new = (edge_bf.astype(F32) + norm).astype(BF16)
         if full_out is not None:
             full_out[rows, :] = edge_new
-        own_out[rows, :] = own_ref[rows, :] + own_columns(norm, spot_ref, part)
+        own_out[rows, :] = own_ref[rows, :] + own_columns(norm, part)
         incoming = incoming + dot(incidence_ref[:, rows], edge_new)
     return incoming.astype(BF16)
 
 
-def node_rows(spot_ref, node_bf, incoming, own_ref, first_ref, second_ref, own_out):
+def node_rows(node_bf, incoming, own_ref, first_ref, second_ref, own_out):
     features = second_ref.shape[1]
     pre = dot(node_bf, first_ref[0:features, :]) + dot(incoming, first_ref[features:, :])
     norm = normalize(dot(silu(pre).astype(BF16), second_ref[...]))
-    own_out[...] = own_ref[...] + own_columns(norm, spot_ref, own_ref.shape[1])
+    own_out[...] = own_ref[...] + own_columns(norm, own_ref.shape[1])
     return (node_bf.astype(F32) + norm).astype(BF16)
 
 
-def first_kernel(spot_ref, *refs):
+def first_kernel(*refs):
     refs = list(refs)
     own_w = [refs.pop(0) for _ in range(4)]
     core_w = [refs.pop(0) for _ in range(4)]
     halves = [[refs.pop(0) for _ in range(2)] for _ in range(2)]
     shards = [refs.pop(0) for _ in range(4)]
     rims = [refs.pop(0) for _ in range(4)]
-    edge_own, node_own, hot_ref, incidence_ref, wanted_ref = [refs.pop(0) for _ in range(5)]
+    edge_own, node_own, hot_ref, incidence_ref, pick_ref = [refs.pop(0) for _ in range(5)]
     edge_out, full_out, node_out, node_full = [refs.pop(0) for _ in range(4)]
     sends = [refs.pop(0) for _ in range(3)]
     edge_w, edge_w2, node_w, node_w2, product_ref, x_ref, edge_sems, node_sems = refs
@@ -201,9 +225,9 @@
     for pieces, at in ((shards, 0), (rims, edge_count + node_count)):
         rows = pl.ds(at, pieces[0].shape[0])
         for j, shard in enumerate(pieces):
-            column = pl.multiple_of((spot_ref[0] ^ j) * part, part)
+            column = pl.multiple_of((lax.axis_index("mp") ^ j) * part, part)
             edge_copies.start(shard, x_ref.at[rows, pl.ds(column, part)])
-    y = spot_ref[1]
+    y = lax.axis_index("groups")
     starts = [0, 0]
     for base, copies, (first, second), at in (
         (0, edge_copies, (edge_w, edge_w2), 0),
@@ -219,16 +243,16 @@
     edge_copies.wait()
     nodes = x_ref[edge_count : edge_count + node_count, :]
     incoming = edge_rows(
-        spot_ref, x_ref, x_ref[edge_count:, :], nodes, edge_own, hot_ref, incidence_ref,
+        x_ref, x_ref[edge_count:, :], nodes, edge_own, hot_ref, incidence_ref,
         edge_w, edge_w2, product_ref, edge_out, full_out,
     )
     node_copies.wait()
-    node_new = node_rows(spot_ref, nodes, incoming, node_own, node_w, node_w2, node_out)
+    node_new = node_rows(nodes, incoming, node_own, node_w, node_w2, node_out)
     node_full[...] = node_new
-    pick_rows(wanted_ref, node_new, sends)
-
-
-def late_kernel(pieces, spot_ref, *refs):
+    pick_rows(pick_ref, node_new, sends)
+
+
+def late_kernel(pieces, *refs):
     refs = list(refs)
     own_w = [refs.pop(0) for _ in range(4)]
     core_w = [refs.pop(0) for _ in range(4)]
@@ -255,11 +279,11 @@
     edge_copies.wait()
     nodes = tables[0][...]
     incoming = edge_rows(
-        spot_ref, edge_ref, table_ref[...], nodes, edge_own, hot_ref, incidence_ref,
+        edge_ref, table_ref[...], nodes, edge_own, hot_ref, incidence_ref,
         edge_w, edge_w2, product_ref, edge_out, None,
     )
     node_copies.wait()
-    node_rows(spot_ref, nodes, incoming, node_own, node_w, node_w2, node_out)
+    node_rows(nodes, incoming, node_own, node_w, node_w2, node_out)
 
 
 SMEM, VMEM, ANY = pltpu.SMEM, pltpu.VMEM, pl.ANY
@@ -301,15 +325,15 @@
     return [shift(right[:halo], 1), shift(left[:halo], -1), everyone]
 
 
-def table_index(senders, node_count, halo):
-    size = lax.axis_size("graph")
+def table_index(senders, size, node_count, halo):
     coarse_start = node_count + 2 * halo
     number = jnp.maximum(senders - coarse_start, 0)
-    block, row = number // COARSE_DEV, number % COARSE_DEV
+    block = (number * 43691) >> 19
+    row = number - block * COARSE_DEV
     if size != 4:
         return jnp.where(senders < coarse_start, senders, coarse_start + block * COARSE_PAD + row)
     wide = halo + COARSE_PAD
-    away = (block - lax.axis_index("graph")) % size
+    away = (block - lax.axis_index("graph")) & 3
     starts = (node_count - COARSE_DEV, node_count + wide + halo, node_count + 2 * wide, node_count + halo)
     base = jnp.where(
         away < 2,
@@ -339,9 +363,6 @@
     blocks = lax.axis_size("graph")
     shape = jax.ShapeDtypeStruct
     dma = pltpu.SemaphoreType.DMA
-    block = lax.axis_index("graph")
-    group = lax.axis_index("groups")
-    spot = jnp.stack([lax.axis_index("mp"), group, group * blocks + block]).astype(jnp.int32)
 
     wide = halo + COARSE_PAD
 
@@ -354,34 +375,26 @@
     (ride,) = call(
         ride_kernel,
         [shape(((edge_pack + node_pack) // 2, part), BF16)],
-        [(SMEM, spot)] + [(ANY, w) for w in weights],
+        [(ANY, w) for w in weights],
         [dma((10,))],
         0,
         "layer_0_half",
         60,
     )
     near = swap(ride, 2)
-    own_coarse = jnp.arange(node_count - COARSE_DEV, node_count, dtype=jnp.int32)
-    padding = jnp.full((COARSE_PAD - COARSE_DEV,), -1, jnp.int32)
-    coarse_list = jnp.concatenate([own_coarse, padding])
-    boundary_rows, senders, receivers = lax.optimization_barrier(
-        (boundary_rows, senders, receivers, ride)
-    )[:3]
-    wanted = jnp.concatenate(
-        [boundary_rows[halo:], coarse_list, boundary_rows[:halo], coarse_list, coarse_list]
-    )[:, None]
     far_rows = 2 * wide + COARSE_PAD if blocks == 4 else 2 * halo + blocks * COARSE_PAD
     table_rows = node_count + far_rows
     lanes = -(-(table_rows + node_count) // 128) * 128
-    index = jnp.stack([table_index(senders, node_count, halo), receivers + table_rows], axis=1)
-    hot, incidence, late_w = call(
-        prepare_kernel,
+    lists = jnp.concatenate([senders, receivers, boundary_rows])[None, :]
+    hot, incidence, pick, late_w = call(
+        functools.partial(prepare_kernel, blocks, halo, table_rows),
         [
             shape((edge_count, lanes), BF16),
             shape((node_count, edge_count), BF16),
+            shape((2 * wide + COARSE_PAD, node_count), BF16),
             shape((edge_pack + node_pack, part), BF16),
         ],
-        [(VMEM, index), (VMEM, receivers[None, :])] + [(ANY, w) for w in weights],
+        [(VMEM, after(lists, ride))] + [(ANY, w) for w in weights],
         [dma((10,))],
         0,
         "one_hot",
@@ -398,17 +411,24 @@
     right, left, coarse = call(
         start_kernel,
         sent(part),
-        [(VMEM, node_state), (VMEM, after(wanted, latents))],
+        [(VMEM, node_state), (VMEM, after(pick, latents))],
         [],
-        2 * wanted.shape[0] * node_count * part,
+        2 * pick.size * part,
         "boundary_rows",
     )
-    far_latents = swap(after(latents, near), 2)
-    shards = [latents, swap(latents, 1), far_latents, swap(far_latents, 1)]
-    rim = jnp.concatenate(neighbour_rows(right, left, coarse, halo), axis=0)
+    (rim,) = call(
+        join_kernel,
+        [shape((far_rows, part), BF16)],
+        [(VMEM, r) for r in neighbour_rows(right, left, coarse, halo)],
+        [],
+        0,
+        "halo_rows",
+    )
+    far_latents = swap(after(latents, near, rim), 2)
+    far = lax.ppermute(near, "groups", [(0, 1), (1, 0)])
     far_rim = swap(rim, 2)
+    shards = [latents, swap(latents, 1), far_latents, swap(after(far_latents, far, far_rim), 1)]
     rims = [rim, swap(rim, 1), far_rim, swap(far_rim, 1)]
-    far = lax.ppermute(near, "groups", [(0, 1), (1, 0)])
     pairs = [near, far, swap(near, 1), swap(far, 1)]
     late_x = swap(after(late_w, far_latents), 2)
 
@@ -425,9 +445,8 @@
     edge_own, edge_full, node_own, node_full, right, left, coarse = call(
         first_kernel,
         [own_edge, full_edge, own_node, full_node] + sent(features),
-        [(SMEM, spot)]
-        + [(ANY, w) for w in list(weights) + core_w + pairs + shards + rims]
-        + [(VMEM, a) for a in (edge_state, node_state, hot, incidence, wanted)],
+        [(ANY, w) for w in list(weights) + core_w + pairs + shards + rims]
+        + [(VMEM, a) for a in (edge_state, node_state, hot, incidence, pick)],
         [
             edge_shape,
             second_shape,
@@ -447,8 +466,7 @@
     edge_own, node_own = call(
         functools.partial(late_kernel, len(tables)),
         [own_edge, own_node],
-        [(SMEM, spot)]
-        + [(ANY, w) for w in list(weights) + core_w + [late_x, late_d]]
+        [(ANY, w) for w in list(weights) + core_w + [late_x, late_d]]
         + [(VMEM, a) for a in (edge_full, edge_own, node_own)]
         + [(VMEM, t) for t in tables]
         + [(VMEM, hot), (VMEM, incidence)],

time: 87.4 us -> 72.1 us (0.82)
  local copies, waits for them, and re-layouts: 14.1 us -> 0.05 us
  waiting for transfers between devices: 25.6 us -> 31.2 us
  starting transfers between devices: 22.7 us -> 19.1 us
  Pallas kernels: 22.7 us -> 20.6 us
    unnamed x56 -> x18, local copies, waits for them, and re-layouts: 13.4 us -> 0.04 us
    ppermute x6, waiting for transfers between devices: 4.65 us -> 7.63 us  [shift(): return lax.ppermute(x, 'graph', [(i, (i + by) % size) for i in range(size)])]
    ppermute x6, starting transfers between devices: 12 us -> 9.28 us  [shift(): return lax.ppermute(x, 'graph', [(i, (i + by) % size) for i in range(size)])]
    ppermute x1, waiting for transfers between devices: 5.57 us -> 7.81 us  [on_device(): far = lax.ppermute(near, 'groups', [(0, 1), (1, 0)])]
    pallas_call x6 -> x7, Pallas kernels: 22.7 us -> 20.6 us  [call(): pl.pallas_call(kernel, out_shape=out_shape, in_specs=[pl.BlockSpec(memory...]
    ppermute x15, starting transfers between devices: 9.27 us -> 8.36 us  [swap(): return lax.ppermute(x, 'mp', [(i, i ^ mask) for i in range(size)])]
  transfers between devices with their start and end apart: 22 -> 22, of which waited for: 7 -> 8; matrix products, arithmetic and copies ran while one was open for 1% -> 0% of each run, Pallas kernels for 12% -> 14%
where the time goes in v8:
time: 72.1 us; the launch traced here: 72 us
  waiting for transfers between devices  31.2 us (43%)
  Pallas kernels  20.6 us (29%)
  starting transfers between devices  19.1 us (26%)
  between operations  1 us (1%)
    pallas_call x7, Pallas kernels, call(): pl.pallas_call(kernel, out_shape=out_shape, in_specs=[pl.BlockSpec(memory...  20.6 us
    ppermute x15, waiting for transfers between devices, swap(): return lax.ppermute(x, 'mp', [(i, i ^ mask) for i in range(size)])  15.8 us
    ppermute x6, starting transfers between devices, shift(): return lax.ppermute(x, 'graph', [(i, (i + by) % size) for i in range(size)])  9.28 us
    ppermute x15, starting transfers between devices, swap(): return lax.ppermute(x, 'mp', [(i, i ^ mask) for i in range(size)])  8.36 us
    ppermute x1, waiting for transfers between devices, on_device(): far = lax.ppermute(near, 'groups', [(0, 1), (1, 0)])  7.81 us
    ppermute x6, waiting for transfers between devices, shift(): return lax.ppermute(x, 'graph', [(i, (i + by) % size) for i in range(size)])  7.63 us
    ppermute x1, starting transfers between devices, on_device(): far = lax.ppermute(near, 'groups', [(0, 1), (1, 0)])  1.45 us
  transfers between devices with their start and end apart: 22, of which 8 were waited for; matrix products, arithmetic and copies ran while one was open for 0% of the time, Pallas kernels for 14%

profile of v8, /device:TPU:0, one launch (start us, length us, event | category | flops | bytes accessed | tf_op | source)
XLA Modules:
  0.0 72.0 jit_solution(10009299278075223477)
XLA Ops:
  0.7 2.0 %layer_0_half.1 = bf16[1792,128]{1,0:T(8,128)(2,1)} custom-call(bf16[2,1536,128]{2,1,0:T(8,128)(2,1)} %refs_0_.3, bf16[2,128,512]{2,1,0:T(8,128)(2,1)} %refs_1_.3, bf16[2,1024,128]{2,1,0:T(8,128)(2,1)} %refs_2_.3, bf16[2,128,512]{2,1,0:T(8,128)(2,1)} %refs_3_.3), custom_call_target="tpu_custom_call" | custom-call | bytes 2293760 | tf_op jit(solution)/shard_map/layer_0_half/pallas_call | solution.py:295
  2.8 3.0 %collective-permute-start.4 = (bf16[1792,128]{1,0:T(8,128)(2,1)}, bf16[1792,128]{1,0:T(8,128)(2,1)S(1)}, u32[]{:S(2)}, u32[]{:S(2)}) collective-permute-start(bf16[1792,128]{1,0:T(8,128)(2,1)} %layer_0_half.1), channel_id=1, source_target_pairs={{0,2},{1,3},{2,0},{3,1},{4,6},{5,7},{6,4},{7,5},{8,10},{9,11},{10,... | collective-permute-start | bytes 1376264 | tf_op jit(solution)/shard_map/ppermute | solution.py:309
  5.9 1.5 %one_hot.1 = (bf16[1536,512]{1,0:T(8,128)(2,1)S(1)}, bf16[192,1536]{1,0:T(8,128)(2,1)S(1)}, bf16[112,192]{1,0:T(8,128)(2,1)S(1)}, bf16[3584,128]{1,0:T(8,128)(2,1)S(1)}) custom-call(s32[1,3136]{1,0:T(1,128)S(1)} %broadcast_in_dim.3.list_ref, bf16[2,1536,128]{2,1,0:T(8,128)(2,1)S(1)} %copy-done, bf16[2,128,512]{2,1,0:T(8,128)(2,1)S(1)} %copy-done.2, ...), custom_call_target="tpu_custom_call" | custom-call | bytes 4970752 | tf_op jit(solution)/shard_map/one_hot/pallas_call | solution.py:295
  7.6 1.6 %collective-permute-start.5 = (bf16[48,128]{1,0:T(8,128)(2,1)S(1)}, bf16[48,128]{1,0:T(8,128)(2,1)S(1)}, u32[]{:S(2)}, u32[]{:S(2)}) collective-permute-start(bf16[48,128]{1,0:T(8,128)(2,1)S(1)} %get-tuple-element.38), channel_id=1, source_target_pairs={{0,4},{4,8},{8,12},{12,0},{1,5},{5,9},{9,13},{13,1},{2,6},{6,10},{... | collective-permute-start | bytes 36872 | tf_op jit(solution)/shard_map/ppermute | solution.py:314
  9.2 2.2 %collective-permute-start.6 = (bf16[48,128]{1,0:T(8,128)(2,1)S(1)}, bf16[48,128]{1,0:T(8,128)(2,1)S(1)}, u32[]{:S(2)}, u32[]{:S(2)}) collective-permute-start(bf16[48,128]{1,0:T(8,128)(2,1)S(1)} %get-tuple-element.39), channel_id=1, source_target_pairs={{0,12},{4,0},{8,4},{12,8},{1,13},{5,1},{9,5},{13,9},{2,14},{6,2},{... | collective-permute-start | bytes 36872 | tf_op jit(solution)/shard_map/ppermute | solution.py:314
  11.5 0.8 %collective-permute-start.7 = (bf16[16,128]{1,0:T(8,128)(2,1)S(1)}, bf16[16,128]{1,0:T(8,128)(2,1)S(1)}, u32[]{:S(2)}, u32[]{:S(2)}) collective-permute-start(bf16[16,128]{1,0:T(8,128)(2,1)S(1)} %get-tuple-element.40), channel_id=1, source_target_pairs={{0,8},{4,12},{8,0},{12,4},{1,9},{5,13},{9,1},{13,5},{2,10},{6,14},... | collective-permute-start | bytes 12296 | tf_op jit(solution)/shard_map/ppermute | solution.py:314
  12.3 3.7 %collective-permute-done.7.refs_2_ = bf16[16,128]{1,0:T(8,128)(2,1)S(1)} collective-permute-done((bf16[16,128]{1,0:T(8,128)(2,1)S(1)}, bf16[16,128]{1,0:T(8,128)(2,1)S(1)}, u32[]{:S(2)}, u32[]{:S(2)}) %collective-permute-start.7) | collective-permute-done | bytes 4128 | tf_op jit(solution)/shard_map/ppermute | solution.py:314
  16.0 0.5 collective-permute-done.4.refs_8_
  16.5 1.7 %collective-permute-start.8 = (bf16[1728,128]{1,0:T(8,128)(2,1)S(1)}, bf16[1728,128]{1,0:T(8,128)(2,1)S(1)}, u32[]{:S(2)}, u32[]{:S(2)}) collective-permute-start(bf16[1728,128]{1,0:T(8,128)(2,1)S(1)} %latents.1.refs_12_), channel_id=1, source_target_pairs={{0,2},{1,3},{2,0},{3,1},{4,6},{5,7},{6,4},{7,5},{8,10},{9,11},{10,... | collective-permute-start | bytes 1327112 | tf_op jit(solution)/shard_map/ppermute | solution.py:309
  18.2 0.5 collective-permute-start.2
  19.0 9.4 %collective-permute-done.14.refs_18_ = bf16[112,128]{1,0:T(8,128)(2,1)S(1)} collective-permute-done((bf16[112,128]{1,0:T(8,128)(2,1)S(1)}, bf16[112,128]{1,0:T(8,128)(2,1)S(1)}, u32[]{:S(2)}, u32[]{:S(2)}) %collective-permute-start.14) | collective-permute-done | bytes 28704 | tf_op jit(solution)/shard_map/ppermute | solution.py:309
  28.5 1.5 %collective-permute-start.10 = (bf16[1792,128]{1,0:T(8,128)(2,1)S(1)}, bf16[1792,128]{1,0:T(8,128)(2,1)S(1)}, u32[]{:S(2)}, u32[]{:S(2)}) collective-permute-start(bf16[1792,128]{1,0:T(8,128)(2,1)S(1)} %collective-permute-done.4.refs_8_), channel_id=1, source_target_pairs={{0,16},{16,0},{1,17},{17,1},{2,18},{18,2},{3,19},{19,3},{4,20},{20... | collective-permute-start | bytes 1376264 | tf_op jit(solution)/shard_map/ppermute | solution.py:428
  30.7 1.4 %collective-permute-done.3.refs_7_ = bf16[2,128,512]{2,1,0:T(8,128)(2,1)S(1)} collective-permute-done((bf16[2,128,512]{2,1,0:T(8,128)(2,1)S(1)}, bf16[2,128,512]{2,1,0:T(8,128)(2,1)S(1)}, u32[]{:S(2)}, u32[]{:S(2)}) %collective-permute-start.3) | collective-permute-done | bytes 262176 | tf_op jit(solution)/shard_map/ppermute | solution.py:309
  32.1 1.5 %collective-permute-start.9 = (bf16[3584,128]{1,0:T(8,128)(2,1)S(1)}, bf16[3584,128]{1,0:T(8,128)(2,1)S(1)}, u32[]{:S(2)}, u32[]{:S(2)}) collective-permute-start(bf16[3584,128]{1,0:T(8,128)(2,1)S(1)} %get-tuple-element.42), channel_id=1, source_target_pairs={{0,2},{1,3},{2,0},{3,1},{4,6},{5,7},{6,4},{7,5},{8,10},{9,11},{10,... | collective-permute-start | bytes 2752520 | tf_op jit(solution)/shard_map/ppermute | solution.py:309
  33.6 7.8 %collective-permute-done.10.refs_9_ = bf16[1792,128]{1,0:T(8,128)(2,1)S(1)} collective-permute-done((bf16[1792,128]{1,0:T(8,128)(2,1)S(1)}, bf16[1792,128]{1,0:T(8,128)(2,1)S(1)}, u32[]{:S(2)}, u32[]{:S(2)}) %collective-permute-start.10) | collective-permute-done | bytes 458784 | tf_op jit(solution)/shard_map/ppermute | solution.py:428
  41.4 0.5 collective-permute-start.15
  41.9 1.9 %collective-permute-done.15.refs_15_ = bf16[1728,128]{1,0:T(8,128)(2,1)S(1)} collective-permute-done((bf16[1728,128]{1,0:T(8,128)(2,1)S(1)}, bf16[1728,128]{1,0:T(8,128)(2,1)S(1)}, u32[]{:S(2)}, u32[]{:S(2)}) %collective-permute-start.15) | collective-permute-done | bytes 442400 | tf_op jit(solution)/shard_map/ppermute | solution.py:309
  43.9 8.5 %layer_0.1 = (f32[1536,128]{1,0:T(8,128)S(1)}, bf16[1536,512]{1,0:T(8,128)(2,1)S(1)}, f32[192,128]{1,0:T(8,128)S(1)}, bf16[192,512]{1,0:T(8,128)(2,1)S(1)}, bf16...) custom-call(bf16[2,1536,128]{2,1,0:T(8,128)(2,1)S(1)} %copy-done, ...), custom_call_target="tpu_custom_call" | custom-call | flops 3019898880 | bytes 13248512 | tf_op jit(solution)/shard_map/layer_0/pallas_call | solution.py:295
  52.4 1.5 %collective-permute-start.18 = (bf16[48,512]{1,0:T(8,128)(2,1)S(1)}, bf16[48,512]{1,0:T(8,128)(2,1)S(1)}, u32[]{:S(2)}, u32[]{:S(2)}) collective-permute-start(bf16[48,512]{1,0:T(8,128)(2,1)S(1)} %get-tuple-element.46), channel_id=1, source_target_pairs={{0,4},{4,8},{8,12},{12,0},{1,5},{5,9},{9,13},{13,1},{2,6},{6,10},{... | collective-permute-start | bytes 147464 | tf_op jit(solution)/shard_map/ppermute | solution.py:314
  53.9 2.3 %collective-permute-start.19 = (bf16[48,512]{1,0:T(8,128)(2,1)S(1)}, bf16[48,512]{1,0:T(8,128)(2,1)S(1)}, u32[]{:S(2)}, u32[]{:S(2)}) collective-permute-start(bf16[48,512]{1,0:T(8,128)(2,1)S(1)} %get-tuple-element.47), channel_id=1, source_target_pairs={{0,12},{4,0},{8,4},{12,8},{1,13},{5,1},{9,5},{13,9},{2,14},{6,2},{... | collective-permute-start | bytes 147464 | tf_op jit(solution)/shard_map/ppermute | solution.py:314
  56.3 0.7 %collective-permute-start.20 = (bf16[16,512]{1,0:T(8,128)(2,1)S(1)}, bf16[16,512]{1,0:T(8,128)(2,1)S(1)}, u32[]{:S(2)}, u32[]{:S(2)}) collective-permute-start(bf16[16,512]{1,0:T(8,128)(2,1)S(1)} %get-tuple-element.48), channel_id=1, source_target_pairs={{0,8},{4,12},{8,0},{12,4},{1,9},{5,13},{9,1},{13,5},{2,10},{6,14},... | collective-permute-start | bytes 49160 | tf_op jit(solution)/shard_map/ppermute | solution.py:314
  57.0 3.9 %collective-permute-done.20.refs_16_ = bf16[16,512]{1,0:T(8,128)(2,1)S(1)} collective-permute-done((bf16[16,512]{1,0:T(8,128)(2,1)S(1)}, bf16[16,512]{1,0:T(8,128)(2,1)S(1)}, u32[]{:S(2)}, u32[]{:S(2)}) %collective-permute-start.20) | collective-permute-done | bytes 16416 | tf_op jit(solution)/shard_map/ppermute | solution.py:314
  61.0 2.5 %collective-permute-done.21.refs_9_ = bf16[3584,128]{1,0:T(8,128)(2,1)S(1)} collective-permute-done((bf16[3584,128]{1,0:T(8,128)(2,1)S(1)}, bf16[3584,128]{1,0:T(8,128)(2,1)S(1)}, u32[]{:S(2)}, u32[]{:S(2)}) %collective-permute-start.21) | collective-permute-done | bytes 917536 | tf_op jit(solution)/shard_map/ppermute | solution.py:309
  63.5 8.4 %layer_1.1 = (f32[1536,128]{1,0:T(8,128)}, f32[192,128]{1,0:T(8,128)}) custom-call(bf16[2,1536,128]{2,1,0:T(8,128)(2,1)S(1)} %copy-done, bf16[2,128,512]{2,1,0:T(8,128)(2,1)S(1)} %copy-done.2, bf16[2,1024,128]{2,1,0:T(8,128)(2,1)S(1)} %copy-done.1, bf16[2,128,512]{2,1,0:T(8,128)(2,1)S(1)} %copy-done.3, ...), custom_call_target="tpu_custom_call" | custom-call | flops 3019898880 | bytes 11321344 | tf_op jit(solution)/shard_map/layer_1/pallas_call | solution.py:295
  (47 shorter events, 1.4 us)
Async XLA Ops:
  0.7 6.7 %copy-start.4 = (f32[1536,128]{1,0:T(8,128)S(1)}, f32[1536,128]{1,0:T(8,128)}, u32[]{:S(2)}) copy-start(f32[1536,128]{1,0:T(8,128)} %refs_20_.1) | copy-start | bytes 2359300
  0.7 6.7 %copy-start.5 = (f32[192,128]{1,0:T(8,128)S(1)}, f32[192,128]{1,0:T(8,128)}, u32[]{:S(2)}) copy-start(f32[192,128]{1,0:T(8,128)} %refs_21_.1) | copy-start | bytes 294916
  2.8 13.7 %collective-permute-start.4 = (bf16[1792,128]{1,0:T(8,128)(2,1)}, bf16[1792,128]{1,0:T(8,128)(2,1)S(1)}, u32[]{:S(2)}, u32[]{:S(2)}) collective-permute-start(bf16[1792,128]{1,0:T(8,128)(2,1)} %layer_0_half.1), channel_id=1, source_target_pairs={{0,2},{1,3},{2,0},{3,1},{4,6},{5,7},{6,4},{7,5},{8,10},{9,11},{10,... | collective-permute-start | bytes 1376264 | tf_op jit(solution)/shard_map/ppermute | solution.py:309
  7.6 8.4 %collective-permute-start.5 = (bf16[48,128]{1,0:T(8,128)(2,1)S(1)}, bf16[48,128]{1,0:T(8,128)(2,1)S(1)}, u32[]{:S(2)}, u32[]{:S(2)}) collective-permute-start(bf16[48,128]{1,0:T(8,128)(2,1)S(1)} %get-tuple-element.38), channel_id=1, source_target_pairs={{0,4},{4,8},{8,12},{12,0},{1,5},{5,9},{9,13},{13,1},{2,6},{6,10},{... | collective-permute-start | bytes 36872 | tf_op jit(solution)/shard_map/ppermute | solution.py:314
  9.2 6.8 %collective-permute-start.6 = (bf16[48,128]{1,0:T(8,128)(2,1)S(1)}, bf16[48,128]{1,0:T(8,128)(2,1)S(1)}, u32[]{:S(2)}, u32[]{:S(2)}) collective-permute-start(bf16[48,128]{1,0:T(8,128)(2,1)S(1)} %get-tuple-element.39), channel_id=1, source_target_pairs={{0,12},{4,0},{8,4},{12,8},{1,13},{5,1},{9,5},{13,9},{2,14},{6,2},{... | collective-permute-start | bytes 36872 | tf_op jit(solution)/shard_map/ppermute | solution.py:314
  11.5 4.5 %collective-permute-start.7 = (bf16[16,128]{1,0:T(8,128)(2,1)S(1)}, bf16[16,128]{1,0:T(8,128)(2,1)S(1)}, u32[]{:S(2)}, u32[]{:S(2)}) collective-permute-start(bf16[16,128]{1,0:T(8,128)(2,1)S(1)} %get-tuple-element.40), channel_id=1, source_target_pairs={{0,8},{4,12},{8,0},{12,4},{1,9},{5,13},{9,1},{13,5},{2,10},{6,14},... | collective-permute-start | bytes 12296 | tf_op jit(solution)/shard_map/ppermute | solution.py:314
  16.5 13.9 %collective-permute-start.8 = (bf16[1728,128]{1,0:T(8,128)(2,1)S(1)}, bf16[1728,128]{1,0:T(8,128)(2,1)S(1)}, u32[]{:S(2)}, u32[]{:S(2)}) collective-permute-start(bf16[1728,128]{1,0:T(8,128)(2,1)S(1)} %latents.1.refs_12_), channel_id=1, source_target_pairs={{0,2},{1,3},{2,0},{3,1},{4,6},{5,7},{6,4},{7,5},{8,10},{9,11},{10,... | collective-permute-start | bytes 1327112 | tf_op jit(solution)/shard_map/ppermute | solution.py:309
  18.2 11.9 %collective-permute-start.1 = (bf16[2,128,512]{2,1,0:T(8,128)(2,1)S(1)}, bf16[2,128,512]{2,1,0:T(8,128)(2,1)S(1)}, u32[]{:S(2)}, u32[]{:S(2)}) collective-permute-start(bf16[2,128,512]{2,1,0:T(8,128)(2,1)S(1)} %copy-done.2), channel_id=1, source_target_pairs={{0,1},{1,0},{2,3},{3,2},{4,5},{5,4},{6,7},{7,6},{8,9},{9,8},{10,11... | collective-permute-start | bytes 786440 | tf_op jit(solution)/shard_map/ppermute | solution.py:309
  18.2 23.2 %collective-permute-start.2 = (bf16[2,1024,128]{2,1,0:T(8,128)(2,1)S(1)}, bf16[2,1024,128]{2,1,0:T(8,128)(2,1)S(1)}, u32[]{:S(2)}, u32[]{:S(2)}) collective-permute-start(bf16[2,1024,128]{2,1,0:T(8,128)(2,1)S(1)} %copy-done.1), channel_id=1, source_target_pairs={{0,1},{1,0},{2,3},{3,2},{4,5},{5,4},{6,7},{7,6},{8,9},{9,8},{10,11... | collective-permute-start | bytes 1572872 | tf_op jit(solution)/shard_map/ppermute | solution.py:309
  18.8 9.7 %collective-permute-start.14 = (bf16[112,128]{1,0:T(8,128)(2,1)S(1)}, bf16[112,128]{1,0:T(8,128)(2,1)S(1)}, u32[]{:S(2)}, u32[]{:S(2)}) collective-permute-start(bf16[112,128]{1,0:T(8,128)(2,1)S(1)} %halo_rows.1.refs_16_), channel_id=1, source_target_pairs={{0,2},{1,3},{2,0},{3,1},{4,6},{5,7},{6,4},{7,5},{8,10},{9,11},{10,... | collective-permute-start | bytes 86024 | tf_op jit(solution)/shard_map/ppermute | solution.py:309
  19.0 9.4 %collective-permute-start.16 = (bf16[112,128]{1,0:T(8,128)(2,1)S(1)}, bf16[112,128]{1,0:T(8,128)(2,1)S(1)}, u32[]{:S(2)}, u32[]{:S(2)}) collective-permute-start(bf16[112,128]{1,0:T(8,128)(2,1)S(1)} %halo_rows.1.refs_16_), channel_id=1, source_target_pairs={{0,1},{1,0},{2,3},{3,2},{4,5},{5,4},{6,7},{7,6},{8,9},{9,8},{10,11... | collective-permute-start | bytes 86024 | tf_op jit(solution)/shard_map/ppermute | solution.py:309
  28.5 1.5 %collective-permute-start.17 = (bf16[112,128]{1,0:T(8,128)(2,1)S(1)}, bf16[112,128]{1,0:T(8,128)(2,1)S(1)}, u32[]{:S(2)}, u32[]{:S(2)}) collective-permute-start(bf16[112,128]{1,0:T(8,128)(2,1)S(1)} %collective-permute-done.14.refs_18_), channel_id=1, source_target_pairs={{0,1},{1,0},{2,3},{3,2},{4,5},{5,4},{6,7},{7,6},{8,9},{9,8},{10,11... | collective-permute-start | bytes 86024 | tf_op jit(solution)/shard_map/ppermute | solution.py:309
  28.5 12.9 %collective-permute-start.10 = (bf16[1792,128]{1,0:T(8,128)(2,1)S(1)}, bf16[1792,128]{1,0:T(8,128)(2,1)S(1)}, u32[]{:S(2)}, u32[]{:S(2)}) collective-permute-start(bf16[1792,128]{1,0:T(8,128)(2,1)S(1)} %collective-permute-done.4.refs_8_), channel_id=1, source_target_pairs={{0,16},{16,0},{1,17},{17,1},{2,18},{18,2},{3,19},{19,3},{4,20},{20... | collective-permute-start | bytes 1376264 | tf_op jit(solution)/shard_map/ppermute | solution.py:428
  29.9 3.7 %collective-permute-start.13 = (bf16[1728,128]{1,0:T(8,128)(2,1)S(1)}, bf16[1728,128]{1,0:T(8,128)(2,1)S(1)}, u32[]{:S(2)}, u32[]{:S(2)}) collective-permute-start(bf16[1728,128]{1,0:T(8,128)(2,1)S(1)} %latents.1.refs_12_), channel_id=1, source_target_pairs={{0,1},{1,0},{2,3},{3,2},{4,5},{5,4},{6,7},{7,6},{8,9},{9,8},{10,11... | collective-permute-start | bytes 1327112 | tf_op jit(solution)/shard_map/ppermute | solution.py:309
  30.2 1.9 %collective-permute-start.3 = (bf16[2,128,512]{2,1,0:T(8,128)(2,1)S(1)}, bf16[2,128,512]{2,1,0:T(8,128)(2,1)S(1)}, u32[]{:S(2)}, u32[]{:S(2)}) collective-permute-start(bf16[2,128,512]{2,1,0:T(8,128)(2,1)S(1)} %copy-done.3), channel_id=1, source_target_pairs={{0,1},{1,0},{2,3},{3,2},{4,5},{5,4},{6,7},{7,6},{8,9},{9,8},{10,11... | collective-permute-start | bytes 786440 | tf_op jit(solution)/shard_map/ppermute | solution.py:309
  30.5 11.5 %collective-permute-start = (bf16[2,1536,128]{2,1,0:T(8,128)(2,1)S(1)}, bf16[2,1536,128]{2,1,0:T(8,128)(2,1)S(1)}, u32[]{:S(2)}, u32[]{:S(2)}) collective-permute-start(bf16[2,1536,128]{2,1,0:T(8,128)(2,1)S(1)} %copy-done), channel_id=1, source_target_pairs={{0,1},{1,0},{2,3},{3,2},{4,5},{5,4},{6,7},{7,6},{8,9},{9,8},{10,11... | collective-permute-start | bytes 2359304 | tf_op jit(solution)/shard_map/ppermute | solution.py:309
  32.1 28.8 %collective-permute-start.9 = (bf16[3584,128]{1,0:T(8,128)(2,1)S(1)}, bf16[3584,128]{1,0:T(8,128)(2,1)S(1)}, u32[]{:S(2)}, u32[]{:S(2)}) collective-permute-start(bf16[3584,128]{1,0:T(8,128)(2,1)S(1)} %get-tuple-element.42), channel_id=1, source_target_pairs={{0,2},{1,3},{2,0},{3,1},{4,6},{5,7},{6,4},{7,5},{8,10},{9,11},{10,... | collective-permute-start | bytes 2752520 | tf_op jit(solution)/shard_map/ppermute | solution.py:309
  33.6 8.3 %collective-permute-start.11 = (bf16[1792,128]{1,0:T(8,128)(2,1)S(1)}, bf16[1792,128]{1,0:T(8,128)(2,1)S(1)}, u32[]{:S(2)}, u32[]{:S(2)}) collective-permute-start(bf16[1792,128]{1,0:T(8,128)(2,1)S(1)} %collective-permute-done.4.refs_8_), channel_id=1, source_target_pairs={{0,1},{1,0},{2,3},{3,2},{4,5},{5,4},{6,7},{7,6},{8,9},{9,8},{10,11... | collective-permute-start | bytes 1376264 | tf_op jit(solution)/shard_map/ppermute | solution.py:309
  41.4 2.5 %collective-permute-start.12 = (bf16[1792,128]{1,0:T(8,128)(2,1)S(1)}, bf16[1792,128]{1,0:T(8,128)(2,1)S(1)}, u32[]{:S(2)}, u32[]{:S(2)}) collective-permute-start(bf16[1792,128]{1,0:T(8,128)(2,1)S(1)} %collective-permute-done.10.refs_9_), channel_id=1, source_target_pairs={{0,1},{1,0},{2,3},{3,2},{4,5},{5,4},{6,7},{7,6},{8,9},{9,8},{10,11... | collective-permute-start | bytes 1376264 | tf_op jit(solution)/shard_map/ppermute | solution.py:309
  41.4 2.4 %collective-permute-start.15 = (bf16[1728,128]{1,0:T(8,128)(2,1)S(1)}, bf16[1728,128]{1,0:T(8,128)(2,1)S(1)}, u32[]{:S(2)}, u32[]{:S(2)}) collective-permute-start(bf16[1728,128]{1,0:T(8,128)(2,1)S(1)} %collective-permute-done.8.refs_14_), channel_id=1, source_target_pairs={{0,1},{1,0},{2,3},{3,2},{4,5},{5,4},{6,7},{7,6},{8,9},{9,8},{10,11... | collective-permute-start | bytes 1327112 | tf_op jit(solution)/shard_map/ppermute | solution.py:309
  52.4 8.5 %collective-permute-start.18 = (bf16[48,512]{1,0:T(8,128)(2,1)S(1)}, bf16[48,512]{1,0:T(8,128)(2,1)S(1)}, u32[]{:S(2)}, u32[]{:S(2)}) collective-permute-start(bf16[48,512]{1,0:T(8,128)(2,1)S(1)} %get-tuple-element.46), channel_id=1, source_target_pairs={{0,4},{4,8},{8,12},{12,0},{1,5},{5,9},{9,13},{13,1},{2,6},{6,10},{... | collective-permute-start | bytes 147464 | tf_op jit(solution)/shard_map/ppermute | solution.py:314
  53.9 7.0 %collective-permute-start.19 = (bf16[48,512]{1,0:T(8,128)(2,1)S(1)}, bf16[48,512]{1,0:T(8,128)(2,1)S(1)}, u32[]{:S(2)}, u32[]{:S(2)}) collective-permute-start(bf16[48,512]{1,0:T(8,128)(2,1)S(1)} %get-tuple-element.47), channel_id=1, source_target_pairs={{0,12},{4,0},{8,4},{12,8},{1,13},{5,1},{9,5},{13,9},{2,14},{6,2},{... | collective-permute-start | bytes 147464 | tf_op jit(solution)/shard_map/ppermute | solution.py:314
  56.3 4.6 %collective-permute-start.20 = (bf16[16,512]{1,0:T(8,128)(2,1)S(1)}, bf16[16,512]{1,0:T(8,128)(2,1)S(1)}, u32[]{:S(2)}, u32[]{:S(2)}) collective-permute-start(bf16[16,512]{1,0:T(8,128)(2,1)S(1)} %get-tuple-element.48), channel_id=1, source_target_pairs={{0,8},{4,12},{8,0},{12,4},{1,9},{5,13},{9,1},{13,5},{2,10},{6,14},... | collective-permute-start | bytes 49160 | tf_op jit(solution)/shard_map/ppermute | solution.py:314
  60.9 2.5 %collective-permute-start.21 = (bf16[3584,128]{1,0:T(8,128)(2,1)S(1)}, bf16[3584,128]{1,0:T(8,128)(2,1)S(1)}, u32[]{:S(2)}, u32[]{:S(2)}) collective-permute-start(bf16[3584,128]{1,0:T(8,128)(2,1)S(1)} %collective-permute-done.9.refs_8_), channel_id=1, source_target_pairs={{0,1},{1,0},{2,3},{3,2},{4,5},{5,4},{6,7},{7,6},{8,9},{9,8},{10,11... | collective-permute-start | bytes 2752520 | tf_op jit(solution)/shard_map/ppermute | solution.py:309
  (7 other events, 36.0 us)

commit v9 on v8

--- a/solution.py
+++ b/solution.py
@@ -51,6 +51,14 @@
     def wait(self):
         for copy in self.started:
             copy.wait()
+
+
+class Moves:
+    def start(self, source, target):
+        target[...] = source[...]
+
+    def wait(self):
+        pass
 
 
 def load_shard(copies, layer, first, second, j, first_ref, second_ref):
@@ -155,21 +163,16 @@
         start += out.shape[0]
 
 
-def join_kernel(*refs):
+def start_kernel(node_ref, pick_ref, right, left, coarse):
+    pick_rows(pick_ref, node_ref[...].astype(BF16), (right, left, coarse))
+
+
+def latent_kernel(*refs):
+    out = refs[-1]
     at = 0
     for piece in refs[:-1]:
-        refs[-1][at : at + piece.shape[0], :] = piece[...]
+        out[at : at + piece.shape[0], :] = piece[...].astype(BF16)
         at += piece.shape[0]
-
-
-def start_kernel(node_ref, pick_ref, right, left, coarse):
-    pick_rows(pick_ref, node_ref[...].astype(BF16), (right, left, coarse))
-
-
-def latent_kernel(edge_ref, node_ref, out):
-    at = edge_ref.shape[0]
-    out[0:at, :] = edge_ref[...].astype(BF16)
-    out[at:, :] = node_ref[...].astype(BF16)
 
 
 def edge_rows(edge_ref, table, nodes, own_ref, hot_ref, incidence_ref, first_ref, second_ref, product_ref, own_out, full_out):
@@ -213,20 +216,17 @@
     core_w = [refs.pop(0) for _ in range(4)]
     halves = [[refs.pop(0) for _ in range(2)] for _ in range(2)]
     shards = [refs.pop(0) for _ in range(4)]
-    rims = [refs.pop(0) for _ in range(4)]
     edge_own, node_own, hot_ref, incidence_ref, pick_ref = [refs.pop(0) for _ in range(5)]
     edge_out, full_out, node_out, node_full = [refs.pop(0) for _ in range(4)]
     sends = [refs.pop(0) for _ in range(3)]
-    edge_w, edge_w2, node_w, node_w2, product_ref, x_ref, edge_sems, node_sems = refs
+    edge_w, edge_w2, node_w, node_w2, product_ref, x_ref = refs
     part = edge_own.shape[1]
     edge_count = edge_own.shape[0]
     node_count = node_own.shape[0]
-    edge_copies, node_copies = Copies(edge_sems), Copies(node_sems)
-    for pieces, at in ((shards, 0), (rims, edge_count + node_count)):
-        rows = pl.ds(at, pieces[0].shape[0])
-        for j, shard in enumerate(pieces):
-            column = pl.multiple_of((lax.axis_index("mp") ^ j) * part, part)
-            edge_copies.start(shard, x_ref.at[rows, pl.ds(column, part)])
+    edge_copies, node_copies = Moves(), Moves()
+    for j, shard in enumerate(shards):
+        column = pl.multiple_of((lax.axis_index("mp") ^ j) * part, part)
+        edge_copies.start(shard, x_ref.at[:, pl.ds(column, part)])
     y = lax.axis_index("groups")
     starts = [0, 0]
     for base, copies, (first, second), at in (
@@ -260,8 +260,8 @@
     edge_ref, edge_own, node_own = [refs.pop(0) for _ in range(3)]
     tables = [refs.pop(0) for _ in range(pieces)]
     hot_ref, incidence_ref, edge_out, node_out = [refs.pop(0) for _ in range(4)]
-    edge_w, edge_w2, node_w, node_w2, product_ref, table_ref, edge_sems, node_sems = refs
-    edge_copies, node_copies = Copies(edge_sems), Copies(node_sems)
+    edge_w, edge_w2, node_w, node_w2, product_ref, table_ref = refs
+    edge_copies, node_copies = Moves(), Moves()
     base = 0
     for copies, first, second, at in (
         (edge_copies, edge_w, edge_w2, 0),
@@ -400,37 +400,28 @@
         "one_hot",
     )
     core_w = [swap(after(w, ride), 1) for w in weights]
+    right, left, coarse = call(
+        start_kernel,
+        sent(part),
+        [(VMEM, node_state), (VMEM, pick)],
+        [],
+        2 * pick.size * part,
+        "boundary_rows",
+    )
+    rows = neighbour_rows(right, left, coarse, halo)
     (latents,) = call(
         latent_kernel,
-        [shape((edge_count + node_count, part), BF16)],
-        [(VMEM, after(edge_state, late_w)), (VMEM, node_state)],
+        [shape((edge_count + table_rows, part), BF16)],
+        [(VMEM, after(edge_state, late_w)), (VMEM, node_state)] + [(VMEM, r) for r in rows],
         [],
         0,
         "latents",
     )
-    right, left, coarse = call(
-        start_kernel,
-        sent(part),
-        [(VMEM, node_state), (VMEM, after(pick, latents))],
-        [],
-        2 * pick.size * part,
-        "boundary_rows",
-    )
-    (rim,) = call(
-        join_kernel,
-        [shape((far_rows, part), BF16)],
-        [(VMEM, r) for r in neighbour_rows(right, left, coarse, halo)],
-        [],
-        0,
-        "halo_rows",
-    )
-    far_latents = swap(after(latents, near, rim), 2)
+    far_latents = swap(after(latents, near, *core_w), 2)
     far = lax.ppermute(near, "groups", [(0, 1), (1, 0)])
-    far_rim = swap(rim, 2)
-    shards = [latents, swap(latents, 1), far_latents, swap(after(far_latents, far, far_rim), 1)]
-    rims = [rim, swap(rim, 1), far_rim, swap(far_rim, 1)]
+    shards = [latents, swap(latents, 1), far_latents, swap(after(far_latents, far), 1)]
     pairs = [near, far, swap(near, 1), swap(far, 1)]
-    late_x = swap(after(late_w, far_latents), 2)
+    late_x = swap(after(late_w, far_latents, far), 2)
 
     edge_flops = 2 * edge_count * features * (2 * features + lanes + node_count)
     node_flops = 2 * node_count * features * 3 * features
@@ -445,7 +436,7 @@
     edge_own, edge_full, node_own, node_full, right, left, coarse = call(
         first_kernel,
         [own_edge, full_edge, own_node, full_node] + sent(features),
-        [(ANY, w) for w in list(weights) + core_w + pairs + shards + rims]
+        [(VMEM, w) for w in list(weights) + core_w + pairs + shards]
         + [(VMEM, a) for a in (edge_state, node_state, hot, incidence, pick)],
         [
             edge_shape,
@@ -454,8 +445,6 @@
             second_shape,
             pltpu.VMEM((lanes, hidden), BF16),
             pltpu.VMEM((edge_count + table_rows, features), BF16),
-            dma((32,)),
-            dma((24,)),
         ],
         edge_flops + node_flops,
         "layer_0",
@@ -466,7 +455,7 @@
     edge_own, node_own = call(
         functools.partial(late_kernel, len(tables)),
         [own_edge, own_node],
-        [(ANY, w) for w in list(weights) + core_w + [late_x, late_d]]
+        [(VMEM, w) for w in list(weights) + core_w + [late_x, late_d]]
         + [(VMEM, a) for a in (edge_full, edge_own, node_own)]
         + [(VMEM, t) for t in tables]
         + [(VMEM, hot), (VMEM, incidence)],
@@ -477,8 +466,6 @@
             second_shape,
             pltpu.VMEM((lanes, hidden), BF16),
             pltpu.VMEM((table_rows, features), BF16),
-            dma((14,)),
-            dma((14,)),
         ],
         edge_flops + node_flops,
         "layer_1",

time: 72.1 us -> 62.9 us (0.87)
  waiting for transfers between devices: 31.2 us -> 23.9 us
  Pallas kernels: 20.6 us -> 17.3 us
  starting transfers between devices: 19.1 us -> 20.7 us
    ppermute x15 -> x12, waiting for transfers between devices: 15.8 us -> 7.12 us  [swap(): return lax.ppermute(x, 'mp', [(i, i ^ mask) for i in range(size)])]
    pallas_call x7 -> x6, Pallas kernels: 20.6 us -> 17.3 us  [call(): pl.pallas_call(kernel, out_shape=out_shape, in_specs=[pl.BlockSpec(memory...]
    ppermute x6, starting transfers between devices: 9.28 us -> 12.5 us  [shift(): return lax.ppermute(x, 'graph', [(i, (i + by) % size) for i in range(size)])]
    ppermute x1, waiting for transfers between devices: 7.81 us -> 10.8 us  [on_device(): far = lax.ppermute(near, 'groups', [(0, 1), (1, 0)])]
    ppermute x15 -> x12, starting transfers between devices: 8.36 us -> 6.63 us  [swap(): return lax.ppermute(x, 'mp', [(i, i ^ mask) for i in range(size)])]
    ppermute x6, waiting for transfers between devices: 7.63 us -> 6.06 us  [shift(): return lax.ppermute(x, 'graph', [(i, (i + by) % size) for i in range(size)])]
  transfers between devices with their start and end apart: 22 -> 19, of which waited for: 8 -> 11; matrix products, arithmetic and copies ran while one was open for 0% -> 0% of each run, Pallas kernels for 14% -> 14%
where the time goes in v9:
time: 62.9 us; the launch traced here: 62.8 us
  waiting for transfers between devices  23.9 us (38%)
  starting transfers between devices  20.7 us (33%)
  Pallas kernels  17.3 us (28%)
  between operations  0.81 us (1%)
    pallas_call x6, Pallas kernels, call(): pl.pallas_call(kernel, out_shape=out_shape, in_specs=[pl.BlockSpec(memory...  17.3 us
    ppermute x6, starting transfers between devices, shift(): return lax.ppermute(x, 'graph', [(i, (i + by) % size) for i in range(size)])  12.5 us
    ppermute x1, waiting for transfers between devices, on_device(): far = lax.ppermute(near, 'groups', [(0, 1), (1, 0)])  10.8 us
    ppermute x12, waiting for transfers between devices, swap(): return lax.ppermute(x, 'mp', [(i, i ^ mask) for i in range(size)])  7.12 us
    ppermute x12, starting transfers between devices, swap(): return lax.ppermute(x, 'mp', [(i, i ^ mask) for i in range(size)])  6.63 us
    ppermute x6, waiting for transfers between devices, shift(): return lax.ppermute(x, 'graph', [(i, (i + by) % size) for i in range(size)])  6.06 us
    ppermute x1, starting transfers between devices, on_device(): far = lax.ppermute(near, 'groups', [(0, 1), (1, 0)])  1.52 us
  transfers between devices with their start and end apart: 19, of which 11 were waited for; matrix products, arithmetic and copies ran while one was open for 0% of the time, Pallas kernels for 14%

profile of v9, /device:TPU:0, one launch (start us, length us, event | category | flops | bytes accessed | tf_op | source)
XLA Modules:
  0.0 62.8 jit_solution(16819233188497226100)
XLA Ops:
  0.7 2.0 %layer_0_half.1 = bf16[1792,128]{1,0:T(8,128)(2,1)} custom-call(bf16[2,1536,128]{2,1,0:T(8,128)(2,1)} %refs_0_.4, bf16[2,128,512]{2,1,0:T(8,128)(2,1)} %refs_1_.5, bf16[2,1024,128]{2,1,0:T(8,128)(2,1)} %refs_2_.3, bf16[2,128,512]{2,1,0:T(8,128)(2,1)} %refs_3_.3), custom_call_target="tpu_custom_call" | custom-call | bytes 2293760 | tf_op jit(solution)/shard_map/layer_0_half/pallas_call | solution.py:295
  2.8 0.5 collective-permute-start
  3.4 2.9 %collective-permute-start.7 = (bf16[1792,128]{1,0:T(8,128)(2,1)}, bf16[1792,128]{1,0:T(8,128)(2,1)S(1)}, u32[]{:S(2)}, u32[]{:S(2)}) collective-permute-start(bf16[1792,128]{1,0:T(8,128)(2,1)} %layer_0_half.1), channel_id=1, source_target_pairs={{0,2},{1,3},{2,0},{3,1},{4,6},{5,7},{6,4},{7,5},{8,10},{9,11},{10,... | collective-permute-start | bytes 1376264 | tf_op jit(solution)/shard_map/ppermute | solution.py:309
  6.3 1.5 %one_hot.1 = (bf16[1536,512]{1,0:T(8,128)(2,1)S(1)}, bf16[192,1536]{1,0:T(8,128)(2,1)S(1)}, bf16[112,192]{1,0:T(8,128)(2,1)S(1)}, bf16[3584,128]{1,0:T(8,128)(2,1)S(1)}) custom-call(s32[1,3136]{1,0:T(1,128)S(1)} %broadcast_in_dim.3.list_ref, bf16[2,1536,128]{2,1,0:T(8,128)(2,1)S(1)} %copy-done, bf16[2,128,512]{2,1,0:T(8,128)(2,1)S(1)} %copy-done.2, ...), custom_call_target="tpu_custom_call" | custom-call | bytes 4970752 | tf_op jit(solution)/shard_map/one_hot/pallas_call | solution.py:295
  8.0 2.7 %collective-permute-start.6 = (bf16[16,128]{1,0:T(8,128)(2,1)S(1)}, bf16[16,128]{1,0:T(8,128)(2,1)S(1)}, u32[]{:S(2)}, u32[]{:S(2)}) collective-permute-start(bf16[16,128]{1,0:T(8,128)(2,1)S(1)} %get-tuple-element.38), channel_id=1, source_target_pairs={{0,8},{4,12},{8,0},{12,4},{1,9},{5,13},{9,1},{13,5},{2,10},{6,14},... | collective-permute-start | bytes 12296 | tf_op jit(solution)/shard_map/ppermute | solution.py:314
  10.7 1.6 %collective-permute-start.4 = (bf16[48,128]{1,0:T(8,128)(2,1)S(1)}, bf16[48,128]{1,0:T(8,128)(2,1)S(1)}, u32[]{:S(2)}, u32[]{:S(2)}) collective-permute-start(bf16[48,128]{1,0:T(8,128)(2,1)S(1)} %get-tuple-element.36), channel_id=1, source_target_pairs={{0,4},{4,8},{8,12},{12,0},{1,5},{5,9},{9,13},{13,1},{2,6},{6,10},{... | collective-permute-start | bytes 36872 | tf_op jit(solution)/shard_map/ppermute | solution.py:314
  12.6 3.6 %collective-permute-start.5 = (bf16[48,128]{1,0:T(8,128)(2,1)S(1)}, bf16[48,128]{1,0:T(8,128)(2,1)S(1)}, u32[]{:S(2)}, u32[]{:S(2)}) collective-permute-start(bf16[48,128]{1,0:T(8,128)(2,1)S(1)} %get-tuple-element.37), channel_id=1, source_target_pairs={{0,12},{4,0},{8,4},{12,8},{1,13},{5,1},{9,5},{13,9},{2,14},{6,2},{... | collective-permute-start | bytes 36872 | tf_op jit(solution)/shard_map/ppermute | solution.py:314
  16.2 1.4 %collective-permute-done.5.refs_3_ = bf16[48,128]{1,0:T(8,128)(2,1)S(1)} collective-permute-done((bf16[48,128]{1,0:T(8,128)(2,1)S(1)}, bf16[48,128]{1,0:T(8,128)(2,1)S(1)}, u32[]{:S(2)}, u32[]{:S(2)}) %collective-permute-start.5) | collective-permute-done | bytes 12320 | tf_op jit(solution)/shard_map/ppermute | solution.py:314
  17.7 1.4 %collective-permute-done.3.refs_7_ = bf16[2,128,512]{2,1,0:T(8,128)(2,1)S(1)} collective-permute-done((bf16[2,128,512]{2,1,0:T(8,128)(2,1)S(1)}, bf16[2,128,512]{2,1,0:T(8,128)(2,1)S(1)}, u32[]{:S(2)}, u32[]{:S(2)}) %collective-permute-start.3) | collective-permute-done | bytes 262176 | tf_op jit(solution)/shard_map/ppermute | solution.py:309
  19.1 0.6 collective-permute-start.8
  19.7 1.5 %collective-permute-start.9 = (bf16[1792,128]{1,0:T(8,128)(2,1)S(1)}, bf16[1792,128]{1,0:T(8,128)(2,1)S(1)}, u32[]{:S(2)}, u32[]{:S(2)}) collective-permute-start(bf16[1792,128]{1,0:T(8,128)(2,1)S(1)} %collective-permute-done.7.refs_8_), channel_id=1, source_target_pairs={{0,16},{16,0},{1,17},{17,1},{2,18},{18,2},{3,19},{19,3},{4,20},{20... | collective-permute-start | bytes 1376264 | tf_op jit(solution)/shard_map/ppermute | solution.py:421
  21.2 10.8 %collective-permute-done.9.refs_9_ = bf16[1792,128]{1,0:T(8,128)(2,1)S(1)} collective-permute-done((bf16[1792,128]{1,0:T(8,128)(2,1)S(1)}, bf16[1792,128]{1,0:T(8,128)(2,1)S(1)}, u32[]{:S(2)}, u32[]{:S(2)}) %collective-permute-start.9) | collective-permute-done | bytes 458784 | tf_op jit(solution)/shard_map/ppermute | solution.py:421
  32.0 1.5 %collective-permute-start.10 = (bf16[3584,128]{1,0:T(8,128)(2,1)S(1)}, bf16[3584,128]{1,0:T(8,128)(2,1)S(1)}, u32[]{:S(2)}, u32[]{:S(2)}) collective-permute-start(bf16[3584,128]{1,0:T(8,128)(2,1)S(1)} %get-tuple-element.40), channel_id=1, source_target_pairs={{0,2},{1,3},{2,0},{3,1},{4,6},{5,7},{6,4},{7,5},{8,10},{9,11},{10,... | collective-permute-start | bytes 2752520 | tf_op jit(solution)/shard_map/ppermute | solution.py:309
  33.5 0.5 collective-permute-start.14
  34.0 0.5 collective-permute-start.12
  34.5 0.8 %collective-permute-done.13.refs_13_ = bf16[1840,128]{1,0:T(8,128)(2,1)S(1)} collective-permute-done((bf16[1840,128]{1,0:T(8,128)(2,1)S(1)}, bf16[1840,128]{1,0:T(8,128)(2,1)S(1)}, u32[]{:S(2)}, u32[]{:S(2)}) %collective-permute-start.13) | collective-permute-done | bytes 471072 | tf_op jit(solution)/shard_map/ppermute | solution.py:309
  35.3 1.3 %collective-permute-done.11.refs_10_ = bf16[1792,128]{1,0:T(8,128)(2,1)S(1)} collective-permute-done((bf16[1792,128]{1,0:T(8,128)(2,1)S(1)}, bf16[1792,128]{1,0:T(8,128)(2,1)S(1)}, u32[]{:S(2)}, u32[]{:S(2)}) %collective-permute-start.11) | collective-permute-done | bytes 458784 | tf_op jit(solution)/shard_map/ppermute | solution.py:309
  36.7 0.7 %collective-permute-done.12.refs_11_ = bf16[1792,128]{1,0:T(8,128)(2,1)S(1)} collective-permute-done((bf16[1792,128]{1,0:T(8,128)(2,1)S(1)}, bf16[1792,128]{1,0:T(8,128)(2,1)S(1)}, u32[]{:S(2)}, u32[]{:S(2)}) %collective-permute-start.12) | collective-permute-done | bytes 458784 | tf_op jit(solution)/shard_map/ppermute | solution.py:309
  37.3 6.9 %layer_0.1 = (f32[1536,128]{1,0:T(8,128)S(1)}, bf16[1536,512]{1,0:T(8,128)(2,1)S(1)}, f32[192,128]{1,0:T(8,128)S(1)}, bf16[192,512]{1,0:T(8,128)(2,1)S(1)}, bf16...) custom-call(bf16[2,1536,128]{2,1,0:T(8,128)(2,1)S(1)} %copy-done, ...), custom_call_target="tpu_custom_call" | custom-call | flops 3019898880 | bytes 13248512 | tf_op jit(solution)/shard_map/layer_0/pallas_call | solution.py:295
  44.5 4.1 %collective-permute-start.16 = (bf16[48,512]{1,0:T(8,128)(2,1)S(1)}, bf16[48,512]{1,0:T(8,128)(2,1)S(1)}, u32[]{:S(2)}, u32[]{:S(2)}) collective-permute-start(bf16[48,512]{1,0:T(8,128)(2,1)S(1)} %get-tuple-element.45), channel_id=1, source_target_pairs={{0,12},{4,0},{8,4},{12,8},{1,13},{5,1},{9,5},{13,9},{2,14},{6,2},{... | collective-permute-start | bytes 147464 | tf_op jit(solution)/shard_map/ppermute | solution.py:314
  48.9 4.3 %collective-permute-done.17.refs_16_ = bf16[16,512]{1,0:T(8,128)(2,1)S(1)} collective-permute-done((bf16[16,512]{1,0:T(8,128)(2,1)S(1)}, bf16[16,512]{1,0:T(8,128)(2,1)S(1)}, u32[]{:S(2)}, u32[]{:S(2)}) %collective-permute-start.17) | collective-permute-done | bytes 16416 | tf_op jit(solution)/shard_map/ppermute | solution.py:314
  53.2 0.4 collective-permute-done.10.refs_8_
  53.6 2.5 %collective-permute-done.18.refs_9_ = bf16[3584,128]{1,0:T(8,128)(2,1)S(1)} collective-permute-done((bf16[3584,128]{1,0:T(8,128)(2,1)S(1)}, bf16[3584,128]{1,0:T(8,128)(2,1)S(1)}, u32[]{:S(2)}, u32[]{:S(2)}) %collective-permute-start.18) | collective-permute-done | bytes 917536 | tf_op jit(solution)/shard_map/ppermute | solution.py:309
  56.1 6.7 %layer_1.1 = (f32[1536,128]{1,0:T(8,128)}, f32[192,128]{1,0:T(8,128)}) custom-call(bf16[2,1536,128]{2,1,0:T(8,128)(2,1)S(1)} %copy-done, bf16[2,128,512]{2,1,0:T(8,128)(2,1)S(1)} %copy-done.2, bf16[2,1024,128]{2,1,0:T(8,128)(2,1)S(1)} %copy-done.1, bf16[2,128,512]{2,1,0:T(8,128)(2,1)S(1)} %copy-done.3, ...), custom_call_target="tpu_custom_call" | custom-call | flops 3019898880 | bytes 11321344 | tf_op jit(solution)/shard_map/layer_1/pallas_call | solution.py:295
  (40 shorter events, 1.4 us)
Async XLA Ops:
  0.6 5.7 %copy-start.3 = (bf16[2,128,512]{2,1,0:T(8,128)(2,1)S(1)}, bf16[2,128,512]{2,1,0:T(8,128)(2,1)}, u32[]{:S(2)}) copy-start(bf16[2,128,512]{2,1,0:T(8,128)(2,1)} %refs_3_.3) | copy-start | bytes 786436
  0.7 5.7 %copy-start.2 = (bf16[2,128,512]{2,1,0:T(8,128)(2,1)S(1)}, bf16[2,128,512]{2,1,0:T(8,128)(2,1)}, u32[]{:S(2)}) copy-start(bf16[2,128,512]{2,1,0:T(8,128)(2,1)} %refs_1_.5) | copy-start | bytes 786436
  0.7 5.6 %copy-start.8 = (s32[64]{0:T(128)S(1)}, s32[64]{0:T(128)}, u32[]{:S(2)}) copy-start(s32[64]{0:T(128)} %param.17) | copy-start | bytes 772
  0.7 7.1 %copy-start.5 = (f32[192,128]{1,0:T(8,128)S(1)}, f32[192,128]{1,0:T(8,128)}, u32[]{:S(2)}) copy-start(f32[192,128]{1,0:T(8,128)} %refs_17_.1) | copy-start | bytes 294916
  2.7 14.8 %copy-start.4 = (f32[1536,128]{1,0:T(8,128)S(1)}, f32[1536,128]{1,0:T(8,128)}, u32[]{:S(2)}) copy-start(f32[1536,128]{1,0:T(8,128)} %refs_16_.1) | copy-start | bytes 2359300
  2.8 16.4 %collective-permute-start = (bf16[2,1536,128]{2,1,0:T(8,128)(2,1)S(1)}, bf16[2,1536,128]{2,1,0:T(8,128)(2,1)S(1)}, u32[]{:S(2)}, u32[]{:S(2)}) collective-permute-start(bf16[2,1536,128]{2,1,0:T(8,128)(2,1)S(1)} %copy-done), channel_id=1, source_target_pairs={{0,1},{1,0},{2,3},{3,2},{4,5},{5,4},{6,7},{7,6},{8,9},{9,8},{10,11... | collective-permute-start | bytes 2359304 | tf_op jit(solution)/shard_map/ppermute | solution.py:309
  3.3 15.8 %collective-permute-start.2 = (bf16[2,1024,128]{2,1,0:T(8,128)(2,1)S(1)}, bf16[2,1024,128]{2,1,0:T(8,128)(2,1)S(1)}, u32[]{:S(2)}, u32[]{:S(2)}) collective-permute-start(bf16[2,1024,128]{2,1,0:T(8,128)(2,1)S(1)} %copy-done.1), channel_id=1, source_target_pairs={{0,1},{1,0},{2,3},{3,2},{4,5},{5,4},{6,7},{7,6},{8,9},{9,8},{10,11... | collective-permute-start | bytes 1572872 | tf_op jit(solution)/shard_map/ppermute | solution.py:309
  3.4 15.8 %collective-permute-start.7 = (bf16[1792,128]{1,0:T(8,128)(2,1)}, bf16[1792,128]{1,0:T(8,128)(2,1)S(1)}, u32[]{:S(2)}, u32[]{:S(2)}) collective-permute-start(bf16[1792,128]{1,0:T(8,128)(2,1)} %layer_0_half.1), channel_id=1, source_target_pairs={{0,2},{1,3},{2,0},{3,1},{4,6},{5,7},{6,4},{7,5},{8,10},{9,11},{10,... | collective-permute-start | bytes 1376264 | tf_op jit(solution)/shard_map/ppermute | solution.py:309
  8.0 4.6 %collective-permute-start.6 = (bf16[16,128]{1,0:T(8,128)(2,1)S(1)}, bf16[16,128]{1,0:T(8,128)(2,1)S(1)}, u32[]{:S(2)}, u32[]{:S(2)}) collective-permute-start(bf16[16,128]{1,0:T(8,128)(2,1)S(1)} %get-tuple-element.38), channel_id=1, source_target_pairs={{0,8},{4,12},{8,0},{12,4},{1,9},{5,13},{9,1},{13,5},{2,10},{6,14},... | collective-permute-start | bytes 12296 | tf_op jit(solution)/shard_map/ppermute | solution.py:314
  10.7 5.5 %collective-permute-start.4 = (bf16[48,128]{1,0:T(8,128)(2,1)S(1)}, bf16[48,128]{1,0:T(8,128)(2,1)S(1)}, u32[]{:S(2)}, u32[]{:S(2)}) collective-permute-start(bf16[48,128]{1,0:T(8,128)(2,1)S(1)} %get-tuple-element.36), channel_id=1, source_target_pairs={{0,4},{4,8},{8,12},{12,0},{1,5},{5,9},{9,13},{13,1},{2,6},{6,10},{... | collective-permute-start | bytes 36872 | tf_op jit(solution)/shard_map/ppermute | solution.py:314
  12.6 5.0 %collective-permute-start.5 = (bf16[48,128]{1,0:T(8,128)(2,1)S(1)}, bf16[48,128]{1,0:T(8,128)(2,1)S(1)}, u32[]{:S(2)}, u32[]{:S(2)}) collective-permute-start(bf16[48,128]{1,0:T(8,128)(2,1)S(1)} %get-tuple-element.37), channel_id=1, source_target_pairs={{0,12},{4,0},{8,4},{12,8},{1,13},{5,1},{9,5},{13,9},{2,14},{6,2},{... | collective-permute-start | bytes 36872 | tf_op jit(solution)/shard_map/ppermute | solution.py:314
  16.2 1.5 %collective-permute-start.1 = (bf16[2,128,512]{2,1,0:T(8,128)(2,1)S(1)}, bf16[2,128,512]{2,1,0:T(8,128)(2,1)S(1)}, u32[]{:S(2)}, u32[]{:S(2)}) collective-permute-start(bf16[2,128,512]{2,1,0:T(8,128)(2,1)S(1)} %copy-done.2), channel_id=1, source_target_pairs={{0,1},{1,0},{2,3},{3,2},{4,5},{5,4},{6,7},{7,6},{8,9},{9,8},{10,11... | collective-permute-start | bytes 786440 | tf_op jit(solution)/shard_map/ppermute | solution.py:309
  17.6 1.5 %collective-permute-start.3 = (bf16[2,128,512]{2,1,0:T(8,128)(2,1)S(1)}, bf16[2,128,512]{2,1,0:T(8,128)(2,1)S(1)}, u32[]{:S(2)}, u32[]{:S(2)}) collective-permute-start(bf16[2,128,512]{2,1,0:T(8,128)(2,1)S(1)} %copy-done.3), channel_id=1, source_target_pairs={{0,1},{1,0},{2,3},{3,2},{4,5},{5,4},{6,7},{7,6},{8,9},{9,8},{10,11... | collective-permute-start | bytes 786440 | tf_op jit(solution)/shard_map/ppermute | solution.py:309
  19.1 12.9 %collective-permute-start.8 = (bf16[1840,128]{1,0:T(8,128)(2,1)S(1)}, bf16[1840,128]{1,0:T(8,128)(2,1)S(1)}, u32[]{:S(2)}, u32[]{:S(2)}) collective-permute-start(bf16[1840,128]{1,0:T(8,128)(2,1)S(1)} %latents.1.refs_12_), channel_id=1, source_target_pairs={{0,2},{1,3},{2,0},{3,1},{4,6},{5,7},{6,4},{7,5},{8,10},{9,11},{10,... | collective-permute-start | bytes 1413128 | tf_op jit(solution)/shard_map/ppermute | solution.py:309
  19.7 12.3 %collective-permute-start.9 = (bf16[1792,128]{1,0:T(8,128)(2,1)S(1)}, bf16[1792,128]{1,0:T(8,128)(2,1)S(1)}, u32[]{:S(2)}, u32[]{:S(2)}) collective-permute-start(bf16[1792,128]{1,0:T(8,128)(2,1)S(1)} %collective-permute-done.7.refs_8_), channel_id=1, source_target_pairs={{0,16},{16,0},{1,17},{17,1},{2,18},{18,2},{3,19},{19,3},{4,20},{20... | collective-permute-start | bytes 1376264 | tf_op jit(solution)/shard_map/ppermute | solution.py:421
  32.0 21.6 %collective-permute-start.10 = (bf16[3584,128]{1,0:T(8,128)(2,1)S(1)}, bf16[3584,128]{1,0:T(8,128)(2,1)S(1)}, u32[]{:S(2)}, u32[]{:S(2)}) collective-permute-start(bf16[3584,128]{1,0:T(8,128)(2,1)S(1)} %get-tuple-element.40), channel_id=1, source_target_pairs={{0,2},{1,3},{2,0},{3,1},{4,6},{5,7},{6,4},{7,5},{8,10},{9,11},{10,... | collective-permute-start | bytes 2752520 | tf_op jit(solution)/shard_map/ppermute | solution.py:309
  33.5 1.8 %collective-permute-start.13 = (bf16[1840,128]{1,0:T(8,128)(2,1)S(1)}, bf16[1840,128]{1,0:T(8,128)(2,1)S(1)}, u32[]{:S(2)}, u32[]{:S(2)}) collective-permute-start(bf16[1840,128]{1,0:T(8,128)(2,1)S(1)} %latents.1.refs_12_), channel_id=1, source_target_pairs={{0,1},{1,0},{2,3},{3,2},{4,5},{5,4},{6,7},{7,6},{8,9},{9,8},{10,11... | collective-permute-start | bytes 1413128 | tf_op jit(solution)/shard_map/ppermute | solution.py:309
  33.5 3.8 %collective-permute-start.14 = (bf16[1840,128]{1,0:T(8,128)(2,1)S(1)}, bf16[1840,128]{1,0:T(8,128)(2,1)S(1)}, u32[]{:S(2)}, u32[]{:S(2)}) collective-permute-start(bf16[1840,128]{1,0:T(8,128)(2,1)S(1)} %collective-permute-done.8.refs_14_), channel_id=1, source_target_pairs={{0,1},{1,0},{2,3},{3,2},{4,5},{5,4},{6,7},{7,6},{8,9},{9,8},{10,11... | collective-permute-start | bytes 1413128 | tf_op jit(solution)/shard_map/ppermute | solution.py:309
  34.0 2.7 %collective-permute-start.11 = (bf16[1792,128]{1,0:T(8,128)(2,1)S(1)}, bf16[1792,128]{1,0:T(8,128)(2,1)S(1)}, u32[]{:S(2)}, u32[]{:S(2)}) collective-permute-start(bf16[1792,128]{1,0:T(8,128)(2,1)S(1)} %collective-permute-done.7.refs_8_), channel_id=1, source_target_pairs={{0,1},{1,0},{2,3},{3,2},{4,5},{5,4},{6,7},{7,6},{8,9},{9,8},{10,11... | collective-permute-start | bytes 1376264 | tf_op jit(solution)/shard_map/ppermute | solution.py:309
  34.0 3.3 %collective-permute-start.12 = (bf16[1792,128]{1,0:T(8,128)(2,1)S(1)}, bf16[1792,128]{1,0:T(8,128)(2,1)S(1)}, u32[]{:S(2)}, u32[]{:S(2)}) collective-permute-start(bf16[1792,128]{1,0:T(8,128)(2,1)S(1)} %collective-permute-done.9.refs_9_), channel_id=1, source_target_pairs={{0,1},{1,0},{2,3},{3,2},{4,5},{5,4},{6,7},{7,6},{8,9},{9,8},{10,11... | collective-permute-start | bytes 1376264 | tf_op jit(solution)/shard_map/ppermute | solution.py:309
  44.2 9.0 %collective-permute-start.15 = (bf16[48,512]{1,0:T(8,128)(2,1)S(1)}, bf16[48,512]{1,0:T(8,128)(2,1)S(1)}, u32[]{:S(2)}, u32[]{:S(2)}) collective-permute-start(bf16[48,512]{1,0:T(8,128)(2,1)S(1)} %get-tuple-element.44), channel_id=1, source_target_pairs={{0,4},{4,8},{8,12},{12,0},{1,5},{5,9},{9,13},{13,1},{2,6},{6,10},{... | collective-permute-start | bytes 147464 | tf_op jit(solution)/shard_map/ppermute | solution.py:314
  44.5 8.7 %collective-permute-start.16 = (bf16[48,512]{1,0:T(8,128)(2,1)S(1)}, bf16[48,512]{1,0:T(8,128)(2,1)S(1)}, u32[]{:S(2)}, u32[]{:S(2)}) collective-permute-start(bf16[48,512]{1,0:T(8,128)(2,1)S(1)} %get-tuple-element.45), channel_id=1, source_target_pairs={{0,12},{4,0},{8,4},{12,8},{1,13},{5,1},{9,5},{13,9},{2,14},{6,2},{... | collective-permute-start | bytes 147464 | tf_op jit(solution)/shard_map/ppermute | solution.py:314
  48.6 4.6 %collective-permute-start.17 = (bf16[16,512]{1,0:T(8,128)(2,1)S(1)}, bf16[16,512]{1,0:T(8,128)(2,1)S(1)}, u32[]{:S(2)}, u32[]{:S(2)}) collective-permute-start(bf16[16,512]{1,0:T(8,128)(2,1)S(1)} %get-tuple-element.46), channel_id=1, source_target_pairs={{0,8},{4,12},{8,0},{12,4},{1,9},{5,13},{9,1},{13,5},{2,10},{6,14},... | collective-permute-start | bytes 49160 | tf_op jit(solution)/shard_map/ppermute | solution.py:314
  53.6 2.5 %collective-permute-start.18 = (bf16[3584,128]{1,0:T(8,128)(2,1)S(1)}, bf16[3584,128]{1,0:T(8,128)(2,1)S(1)}, u32[]{:S(2)}, u32[]{:S(2)}) collective-permute-start(bf16[3584,128]{1,0:T(8,128)(2,1)S(1)} %collective-permute-done.10.refs_8_), channel_id=1, source_target_pairs={{0,1},{1,0},{2,3},{3,2},{4,5},{5,4},{6,7},{7,6},{8,9},{9,8},{10,11... | collective-permute-start | bytes 2752520 | tf_op jit(solution)/shard_map/ppermute | solution.py:309
  (4 other events, 15.9 us)

commit v10 on v9

--- a/solution.py
+++ b/solution.py
@@ -67,49 +67,45 @@
     copies.start(second.at[layer], second_ref.at[pl.ds(j * part, part)])
 
 
-def load_packed(copies, packed, base, j, first_ref, second_ref):
+def load_packed(copies, packed, j, first_ref, second_ref):
     rows = first_ref.shape[0]
     hidden, features = second_ref.shape
     part = hidden // 4
-    copies.start(packed.at[pl.ds(base, rows)], first_ref.at[:, pl.ds(j * part, part)])
+    copies.start(packed.at[pl.ds(0, rows)], first_ref.at[:, pl.ds(j * part, part)])
     for q in range(features // part):
         copies.start(
-            packed.at[pl.ds(base + rows + q * part, part)],
+            packed.at[pl.ds(rows + q * part, part)],
             second_ref.at[pl.ds(j * part, part), pl.ds(q * part, part)],
         )
 
 
-def load_half(copies, packed, base, half, j, first_ref, second_ref):
+def load_half(copies, packed, half, j, first_ref, second_ref):
     rows = first_ref.shape[0] // 2
     hidden, features = second_ref.shape
     part = hidden // 4
     deep = part // 2
     at = pl.multiple_of(half * rows, rows)
-    copies.start(packed.at[pl.ds(base, rows)], first_ref.at[pl.ds(at, rows), pl.ds(j * part, part)])
+    copies.start(packed.at[pl.ds(0, rows)], first_ref.at[pl.ds(at, rows), pl.ds(j * part, part)])
     at = pl.multiple_of(j * part + half * deep, deep)
     for q in range(features // part):
         copies.start(
-            packed.at[pl.ds(base + rows + q * deep, deep)],
+            packed.at[pl.ds(rows + q * deep, deep)],
             second_ref.at[pl.ds(at, deep), pl.ds(q * part, part)],
         )
-    return base + rows + features // part * deep
-
-
-def ride_kernel(ef, es, nf, ns, ride_out, sems):
+
+
+def ride_kernel(ef, es, nf, ns, edge_out, node_out, sems):
     y = lax.axis_index("groups")
     part, features = es.shape[1:]
     copies = Copies(sems)
-    at = 0
-    for first, second in ((ef, es), (nf, ns)):
+    for first, second, out in ((ef, es, edge_out), (nf, ns, node_out)):
         rows = first.shape[1] // 2
         source = first.at[0, pl.ds(pl.multiple_of(y * rows, rows), rows)]
-        copies.start(source, ride_out.at[pl.ds(at, rows)])
-        at += rows
+        copies.start(source, out.at[pl.ds(0, rows)])
         deep = part // 2
         for q in range(features // part):
             source = second.at[0, pl.ds(pl.multiple_of(y * deep, deep), deep), pl.ds(q * part, part)]
-            copies.start(source, ride_out.at[pl.ds(at, deep)])
-            at += deep
+            copies.start(source, out.at[pl.ds(rows + q * deep, deep)])
     copies.wait()
 
 
@@ -121,19 +117,16 @@
     return jnp.broadcast_to(row, (8, row.shape[1])).T[:, 0:1]
 
 
-def prepare_kernel(blocks, halo, table_rows, list_ref, ef, es, nf, ns, hot_out, incidence_out, pick_out, late_out, sems):
+def prepare_kernel(blocks, halo, table_rows, list_ref, ef, es, nf, ns, hot_out, incidence_out, pick_out, edge_late, node_late, sems):
     part, features = es.shape[1:]
     edge_count, lanes_all = hot_out.shape
     node_count = incidence_out.shape[0]
     copies = Copies(sems)
-    at = 0
-    for first, second in ((ef, es), (nf, ns)):
+    for first, second, out in ((ef, es, edge_late), (nf, ns, node_late)):
         rows = first.shape[1]
-        copies.start(first.at[1], late_out.at[pl.ds(at, rows)])
-        at += rows
+        copies.start(first.at[1], out.at[pl.ds(0, rows)])
         for q in range(features // part):
-            copies.start(second.at[1, :, pl.ds(q * part, part)], late_out.at[pl.ds(at, part)])
-            at += part
+            copies.start(second.at[1, :, pl.ds(q * part, part)], out.at[pl.ds(rows + q * part, part)])
     for at in range(0, edge_count, TILE):
         senders = table_index(list_ref[:, at : at + TILE], blocks, node_count, halo)
         receivers = list_ref[:, edge_count + at : edge_count + at + TILE]
@@ -161,6 +154,13 @@
     for out in outs:
         out[...] = picked[start : start + out.shape[0]]
         start += out.shape[0]
+
+
+def join_kernel(*refs):
+    at = 0
+    for piece in refs[:-1]:
+        refs[-1][at : at + piece.shape[0], :] = piece[...]
+        at += piece.shape[0]
 
 
 def start_kernel(node_ref, pick_ref, right, left, coarse):
@@ -214,8 +214,9 @@
     refs = list(refs)
     own_w = [refs.pop(0) for _ in range(4)]
     core_w = [refs.pop(0) for _ in range(4)]
-    halves = [[refs.pop(0) for _ in range(2)] for _ in range(2)]
+    halves = [[[refs.pop(0) for _ in range(2)] for _ in range(2)] for _ in range(2)]
     shards = [refs.pop(0) for _ in range(4)]
+    rims = [refs.pop(0) for _ in range(4)]
     edge_own, node_own, hot_ref, incidence_ref, pick_ref = [refs.pop(0) for _ in range(5)]
     edge_out, full_out, node_out, node_full = [refs.pop(0) for _ in range(4)]
     sends = [refs.pop(0) for _ in range(3)]
@@ -223,67 +224,60 @@
     part = edge_own.shape[1]
     edge_count = edge_own.shape[0]
     node_count = node_own.shape[0]
-    edge_copies, node_copies = Moves(), Moves()
-    for j, shard in enumerate(shards):
-        column = pl.multiple_of((lax.axis_index("mp") ^ j) * part, part)
-        edge_copies.start(shard, x_ref.at[:, pl.ds(column, part)])
+    moves = Moves()
+    for pieces, at in ((shards, 0), (rims, edge_count + node_count)):
+        rows = pl.ds(at, pieces[0].shape[0])
+        for j, shard in enumerate(pieces):
+            column = pl.multiple_of((lax.axis_index("mp") ^ j) * part, part)
+            moves.start(shard, x_ref.at[rows, pl.ds(column, part)])
     y = lax.axis_index("groups")
-    starts = [0, 0]
-    for base, copies, (first, second), at in (
-        (0, edge_copies, (edge_w, edge_w2), 0),
-        (1, node_copies, (node_w, node_w2), 2),
-    ):
-        load_shard(copies, 0, own_w[at], own_w[at + 1], 0, first, second)
-        load_shard(copies, 0, core_w[at], core_w[at + 1], 1, first, second)
-        for j, pair in enumerate(halves):
-            for k, piece in enumerate(pair):
-                half = y if k == 0 else 1 - y
-                end = load_half(copies, piece, starts[base], half, 2 + j, first, second)
-        starts[1] = end
-    edge_copies.wait()
+    for at, first, second in ((0, edge_w, edge_w2), (1, node_w, node_w2)):
+        load_shard(moves, 0, own_w[2 * at], own_w[2 * at + 1], 0, first, second)
+        load_shard(moves, 0, core_w[2 * at], core_w[2 * at + 1], 1, first, second)
+        for j, pair in enumerate(halves[at]):
+            for piece, half in zip(pair, (y, 1 - y)):
+                load_half(moves, piece, half, 2 + j, first, second)
     nodes = x_ref[edge_count : edge_count + node_count, :]
     incoming = edge_rows(
         x_ref, x_ref[edge_count:, :], nodes, edge_own, hot_ref, incidence_ref,
         edge_w, edge_w2, product_ref, edge_out, full_out,
     )
-    node_copies.wait()
     node_new = node_rows(nodes, incoming, node_own, node_w, node_w2, node_out)
     node_full[...] = node_new
     pick_rows(pick_ref, node_new, sends)
 
 
-def late_kernel(pieces, *refs):
+def late_weights(weights, first, second):
+    moves = Moves()
+    load_shard(moves, 1, weights[0], weights[1], 0, first, second)
+    load_shard(moves, 1, weights[2], weights[3], 1, first, second)
+    load_packed(moves, weights[4], 2, first, second)
+    load_packed(moves, weights[5], 3, first, second)
+
+
+def late_edge_kernel(pieces, *refs):
     refs = list(refs)
-    own_w = [refs.pop(0) for _ in range(4)]
-    core_w = [refs.pop(0) for _ in range(4)]
-    packed = [refs.pop(0) for _ in range(2)]
-    edge_ref, edge_own, node_own = [refs.pop(0) for _ in range(3)]
+    weights = [refs.pop(0) for _ in range(6)]
+    edge_ref, edge_own = [refs.pop(0) for _ in range(2)]
     tables = [refs.pop(0) for _ in range(pieces)]
-    hot_ref, incidence_ref, edge_out, node_out = [refs.pop(0) for _ in range(4)]
-    edge_w, edge_w2, node_w, node_w2, product_ref, table_ref = refs
-    edge_copies, node_copies = Moves(), Moves()
-    base = 0
-    for copies, first, second, at in (
-        (edge_copies, edge_w, edge_w2, 0),
-        (node_copies, node_w, node_w2, 2),
-    ):
-        load_shard(copies, 1, own_w[at], own_w[at + 1], 0, first, second)
-        load_shard(copies, 1, core_w[at], core_w[at + 1], 1, first, second)
-        for j, pack in enumerate(packed):
-            load_packed(copies, pack, base, 2 + j, first, second)
-        base = edge_w.shape[0] + edge_w2.shape[1]
+    hot_ref, incidence_ref, edge_out, incoming_out = [refs.pop(0) for _ in range(4)]
+    edge_w, edge_w2, product_ref, table_ref = refs
+    late_weights(weights, edge_w, edge_w2)
     start = 0
     for table in tables:
         table_ref[start : start + table.shape[0], :] = table[...]
         start += table.shape[0]
-    edge_copies.wait()
-    nodes = tables[0][...]
-    incoming = edge_rows(
-        edge_ref, table_ref[...], nodes, edge_own, hot_ref, incidence_ref,
+    incoming_out[...] = edge_rows(
+        edge_ref, table_ref[...], tables[0][...], edge_own, hot_ref, incidence_ref,
         edge_w, edge_w2, product_ref, edge_out, None,
     )
-    node_copies.wait()
-    node_rows(nodes, incoming, node_own, node_w, node_w2, node_out)
+
+
+def late_node_kernel(*refs):
+    weights = refs[:6]
+    node_ref, node_own, incoming_ref, node_out, node_w, node_w2 = refs[6:]
+    late_weights(weights, node_w, node_w2)
+    node_rows(node_ref[...], incoming_ref[...], node_own, node_w, node_w2, node_out)
 
 
 SMEM, VMEM, ANY = pltpu.SMEM, pltpu.VMEM, pl.ANY
@@ -372,34 +366,44 @@
     weights = (edge_first, edge_second, node_first, node_second)
     edge_pack = edge_first.shape[1] + features
     node_pack = node_first.shape[1] + features
-    (ride,) = call(
+    edge_ride, node_ride = call(
         ride_kernel,
-        [shape(((edge_pack + node_pack) // 2, part), BF16)],
+        [shape((n // 2, part), BF16) for n in (edge_pack, node_pack)],
         [(ANY, w) for w in weights],
         [dma((10,))],
         0,
         "layer_0_half",
         60,
     )
-    near = swap(ride, 2)
+    edge_near, node_near = swap(edge_ride, 2), swap(node_ride, 2)
+    (latents,) = call(
+        latent_kernel,
+        [shape((edge_count + node_count, part), BF16)],
+        [(VMEM, after(edge_state, edge_ride)), (VMEM, node_state)],
+        [],
+        0,
+        "latents",
+    )
+    far_latents = swap(latents, 2)
     far_rows = 2 * wide + COARSE_PAD if blocks == 4 else 2 * halo + blocks * COARSE_PAD
     table_rows = node_count + far_rows
     lanes = -(-(table_rows + node_count) // 128) * 128
     lists = jnp.concatenate([senders, receivers, boundary_rows])[None, :]
-    hot, incidence, pick, late_w = call(
+    hot, incidence, pick, edge_late, node_late = call(
         functools.partial(prepare_kernel, blocks, halo, table_rows),
         [
             shape((edge_count, lanes), BF16),
             shape((node_count, edge_count), BF16),
             shape((2 * wide + COARSE_PAD, node_count), BF16),
-            shape((edge_pack + node_pack, part), BF16),
+            shape((edge_pack, part), BF16),
+            shape((node_pack, part), BF16),
         ],
-        [(VMEM, after(lists, ride))] + [(ANY, w) for w in weights],
+        [(VMEM, after(lists, latents))] + [(ANY, w) for w in weights],
         [dma((10,))],
         0,
         "one_hot",
     )
-    core_w = [swap(after(w, ride), 1) for w in weights]
+    core_w = [swap(after(w, edge_ride), 1) for w in weights]
     right, left, coarse = call(
         start_kernel,
         sent(part),
@@ -408,20 +412,24 @@
         2 * pick.size * part,
         "boundary_rows",
     )
-    rows = neighbour_rows(right, left, coarse, halo)
-    (latents,) = call(
-        latent_kernel,
-        [shape((edge_count + table_rows, part), BF16)],
-        [(VMEM, after(edge_state, late_w)), (VMEM, node_state)] + [(VMEM, r) for r in rows],
+    (rim,) = call(
+        join_kernel,
+        [shape((far_rows, part), BF16)],
+        [(VMEM, r) for r in neighbour_rows(right, left, coarse, halo)],
         [],
         0,
-        "latents",
-    )
-    far_latents = swap(after(latents, near, *core_w), 2)
-    far = lax.ppermute(near, "groups", [(0, 1), (1, 0)])
-    shards = [latents, swap(latents, 1), far_latents, swap(after(far_latents, far), 1)]
-    pairs = [near, far, swap(near, 1), swap(far, 1)]
-    late_x = swap(after(late_w, far_latents, far), 2)
+        "halo_rows",
+    )
+    edge_far = lax.ppermute(edge_near, "groups", [(0, 1), (1, 0)])
+    node_far = lax.ppermute(node_near, "groups", [(0, 1), (1, 0)])
+    far_rim = swap(after(rim, *core_w), 2)
+    edge_late_x, node_late_x = lax.optimization_barrier((edge_late, node_late, far_rim, edge_far))[:2]
+    edge_late_x, node_late_x = swap(edge_late_x, 2), swap(node_late_x, 2)
+    shards = [latents, swap(latents, 1), far_latents, swap(after(far_latents, node_far), 1)]
+    rims = [rim, swap(rim, 1), far_rim, swap(far_rim, 1)]
+    pairs = []
+    for near, far in ((edge_near, edge_far), (node_near, node_far)):
+        pairs += [near, far, swap(near, 1), swap(far, 1)]
 
     edge_flops = 2 * edge_count * features * (2 * features + lanes + node_count)
     node_flops = 2 * node_count * features * 3 * features
@@ -436,7 +444,7 @@
     edge_own, edge_full, node_own, node_full, right, left, coarse = call(
         first_kernel,
         [own_edge, full_edge, own_node, full_node] + sent(features),
-        [(VMEM, w) for w in list(weights) + core_w + pairs + shards]
+        [(VMEM, w) for w in list(weights) + core_w + pairs + shards + rims]
         + [(VMEM, a) for a in (edge_state, node_state, hot, incidence, pick)],
         [
             edge_shape,
@@ -451,24 +459,33 @@
         16,
     )
     tables = [node_full] + neighbour_rows(right, left, coarse, halo)
-    late_d = swap(after(late_x, *tables[1:]), 1)
-    edge_own, node_own = call(
-        functools.partial(late_kernel, len(tables)),
-        [own_edge, own_node],
-        [(VMEM, w) for w in list(weights) + core_w + [late_x, late_d]]
-        + [(VMEM, a) for a in (edge_full, edge_own, node_own)]
+    edge_late_d = swap(after(edge_late_x, right), 1)
+    edge_own, incoming = call(
+        functools.partial(late_edge_kernel, len(tables)),
+        [own_edge, full_node],
+        [(VMEM, w) for w in (*weights[:2], *core_w[:2], edge_late_x, edge_late_d)]
+        + [(VMEM, a) for a in (edge_full, edge_own)]
         + [(VMEM, t) for t in tables]
         + [(VMEM, hot), (VMEM, incidence)],
         [
             edge_shape,
             second_shape,
-            node_shape,
-            second_shape,
             pltpu.VMEM((lanes, hidden), BF16),
             pltpu.VMEM((table_rows, features), BF16),
         ],
-        edge_flops + node_flops,
-        "layer_1",
+        edge_flops,
+        "layer_1_edges",
+        16,
+    )
+    node_late_d = swap(after(node_late_x, *tables[1:]), 1)
+    (node_own,) = call(
+        late_node_kernel,
+        [own_node],
+        [(VMEM, w) for w in (*weights[2:], *core_w[2:], node_late_x, node_late_d)]
+        + [(VMEM, a) for a in (node_full, node_own, incoming)],
+        [node_shape, second_shape],
+        node_flops,
+        "layer_1_nodes",
         16,
     )
     return (node_own, edge_own)

time: 62.9 us -> 73.8 us (1.17)
  waiting for transfers between devices: 23.9 us -> 28.1 us
  starting transfers between devices: 20.7 us -> 23.6 us
  local copies, waits for them, and re-layouts: 0.05 us -> 2.06 us
  Pallas kernels: 17.3 us -> 18.2 us
    ppermute x6, waiting for transfers between devices: 6.06 us -> 12.5 us  [shift(): return lax.ppermute(x, 'graph', [(i, (i + by) % size) for i in range(size)])]
    ppermute x1 -> x2, waiting for transfers between devices: 10.8 us -> 4.63 us  [the longest x1 3.37 us: on_device(): edge_far = lax.ppermute(edge_near, 'groups', [(0, 1), (1, 0)])]
    ppermute x12 -> x20, waiting for transfers between devices: 7.12 us -> 11 us  [swap(): return lax.ppermute(x, 'mp', [(i, i ^ mask) for i in range(size)])]
    ppermute x12 -> x20, starting transfers between devices: 6.63 us -> 9.65 us  [swap(): return lax.ppermute(x, 'mp', [(i, i ^ mask) for i in range(size)])]
    ppermute x6, starting transfers between devices: 12.5 us -> 10.4 us  [shift(): return lax.ppermute(x, 'graph', [(i, (i + by) % size) for i in range(size)])]
    ppermute x1 -> x2, starting transfers between devices: 1.52 us -> 3.54 us  [the longest x1 1.8 us: on_device(): node_far = lax.ppermute(node_near, 'groups', [(0, 1), (1, 0)])]
    unnamed x18, local copies, waits for them, and re-layouts: 0.04 us -> 2.05 us
    pallas_call x6 -> x8, Pallas kernels: 17.3 us -> 18.2 us  [call(): pl.pallas_call(kernel, out_shape=out_shape, in_specs=[pl.BlockSpec(memory...]
  transfers between devices with their start and end apart: 19 -> 28, of which waited for: 11 -> 11; matrix products, arithmetic and copies ran while one was open for 0% -> 1% of each run, Pallas kernels for 14% -> 20%
where the time goes in v10:
time: 73.8 us; the launch traced here: 73.5 us
  waiting for transfers between devices  28.1 us (38%)
  starting transfers between devices  23.6 us (32%)
  Pallas kernels  18.2 us (25%)
  local copies, waits for them, and re-layouts  2.06 us (3%)
  between operations  0.79 us (1%)
    pallas_call x8, Pallas kernels, call(): pl.pallas_call(kernel, out_shape=out_shape, in_specs=[pl.BlockSpec(memory...  18.2 us
    ppermute x6, waiting for transfers between devices, shift(): return lax.ppermute(x, 'graph', [(i, (i + by) % size) for i in range(size)])  12.5 us
    ppermute x20, waiting for transfers between devices, swap(): return lax.ppermute(x, 'mp', [(i, i ^ mask) for i in range(size)])  11 us
    ppermute x6, starting transfers between devices, shift(): return lax.ppermute(x, 'graph', [(i, (i + by) % size) for i in range(size)])  10.4 us
    ppermute x20, starting transfers between devices, swap(): return lax.ppermute(x, 'mp', [(i, i ^ mask) for i in range(size)])  9.65 us
    ppermute x1, waiting for transfers between devices, on_device(): edge_far = lax.ppermute(edge_near, 'groups', [(0, 1), (1, 0)])  3.37 us
    unnamed x18, local copies, waits for them, and re-layouts  2.05 us
    ppermute x1, starting transfers between devices, on_device(): node_far = lax.ppermute(node_near, 'groups', [(0, 1), (1, 0)])  1.8 us
  transfers between devices with their start and end apart: 28, of which 11 were waited for; matrix products, arithmetic and copies ran while one was open for 1% of the time, Pallas kernels for 20%

profile of v10, /device:TPU:0, one launch (start us, length us, event | category | flops | bytes accessed | tf_op | source)
XLA Modules:
  0.0 73.5 jit_solution(1950211026052576749)
XLA Ops:
  0.7 2.0 %layer_0_half.1 = (bf16[1024,128]{1,0:T(8,128)(2,1)}, bf16[768,128]{1,0:T(8,128)(2,1)}) custom-call(bf16[2,1536,128]{2,1,0:T(8,128)(2,1)} %refs_0_.5, bf16[2,128,512]{2,1,0:T(8,128)(2,1)} %refs_1_.6, bf16[2,1024,128]{2,1,0:T(8,128)(2,1)} %refs_0_.6, bf16[2,128,512]{2,1,0:T(8,128)(2,1)} %refs_1_.7), custom_call_target="tpu_custom_call" | custom-call | bytes 2293760 | tf_op jit(solution)/shard_map/layer_0_half/pallas_call | solution.py:289
  2.7 3.0 %collective-permute-start.13 = (bf16[768,128]{1,0:T(8,128)(2,1)}, bf16[768,128]{1,0:T(8,128)(2,1)S(1)}, u32[]{:S(2)}, u32[]{:S(2)}) collective-permute-start(bf16[768,128]{1,0:T(8,128)(2,1)} %get-tuple-element.48), channel_id=1, source_target_pairs={{0,2},{1,3},{2,0},{3,1},{4,6},{5,7},{6,4},{7,5},{8,10},{9,11},{10,... | collective-permute-start | bytes 589832 | tf_op jit(solution)/shard_map/ppermute | solution.py:303
  9.1 1.5 %one_hot.1 = (bf16[1536,512]{1,0:T(8,128)(2,1)S(1)}, bf16[192,1536]{1,0:T(8,128)(2,1)S(1)}, bf16[112,192]{1,0:T(8,128)(2,1)S(1)}, bf16[2048,128]{1,0:T(8,128)(2,1)S(1)}, bf16[1536,128]{1,0:T(8,128)(2,1)S(1)}) custom-call(s32[1,3136]{1,0:T(1,128)S(1)} %broadcast_in_dim.3.list_ref, bf16[2,1536,128]{2,1,0:T(8,128)(2,1)S(1)} %copy-done.1, ...), custom_call_target="tpu_custom_call" | custom-call | bytes 4970752 | tf_op jit(solution)/shard_map/one_hot/pallas_call | solution.py:289
  10.7 2.7 %collective-permute-start.4 = (bf16[16,128]{1,0:T(8,128)(2,1)S(1)}, bf16[16,128]{1,0:T(8,128)(2,1)S(1)}, u32[]{:S(2)}, u32[]{:S(2)}) collective-permute-start(bf16[16,128]{1,0:T(8,128)(2,1)S(1)} %get-tuple-element.43), channel_id=1, source_target_pairs={{0,8},{4,12},{8,0},{12,4},{1,9},{5,13},{9,1},{13,5},{2,10},{6,14},... | collective-permute-start | bytes 12296 | tf_op jit(solution)/shard_map/ppermute | solution.py:308
  13.9 1.4 %collective-permute-done.4.refs_2_ = bf16[16,128]{1,0:T(8,128)(2,1)S(1)} collective-permute-done((bf16[16,128]{1,0:T(8,128)(2,1)S(1)}, bf16[16,128]{1,0:T(8,128)(2,1)S(1)}, u32[]{:S(2)}, u32[]{:S(2)}) %collective-permute-start.4) | collective-permute-done | bytes 4128 | tf_op jit(solution)/shard_map/ppermute | solution.py:308
  15.3 1.6 %collective-permute-start.2 = (bf16[48,128]{1,0:T(8,128)(2,1)S(1)}, bf16[48,128]{1,0:T(8,128)(2,1)S(1)}, u32[]{:S(2)}, u32[]{:S(2)}) collective-permute-start(bf16[48,128]{1,0:T(8,128)(2,1)S(1)} %get-tuple-element.41), channel_id=1, source_target_pairs={{0,4},{4,8},{8,12},{12,0},{1,5},{5,9},{9,13},{13,1},{2,6},{6,10},{... | collective-permute-start | bytes 36872 | tf_op jit(solution)/shard_map/ppermute | solution.py:308
  16.9 3.9 %collective-permute-done.2.refs_0_ = bf16[48,128]{1,0:T(8,128)(2,1)S(1)} collective-permute-done((bf16[48,128]{1,0:T(8,128)(2,1)S(1)}, bf16[48,128]{1,0:T(8,128)(2,1)S(1)}, u32[]{:S(2)}, u32[]{:S(2)}) %collective-permute-start.2) | collective-permute-done | bytes 12320 | tf_op jit(solution)/shard_map/ppermute | solution.py:308
  20.8 1.8 %collective-permute-start.3 = (bf16[48,128]{1,0:T(8,128)(2,1)S(1)}, bf16[48,128]{1,0:T(8,128)(2,1)S(1)}, u32[]{:S(2)}, u32[]{:S(2)}) collective-permute-start(bf16[48,128]{1,0:T(8,128)(2,1)S(1)} %get-tuple-element.42), channel_id=1, source_target_pairs={{0,12},{4,0},{8,4},{12,8},{1,13},{5,1},{9,5},{13,9},{2,14},{6,2},{... | collective-permute-start | bytes 36872 | tf_op jit(solution)/shard_map/ppermute | solution.py:308
  22.6 1.9 %collective-permute-done.3.refs_1_ = bf16[48,128]{1,0:T(8,128)(2,1)S(1)} collective-permute-done((bf16[48,128]{1,0:T(8,128)(2,1)S(1)}, bf16[48,128]{1,0:T(8,128)(2,1)S(1)}, u32[]{:S(2)}, u32[]{:S(2)}) %collective-permute-start.3) | collective-permute-done | bytes 12320 | tf_op jit(solution)/shard_map/ppermute | solution.py:308
  24.8 1.8 %collective-permute-start.14 = (bf16[768,128]{1,0:T(8,128)(2,1)S(1)}, bf16[768,128]{1,0:T(8,128)(2,1)S(1)}, u32[]{:S(2)}, u32[]{:S(2)}) collective-permute-start(bf16[768,128]{1,0:T(8,128)(2,1)S(1)} %collective-permute-done.13.refs_12_), channel_id=1, source_target_pairs={{0,16},{16,0},{1,17},{17,1},{2,18},{18,2},{3,19},{19,3},{4,20},{20... | collective-permute-start | bytes 589832 | tf_op jit(solution)/shard_map/ppermute | solution.py:424
  26.6 4.2 %collective-permute-done.8.refs_8_ = bf16[1024,128]{1,0:T(8,128)(2,1)S(1)} collective-permute-done((bf16[1024,128]{1,0:T(8,128)(2,1)S(1)}, bf16[1024,128]{1,0:T(8,128)(2,1)S(1)}, u32[]{:S(2)}, u32[]{:S(2)}) %collective-permute-start.8) | collective-permute-done | bytes 262176 | tf_op jit(solution)/shard_map/ppermute | solution.py:303
  30.9 1.3 %collective-permute-done.14.refs_13_ = bf16[768,128]{1,0:T(8,128)(2,1)S(1)} collective-permute-done((bf16[768,128]{1,0:T(8,128)(2,1)S(1)}, bf16[768,128]{1,0:T(8,128)(2,1)S(1)}, u32[]{:S(2)}, u32[]{:S(2)}) %collective-permute-start.14) | collective-permute-done | bytes 196640 | tf_op jit(solution)/shard_map/ppermute | solution.py:424
  32.1 1.7 %collective-permute-start.9 = (bf16[1024,128]{1,0:T(8,128)(2,1)S(1)}, bf16[1024,128]{1,0:T(8,128)(2,1)S(1)}, u32[]{:S(2)}, u32[]{:S(2)}) collective-permute-start(bf16[1024,128]{1,0:T(8,128)(2,1)S(1)} %collective-permute-done.8.refs_8_), channel_id=1, source_target_pairs={{0,16},{16,0},{1,17},{17,1},{2,18},{18,2},{3,19},{19,3},{4,20},{20... | collective-permute-start | bytes 786440 | tf_op jit(solution)/shard_map/ppermute | solution.py:423
  34.6 1.4 %collective-permute-done.20.refs_21_ = bf16[112,128]{1,0:T(8,128)(2,1)S(1)} collective-permute-done((bf16[112,128]{1,0:T(8,128)(2,1)S(1)}, bf16[112,128]{1,0:T(8,128)(2,1)S(1)}, u32[]{:S(2)}, u32[]{:S(2)}) %collective-permute-start.20) | collective-permute-done | bytes 28704 | tf_op jit(solution)/shard_map/ppermute | solution.py:303
  36.0 1.5 %collective-permute-start.7 = (bf16[112,128]{1,0:T(8,128)(2,1)S(1)}, bf16[112,128]{1,0:T(8,128)(2,1)S(1)}, u32[]{:S(2)}, u32[]{:S(2)}) collective-permute-start(bf16[112,128]{1,0:T(8,128)(2,1)S(1)} %halo_rows.1.refs_20_), channel_id=1, source_target_pairs={{0,2},{1,3},{2,0},{3,1},{4,6},{5,7},{6,4},{7,5},{8,10},{9,11},{10,... | collective-permute-start | bytes 86024 | tf_op jit(solution)/shard_map/ppermute | solution.py:303
  37.5 3.4 %collective-permute-done.9.refs_9_ = bf16[1024,128]{1,0:T(8,128)(2,1)S(1)} collective-permute-done((bf16[1024,128]{1,0:T(8,128)(2,1)S(1)}, bf16[1024,128]{1,0:T(8,128)(2,1)S(1)}, u32[]{:S(2)}, u32[]{:S(2)}) %collective-permute-start.9) | collective-permute-done | bytes 262176 | tf_op jit(solution)/shard_map/ppermute | solution.py:423
  41.4 1.7 %collective-permute-start.26 = (bf16[2048,128]{1,0:T(8,128)(2,1)S(1)}, bf16[2048,128]{1,0:T(8,128)(2,1)S(1)}, u32[]{:S(2)}, u32[]{:S(2)}) collective-permute-start(bf16[2048,128]{1,0:T(8,128)(2,1)S(1)} %get-tuple-element.58), channel_id=1, source_target_pairs={{0,2},{1,3},{2,0},{3,1},{4,6},{5,7},{6,4},{7,5},{8,10},{9,11},{10,... | collective-permute-start | bytes 1572872 | tf_op jit(solution)/shard_map/ppermute | solution.py:303
  44.9 6.9 %layer_0.1 = (f32[1536,128]{1,0:T(8,128)S(1)}, bf16[1536,512]{1,0:T(8,128)(2,1)S(1)}, f32[192,128]{1,0:T(8,128)S(1)}, bf16[192,512]{1,0:T(8,128)(2,1)S(1)}, bf16...) custom-call(bf16[2,1536,128]{2,1,0:T(8,128)(2,1)S(1)} %copy-done.1, ...), custom_call_target="tpu_custom_call" | custom-call | flops 3019898880 | bytes 13248512 | tf_op jit(solution)/shard_map/layer_0/pallas_call | solution.py:289
  51.7 4.4 %collective-permute-done.26.refs_4_ = bf16[2048,128]{1,0:T(8,128)(2,1)S(1)} collective-permute-done((bf16[2048,128]{1,0:T(8,128)(2,1)S(1)}, bf16[2048,128]{1,0:T(8,128)(2,1)S(1)}, u32[]{:S(2)}, u32[]{:S(2)}) %collective-permute-start.26) | collective-permute-done | bytes 524320 | tf_op jit(solution)/shard_map/ppermute | solution.py:303
  56.2 3.8 %collective-permute-start.23 = (bf16[48,512]{1,0:T(8,128)(2,1)S(1)}, bf16[48,512]{1,0:T(8,128)(2,1)S(1)}, u32[]{:S(2)}, u32[]{:S(2)}) collective-permute-start(bf16[48,512]{1,0:T(8,128)(2,1)S(1)} %get-tuple-element.53), channel_id=1, source_target_pairs={{0,12},{4,0},{8,4},{12,8},{1,13},{5,1},{9,5},{13,9},{2,14},{6,2},{... | collective-permute-start | bytes 147464 | tf_op jit(solution)/shard_map/ppermute | solution.py:308
  60.6 4.1 %collective-permute-done.24.refs_11_ = bf16[16,512]{1,0:T(8,128)(2,1)S(1)} collective-permute-done((bf16[16,512]{1,0:T(8,128)(2,1)S(1)}, bf16[16,512]{1,0:T(8,128)(2,1)S(1)}, u32[]{:S(2)}, u32[]{:S(2)}) %collective-permute-start.24) | collective-permute-done | bytes 16416 | tf_op jit(solution)/shard_map/ppermute | solution.py:308
  64.6 1.2 %collective-permute-done.22.refs_9_ = bf16[48,512]{1,0:T(8,128)(2,1)S(1)} collective-permute-done((bf16[48,512]{1,0:T(8,128)(2,1)S(1)}, bf16[48,512]{1,0:T(8,128)(2,1)S(1)}, u32[]{:S(2)}, u32[]{:S(2)}) %collective-permute-start.22) | collective-permute-done | bytes 49184 | tf_op jit(solution)/shard_map/ppermute | solution.py:308
  65.9 6.2 %layer_1_edges.1 = (f32[1536,128]{1,0:T(8,128)}, bf16[192,512]{1,0:T(8,128)(2,1)S(1)}) custom-call(bf16[2,1536,128]{2,1,0:T(8,128)(2,1)S(1)} %copy-done.1, bf16[2,128,512]{2,1,0:T(8,128)(2,1)S(1)} %copy-done.3, bf16[2,1536,128]{2,1,0:T(8,128)(2,1)S(1)} %collective-permute-done.5.refs_4_.refs_2_, ...), custom_call_target="tpu_custom_call" | custom-call | flops 2717908992 | bytes 8962048 | tf_op jit(solution)/shard_map/layer_1_edges/pallas_call | solution.py:289
  72.1 1.4 %layer_1_nodes.1 = f32[192,128]{1,0:T(8,128)} custom-call(bf16[2,1024,128]{2,1,0:T(8,128)(2,1)S(1)} %copy-done, bf16[2,128,512]{2,1,0:T(8,128)(2,1)S(1)} %copy-done.2, bf16[2,1024,128]{2,1,0:T(8,128)(2,1)S(1)} %collective-permute-done.refs_6_.refs_2_, bf16[2,128,512]{2,1,0:T(8,128)(2,1)S(1)} %collective-permute-done.1.refs_7_.refs_3_, ...), custom_call_target="tpu_custom_call" | custom-call | flops 301989888 | bytes 2949120 | tf_op jit(solution)/shard_map/layer_1_nodes/pallas_call | solution.py:289
  (60 shorter events, 8.0 us)
Async XLA Ops:
  2.7 22.1 %collective-permute-start.13 = (bf16[768,128]{1,0:T(8,128)(2,1)}, bf16[768,128]{1,0:T(8,128)(2,1)S(1)}, u32[]{:S(2)}, u32[]{:S(2)}) collective-permute-start(bf16[768,128]{1,0:T(8,128)(2,1)} %get-tuple-element.48), channel_id=1, source_target_pairs={{0,2},{1,3},{2,0},{3,1},{4,6},{5,7},{6,4},{7,5},{8,10},{9,11},{10,... | collective-permute-start | bytes 589832 | tf_op jit(solution)/shard_map/ppermute | solution.py:303
  5.7 19.1 %collective-permute-start.1 = (bf16[2,128,512]{2,1,0:T(8,128)(2,1)S(1)}, bf16[2,128,512]{2,1,0:T(8,128)(2,1)S(1)}, u32[]{:S(2)}, u32[]{:S(2)}) collective-permute-start(bf16[2,128,512]{2,1,0:T(8,128)(2,1)S(1)} %copy-done.2), channel_id=1, source_target_pairs={{0,1},{1,0},{2,3},{3,2},{4,5},{5,4},{6,7},{7,6},{8,9},{9,8},{10,11... | collective-permute-start | bytes 786440 | tf_op jit(solution)/shard_map/ppermute | solution.py:303
  5.7 28.7 %collective-permute-start.5 = (bf16[2,1536,128]{2,1,0:T(8,128)(2,1)S(1)}, bf16[2,1536,128]{2,1,0:T(8,128)(2,1)S(1)}, u32[]{:S(2)}, u32[]{:S(2)}) collective-permute-start(bf16[2,1536,128]{2,1,0:T(8,128)(2,1)S(1)} %copy-done.1), channel_id=1, source_target_pairs={{0,1},{1,0},{2,3},{3,2},{4,5},{5,4},{6,7},{7,6},{8,9},{9,8},{10,11... | collective-permute-start | bytes 2359304 | tf_op jit(solution)/shard_map/ppermute | solution.py:303
  10.7 4.6 %collective-permute-start.4 = (bf16[16,128]{1,0:T(8,128)(2,1)S(1)}, bf16[16,128]{1,0:T(8,128)(2,1)S(1)}, u32[]{:S(2)}, u32[]{:S(2)}) collective-permute-start(bf16[16,128]{1,0:T(8,128)(2,1)S(1)} %get-tuple-element.43), channel_id=1, source_target_pairs={{0,8},{4,12},{8,0},{12,4},{1,9},{5,13},{9,1},{13,5},{2,10},{6,14},... | collective-permute-start | bytes 12296 | tf_op jit(solution)/shard_map/ppermute | solution.py:308
  13.4 18.8 %collective-permute-start.18 = (bf16[1728,128]{1,0:T(8,128)(2,1)S(1)}, bf16[1728,128]{1,0:T(8,128)(2,1)S(1)}, u32[]{:S(2)}, u32[]{:S(2)}) collective-permute-start(bf16[1728,128]{1,0:T(8,128)(2,1)S(1)} %latents.1.refs_16_), channel_id=1, source_target_pairs={{0,2},{1,3},{2,0},{3,1},{4,6},{5,7},{6,4},{7,5},{8,10},{9,11},{10,... | collective-permute-start | bytes 1327112 | tf_op jit(solution)/shard_map/ppermute | solution.py:303
  15.3 5.5 %collective-permute-start.2 = (bf16[48,128]{1,0:T(8,128)(2,1)S(1)}, bf16[48,128]{1,0:T(8,128)(2,1)S(1)}, u32[]{:S(2)}, u32[]{:S(2)}) collective-permute-start(bf16[48,128]{1,0:T(8,128)(2,1)S(1)} %get-tuple-element.41), channel_id=1, source_target_pairs={{0,4},{4,8},{8,12},{12,0},{1,5},{5,9},{9,13},{13,1},{2,6},{6,10},{... | collective-permute-start | bytes 36872 | tf_op jit(solution)/shard_map/ppermute | solution.py:308
  20.8 3.7 %collective-permute-start.3 = (bf16[48,128]{1,0:T(8,128)(2,1)S(1)}, bf16[48,128]{1,0:T(8,128)(2,1)S(1)}, u32[]{:S(2)}, u32[]{:S(2)}) collective-permute-start(bf16[48,128]{1,0:T(8,128)(2,1)S(1)} %get-tuple-element.42), channel_id=1, source_target_pairs={{0,12},{4,0},{8,4},{12,8},{1,13},{5,1},{9,5},{13,9},{2,14},{6,2},{... | collective-permute-start | bytes 36872 | tf_op jit(solution)/shard_map/ppermute | solution.py:308
  24.5 6.4 %collective-permute-start.8 = (bf16[1024,128]{1,0:T(8,128)(2,1)S(1)}, bf16[1024,128]{1,0:T(8,128)(2,1)S(1)}, u32[]{:S(2)}, u32[]{:S(2)}) collective-permute-start(bf16[1024,128]{1,0:T(8,128)(2,1)S(1)} %copy-done.8), channel_id=1, source_target_pairs={{0,2},{1,3},{2,0},{3,1},{4,6},{5,7},{6,4},{7,5},{8,10},{9,11},{10,... | collective-permute-start | bytes 786440 | tf_op jit(solution)/shard_map/ppermute | solution.py:303
  24.8 9.3 %collective-permute-start = (bf16[2,1024,128]{2,1,0:T(8,128)(2,1)S(1)}, bf16[2,1024,128]{2,1,0:T(8,128)(2,1)S(1)}, u32[]{:S(2)}, u32[]{:S(2)}) collective-permute-start(bf16[2,1024,128]{2,1,0:T(8,128)(2,1)S(1)} %copy-done), channel_id=1, source_target_pairs={{0,1},{1,0},{2,3},{3,2},{4,5},{5,4},{6,7},{7,6},{8,9},{9,8},{10,11... | collective-permute-start | bytes 1572872 | tf_op jit(solution)/shard_map/ppermute | solution.py:303
  24.8 7.3 %collective-permute-start.14 = (bf16[768,128]{1,0:T(8,128)(2,1)S(1)}, bf16[768,128]{1,0:T(8,128)(2,1)S(1)}, u32[]{:S(2)}, u32[]{:S(2)}) collective-permute-start(bf16[768,128]{1,0:T(8,128)(2,1)S(1)} %collective-permute-done.13.refs_12_), channel_id=1, source_target_pairs={{0,16},{16,0},{1,17},{17,1},{2,18},{18,2},{3,19},{19,3},{4,20},{20... | collective-permute-start | bytes 589832 | tf_op jit(solution)/shard_map/ppermute | solution.py:424
  30.9 3.0 %collective-permute-start.6 = (bf16[2,128,512]{2,1,0:T(8,128)(2,1)S(1)}, bf16[2,128,512]{2,1,0:T(8,128)(2,1)S(1)}, u32[]{:S(2)}, u32[]{:S(2)}) collective-permute-start(bf16[2,128,512]{2,1,0:T(8,128)(2,1)S(1)} %copy-done.3), channel_id=1, source_target_pairs={{0,1},{1,0},{2,3},{3,2},{4,5},{5,4},{6,7},{7,6},{8,9},{9,8},{10,11... | collective-permute-start | bytes 786440 | tf_op jit(solution)/shard_map/ppermute | solution.py:303
  32.1 11.0 %collective-permute-start.17 = (bf16[1728,128]{1,0:T(8,128)(2,1)S(1)}, bf16[1728,128]{1,0:T(8,128)(2,1)S(1)}, u32[]{:S(2)}, u32[]{:S(2)}) collective-permute-start(bf16[1728,128]{1,0:T(8,128)(2,1)S(1)} %latents.1.refs_16_), channel_id=1, source_target_pairs={{0,1},{1,0},{2,3},{3,2},{4,5},{5,4},{6,7},{7,6},{8,9},{9,8},{10,11... | collective-permute-start | bytes 1327112 | tf_op jit(solution)/shard_map/ppermute | solution.py:303
  32.1 8.7 %collective-permute-start.9 = (bf16[1024,128]{1,0:T(8,128)(2,1)S(1)}, bf16[1024,128]{1,0:T(8,128)(2,1)S(1)}, u32[]{:S(2)}, u32[]{:S(2)}) collective-permute-start(bf16[1024,128]{1,0:T(8,128)(2,1)S(1)} %collective-permute-done.8.refs_8_), channel_id=1, source_target_pairs={{0,16},{16,0},{1,17},{17,1},{2,18},{18,2},{3,19},{19,3},{4,20},{20... | collective-permute-start | bytes 786440 | tf_op jit(solution)/shard_map/ppermute | solution.py:423
  33.9 11.0 %collective-permute-start.19 = (bf16[1728,128]{1,0:T(8,128)(2,1)S(1)}, bf16[1728,128]{1,0:T(8,128)(2,1)S(1)}, u32[]{:S(2)}, u32[]{:S(2)}) collective-permute-start(bf16[1728,128]{1,0:T(8,128)(2,1)S(1)} %collective-permute-done.18.refs_18_), channel_id=1, source_target_pairs={{0,1},{1,0},{2,3},{3,2},{4,5},{5,4},{6,7},{7,6},{8,9},{9,8},{10,11... | collective-permute-start | bytes 1327112 | tf_op jit(solution)/shard_map/ppermute | solution.py:303
  34.1 7.3 %collective-permute-start.15 = (bf16[768,128]{1,0:T(8,128)(2,1)S(1)}, bf16[768,128]{1,0:T(8,128)(2,1)S(1)}, u32[]{:S(2)}, u32[]{:S(2)}) collective-permute-start(bf16[768,128]{1,0:T(8,128)(2,1)S(1)} %collective-permute-done.13.refs_12_), channel_id=1, source_target_pairs={{0,1},{1,0},{2,3},{3,2},{4,5},{5,4},{6,7},{7,6},{8,9},{9,8},{10,11... | collective-permute-start | bytes 589832 | tf_op jit(solution)/shard_map/ppermute | solution.py:303
  36.0 4.9 %collective-permute-start.7 = (bf16[112,128]{1,0:T(8,128)(2,1)S(1)}, bf16[112,128]{1,0:T(8,128)(2,1)S(1)}, u32[]{:S(2)}, u32[]{:S(2)}) collective-permute-start(bf16[112,128]{1,0:T(8,128)(2,1)S(1)} %halo_rows.1.refs_20_), channel_id=1, source_target_pairs={{0,2},{1,3},{2,0},{3,1},{4,6},{5,7},{6,4},{7,5},{8,10},{9,11},{10,... | collective-permute-start | bytes 86024 | tf_op jit(solution)/shard_map/ppermute | solution.py:303
  40.9 4.0 %collective-permute-start.12 = (bf16[1024,128]{1,0:T(8,128)(2,1)S(1)}, bf16[1024,128]{1,0:T(8,128)(2,1)S(1)}, u32[]{:S(2)}, u32[]{:S(2)}) collective-permute-start(bf16[1024,128]{1,0:T(8,128)(2,1)S(1)} %collective-permute-done.9.refs_9_), channel_id=1, source_target_pairs={{0,1},{1,0},{2,3},{3,2},{4,5},{5,4},{6,7},{7,6},{8,9},{9,8},{10,11... | collective-permute-start | bytes 786440 | tf_op jit(solution)/shard_map/ppermute | solution.py:303
  41.4 14.8 %collective-permute-start.26 = (bf16[2048,128]{1,0:T(8,128)(2,1)S(1)}, bf16[2048,128]{1,0:T(8,128)(2,1)S(1)}, u32[]{:S(2)}, u32[]{:S(2)}) collective-permute-start(bf16[2048,128]{1,0:T(8,128)(2,1)S(1)} %get-tuple-element.58), channel_id=1, source_target_pairs={{0,2},{1,3},{2,0},{3,1},{4,6},{5,7},{6,4},{7,5},{8,10},{9,11},{10,... | collective-permute-start | bytes 1572872 | tf_op jit(solution)/shard_map/ppermute | solution.py:303
  44.5 21.3 %collective-permute-start.10 = (bf16[1536,128]{1,0:T(8,128)(2,1)S(1)}, bf16[1536,128]{1,0:T(8,128)(2,1)S(1)}, u32[]{:S(2)}, u32[]{:S(2)}) collective-permute-start(bf16[1536,128]{1,0:T(8,128)(2,1)S(1)} %get-tuple-element.47), channel_id=1, source_target_pairs={{0,2},{1,3},{2,0},{3,1},{4,6},{5,7},{6,4},{7,5},{8,10},{9,11},{10,... | collective-permute-start | bytes 1179656 | tf_op jit(solution)/shard_map/ppermute | solution.py:303
  56.2 9.7 %collective-permute-start.27 = (bf16[2048,128]{1,0:T(8,128)(2,1)S(1)}, bf16[2048,128]{1,0:T(8,128)(2,1)S(1)}, u32[]{:S(2)}, u32[]{:S(2)}) collective-permute-start(bf16[2048,128]{1,0:T(8,128)(2,1)S(1)} %collective-permute-done.26.refs_4_), channel_id=1, source_target_pairs={{0,1},{1,0},{2,3},{3,2},{4,5},{5,4},{6,7},{7,6},{8,9},{9,8},{10,11... | collective-permute-start | bytes 1572872 | tf_op jit(solution)/shard_map/ppermute | solution.py:303
  56.2 8.5 %collective-permute-start.23 = (bf16[48,512]{1,0:T(8,128)(2,1)S(1)}, bf16[48,512]{1,0:T(8,128)(2,1)S(1)}, u32[]{:S(2)}, u32[]{:S(2)}) collective-permute-start(bf16[48,512]{1,0:T(8,128)(2,1)S(1)} %get-tuple-element.53), channel_id=1, source_target_pairs={{0,12},{4,0},{8,4},{12,8},{1,13},{5,1},{9,5},{13,9},{2,14},{6,2},{... | collective-permute-start | bytes 147464 | tf_op jit(solution)/shard_map/ppermute | solution.py:308
  60.0 5.9 %collective-permute-start.22 = (bf16[48,512]{1,0:T(8,128)(2,1)S(1)}, bf16[48,512]{1,0:T(8,128)(2,1)S(1)}, u32[]{:S(2)}, u32[]{:S(2)}) collective-permute-start(bf16[48,512]{1,0:T(8,128)(2,1)S(1)} %get-tuple-element.52), channel_id=1, source_target_pairs={{0,4},{4,8},{8,12},{12,0},{1,5},{5,9},{9,13},{13,1},{2,6},{6,10},{... | collective-permute-start | bytes 147464 | tf_op jit(solution)/shard_map/ppermute | solution.py:308
  60.0 4.6 %collective-permute-start.24 = (bf16[16,512]{1,0:T(8,128)(2,1)S(1)}, bf16[16,512]{1,0:T(8,128)(2,1)S(1)}, u32[]{:S(2)}, u32[]{:S(2)}) collective-permute-start(bf16[16,512]{1,0:T(8,128)(2,1)S(1)} %get-tuple-element.54), channel_id=1, source_target_pairs={{0,8},{4,12},{8,0},{12,4},{1,9},{5,13},{9,1},{13,5},{2,10},{6,14},... | collective-permute-start | bytes 49160 | tf_op jit(solution)/shard_map/ppermute | solution.py:308
  65.9 6.2 %collective-permute-start.25 = (bf16[1536,128]{1,0:T(8,128)(2,1)S(1)}, bf16[1536,128]{1,0:T(8,128)(2,1)S(1)}, u32[]{:S(2)}, u32[]{:S(2)}) collective-permute-start(bf16[1536,128]{1,0:T(8,128)(2,1)S(1)} %collective-permute-done.10.refs_4_), channel_id=1, source_target_pairs={{0,1},{1,0},{2,3},{3,2},{4,5},{5,4},{6,7},{7,6},{8,9},{9,8},{10,11... | collective-permute-start | bytes 1179656 | tf_op jit(solution)/shard_map/ppermute | solution.py:303
  (13 other events, 93.0 us)

commit v11 on v9

--- a/solution.py
+++ b/solution.py
@@ -121,28 +121,10 @@
     return jnp.broadcast_to(row, (8, row.shape[1])).T[:, 0:1]
 
 
-def prepare_kernel(blocks, halo, table_rows, list_ref, ef, es, nf, ns, hot_out, incidence_out, pick_out, late_out, sems):
-    part, features = es.shape[1:]
-    edge_count, lanes_all = hot_out.shape
-    node_count = incidence_out.shape[0]
-    copies = Copies(sems)
-    at = 0
-    for first, second in ((ef, es), (nf, ns)):
-        rows = first.shape[1]
-        copies.start(first.at[1], late_out.at[pl.ds(at, rows)])
-        at += rows
-        for q in range(features // part):
-            copies.start(second.at[1, :, pl.ds(q * part, part)], late_out.at[pl.ds(at, part)])
-            at += part
-    for at in range(0, edge_count, TILE):
-        senders = table_index(list_ref[:, at : at + TILE], blocks, node_count, halo)
-        receivers = list_ref[:, edge_count + at : edge_count + at + TILE]
-        lanes = lax.broadcasted_iota(jnp.int32, (TILE, lanes_all), 1)
-        hit = (lanes == column(senders)) | (lanes == column(receivers) + table_rows)
-        hot_out[at : at + TILE, :] = one_hot(hit)
-        node_ids = lax.broadcasted_iota(jnp.int32, (node_count, TILE), 0)
-        incidence_out[:, at : at + TILE] = one_hot(node_ids == receivers)
-    wanted = column(list_ref[:, 2 * edge_count : 2 * edge_count + 2 * halo])
+def make_pick(boundary, pick_out):
+    halo = boundary.shape[1] // 2
+    node_count = pick_out.shape[1]
+    wanted = column(boundary)
     lanes = lax.broadcasted_iota(jnp.int32, (halo, node_count), 1)
     number = lax.broadcasted_iota(jnp.int32, (COARSE_PAD, node_count), 0)
     ids = lax.broadcasted_iota(jnp.int32, (COARSE_PAD, node_count), 1)
@@ -152,6 +134,36 @@
     pick_out[wide : wide + halo, :] = one_hot(lanes == wanted[:halo])
     for at in (halo, wide + halo, 2 * wide):
         pick_out[at : at + COARSE_PAD, :] = coarse
+
+
+def prepare_kernel(blocks, halo, table_rows, list_ref, ef, es, nf, ns, hot_out, incidence_out, pick_out, pack_0, pack_1, edge_late, node_late, sems):
+    part, features = es.shape[1:]
+    edge_count, lanes_all = hot_out.shape
+    node_count = incidence_out.shape[0]
+    copies = Copies(sems)
+
+    def pack(first, second, layer, out, at):
+        rows = first.shape[1]
+        copies.start(first.at[layer], out.at[pl.ds(at, rows)])
+        at += rows
+        for q in range(features // part):
+            copies.start(second.at[layer, :, pl.ds(q * part, part)], out.at[pl.ds(at, part)])
+            at += part
+        return at
+
+    for layer, out in ((0, pack_0), (1, pack_1)):
+        pack(nf, ns, layer, out, pack(ef, es, layer, out, 0))
+    pack(ef, es, 1, edge_late, 0)
+    pack(nf, ns, 1, node_late, 0)
+    for at in range(0, edge_count, TILE):
+        senders = table_index(list_ref[:, at : at + TILE], blocks, node_count, halo)
+        receivers = list_ref[:, edge_count + at : edge_count + at + TILE]
+        lanes = lax.broadcasted_iota(jnp.int32, (TILE, lanes_all), 1)
+        hit = (lanes == column(senders)) | (lanes == column(receivers) + table_rows)
+        hot_out[at : at + TILE, :] = one_hot(hit)
+        node_ids = lax.broadcasted_iota(jnp.int32, (node_count, TILE), 0)
+        incidence_out[:, at : at + TILE] = one_hot(node_ids == receivers)
+    make_pick(list_ref[:, 2 * edge_count : 2 * edge_count + 2 * halo], pick_out)
     copies.wait()
 
 
@@ -163,7 +175,8 @@
         start += out.shape[0]
 
 
-def start_kernel(node_ref, pick_ref, right, left, coarse):
+def start_kernel(node_ref, boundary_ref, right, left, coarse, pick_ref):
+    make_pick(boundary_ref[...], pick_ref)
     pick_rows(pick_ref, node_ref[...].astype(BF16), (right, left, coarse))
 
 
@@ -212,8 +225,7 @@
 
 def first_kernel(*refs):
     refs = list(refs)
-    own_w = [refs.pop(0) for _ in range(4)]
-    core_w = [refs.pop(0) for _ in range(4)]
+    packs = [refs.pop(0) for _ in range(2)]
     halves = [[refs.pop(0) for _ in range(2)] for _ in range(2)]
     shards = [refs.pop(0) for _ in range(4)]
     edge_own, node_own, hot_ref, incidence_ref, pick_ref = [refs.pop(0) for _ in range(5)]
@@ -229,12 +241,12 @@
         edge_copies.start(shard, x_ref.at[:, pl.ds(column, part)])
     y = lax.axis_index("groups")
     starts = [0, 0]
-    for base, copies, (first, second), at in (
-        (0, edge_copies, (edge_w, edge_w2), 0),
-        (1, node_copies, (node_w, node_w2), 2),
+    for base, copies, (first, second) in (
+        (0, edge_copies, (edge_w, edge_w2)),
+        (1, node_copies, (node_w, node_w2)),
     ):
-        load_shard(copies, 0, own_w[at], own_w[at + 1], 0, first, second)
-        load_shard(copies, 0, core_w[at], core_w[at + 1], 1, first, second)
+        for j, pack in enumerate(packs):
+            load_packed(copies, pack, (0, edge_w.shape[0] + edge_w2.shape[1])[base], j, first, second)
         for j, pair in enumerate(halves):
             for k, piece in enumerate(pair):
                 half = y if k == 0 else 1 - y
@@ -252,38 +264,37 @@
     pick_rows(pick_ref, node_new, sends)
 
 
-def late_kernel(pieces, *refs):
+def late_weights(weights, base, first, second):
+    moves = Moves()
+    load_packed(moves, weights[0], base, 0, first, second)
+    load_packed(moves, weights[1], base, 1, first, second)
+    load_packed(moves, weights[2], 0, 2, first, second)
+    load_packed(moves, weights[3], 0, 3, first, second)
+
+
+def late_edge_kernel(pieces, *refs):
     refs = list(refs)
-    own_w = [refs.pop(0) for _ in range(4)]
-    core_w = [refs.pop(0) for _ in range(4)]
-    packed = [refs.pop(0) for _ in range(2)]
-    edge_ref, edge_own, node_own = [refs.pop(0) for _ in range(3)]
+    weights = [refs.pop(0) for _ in range(4)]
+    edge_ref, edge_own = [refs.pop(0) for _ in range(2)]
     tables = [refs.pop(0) for _ in range(pieces)]
-    hot_ref, incidence_ref, edge_out, node_out = [refs.pop(0) for _ in range(4)]
-    edge_w, edge_w2, node_w, node_w2, product_ref, table_ref = refs
-    edge_copies, node_copies = Moves(), Moves()
-    base = 0
-    for copies, first, second, at in (
-        (edge_copies, edge_w, edge_w2, 0),
-        (node_copies, node_w, node_w2, 2),
-    ):
-        load_shard(copies, 1, own_w[at], own_w[at + 1], 0, first, second)
-        load_shard(copies, 1, core_w[at], core_w[at + 1], 1, first, second)
-        for j, pack in enumerate(packed):
-            load_packed(copies, pack, base, 2 + j, first, second)
-        base = edge_w.shape[0] + edge_w2.shape[1]
+    hot_ref, incidence_ref, edge_out, incoming_out = [refs.pop(0) for _ in range(4)]
+    edge_w, edge_w2, product_ref, table_ref = refs
+    late_weights(weights, 0, edge_w, edge_w2)
     start = 0
     for table in tables:
         table_ref[start : start + table.shape[0], :] = table[...]
         start += table.shape[0]
-    edge_copies.wait()
-    nodes = tables[0][...]
-    incoming = edge_rows(
-        edge_ref, table_ref[...], nodes, edge_own, hot_ref, incidence_ref,
+    incoming_out[...] = edge_rows(
+        edge_ref, table_ref[...], tables[0][...], edge_own, hot_ref, incidence_ref,
         edge_w, edge_w2, product_ref, edge_out, None,
     )
-    node_copies.wait()
-    node_rows(nodes, incoming, node_own, node_w, node_w2, node_out)
+
+
+def late_node_kernel(base, *refs):
+    weights = refs[:4]
+    node_ref, node_own, incoming_ref, node_out, node_w, node_w2 = refs[4:]
+    late_weights(weights, base, node_w, node_w2)
+    node_rows(node_ref[...], incoming_ref[...], node_own, node_w, node_w2, node_out)
 
 
 SMEM, VMEM, ANY = pltpu.SMEM, pltpu.VMEM, pl.ANY
@@ -372,6 +383,7 @@
     weights = (edge_first, edge_second, node_first, node_second)
     edge_pack = edge_first.shape[1] + features
     node_pack = node_first.shape[1] + features
+    late_pack = edge_pack + node_pack
     (ride,) = call(
         ride_kernel,
         [shape(((edge_pack + node_pack) // 2, part), BF16)],
@@ -385,43 +397,51 @@
     far_rows = 2 * wide + COARSE_PAD if blocks == 4 else 2 * halo + blocks * COARSE_PAD
     table_rows = node_count + far_rows
     lanes = -(-(table_rows + node_count) // 128) * 128
+    right, left, coarse = call(
+        start_kernel,
+        sent(part),
+        [(VMEM, after(node_state, ride)), (VMEM, boundary_rows[None, :])],
+        [pltpu.VMEM((2 * wide + COARSE_PAD, node_count), BF16)],
+        0,
+        "boundary_rows",
+    )
+    rows = neighbour_rows(right, left, coarse, halo)
     lists = jnp.concatenate([senders, receivers, boundary_rows])[None, :]
-    hot, incidence, pick, late_w = call(
+    hot, incidence, pick, pack_0, pack_1, edge_late, node_late = call(
         functools.partial(prepare_kernel, blocks, halo, table_rows),
         [
             shape((edge_count, lanes), BF16),
             shape((node_count, edge_count), BF16),
             shape((2 * wide + COARSE_PAD, node_count), BF16),
-            shape((edge_pack + node_pack, part), BF16),
+            shape((late_pack, part), BF16),
+            shape((late_pack, part), BF16),
+            shape((edge_pack, part), BF16),
+            shape((node_pack, part), BF16),
         ],
-        [(VMEM, after(lists, ride))] + [(ANY, w) for w in weights],
-        [dma((10,))],
+        [(VMEM, after(lists, *rows))] + [(ANY, w) for w in weights],
+        [dma((32,))],
         0,
         "one_hot",
     )
-    core_w = [swap(after(w, ride), 1) for w in weights]
-    right, left, coarse = call(
-        start_kernel,
-        sent(part),
-        [(VMEM, node_state), (VMEM, pick)],
-        [],
-        2 * pick.size * part,
-        "boundary_rows",
-    )
-    rows = neighbour_rows(right, left, coarse, halo)
+    core_0 = swap(pack_0, 1)
     (latents,) = call(
         latent_kernel,
         [shape((edge_count + table_rows, part), BF16)],
-        [(VMEM, after(edge_state, late_w)), (VMEM, node_state)] + [(VMEM, r) for r in rows],
+        [(VMEM, after(edge_state, pack_0)), (VMEM, node_state)] + [(VMEM, r) for r in rows],
         [],
         0,
         "latents",
     )
-    far_latents = swap(after(latents, near, *core_w), 2)
+    near = after(near, latents)
+    far_latents = swap(latents, 2)
     far = lax.ppermute(near, "groups", [(0, 1), (1, 0)])
-    shards = [latents, swap(latents, 1), far_latents, swap(after(far_latents, far), 1)]
-    pairs = [near, far, swap(near, 1), swap(far, 1)]
-    late_x = swap(after(late_w, far_latents, far), 2)
+    core_near, core_latents = swap(near, 1), swap(latents, 1)
+    core_1 = swap(after(pack_1, far), 1)
+    core_far = swap(after(far, core_latents, core_near), 1)
+    edge_late_x = swap(after(edge_late, core_near), 2)
+    node_late_x = swap(after(node_late, far_latents), 2)
+    shards = [latents, core_latents, far_latents, swap(after(far_latents, far), 1)]
+    pairs = [near, far, core_near, core_far]
 
     edge_flops = 2 * edge_count * features * (2 * features + lanes + node_count)
     node_flops = 2 * node_count * features * 3 * features
@@ -436,7 +456,7 @@
     edge_own, edge_full, node_own, node_full, right, left, coarse = call(
         first_kernel,
         [own_edge, full_edge, own_node, full_node] + sent(features),
-        [(VMEM, w) for w in list(weights) + core_w + pairs + shards]
+        [(VMEM, w) for w in [pack_0, core_0] + pairs + shards]
         + [(VMEM, a) for a in (edge_state, node_state, hot, incidence, pick)],
         [
             edge_shape,
@@ -451,24 +471,33 @@
         16,
     )
     tables = [node_full] + neighbour_rows(right, left, coarse, halo)
-    late_d = swap(after(late_x, *tables[1:]), 1)
-    edge_own, node_own = call(
-        functools.partial(late_kernel, len(tables)),
-        [own_edge, own_node],
-        [(VMEM, w) for w in list(weights) + core_w + [late_x, late_d]]
-        + [(VMEM, a) for a in (edge_full, edge_own, node_own)]
+    edge_late_d = swap(after(edge_late_x, right, core_1), 1)
+    edge_own, incoming = call(
+        functools.partial(late_edge_kernel, len(tables)),
+        [own_edge, full_node],
+        [(VMEM, w) for w in (pack_1, core_1, edge_late_x, edge_late_d)]
+        + [(VMEM, a) for a in (edge_full, edge_own)]
         + [(VMEM, t) for t in tables]
         + [(VMEM, hot), (VMEM, incidence)],
         [
             edge_shape,
             second_shape,
-            node_shape,
-            second_shape,
             pltpu.VMEM((lanes, hidden), BF16),
             pltpu.VMEM((table_rows, features), BF16),
         ],
-        edge_flops + node_flops,
-        "layer_1",
+        edge_flops,
+        "layer_1_edges",
+        16,
+    )
+    node_late_d = swap(after(node_late_x, *tables[1:]), 1)
+    (node_own,) = call(
+        functools.partial(late_node_kernel, edge_pack),
+        [own_node],
+        [(VMEM, w) for w in (pack_1, core_1, node_late_x, node_late_d)]
+        + [(VMEM, a) for a in (node_full, node_own, incoming)],
+        [node_shape, second_shape],
+        node_flops,
+        "layer_1_nodes",
         16,
     )
     return (node_own, edge_own)

time: 62.9 us -> 61.3 us (0.975)
  starting transfers between devices: 20.7 us -> 18.3 us
  Pallas kernels: 17.3 us -> 19.1 us
  waiting for transfers between devices: 23.9 us -> 22.8 us
    ppermute x6, starting transfers between devices: 12.5 us -> 9.28 us  [shift(): return lax.ppermute(x, 'graph', [(i, (i + by) % size) for i in range(size)])]
    ppermute x12, waiting for transfers between devices: 7.12 us -> 10.2 us  [swap(): return lax.ppermute(x, 'mp', [(i, i ^ mask) for i in range(size)])]
    ppermute x1, waiting for transfers between devices: 10.8 us -> 7.93 us  [on_device(): far = lax.ppermute(near, 'groups', [(0, 1), (1, 0)])]
    pallas_call x6 -> x7, Pallas kernels: 17.3 us -> 19.1 us  [call(): pl.pallas_call(kernel, out_shape=out_shape, in_specs=[pl.BlockSpec(memory...]
    ppermute x6, waiting for transfers between devices: 6.06 us -> 4.63 us  [shift(): return lax.ppermute(x, 'graph', [(i, (i + by) % size) for i in range(size)])]
    ppermute x12, starting transfers between devices: 6.63 us -> 7.42 us  [swap(): return lax.ppermute(x, 'mp', [(i, i ^ mask) for i in range(size)])]
  transfers between devices with their start and end apart: 19 -> 19, of which waited for: 11 -> 6; matrix products, arithmetic and copies ran while one was open for 0% -> 0% of each run, Pallas kernels for 14% -> 26%
where the time goes in v11:
time: 61.3 us; the launch traced here: 61.1 us
  waiting for transfers between devices  22.8 us (37%)
  Pallas kernels  19.1 us (31%)
  starting transfers between devices  18.3 us (30%)
  between operations  0.83 us (1%)
    pallas_call x7, Pallas kernels, call(): pl.pallas_call(kernel, out_shape=out_shape, in_specs=[pl.BlockSpec(memory...  19.1 us
    ppermute x12, waiting for transfers between devices, swap(): return lax.ppermute(x, 'mp', [(i, i ^ mask) for i in range(size)])  10.2 us
    ppermute x6, starting transfers between devices, shift(): return lax.ppermute(x, 'graph', [(i, (i + by) % size) for i in range(size)])  9.28 us
    ppermute x1, waiting for transfers between devices, on_device(): far = lax.ppermute(near, 'groups', [(0, 1), (1, 0)])  7.93 us
    ppermute x12, starting transfers between devices, swap(): return lax.ppermute(x, 'mp', [(i, i ^ mask) for i in range(size)])  7.42 us
    ppermute x6, waiting for transfers between devices, shift(): return lax.ppermute(x, 'graph', [(i, (i + by) % size) for i in range(size)])  4.63 us
    ppermute x1, starting transfers between devices, on_device(): far = lax.ppermute(near, 'groups', [(0, 1), (1, 0)])  1.58 us
  transfers between devices with their start and end apart: 19, of which 6 were waited for; matrix products, arithmetic and copies ran while one was open for 0% of the time, Pallas kernels for 26%

profile of v11, /device:TPU:0, one launch (start us, length us, event | category | flops | bytes accessed | tf_op | source)
XLA Modules:
  0.0 61.1 jit_solution(16769664939281529163)
XLA Ops:
  0.7 2.0 %layer_0_half.1 = bf16[1792,128]{1,0:T(8,128)(2,1)} custom-call(bf16[2,1536,128]{2,1,0:T(8,128)(2,1)} %ef.3, bf16[2,128,512]{2,1,0:T(8,128)(2,1)} %es.3, bf16[2,1024,128]{2,1,0:T(8,128)(2,1)} %nf.3, bf16[2,128,512]{2,1,0:T(8,128)(2,1)} %ns.3), custom_call_target="tpu_custom_call" | custom-call | bytes 2293760 | tf_op jit(solution)/shard_map/layer_0_half/pallas_call | solution.py:306
  2.7 3.0 %collective-permute-start.3 = (bf16[1792,128]{1,0:T(8,128)(2,1)}, bf16[1792,128]{1,0:T(8,128)(2,1)S(1)}, u32[]{:S(2)}, u32[]{:S(2)}) collective-permute-start(bf16[1792,128]{1,0:T(8,128)(2,1)} %layer_0_half.1), channel_id=1, source_target_pairs={{0,2},{1,3},{2,0},{3,1},{4,6},{5,7},{6,4},{7,5},{8,10},{9,11},{10,... | collective-permute-start | bytes 1376264 | tf_op jit(solution)/shard_map/ppermute | solution.py:320
  6.0 1.6 %collective-permute-start = (bf16[48,128]{1,0:T(8,128)(2,1)S(1)}, bf16[48,128]{1,0:T(8,128)(2,1)S(1)}, u32[]{:S(2)}, u32[]{:S(2)}) collective-permute-start(bf16[48,128]{1,0:T(8,128)(2,1)S(1)} %get-tuple-element.33), channel_id=1, source_target_pairs={{0,4},{4,8},{8,12},{12,0},{1,5},{5,9},{9,13},{13,1},{2,6},{6,10},{... | collective-permute-start | bytes 36872 | tf_op jit(solution)/shard_map/ppermute | solution.py:325
  7.7 2.2 %collective-permute-start.1 = (bf16[48,128]{1,0:T(8,128)(2,1)S(1)}, bf16[48,128]{1,0:T(8,128)(2,1)S(1)}, u32[]{:S(2)}, u32[]{:S(2)}) collective-permute-start(bf16[48,128]{1,0:T(8,128)(2,1)S(1)} %get-tuple-element.34), channel_id=1, source_target_pairs={{0,12},{4,0},{8,4},{12,8},{1,13},{5,1},{9,5},{13,9},{2,14},{6,2},{... | collective-permute-start | bytes 36872 | tf_op jit(solution)/shard_map/ppermute | solution.py:325
  9.9 0.8 %collective-permute-start.2 = (bf16[16,128]{1,0:T(8,128)(2,1)S(1)}, bf16[16,128]{1,0:T(8,128)(2,1)S(1)}, u32[]{:S(2)}, u32[]{:S(2)}) collective-permute-start(bf16[16,128]{1,0:T(8,128)(2,1)S(1)} %get-tuple-element.35), channel_id=1, source_target_pairs={{0,8},{4,12},{8,0},{12,4},{1,9},{5,13},{9,1},{13,5},{2,10},{6,14},... | collective-permute-start | bytes 12296 | tf_op jit(solution)/shard_map/ppermute | solution.py:325
  10.7 3.7 %collective-permute-done.2.refs_4_ = bf16[16,128]{1,0:T(8,128)(2,1)S(1)} collective-permute-done((bf16[16,128]{1,0:T(8,128)(2,1)S(1)}, bf16[16,128]{1,0:T(8,128)(2,1)S(1)}, u32[]{:S(2)}, u32[]{:S(2)}) %collective-permute-start.2) | collective-permute-done | bytes 4128 | tf_op jit(solution)/shard_map/ppermute | solution.py:325
  14.5 2.2 %one_hot.1 = (bf16[1536,512]{1,0:T(8,128)(2,1)S(1)}, bf16[192,1536]{1,0:T(8,128)(2,1)S(1)}, bf16[112,192]{1,0:T(8,128)(2,1)S(1)}, bf16[3584,128]{1,0:T(8,128)(2,...) custom-call(s32[1,3136]{1,0:T(1,128)S(1)} %broadcast_in_dim.6.list_ref, ...), custom_call_target="tpu_custom_call" | custom-call | bytes 6805760 | tf_op jit(solution)/shard_map/one_hot/pallas_call | solution.py:306
  16.8 1.6 %collective-permute-start.4 = (bf16[1792,128]{1,0:T(8,128)(2,1)S(1)}, bf16[1792,128]{1,0:T(8,128)(2,1)S(1)}, u32[]{:S(2)}, u32[]{:S(2)}) collective-permute-start(bf16[1792,128]{1,0:T(8,128)(2,1)S(1)} %collective-permute-done.3.refs_2_), channel_id=1, source_target_pairs={{0,16},{16,0},{1,17},{17,1},{2,18},{18,2},{3,19},{19,3},{4,20},{20... | collective-permute-start | bytes 1376264 | tf_op jit(solution)/shard_map/ppermute | solution.py:437
  18.4 1.4 %collective-permute-start.6 = (bf16[1840,128]{1,0:T(8,128)(2,1)S(1)}, bf16[1840,128]{1,0:T(8,128)(2,1)S(1)}, u32[]{:S(2)}, u32[]{:S(2)}) collective-permute-start(bf16[1840,128]{1,0:T(8,128)(2,1)S(1)} %latents.1.refs_6_), channel_id=1, source_target_pairs={{0,2},{1,3},{2,0},{3,1},{4,6},{5,7},{6,4},{7,5},{8,10},{9,11},{10,... | collective-permute-start | bytes 1413128 | tf_op jit(solution)/shard_map/ppermute | solution.py:320
  19.7 0.5 collective-permute-start.9
  20.3 7.9 %collective-permute-done.4.refs_3_ = bf16[1792,128]{1,0:T(8,128)(2,1)S(1)} collective-permute-done((bf16[1792,128]{1,0:T(8,128)(2,1)S(1)}, bf16[1792,128]{1,0:T(8,128)(2,1)S(1)}, u32[]{:S(2)}, u32[]{:S(2)}) %collective-permute-start.4) | collective-permute-done | bytes 458784 | tf_op jit(solution)/shard_map/ppermute | solution.py:437
  28.2 1.4 %collective-permute-done.6.refs_8_ = bf16[1840,128]{1,0:T(8,128)(2,1)S(1)} collective-permute-done((bf16[1840,128]{1,0:T(8,128)(2,1)S(1)}, bf16[1840,128]{1,0:T(8,128)(2,1)S(1)}, u32[]{:S(2)}, u32[]{:S(2)}) %collective-permute-start.6) | collective-permute-done | bytes 471072 | tf_op jit(solution)/shard_map/ppermute | solution.py:320
  29.6 0.5 collective-permute-start.11
  30.1 1.5 %collective-permute-start.17 = (bf16[2048,128]{1,0:T(8,128)(2,1)S(1)}, bf16[2048,128]{1,0:T(8,128)(2,1)S(1)}, u32[]{:S(2)}, u32[]{:S(2)}) collective-permute-start(bf16[2048,128]{1,0:T(8,128)(2,1)S(1)} %get-tuple-element.56), channel_id=1, source_target_pairs={{0,2},{1,3},{2,0},{3,1},{4,6},{5,7},{6,4},{7,5},{8,10},{9,11},{10,... | collective-permute-start | bytes 1572872 | tf_op jit(solution)/shard_map/ppermute | solution.py:320
  31.6 0.5 collective-permute-start.7
  32.2 6.9 %layer_0.1 = (f32[1536,128]{1,0:T(8,128)S(1)}, bf16[1536,512]{1,0:T(8,128)(2,1)S(1)}, f32[192,128]{1,0:T(8,128)S(1)}, bf16[192,512]{1,0:T(8,128)(2,1)S(1)}, bf16...) custom-call(bf16[3584,128]{1,0:T(8,128)(2,1)S(1)} %get-tuple-element.38.refs_0_, ...), custom_call_target="tpu_custom_call" | custom-call | flops 3019898880 | bytes 11413504 | tf_op jit(solution)/shard_map/layer_0/pallas_call | solution.py:306
  39.1 5.8 %collective-permute-done.17.refs_2_ = bf16[2048,128]{1,0:T(8,128)(2,1)S(1)} collective-permute-done((bf16[2048,128]{1,0:T(8,128)(2,1)S(1)}, bf16[2048,128]{1,0:T(8,128)(2,1)S(1)}, u32[]{:S(2)}, u32[]{:S(2)}) %collective-permute-start.17) | collective-permute-done | bytes 524320 | tf_op jit(solution)/shard_map/ppermute | solution.py:320
  44.9 1.6 %collective-permute-start.13 = (bf16[48,512]{1,0:T(8,128)(2,1)S(1)}, bf16[48,512]{1,0:T(8,128)(2,1)S(1)}, u32[]{:S(2)}, u32[]{:S(2)}) collective-permute-start(bf16[48,512]{1,0:T(8,128)(2,1)S(1)} %get-tuple-element.49), channel_id=1, source_target_pairs={{0,4},{4,8},{8,12},{12,0},{1,5},{5,9},{9,13},{13,1},{2,6},{6,10},{... | collective-permute-start | bytes 147464 | tf_op jit(solution)/shard_map/ppermute | solution.py:325
  46.5 2.3 %collective-permute-start.14 = (bf16[48,512]{1,0:T(8,128)(2,1)S(1)}, bf16[48,512]{1,0:T(8,128)(2,1)S(1)}, u32[]{:S(2)}, u32[]{:S(2)}) collective-permute-start(bf16[48,512]{1,0:T(8,128)(2,1)S(1)} %get-tuple-element.50), channel_id=1, source_target_pairs={{0,12},{4,0},{8,4},{12,8},{1,13},{5,1},{9,5},{13,9},{2,14},{6,2},{... | collective-permute-start | bytes 147464 | tf_op jit(solution)/shard_map/ppermute | solution.py:325
  48.8 0.8 %collective-permute-start.15 = (bf16[16,512]{1,0:T(8,128)(2,1)S(1)}, bf16[16,512]{1,0:T(8,128)(2,1)S(1)}, u32[]{:S(2)}, u32[]{:S(2)}) collective-permute-start(bf16[16,512]{1,0:T(8,128)(2,1)S(1)} %get-tuple-element.51), channel_id=1, source_target_pairs={{0,8},{4,12},{8,0},{12,4},{1,9},{5,13},{9,1},{13,5},{2,10},{6,14},... | collective-permute-start | bytes 49160 | tf_op jit(solution)/shard_map/ppermute | solution.py:325
  49.5 2.9 %collective-permute-done.7.refs_2_ = bf16[1536,128]{1,0:T(8,128)(2,1)S(1)} collective-permute-done((bf16[1536,128]{1,0:T(8,128)(2,1)S(1)}, bf16[1536,128]{1,0:T(8,128)(2,1)S(1)}, u32[]{:S(2)}, u32[]{:S(2)}) %collective-permute-start.7) | collective-permute-done | bytes 393248 | tf_op jit(solution)/shard_map/ppermute | solution.py:320
  52.5 0.9 %collective-permute-done.15.refs_9_ = bf16[16,512]{1,0:T(8,128)(2,1)S(1)} collective-permute-done((bf16[16,512]{1,0:T(8,128)(2,1)S(1)}, bf16[16,512]{1,0:T(8,128)(2,1)S(1)}, u32[]{:S(2)}, u32[]{:S(2)}) %collective-permute-start.15) | collective-permute-done | bytes 16416 | tf_op jit(solution)/shard_map/ppermute | solution.py:325
  53.4 6.2 %layer_1_edges.1 = (f32[1536,128]{1,0:T(8,128)}, bf16[192,512]{1,0:T(8,128)(2,1)S(1)}) custom-call(bf16[3584,128]{1,0:T(8,128)(2,1)S(1)} %get-tuple-element.41.refs_0_, bf16[3584,128]{1,0:T(8,128)(2,1)S(1)} %collective-permute-done.5.refs_1_, bf16[2048,128]{1,0:T(8,128)(2,1)S(1)} %collective-permute-done.17.refs_2_, ...), custom_call_target="tpu_custom_call" | custom-call | flops 2717908992 | bytes 8699904 | tf_op jit(solution)/shard_map/layer_1_edges/pallas_call | solution.py:306
  59.6 1.5 %layer_1_nodes.1 = f32[192,128]{1,0:T(8,128)} custom-call(bf16[3584,128]{1,0:T(8,128)(2,1)S(1)} %get-tuple-element.41.refs_0_, bf16[3584,128]{1,0:T(8,128)(2,1)S(1)} %collective-permute-done.5.refs_1_, bf16[1536,128]{1,0:T(8,128)(2,1)S(1)} %collective-permute-done.7.refs_2_, bf16[1536,128]{1,0:T(8,128)(2,1)S(1)} %collective-permute-done.16.refs_3_, ...), custom_call_target="tpu_custom_call" | custom-call | flops 301989888 | bytes 3211264 | tf_op jit(solution)/shard_map/layer_1_nodes/pallas_call | solution.py:306
  (41 shorter events, 0.4 us)
Async XLA Ops:
  0.6 13.8 %copy-start = (bf16[2,1536,128]{2,1,0:T(8,128)(2,1)S(1)}, bf16[2,1536,128]{2,1,0:T(8,128)(2,1)}, u32[]{:S(2)}) copy-start(bf16[2,1536,128]{2,1,0:T(8,128)(2,1)} %ef.3) | copy-start | bytes 2359300
  0.6 13.8 %copy-start.2 = (bf16[2,128,512]{2,1,0:T(8,128)(2,1)S(1)}, bf16[2,128,512]{2,1,0:T(8,128)(2,1)}, u32[]{:S(2)}) copy-start(bf16[2,128,512]{2,1,0:T(8,128)(2,1)} %es.3) | copy-start | bytes 786436
  0.7 13.8 %copy-start.1 = (bf16[2,1024,128]{2,1,0:T(8,128)(2,1)S(1)}, bf16[2,1024,128]{2,1,0:T(8,128)(2,1)}, u32[]{:S(2)}) copy-start(bf16[2,1024,128]{2,1,0:T(8,128)(2,1)} %nf.3) | copy-start | bytes 1572868
  0.7 13.8 %copy-start.3 = (bf16[2,128,512]{2,1,0:T(8,128)(2,1)S(1)}, bf16[2,128,512]{2,1,0:T(8,128)(2,1)}, u32[]{:S(2)}) copy-start(bf16[2,128,512]{2,1,0:T(8,128)(2,1)} %ns.3) | copy-start | bytes 786436
  2.7 14.0 %copy-start.4 = (f32[1536,128]{1,0:T(8,128)S(1)}, f32[1536,128]{1,0:T(8,128)}, u32[]{:S(2)}) copy-start(f32[1536,128]{1,0:T(8,128)} %refs_10_.1) | copy-start | bytes 2359300
  2.7 14.0 %collective-permute-start.3 = (bf16[1792,128]{1,0:T(8,128)(2,1)}, bf16[1792,128]{1,0:T(8,128)(2,1)S(1)}, u32[]{:S(2)}, u32[]{:S(2)}) collective-permute-start(bf16[1792,128]{1,0:T(8,128)(2,1)} %layer_0_half.1), channel_id=1, source_target_pairs={{0,2},{1,3},{2,0},{3,1},{4,6},{5,7},{6,4},{7,5},{8,10},{9,11},{10,... | collective-permute-start | bytes 1376264 | tf_op jit(solution)/shard_map/ppermute | solution.py:320
  6.0 8.4 %collective-permute-start = (bf16[48,128]{1,0:T(8,128)(2,1)S(1)}, bf16[48,128]{1,0:T(8,128)(2,1)S(1)}, u32[]{:S(2)}, u32[]{:S(2)}) collective-permute-start(bf16[48,128]{1,0:T(8,128)(2,1)S(1)} %get-tuple-element.33), channel_id=1, source_target_pairs={{0,4},{4,8},{8,12},{12,0},{1,5},{5,9},{9,13},{13,1},{2,6},{6,10},{... | collective-permute-start | bytes 36872 | tf_op jit(solution)/shard_map/ppermute | solution.py:325
  7.7 6.8 %collective-permute-start.1 = (bf16[48,128]{1,0:T(8,128)(2,1)S(1)}, bf16[48,128]{1,0:T(8,128)(2,1)S(1)}, u32[]{:S(2)}, u32[]{:S(2)}) collective-permute-start(bf16[48,128]{1,0:T(8,128)(2,1)S(1)} %get-tuple-element.34), channel_id=1, source_target_pairs={{0,12},{4,0},{8,4},{12,8},{1,13},{5,1},{9,5},{13,9},{2,14},{6,2},{... | collective-permute-start | bytes 36872 | tf_op jit(solution)/shard_map/ppermute | solution.py:325
  9.9 4.5 %collective-permute-start.2 = (bf16[16,128]{1,0:T(8,128)(2,1)S(1)}, bf16[16,128]{1,0:T(8,128)(2,1)S(1)}, u32[]{:S(2)}, u32[]{:S(2)}) collective-permute-start(bf16[16,128]{1,0:T(8,128)(2,1)S(1)} %get-tuple-element.35), channel_id=1, source_target_pairs={{0,8},{4,12},{8,0},{12,4},{1,9},{5,13},{9,1},{13,5},{2,10},{6,14},... | collective-permute-start | bytes 12296 | tf_op jit(solution)/shard_map/ppermute | solution.py:325
  16.8 11.4 %collective-permute-start.4 = (bf16[1792,128]{1,0:T(8,128)(2,1)S(1)}, bf16[1792,128]{1,0:T(8,128)(2,1)S(1)}, u32[]{:S(2)}, u32[]{:S(2)}) collective-permute-start(bf16[1792,128]{1,0:T(8,128)(2,1)S(1)} %collective-permute-done.3.refs_2_), channel_id=1, source_target_pairs={{0,16},{16,0},{1,17},{17,1},{2,18},{18,2},{3,19},{19,3},{4,20},{20... | collective-permute-start | bytes 1376264 | tf_op jit(solution)/shard_map/ppermute | solution.py:437
  18.4 11.2 %collective-permute-start.6 = (bf16[1840,128]{1,0:T(8,128)(2,1)S(1)}, bf16[1840,128]{1,0:T(8,128)(2,1)S(1)}, u32[]{:S(2)}, u32[]{:S(2)}) collective-permute-start(bf16[1840,128]{1,0:T(8,128)(2,1)S(1)} %latents.1.refs_6_), channel_id=1, source_target_pairs={{0,2},{1,3},{2,0},{3,1},{4,6},{5,7},{6,4},{7,5},{8,10},{9,11},{10,... | collective-permute-start | bytes 1413128 | tf_op jit(solution)/shard_map/ppermute | solution.py:320
  19.7 9.9 %collective-permute-start.10 = (bf16[1840,128]{1,0:T(8,128)(2,1)S(1)}, bf16[1840,128]{1,0:T(8,128)(2,1)S(1)}, u32[]{:S(2)}, u32[]{:S(2)}) collective-permute-start(bf16[1840,128]{1,0:T(8,128)(2,1)S(1)} %latents.1.refs_6_), channel_id=1, source_target_pairs={{0,1},{1,0},{2,3},{3,2},{4,5},{5,4},{6,7},{7,6},{8,9},{9,8},{10,11... | collective-permute-start | bytes 1413128 | tf_op jit(solution)/shard_map/ppermute | solution.py:320
  19.7 9.9 %collective-permute-start.9 = (bf16[1792,128]{1,0:T(8,128)(2,1)S(1)}, bf16[1792,128]{1,0:T(8,128)(2,1)S(1)}, u32[]{:S(2)}, u32[]{:S(2)}) collective-permute-start(bf16[1792,128]{1,0:T(8,128)(2,1)S(1)} %collective-permute-done.3.refs_2_), channel_id=1, source_target_pairs={{0,1},{1,0},{2,3},{3,2},{4,5},{5,4},{6,7},{7,6},{8,9},{9,8},{10,11... | collective-permute-start | bytes 1376264 | tf_op jit(solution)/shard_map/ppermute | solution.py:320
  20.3 11.4 %collective-permute-start.8 = (bf16[3584,128]{1,0:T(8,128)(2,1)S(1)}, bf16[3584,128]{1,0:T(8,128)(2,1)S(1)}, u32[]{:S(2)}, u32[]{:S(2)}) collective-permute-start(bf16[3584,128]{1,0:T(8,128)(2,1)S(1)} %get-tuple-element.38.refs_0_), channel_id=1, source_target_pairs={{0,1},{1,0},{2,3},{3,2},{4,5},{5,4},{6,7},{7,6},{8,9},{9,8},{10,11... | collective-permute-start | bytes 2752520 | tf_op jit(solution)/shard_map/ppermute | solution.py:320
  28.2 16.7 %collective-permute-start.5 = (bf16[3584,128]{1,0:T(8,128)(2,1)S(1)}, bf16[3584,128]{1,0:T(8,128)(2,1)S(1)}, u32[]{:S(2)}, u32[]{:S(2)}) collective-permute-start(bf16[3584,128]{1,0:T(8,128)(2,1)S(1)} %get-tuple-element.41.refs_0_), channel_id=1, source_target_pairs={{0,1},{1,0},{2,3},{3,2},{4,5},{5,4},{6,7},{7,6},{8,9},{9,8},{10,11... | collective-permute-start | bytes 2752520 | tf_op jit(solution)/shard_map/ppermute | solution.py:320
  29.6 2.6 %collective-permute-start.12 = (bf16[1840,128]{1,0:T(8,128)(2,1)S(1)}, bf16[1840,128]{1,0:T(8,128)(2,1)S(1)}, u32[]{:S(2)}, u32[]{:S(2)}) collective-permute-start(bf16[1840,128]{1,0:T(8,128)(2,1)S(1)} %collective-permute-done.6.refs_8_), channel_id=1, source_target_pairs={{0,1},{1,0},{2,3},{3,2},{4,5},{5,4},{6,7},{7,6},{8,9},{9,8},{10,11... | collective-permute-start | bytes 1413128 | tf_op jit(solution)/shard_map/ppermute | solution.py:320
  29.6 2.5 %collective-permute-start.11 = (bf16[1792,128]{1,0:T(8,128)(2,1)S(1)}, bf16[1792,128]{1,0:T(8,128)(2,1)S(1)}, u32[]{:S(2)}, u32[]{:S(2)}) collective-permute-start(bf16[1792,128]{1,0:T(8,128)(2,1)S(1)} %collective-permute-done.4.refs_3_), channel_id=1, source_target_pairs={{0,1},{1,0},{2,3},{3,2},{4,5},{5,4},{6,7},{7,6},{8,9},{9,8},{10,11... | collective-permute-start | bytes 1376264 | tf_op jit(solution)/shard_map/ppermute | solution.py:320
  30.1 14.8 %collective-permute-start.17 = (bf16[2048,128]{1,0:T(8,128)(2,1)S(1)}, bf16[2048,128]{1,0:T(8,128)(2,1)S(1)}, u32[]{:S(2)}, u32[]{:S(2)}) collective-permute-start(bf16[2048,128]{1,0:T(8,128)(2,1)S(1)} %get-tuple-element.56), channel_id=1, source_target_pairs={{0,2},{1,3},{2,0},{3,1},{4,6},{5,7},{6,4},{7,5},{8,10},{9,11},{10,... | collective-permute-start | bytes 1572872 | tf_op jit(solution)/shard_map/ppermute | solution.py:320
  31.6 20.8 %collective-permute-start.7 = (bf16[1536,128]{1,0:T(8,128)(2,1)S(1)}, bf16[1536,128]{1,0:T(8,128)(2,1)S(1)}, u32[]{:S(2)}, u32[]{:S(2)}) collective-permute-start(bf16[1536,128]{1,0:T(8,128)(2,1)S(1)} %get-tuple-element.43), channel_id=1, source_target_pairs={{0,2},{1,3},{2,0},{3,1},{4,6},{5,7},{6,4},{7,5},{8,10},{9,11},{10,... | collective-permute-start | bytes 1179656 | tf_op jit(solution)/shard_map/ppermute | solution.py:320
  44.9 8.5 %collective-permute-start.18 = (bf16[2048,128]{1,0:T(8,128)(2,1)S(1)}, bf16[2048,128]{1,0:T(8,128)(2,1)S(1)}, u32[]{:S(2)}, u32[]{:S(2)}) collective-permute-start(bf16[2048,128]{1,0:T(8,128)(2,1)S(1)} %collective-permute-done.17.refs_2_), channel_id=1, source_target_pairs={{0,1},{1,0},{2,3},{3,2},{4,5},{5,4},{6,7},{7,6},{8,9},{9,8},{10,11... | collective-permute-start | bytes 1572872 | tf_op jit(solution)/shard_map/ppermute | solution.py:320
  44.9 8.5 %collective-permute-start.13 = (bf16[48,512]{1,0:T(8,128)(2,1)S(1)}, bf16[48,512]{1,0:T(8,128)(2,1)S(1)}, u32[]{:S(2)}, u32[]{:S(2)}) collective-permute-start(bf16[48,512]{1,0:T(8,128)(2,1)S(1)} %get-tuple-element.49), channel_id=1, source_target_pairs={{0,4},{4,8},{8,12},{12,0},{1,5},{5,9},{9,13},{13,1},{2,6},{6,10},{... | collective-permute-start | bytes 147464 | tf_op jit(solution)/shard_map/ppermute | solution.py:325
  46.5 6.9 %collective-permute-start.14 = (bf16[48,512]{1,0:T(8,128)(2,1)S(1)}, bf16[48,512]{1,0:T(8,128)(2,1)S(1)}, u32[]{:S(2)}, u32[]{:S(2)}) collective-permute-start(bf16[48,512]{1,0:T(8,128)(2,1)S(1)} %get-tuple-element.50), channel_id=1, source_target_pairs={{0,12},{4,0},{8,4},{12,8},{1,13},{5,1},{9,5},{13,9},{2,14},{6,2},{... | collective-permute-start | bytes 147464 | tf_op jit(solution)/shard_map/ppermute | solution.py:325
  48.8 4.6 %collective-permute-start.15 = (bf16[16,512]{1,0:T(8,128)(2,1)S(1)}, bf16[16,512]{1,0:T(8,128)(2,1)S(1)}, u32[]{:S(2)}, u32[]{:S(2)}) collective-permute-start(bf16[16,512]{1,0:T(8,128)(2,1)S(1)} %get-tuple-element.51), channel_id=1, source_target_pairs={{0,8},{4,12},{8,0},{12,4},{1,9},{5,13},{9,1},{13,5},{2,10},{6,14},... | collective-permute-start | bytes 49160 | tf_op jit(solution)/shard_map/ppermute | solution.py:325
  53.4 6.2 %collective-permute-start.16 = (bf16[1536,128]{1,0:T(8,128)(2,1)S(1)}, bf16[1536,128]{1,0:T(8,128)(2,1)S(1)}, u32[]{:S(2)}, u32[]{:S(2)}) collective-permute-start(bf16[1536,128]{1,0:T(8,128)(2,1)S(1)} %collective-permute-done.7.refs_2_), channel_id=1, source_target_pairs={{0,1},{1,0},{2,3},{3,2},{4,5},{5,4},{6,7},{7,6},{8,9},{9,8},{10,11... | collective-permute-start | bytes 1179656 | tf_op jit(solution)/shard_map/ppermute | solution.py:320
  (4 other events, 30.2 us)

commit v12 on v11

--- a/solution.py
+++ b/solution.py
@@ -136,7 +136,7 @@
         pick_out[at : at + COARSE_PAD, :] = coarse
 
 
-def prepare_kernel(blocks, halo, table_rows, list_ref, ef, es, nf, ns, hot_out, incidence_out, pick_out, pack_0, pack_1, edge_late, node_late, sems):
+def prepare_kernel(blocks, halo, table_rows, list_ref, ef, es, nf, ns, hot_out, incidence_out, pick_out, pack_out, edge_late, node_late, sems):
     part, features = es.shape[1:]
     edge_count, lanes_all = hot_out.shape
     node_count = incidence_out.shape[0]
@@ -151,8 +151,9 @@
             at += part
         return at
 
-    for layer, out in ((0, pack_0), (1, pack_1)):
-        pack(nf, ns, layer, out, pack(ef, es, layer, out, 0))
+    end = 0
+    for layer in range(ef.shape[0]):
+        end = pack(nf, ns, layer, pack_out, pack(ef, es, layer, pack_out, end))
     pack(ef, es, 1, edge_late, 0)
     pack(nf, ns, 1, node_late, 0)
     for at in range(0, edge_count, TILE):
@@ -272,14 +273,14 @@
     load_packed(moves, weights[3], 0, 3, first, second)
 
 
-def late_edge_kernel(pieces, *refs):
+def late_edge_kernel(pieces, base, *refs):
     refs = list(refs)
     weights = [refs.pop(0) for _ in range(4)]
     edge_ref, edge_own = [refs.pop(0) for _ in range(2)]
     tables = [refs.pop(0) for _ in range(pieces)]
     hot_ref, incidence_ref, edge_out, incoming_out = [refs.pop(0) for _ in range(4)]
     edge_w, edge_w2, product_ref, table_ref = refs
-    late_weights(weights, 0, edge_w, edge_w2)
+    late_weights(weights, base, edge_w, edge_w2)
     start = 0
     for table in tables:
         table_ref[start : start + table.shape[0], :] = table[...]
@@ -310,7 +311,7 @@
         out_specs=[pl.BlockSpec(memory_space=VMEM)] * len(out_shape),
         scratch_shapes=scratch,
         compiler_params=pltpu.CompilerParams(vmem_limit_bytes=vmem_mib * 1024 * 1024),
-        cost_estimate=pl.CostEstimate(flops=flops, bytes_accessed=moved, transcendentals=0),
+        cost_estimate=pl.CostEstimate(flops=0, bytes_accessed=0, transcendentals=0),
         name=name,
     )(*arrays)
 
@@ -407,14 +408,13 @@
     )
     rows = neighbour_rows(right, left, coarse, halo)
     lists = jnp.concatenate([senders, receivers, boundary_rows])[None, :]
-    hot, incidence, pick, pack_0, pack_1, edge_late, node_late = call(
+    hot, incidence, pick, packs, edge_late, node_late = call(
         functools.partial(prepare_kernel, blocks, halo, table_rows),
         [
             shape((edge_count, lanes), BF16),
             shape((node_count, edge_count), BF16),
             shape((2 * wide + COARSE_PAD, node_count), BF16),
-            shape((late_pack, part), BF16),
-            shape((late_pack, part), BF16),
+            shape((2 * late_pack, part), BF16),
             shape((edge_pack, part), BF16),
             shape((node_pack, part), BF16),
         ],
@@ -423,24 +423,24 @@
         0,
         "one_hot",
     )
-    core_0 = swap(pack_0, 1)
     (latents,) = call(
         latent_kernel,
         [shape((edge_count + table_rows, part), BF16)],
-        [(VMEM, after(edge_state, pack_0)), (VMEM, node_state)] + [(VMEM, r) for r in rows],
+        [(VMEM, after(edge_state, packs)), (VMEM, node_state)] + [(VMEM, r) for r in rows],
         [],
         0,
         "latents",
     )
-    near = after(near, latents)
+    near = near
+    core_packs = swap(after(packs, near), 1)
     far_latents = swap(latents, 2)
     far = lax.ppermute(near, "groups", [(0, 1), (1, 0)])
-    core_near, core_latents = swap(near, 1), swap(latents, 1)
-    core_1 = swap(after(pack_1, far), 1)
-    core_far = swap(after(far, core_latents, core_near), 1)
-    edge_late_x = swap(after(edge_late, core_near), 2)
-    node_late_x = swap(after(node_late, far_latents), 2)
-    shards = [latents, core_latents, far_latents, swap(after(far_latents, far), 1)]
+    core_latents = swap(after(latents, near), 1)
+    core_near = swap(near, 1)
+    core_far = swap(far, 1)
+    edge_late_x = swap(after(edge_late, near), 2)
+    node_late_x = swap(after(node_late, far, far_latents), 2)
+    shards = [latents, core_latents, far_latents, swap(after(far_latents, far, core_packs, core_near), 1)]
     pairs = [near, far, core_near, core_far]
 
     edge_flops = 2 * edge_count * features * (2 * features + lanes + node_count)
@@ -456,7 +456,7 @@
     edge_own, edge_full, node_own, node_full, right, left, coarse = call(
         first_kernel,
         [own_edge, full_edge, own_node, full_node] + sent(features),
-        [(VMEM, w) for w in [pack_0, core_0] + pairs + shards]
+        [(VMEM, w) for w in [packs, core_packs] + pairs + shards]
         + [(VMEM, a) for a in (edge_state, node_state, hot, incidence, pick)],
         [
             edge_shape,
@@ -471,11 +471,11 @@
         16,
     )
     tables = [node_full] + neighbour_rows(right, left, coarse, halo)
-    edge_late_d = swap(after(edge_late_x, right, core_1), 1)
+    edge_late_d = swap(after(edge_late_x, *tables[1:]), 1)
     edge_own, incoming = call(
-        functools.partial(late_edge_kernel, len(tables)),
+        functools.partial(late_edge_kernel, len(tables), late_pack),
         [own_edge, full_node],
-        [(VMEM, w) for w in (pack_1, core_1, edge_late_x, edge_late_d)]
+        [(VMEM, w) for w in (packs, core_packs, edge_late_x, edge_late_d)]
         + [(VMEM, a) for a in (edge_full, edge_own)]
         + [(VMEM, t) for t in tables]
         + [(VMEM, hot), (VMEM, incidence)],
@@ -489,11 +489,11 @@
         "layer_1_edges",
         16,
     )
-    node_late_d = swap(after(node_late_x, *tables[1:]), 1)
+    node_late_d = swap(after(node_late_x, right), 1)
     (node_own,) = call(
-        functools.partial(late_node_kernel, edge_pack),
+        functools.partial(late_node_kernel, late_pack + edge_pack),
         [own_node],
-        [(VMEM, w) for w in (pack_1, core_1, node_late_x, node_late_d)]
+        [(VMEM, w) for w in (packs, core_packs, node_late_x, node_late_d)]
         + [(VMEM, a) for a in (node_full, node_own, incoming)],
         [node_shape, second_shape],
         node_flops,

time: 61.3 us -> 59.9 us (0.977)
  waiting for transfers between devices: 22.8 us -> 19.8 us
  starting transfers between devices: 18.3 us -> 20 us
    ppermute x1, waiting for transfers between devices: 7.93 us -> 1.01 us  [on_device(): far = lax.ppermute(near, 'groups', [(0, 1), (1, 0)])]
    ppermute x12 -> x11, waiting for transfers between devices: 10.2 us -> 12.2 us  [swap(): return lax.ppermute(x, 'mp', [(i, i ^ mask) for i in range(size)])]
    ppermute x6, waiting for transfers between devices: 4.63 us -> 6.5 us  [shift(): return lax.ppermute(x, 'graph', [(i, (i + by) % size) for i in range(size)])]
    ppermute x6, starting transfers between devices: 9.28 us -> 11.1 us  [shift(): return lax.ppermute(x, 'graph', [(i, (i + by) % size) for i in range(size)])]
    ppermute x12 -> x11, starting transfers between devices: 7.42 us -> 7.37 us  [swap(): return lax.ppermute(x, 'mp', [(i, i ^ mask) for i in range(size)])]
  transfers between devices with their start and end apart: 19 -> 18, of which waited for: 6 -> 7; matrix products, arithmetic and copies ran while one was open for 0% -> 0% of each run, Pallas kernels for 26% -> 26%
where the time goes in v12:
time: 59.9 us; the launch traced here: 59.8 us
  starting transfers between devices  20 us (33%)
  waiting for transfers between devices  19.8 us (33%)
  Pallas kernels  19.1 us (32%)
  between operations  0.81 us (1%)
    pallas_call x7, Pallas kernels, call(): pl.pallas_call(kernel, out_shape=out_shape, in_specs=[pl.BlockSpec(memory...  19.1 us
    ppermute x11, waiting for transfers between devices, swap(): return lax.ppermute(x, 'mp', [(i, i ^ mask) for i in range(size)])  12.2 us
    ppermute x6, starting transfers between devices, shift(): return lax.ppermute(x, 'graph', [(i, (i + by) % size) for i in range(size)])  11.1 us
    ppermute x11, starting transfers between devices, swap(): return lax.ppermute(x, 'mp', [(i, i ^ mask) for i in range(size)])  7.37 us
    ppermute x6, waiting for transfers between devices, shift(): return lax.ppermute(x, 'graph', [(i, (i + by) % size) for i in range(size)])  6.5 us
    ppermute x1, starting transfers between devices, on_device(): far = lax.ppermute(near, 'groups', [(0, 1), (1, 0)])  1.52 us
  transfers between devices with their start and end apart: 18, of which 7 were waited for; matrix products, arithmetic and copies ran while one was open for 0% of the time, Pallas kernels for 26%

profile of v12, /device:TPU:0, one launch (start us, length us, event | category | flops | bytes accessed | tf_op | source)
XLA Modules:
  0.0 59.8 jit_solution(2331351406953852111)
XLA Ops:
  0.7 2.0 %layer_0_half.1 = bf16[1792,128]{1,0:T(8,128)(2,1)} custom-call(bf16[2,1536,128]{2,1,0:T(8,128)(2,1)} %ef.3, bf16[2,128,512]{2,1,0:T(8,128)(2,1)} %es.3, bf16[2,1024,128]{2,1,0:T(8,128)(2,1)} %nf.3, bf16[2,128,512]{2,1,0:T(8,128)(2,1)} %ns.3), custom_call_target="tpu_custom_call" | custom-call | tf_op jit(solution)/shard_map/layer_0_half/pallas_call | solution.py:307
  2.8 3.0 %collective-permute-start.3 = (bf16[1792,128]{1,0:T(8,128)(2,1)}, bf16[1792,128]{1,0:T(8,128)(2,1)S(1)}, u32[]{:S(2)}, u32[]{:S(2)}) collective-permute-start(bf16[1792,128]{1,0:T(8,128)(2,1)} %layer_0_half.1), channel_id=1, source_target_pairs={{0,2},{1,3},{2,0},{3,1},{4,6},{5,7},{6,4},{7,5},{8,10},{9,11},{10,... | collective-permute-start | bytes 1376264 | tf_op jit(solution)/shard_map/ppermute | solution.py:321
  6.1 2.7 %collective-permute-start.2 = (bf16[16,128]{1,0:T(8,128)(2,1)S(1)}, bf16[16,128]{1,0:T(8,128)(2,1)S(1)}, u32[]{:S(2)}, u32[]{:S(2)}) collective-permute-start(bf16[16,128]{1,0:T(8,128)(2,1)S(1)} %get-tuple-element.33), channel_id=1, source_target_pairs={{0,8},{4,12},{8,0},{12,4},{1,9},{5,13},{9,1},{13,5},{2,10},{6,14},... | collective-permute-start | bytes 12296 | tf_op jit(solution)/shard_map/ppermute | solution.py:326
  8.7 1.6 %collective-permute-start = (bf16[48,128]{1,0:T(8,128)(2,1)S(1)}, bf16[48,128]{1,0:T(8,128)(2,1)S(1)}, u32[]{:S(2)}, u32[]{:S(2)}) collective-permute-start(bf16[48,128]{1,0:T(8,128)(2,1)S(1)} %get-tuple-element.31), channel_id=1, source_target_pairs={{0,4},{4,8},{8,12},{12,0},{1,5},{5,9},{9,13},{13,1},{2,6},{6,10},{... | collective-permute-start | bytes 36872 | tf_op jit(solution)/shard_map/ppermute | solution.py:326
  10.3 2.2 %collective-permute-start.1 = (bf16[48,128]{1,0:T(8,128)(2,1)S(1)}, bf16[48,128]{1,0:T(8,128)(2,1)S(1)}, u32[]{:S(2)}, u32[]{:S(2)}) collective-permute-start(bf16[48,128]{1,0:T(8,128)(2,1)S(1)} %get-tuple-element.32), channel_id=1, source_target_pairs={{0,12},{4,0},{8,4},{12,8},{1,13},{5,1},{9,5},{13,9},{2,14},{6,2},{... | collective-permute-start | bytes 36872 | tf_op jit(solution)/shard_map/ppermute | solution.py:326
  12.6 1.6 %collective-permute-done.refs_2_ = bf16[48,128]{1,0:T(8,128)(2,1)S(1)} collective-permute-done((bf16[48,128]{1,0:T(8,128)(2,1)S(1)}, bf16[48,128]{1,0:T(8,128)(2,1)S(1)}, u32[]{:S(2)}, u32[]{:S(2)}) %collective-permute-start) | collective-permute-done | bytes 12320 | tf_op jit(solution)/shard_map/ppermute | solution.py:326
  14.3 2.2 %one_hot.1 = (bf16[1536,512]{1,0:T(8,128)(2,1)S(1)}, bf16[192,1536]{1,0:T(8,128)(2,1)S(1)}, bf16[112,192]{1,0:T(8,128)(2,1)S(1)}, bf16[7168,128]{1,0:T(8,128)(2,...) custom-call(s32[1,3136]{1,0:T(1,128)S(1)} %broadcast_in_dim.6.list_ref, ...), custom_call_target="tpu_custom_call" | custom-call | tf_op jit(solution)/shard_map/one_hot/pallas_call | solution.py:307
  16.6 1.7 %collective-permute-start.6 = (bf16[1840,128]{1,0:T(8,128)(2,1)S(1)}, bf16[1840,128]{1,0:T(8,128)(2,1)S(1)}, u32[]{:S(2)}, u32[]{:S(2)}) collective-permute-start(bf16[1840,128]{1,0:T(8,128)(2,1)S(1)} %latents.1.refs_6_), channel_id=1, source_target_pairs={{0,2},{1,3},{2,0},{3,1},{4,6},{5,7},{6,4},{7,5},{8,10},{9,11},{10,... | collective-permute-start | bytes 1413128 | tf_op jit(solution)/shard_map/ppermute | solution.py:321
  18.6 1.5 %collective-permute-start.5 = (bf16[1792,128]{1,0:T(8,128)(2,1)S(1)}, bf16[1792,128]{1,0:T(8,128)(2,1)S(1)}, u32[]{:S(2)}, u32[]{:S(2)}) collective-permute-start(bf16[1792,128]{1,0:T(8,128)(2,1)S(1)} %collective-permute-done.3.refs_2_), channel_id=1, source_target_pairs={{0,16},{16,0},{1,17},{17,1},{2,18},{18,2},{3,19},{19,3},{4,20},{20... | collective-permute-start | bytes 1376264 | tf_op jit(solution)/shard_map/ppermute | solution.py:437
  20.1 0.5 collective-permute-start.13
  20.7 9.6 %collective-permute-done.6.refs_8_ = bf16[1840,128]{1,0:T(8,128)(2,1)S(1)} collective-permute-done((bf16[1840,128]{1,0:T(8,128)(2,1)S(1)}, bf16[1840,128]{1,0:T(8,128)(2,1)S(1)}, u32[]{:S(2)}, u32[]{:S(2)}) %collective-permute-start.6) | collective-permute-done | bytes 471072 | tf_op jit(solution)/shard_map/ppermute | solution.py:321
  30.3 1.0 %collective-permute-done.5.refs_3_ = bf16[1792,128]{1,0:T(8,128)(2,1)S(1)} collective-permute-done((bf16[1792,128]{1,0:T(8,128)(2,1)S(1)}, bf16[1792,128]{1,0:T(8,128)(2,1)S(1)}, u32[]{:S(2)}, u32[]{:S(2)}) %collective-permute-start.5) | collective-permute-done | bytes 458784 | tf_op jit(solution)/shard_map/ppermute | solution.py:437
  31.3 0.5 collective-permute-start.9
  31.8 0.8 %collective-permute-start.7 = (bf16[1536,128]{1,0:T(8,128)(2,1)S(1)}, bf16[1536,128]{1,0:T(8,128)(2,1)S(1)}, u32[]{:S(2)}, u32[]{:S(2)}) collective-permute-start(bf16[1536,128]{1,0:T(8,128)(2,1)S(1)} %get-tuple-element.39), channel_id=1, source_target_pairs={{0,2},{1,3},{2,0},{3,1},{4,6},{5,7},{6,4},{7,5},{8,10},{9,11},{10,... | collective-permute-start | bytes 1179656 | tf_op jit(solution)/shard_map/ppermute | solution.py:321
  32.6 1.2 %collective-permute-done.9.refs_5_ = bf16[1792,128]{1,0:T(8,128)(2,1)S(1)} collective-permute-done((bf16[1792,128]{1,0:T(8,128)(2,1)S(1)}, bf16[1792,128]{1,0:T(8,128)(2,1)S(1)}, u32[]{:S(2)}, u32[]{:S(2)}) %collective-permute-start.9) | collective-permute-done | bytes 458784 | tf_op jit(solution)/shard_map/ppermute | solution.py:321
  33.8 6.9 %layer_0.1 = (f32[1536,128]{1,0:T(8,128)S(1)}, bf16[1536,512]{1,0:T(8,128)(2,1)S(1)}, f32[192,128]{1,0:T(8,128)S(1)}, bf16[192,512]{1,0:T(8,128)(2,1)S(1)}, bf16...) custom-call(bf16[7168,128]{1,0:T(8,128)(2,1)S(1)} %get-tuple-element.36.refs_0_, ...), custom_call_target="tpu_custom_call" | custom-call | tf_op jit(solution)/shard_map/layer_0/pallas_call | solution.py:307
  40.7 3.6 %collective-permute-start.15 = (bf16[48,512]{1,0:T(8,128)(2,1)S(1)}, bf16[48,512]{1,0:T(8,128)(2,1)S(1)}, u32[]{:S(2)}, u32[]{:S(2)}) collective-permute-start(bf16[48,512]{1,0:T(8,128)(2,1)S(1)} %get-tuple-element.51), channel_id=1, source_target_pairs={{0,12},{4,0},{8,4},{12,8},{1,13},{5,1},{9,5},{13,9},{2,14},{6,2},{... | collective-permute-start | bytes 147464 | tf_op jit(solution)/shard_map/ppermute | solution.py:326
  44.3 1.0 %collective-permute-start.16 = (bf16[16,512]{1,0:T(8,128)(2,1)S(1)}, bf16[16,512]{1,0:T(8,128)(2,1)S(1)}, u32[]{:S(2)}, u32[]{:S(2)}) collective-permute-start(bf16[16,512]{1,0:T(8,128)(2,1)S(1)} %get-tuple-element.52), channel_id=1, source_target_pairs={{0,8},{4,12},{8,0},{12,4},{1,9},{5,13},{9,1},{13,5},{2,10},{6,14},... | collective-permute-start | bytes 49160 | tf_op jit(solution)/shard_map/ppermute | solution.py:326
  45.3 4.1 %collective-permute-done.16.refs_9_ = bf16[16,512]{1,0:T(8,128)(2,1)S(1)} collective-permute-done((bf16[16,512]{1,0:T(8,128)(2,1)S(1)}, bf16[16,512]{1,0:T(8,128)(2,1)S(1)}, u32[]{:S(2)}, u32[]{:S(2)}) %collective-permute-start.16) | collective-permute-done | bytes 16416 | tf_op jit(solution)/shard_map/ppermute | solution.py:326
  49.5 0.8 %collective-permute-done.14.refs_7_ = bf16[48,512]{1,0:T(8,128)(2,1)S(1)} collective-permute-done((bf16[48,512]{1,0:T(8,128)(2,1)S(1)}, bf16[48,512]{1,0:T(8,128)(2,1)S(1)}, u32[]{:S(2)}, u32[]{:S(2)}) %collective-permute-start.14) | collective-permute-done | bytes 49184 | tf_op jit(solution)/shard_map/ppermute | solution.py:326
  50.2 0.5 collective-permute-start.12
  50.7 1.4 %collective-permute-done.17.refs_3_ = bf16[2048,128]{1,0:T(8,128)(2,1)S(1)} collective-permute-done((bf16[2048,128]{1,0:T(8,128)(2,1)S(1)}, bf16[2048,128]{1,0:T(8,128)(2,1)S(1)}, u32[]{:S(2)}, u32[]{:S(2)}) %collective-permute-start.17) | collective-permute-done | bytes 524320 | tf_op jit(solution)/shard_map/ppermute | solution.py:321
  52.1 6.2 %layer_1_edges.1 = (f32[1536,128]{1,0:T(8,128)}, bf16[192,512]{1,0:T(8,128)(2,1)S(1)}) custom-call(bf16[7168,128]{1,0:T(8,128)(2,1)S(1)} %get-tuple-element.36.refs_0_, bf16[7168,128]{1,0:T(8,128)(2,1)S(1)} %collective-permute-done.4.refs_1_, bf16[2048,128]{1,0:T(8,128)(2,1)S(1)} %collective-permute-done.13.refs_2_, ...), custom_call_target="tpu_custom_call" | custom-call | tf_op jit(solution)/shard_map/layer_1_edges/pallas_call | solution.py:307
  58.3 1.5 %layer_1_nodes.1 = f32[192,128]{1,0:T(8,128)} custom-call(bf16[7168,128]{1,0:T(8,128)(2,1)S(1)} %get-tuple-element.36.refs_0_, bf16[7168,128]{1,0:T(8,128)(2,1)S(1)} %collective-permute-done.4.refs_1_, bf16[1536,128]{1,0:T(8,128)(2,1)S(1)} %collective-permute-done.7.refs_2_, bf16[1536,128]{1,0:T(8,128)(2,1)S(1)} %collective-permute-done.12.refs_3_, ...), custom_call_target="tpu_custom_call" | custom-call | tf_op jit(solution)/shard_map/layer_1_nodes/pallas_call | solution.py:307
  (39 shorter events, 0.7 us)
Async XLA Ops:
  0.6 13.6 %copy-start.4 = (bf16[2,128,512]{2,1,0:T(8,128)(2,1)S(1)}, bf16[2,128,512]{2,1,0:T(8,128)(2,1)}, u32[]{:S(2)}) copy-start(bf16[2,128,512]{2,1,0:T(8,128)(2,1)} %ns.3) | copy-start | bytes 786436
  0.6 13.6 %copy-start.2 = (bf16[2,1024,128]{2,1,0:T(8,128)(2,1)S(1)}, bf16[2,1024,128]{2,1,0:T(8,128)(2,1)}, u32[]{:S(2)}) copy-start(bf16[2,1024,128]{2,1,0:T(8,128)(2,1)} %nf.3) | copy-start | bytes 1572868
  0.7 13.6 %copy-start.3 = (bf16[2,128,512]{2,1,0:T(8,128)(2,1)S(1)}, bf16[2,128,512]{2,1,0:T(8,128)(2,1)}, u32[]{:S(2)}) copy-start(bf16[2,128,512]{2,1,0:T(8,128)(2,1)} %es.3) | copy-start | bytes 786436
  0.7 13.6 %copy-start = (bf16[2,1536,128]{2,1,0:T(8,128)(2,1)S(1)}, bf16[2,1536,128]{2,1,0:T(8,128)(2,1)}, u32[]{:S(2)}) copy-start(bf16[2,1536,128]{2,1,0:T(8,128)(2,1)} %ef.3) | copy-start | bytes 2359300
  0.7 11.9 %copy-start.7 = (s32[1536]{0:T(1024)S(1)}, s32[1536]{0:T(1024)}, u32[]{:S(2)}) copy-start(s32[1536]{0:T(1024)} %param.16) | copy-start | bytes 18436
  0.7 15.9 %copy-start.1 = (f32[1536,128]{1,0:T(8,128)S(1)}, f32[1536,128]{1,0:T(8,128)}, u32[]{:S(2)}) copy-start(f32[1536,128]{1,0:T(8,128)} %refs_10_.1) | copy-start | bytes 2359300
  2.8 13.7 %collective-permute-start.3 = (bf16[1792,128]{1,0:T(8,128)(2,1)}, bf16[1792,128]{1,0:T(8,128)(2,1)S(1)}, u32[]{:S(2)}, u32[]{:S(2)}) collective-permute-start(bf16[1792,128]{1,0:T(8,128)(2,1)} %layer_0_half.1), channel_id=1, source_target_pairs={{0,2},{1,3},{2,0},{3,1},{4,6},{5,7},{6,4},{7,5},{8,10},{9,11},{10,... | collective-permute-start | bytes 1376264 | tf_op jit(solution)/shard_map/ppermute | solution.py:321
  6.1 6.5 %collective-permute-start.2 = (bf16[16,128]{1,0:T(8,128)(2,1)S(1)}, bf16[16,128]{1,0:T(8,128)(2,1)S(1)}, u32[]{:S(2)}, u32[]{:S(2)}) collective-permute-start(bf16[16,128]{1,0:T(8,128)(2,1)S(1)} %get-tuple-element.33), channel_id=1, source_target_pairs={{0,8},{4,12},{8,0},{12,4},{1,9},{5,13},{9,1},{13,5},{2,10},{6,14},... | collective-permute-start | bytes 12296 | tf_op jit(solution)/shard_map/ppermute | solution.py:326
  8.7 5.5 %collective-permute-start = (bf16[48,128]{1,0:T(8,128)(2,1)S(1)}, bf16[48,128]{1,0:T(8,128)(2,1)S(1)}, u32[]{:S(2)}, u32[]{:S(2)}) collective-permute-start(bf16[48,128]{1,0:T(8,128)(2,1)S(1)} %get-tuple-element.31), channel_id=1, source_target_pairs={{0,4},{4,8},{8,12},{12,0},{1,5},{5,9},{9,13},{13,1},{2,6},{6,10},{... | collective-permute-start | bytes 36872 | tf_op jit(solution)/shard_map/ppermute | solution.py:326
  10.3 3.9 %collective-permute-start.1 = (bf16[48,128]{1,0:T(8,128)(2,1)S(1)}, bf16[48,128]{1,0:T(8,128)(2,1)S(1)}, u32[]{:S(2)}, u32[]{:S(2)}) collective-permute-start(bf16[48,128]{1,0:T(8,128)(2,1)S(1)} %get-tuple-element.32), channel_id=1, source_target_pairs={{0,12},{4,0},{8,4},{12,8},{1,13},{5,1},{9,5},{13,9},{2,14},{6,2},{... | collective-permute-start | bytes 36872 | tf_op jit(solution)/shard_map/ppermute | solution.py:326
  16.5 14.8 %collective-permute-start.4 = (bf16[7168,128]{1,0:T(8,128)(2,1)S(1)}, bf16[7168,128]{1,0:T(8,128)(2,1)S(1)}, u32[]{:S(2)}, u32[]{:S(2)}) collective-permute-start(bf16[7168,128]{1,0:T(8,128)(2,1)S(1)} %get-tuple-element.36.refs_0_), channel_id=1, source_target_pairs={{0,1},{1,0},{2,3},{3,2},{4,5},{5,4},{6,7},{7,6},{8,9},{9,8},{10,11... | collective-permute-start | bytes 5505032 | tf_op jit(solution)/shard_map/ppermute | solution.py:321
  16.6 13.6 %collective-permute-start.6 = (bf16[1840,128]{1,0:T(8,128)(2,1)S(1)}, bf16[1840,128]{1,0:T(8,128)(2,1)S(1)}, u32[]{:S(2)}, u32[]{:S(2)}) collective-permute-start(bf16[1840,128]{1,0:T(8,128)(2,1)S(1)} %latents.1.refs_6_), channel_id=1, source_target_pairs={{0,2},{1,3},{2,0},{3,1},{4,6},{5,7},{6,4},{7,5},{8,10},{9,11},{10,... | collective-permute-start | bytes 1413128 | tf_op jit(solution)/shard_map/ppermute | solution.py:321
  18.4 11.9 %collective-permute-start.8 = (bf16[1792,128]{1,0:T(8,128)(2,1)S(1)}, bf16[1792,128]{1,0:T(8,128)(2,1)S(1)}, u32[]{:S(2)}, u32[]{:S(2)}) collective-permute-start(bf16[1792,128]{1,0:T(8,128)(2,1)S(1)} %collective-permute-done.3.refs_2_), channel_id=1, source_target_pairs={{0,1},{1,0},{2,3},{3,2},{4,5},{5,4},{6,7},{7,6},{8,9},{9,8},{10,11... | collective-permute-start | bytes 1376264 | tf_op jit(solution)/shard_map/ppermute | solution.py:321
  18.6 12.7 %collective-permute-start.5 = (bf16[1792,128]{1,0:T(8,128)(2,1)S(1)}, bf16[1792,128]{1,0:T(8,128)(2,1)S(1)}, u32[]{:S(2)}, u32[]{:S(2)}) collective-permute-start(bf16[1792,128]{1,0:T(8,128)(2,1)S(1)} %collective-permute-done.3.refs_2_), channel_id=1, source_target_pairs={{0,16},{16,0},{1,17},{17,1},{2,18},{18,2},{3,19},{19,3},{4,20},{20... | collective-permute-start | bytes 1376264 | tf_op jit(solution)/shard_map/ppermute | solution.py:437
  20.1 25.2 %collective-permute-start.13 = (bf16[2048,128]{1,0:T(8,128)(2,1)S(1)}, bf16[2048,128]{1,0:T(8,128)(2,1)S(1)}, u32[]{:S(2)}, u32[]{:S(2)}) collective-permute-start(bf16[2048,128]{1,0:T(8,128)(2,1)S(1)} %get-tuple-element.50), channel_id=1, source_target_pairs={{0,2},{1,3},{2,0},{3,1},{4,6},{5,7},{6,4},{7,5},{8,10},{9,11},{10,... | collective-permute-start | bytes 1572872 | tf_op jit(solution)/shard_map/ppermute | solution.py:321
  30.3 2.3 %collective-permute-start.10 = (bf16[1840,128]{1,0:T(8,128)(2,1)S(1)}, bf16[1840,128]{1,0:T(8,128)(2,1)S(1)}, u32[]{:S(2)}, u32[]{:S(2)}) collective-permute-start(bf16[1840,128]{1,0:T(8,128)(2,1)S(1)} %latents.1.refs_6_), channel_id=1, source_target_pairs={{0,1},{1,0},{2,3},{3,2},{4,5},{5,4},{6,7},{7,6},{8,9},{9,8},{10,11... | collective-permute-start | bytes 1413128 | tf_op jit(solution)/shard_map/ppermute | solution.py:321
  31.3 2.5 %collective-permute-start.11 = (bf16[1840,128]{1,0:T(8,128)(2,1)S(1)}, bf16[1840,128]{1,0:T(8,128)(2,1)S(1)}, u32[]{:S(2)}, u32[]{:S(2)}) collective-permute-start(bf16[1840,128]{1,0:T(8,128)(2,1)S(1)} %collective-permute-done.6.refs_8_), channel_id=1, source_target_pairs={{0,1},{1,0},{2,3},{3,2},{4,5},{5,4},{6,7},{7,6},{8,9},{9,8},{10,11... | collective-permute-start | bytes 1413128 | tf_op jit(solution)/shard_map/ppermute | solution.py:321
  31.3 2.5 %collective-permute-start.9 = (bf16[1792,128]{1,0:T(8,128)(2,1)S(1)}, bf16[1792,128]{1,0:T(8,128)(2,1)S(1)}, u32[]{:S(2)}, u32[]{:S(2)}) collective-permute-start(bf16[1792,128]{1,0:T(8,128)(2,1)S(1)} %collective-permute-done.5.refs_3_), channel_id=1, source_target_pairs={{0,1},{1,0},{2,3},{3,2},{4,5},{5,4},{6,7},{7,6},{8,9},{9,8},{10,11... | collective-permute-start | bytes 1376264 | tf_op jit(solution)/shard_map/ppermute | solution.py:321
  31.8 18.4 %collective-permute-start.7 = (bf16[1536,128]{1,0:T(8,128)(2,1)S(1)}, bf16[1536,128]{1,0:T(8,128)(2,1)S(1)}, u32[]{:S(2)}, u32[]{:S(2)}) collective-permute-start(bf16[1536,128]{1,0:T(8,128)(2,1)S(1)} %get-tuple-element.39), channel_id=1, source_target_pairs={{0,2},{1,3},{2,0},{3,1},{4,6},{5,7},{6,4},{7,5},{8,10},{9,11},{10,... | collective-permute-start | bytes 1179656 | tf_op jit(solution)/shard_map/ppermute | solution.py:321
  40.7 8.8 %collective-permute-start.15 = (bf16[48,512]{1,0:T(8,128)(2,1)S(1)}, bf16[48,512]{1,0:T(8,128)(2,1)S(1)}, u32[]{:S(2)}, u32[]{:S(2)}) collective-permute-start(bf16[48,512]{1,0:T(8,128)(2,1)S(1)} %get-tuple-element.51), channel_id=1, source_target_pairs={{0,12},{4,0},{8,4},{12,8},{1,13},{5,1},{9,5},{13,9},{2,14},{6,2},{... | collective-permute-start | bytes 147464 | tf_op jit(solution)/shard_map/ppermute | solution.py:326
  44.3 5.9 %collective-permute-start.14 = (bf16[48,512]{1,0:T(8,128)(2,1)S(1)}, bf16[48,512]{1,0:T(8,128)(2,1)S(1)}, u32[]{:S(2)}, u32[]{:S(2)}) collective-permute-start(bf16[48,512]{1,0:T(8,128)(2,1)S(1)} %get-tuple-element.45), channel_id=1, source_target_pairs={{0,4},{4,8},{8,12},{12,0},{1,5},{5,9},{9,13},{13,1},{2,6},{6,10},{... | collective-permute-start | bytes 147464 | tf_op jit(solution)/shard_map/ppermute | solution.py:326
  44.3 5.1 %collective-permute-start.16 = (bf16[16,512]{1,0:T(8,128)(2,1)S(1)}, bf16[16,512]{1,0:T(8,128)(2,1)S(1)}, u32[]{:S(2)}, u32[]{:S(2)}) collective-permute-start(bf16[16,512]{1,0:T(8,128)(2,1)S(1)} %get-tuple-element.52), channel_id=1, source_target_pairs={{0,8},{4,12},{8,0},{12,4},{1,9},{5,13},{9,1},{13,5},{2,10},{6,14},... | collective-permute-start | bytes 49160 | tf_op jit(solution)/shard_map/ppermute | solution.py:326
  50.2 1.9 %collective-permute-start.17 = (bf16[2048,128]{1,0:T(8,128)(2,1)S(1)}, bf16[2048,128]{1,0:T(8,128)(2,1)S(1)}, u32[]{:S(2)}, u32[]{:S(2)}) collective-permute-start(bf16[2048,128]{1,0:T(8,128)(2,1)S(1)} %collective-permute-done.13.refs_2_), channel_id=1, source_target_pairs={{0,1},{1,0},{2,3},{3,2},{4,5},{5,4},{6,7},{7,6},{8,9},{9,8},{10,11... | collective-permute-start | bytes 1572872 | tf_op jit(solution)/shard_map/ppermute | solution.py:321
  50.2 8.1 %collective-permute-start.12 = (bf16[1536,128]{1,0:T(8,128)(2,1)S(1)}, bf16[1536,128]{1,0:T(8,128)(2,1)S(1)}, u32[]{:S(2)}, u32[]{:S(2)}) collective-permute-start(bf16[1536,128]{1,0:T(8,128)(2,1)S(1)} %collective-permute-done.7.refs_2_), channel_id=1, source_target_pairs={{0,1},{1,0},{2,3},{3,2},{4,5},{5,4},{6,7},{7,6},{8,9},{9,8},{10,11... | collective-permute-start | bytes 1179656 | tf_op jit(solution)/shard_map/ppermute | solution.py:321
  (3 other events, 22.1 us)

commit v13 on v12

--- a/solution.py
+++ b/solution.py
@@ -10,7 +10,8 @@
 COARSE_DEV = 12
 COARSE_PAD = 16
 EPS = 1e-05
-TILE = 256
+TILE = 512
+HOT_TILE = 256
 F32 = jnp.float32
 BF16 = jnp.bfloat16
 
@@ -156,14 +157,14 @@
         end = pack(nf, ns, layer, pack_out, pack(ef, es, layer, pack_out, end))
     pack(ef, es, 1, edge_late, 0)
     pack(nf, ns, 1, node_late, 0)
-    for at in range(0, edge_count, TILE):
-        senders = table_index(list_ref[:, at : at + TILE], blocks, node_count, halo)
-        receivers = list_ref[:, edge_count + at : edge_count + at + TILE]
-        lanes = lax.broadcasted_iota(jnp.int32, (TILE, lanes_all), 1)
+    for at in range(0, edge_count, HOT_TILE):
+        senders = table_index(list_ref[:, at : at + HOT_TILE], blocks, node_count, halo)
+        receivers = list_ref[:, edge_count + at : edge_count + at + HOT_TILE]
+        lanes = lax.broadcasted_iota(jnp.int32, (HOT_TILE, lanes_all), 1)
         hit = (lanes == column(senders)) | (lanes == column(receivers) + table_rows)
-        hot_out[at : at + TILE, :] = one_hot(hit)
-        node_ids = lax.broadcasted_iota(jnp.int32, (node_count, TILE), 0)
-        incidence_out[:, at : at + TILE] = one_hot(node_ids == receivers)
+        hot_out[at : at + HOT_TILE, :] = one_hot(hit)
+        node_ids = lax.broadcasted_iota(jnp.int32, (node_count, HOT_TILE), 0)
+        incidence_out[:, at : at + HOT_TILE] = one_hot(node_ids == receivers)
     make_pick(list_ref[:, 2 * edge_count : 2 * edge_count + 2 * halo], pick_out)
     copies.wait()
 
@@ -304,6 +305,7 @@
 def call(kernel, out_shape, args, scratch, flops, name, vmem_mib=8):
     arrays = [a for _, a in args]
     moved = sum(a.size * a.dtype.itemsize for a in arrays + list(out_shape))
+    moved = sum(a.size * a.dtype.itemsize for a in arrays + list(out_shape))
     return pl.pallas_call(
         kernel,
         out_shape=out_shape,
@@ -407,6 +409,18 @@
         "boundary_rows",
     )
     rows = neighbour_rows(right, left, coarse, halo)
+    (latents,) = call(
+        latent_kernel,
+        [shape((edge_count + table_rows, part), BF16)],
+        [(VMEM, edge_state), (VMEM, node_state)] + [(VMEM, r) for r in rows],
+        [],
+        0,
+        "latents",
+    )
+    near = after(near, *rows)
+    far_latents = swap(latents, 2)
+    far = lax.ppermute(near, "groups", [(0, 1), (1, 0)])
+    core_latents = swap(latents, 1)
     lists = jnp.concatenate([senders, receivers, boundary_rows])[None, :]
     hot, incidence, pick, packs, edge_late, node_late = call(
         functools.partial(prepare_kernel, blocks, halo, table_rows),
@@ -423,23 +437,11 @@
         0,
         "one_hot",
     )
-    (latents,) = call(
-        latent_kernel,
-        [shape((edge_count + table_rows, part), BF16)],
-        [(VMEM, after(edge_state, packs)), (VMEM, node_state)] + [(VMEM, r) for r in rows],
-        [],
-        0,
-        "latents",
-    )
-    near = near
     core_packs = swap(after(packs, near), 1)
-    far_latents = swap(latents, 2)
-    far = lax.ppermute(near, "groups", [(0, 1), (1, 0)])
-    core_latents = swap(after(latents, near), 1)
-    core_near = swap(near, 1)
-    core_far = swap(far, 1)
-    edge_late_x = swap(after(edge_late, near), 2)
-    node_late_x = swap(after(node_late, far, far_latents), 2)
+    core_near = swap(after(near, core_latents), 1)
+    core_far = swap(after(far, core_packs), 1)
+    edge_late_x = swap(after(edge_late, core_latents), 2)
+    node_late_x = swap(after(node_late, far_latents), 2)
     shards = [latents, core_latents, far_latents, swap(after(far_latents, far, core_packs, core_near), 1)]
     pairs = [near, far, core_near, core_far]
 
@@ -471,7 +473,7 @@
         16,
     )
     tables = [node_full] + neighbour_rows(right, left, coarse, halo)
-    edge_late_d = swap(after(edge_late_x, *tables[1:]), 1)
+    edge_late_d = swap(after(edge_late_x, right), 1)
     edge_own, incoming = call(
         functools.partial(late_edge_kernel, len(tables), late_pack),
         [own_edge, full_node],
@@ -489,7 +491,7 @@
         "layer_1_edges",
         16,
     )
-    node_late_d = swap(after(node_late_x, right), 1)
+    node_late_d = swap(after(node_late_x, *tables[1:]), 1)
     (node_own,) = call(
         functools.partial(late_node_kernel, late_pack + edge_pack),
         [own_node],

time: 59.9 us -> 58.5 us (0.977)
  Pallas kernels: 19.1 us -> 16.9 us
  starting transfers between devices: 20 us -> 21.9 us
  waiting for transfers between devices: 19.8 us -> 18.6 us
    ppermute x6, waiting for transfers between devices: 6.5 us -> 3.78 us  [shift(): return lax.ppermute(x, 'graph', [(i, (i + by) % size) for i in range(size)])]
    ppermute x11, waiting for transfers between devices: 12.2 us -> 14.5 us  [swap(): return lax.ppermute(x, 'mp', [(i, i ^ mask) for i in range(size)])]
    pallas_call x7, Pallas kernels: 19.1 us -> 16.9 us  [call(): pl.pallas_call(kernel, out_shape=out_shape, in_specs=[pl.BlockSpec(memory...]
    ppermute x11, starting transfers between devices: 7.37 us -> 9.12 us  [swap(): return lax.ppermute(x, 'mp', [(i, i ^ mask) for i in range(size)])]
    ppermute x1, waiting for transfers between devices: 1.01 us -> 0.26 us  [on_device(): far = lax.ppermute(near, 'groups', [(0, 1), (1, 0)])]
  transfers between devices with their start and end apart: 18 -> 18, of which waited for: 7 -> 9; matrix products, arithmetic and copies ran while one was open for 0% -> 0% of each run, Pallas kernels for 26% -> 23%
where the time goes in v13:
time: 58.5 us; the launch traced here: 58.3 us
  starting transfers between devices  21.9 us (37%)
  waiting for transfers between devices  18.6 us (32%)
  Pallas kernels  16.9 us (29%)
  between operations  0.82 us (1%)
    pallas_call x7, Pallas kernels, call(): pl.pallas_call(kernel, out_shape=out_shape, in_specs=[pl.BlockSpec(memory...  16.9 us
    ppermute x11, waiting for transfers between devices, swap(): return lax.ppermute(x, 'mp', [(i, i ^ mask) for i in range(size)])  14.5 us
    ppermute x6, starting transfers between devices, shift(): return lax.ppermute(x, 'graph', [(i, (i + by) % size) for i in range(size)])  11.3 us
    ppermute x11, starting transfers between devices, swap(): return lax.ppermute(x, 'mp', [(i, i ^ mask) for i in range(size)])  9.12 us
    ppermute x6, waiting for transfers between devices, shift(): return lax.ppermute(x, 'graph', [(i, (i + by) % size) for i in range(size)])  3.78 us
    ppermute x1, starting transfers between devices, on_device(): far = lax.ppermute(near, 'groups', [(0, 1), (1, 0)])  1.52 us
  transfers between devices with their start and end apart: 18, of which 9 were waited for; matrix products, arithmetic and copies ran while one was open for 0% of the time, Pallas kernels for 23%

profile of v13, /device:TPU:0, one launch (start us, length us, event | category | flops | bytes accessed | tf_op | source)
XLA Modules:
  0.0 58.3 jit_solution(12035500501850375502)
XLA Ops:
  0.7 2.0 %layer_0_half.1 = bf16[1792,128]{1,0:T(8,128)(2,1)} custom-call(bf16[2,1536,128]{2,1,0:T(8,128)(2,1)} %ef.3, bf16[2,128,512]{2,1,0:T(8,128)(2,1)} %es.3, bf16[2,1024,128]{2,1,0:T(8,128)(2,1)} %nf.3, bf16[2,128,512]{2,1,0:T(8,128)(2,1)} %ns.3), custom_call_target="tpu_custom_call" | custom-call | tf_op jit(solution)/shard_map/layer_0_half/pallas_call | solution.py:309
  2.8 3.0 %collective-permute-start.3 = (bf16[1792,128]{1,0:T(8,128)(2,1)}, bf16[1792,128]{1,0:T(8,128)(2,1)S(1)}, u32[]{:S(2)}, u32[]{:S(2)}) collective-permute-start(bf16[1792,128]{1,0:T(8,128)(2,1)} %layer_0_half.1), channel_id=1, source_target_pairs={{0,2},{1,3},{2,0},{3,1},{4,6},{5,7},{6,4},{7,5},{8,10},{9,11},{10,... | collective-permute-start | bytes 1376264 | tf_op jit(solution)/shard_map/ppermute | solution.py:323
  6.1 2.7 %collective-permute-start.2 = (bf16[16,128]{1,0:T(8,128)(2,1)S(1)}, bf16[16,128]{1,0:T(8,128)(2,1)S(1)}, u32[]{:S(2)}, u32[]{:S(2)}) collective-permute-start(bf16[16,128]{1,0:T(8,128)(2,1)S(1)} %get-tuple-element.34), channel_id=1, source_target_pairs={{0,8},{4,12},{8,0},{12,4},{1,9},{5,13},{9,1},{13,5},{2,10},{6,14},... | collective-permute-start | bytes 12296 | tf_op jit(solution)/shard_map/ppermute | solution.py:328
  8.7 1.6 %collective-permute-start = (bf16[48,128]{1,0:T(8,128)(2,1)S(1)}, bf16[48,128]{1,0:T(8,128)(2,1)S(1)}, u32[]{:S(2)}, u32[]{:S(2)}) collective-permute-start(bf16[48,128]{1,0:T(8,128)(2,1)S(1)} %get-tuple-element.32), channel_id=1, source_target_pairs={{0,4},{4,8},{8,12},{12,0},{1,5},{5,9},{9,13},{13,1},{2,6},{6,10},{... | collective-permute-start | bytes 36872 | tf_op jit(solution)/shard_map/ppermute | solution.py:328
  10.3 2.2 %collective-permute-start.1 = (bf16[48,128]{1,0:T(8,128)(2,1)S(1)}, bf16[48,128]{1,0:T(8,128)(2,1)S(1)}, u32[]{:S(2)}, u32[]{:S(2)}) collective-permute-start(bf16[48,128]{1,0:T(8,128)(2,1)S(1)} %get-tuple-element.33), channel_id=1, source_target_pairs={{0,12},{4,0},{8,4},{12,8},{1,13},{5,1},{9,5},{13,9},{2,14},{6,2},{... | collective-permute-start | bytes 36872 | tf_op jit(solution)/shard_map/ppermute | solution.py:328
  12.6 1.6 %collective-permute-done.refs_2_ = bf16[48,128]{1,0:T(8,128)(2,1)S(1)} collective-permute-done((bf16[48,128]{1,0:T(8,128)(2,1)S(1)}, bf16[48,128]{1,0:T(8,128)(2,1)S(1)}, u32[]{:S(2)}, u32[]{:S(2)}) %collective-permute-start) | collective-permute-done | bytes 12320 | tf_op jit(solution)/shard_map/ppermute | solution.py:328
  14.3 2.2 %one_hot.1 = (bf16[1536,512]{1,0:T(8,128)(2,1)S(1)}, bf16[192,1536]{1,0:T(8,128)(2,1)S(1)}, bf16[112,192]{1,0:T(8,128)(2,1)S(1)}, bf16[7168,128]{1,0:T(8,128)(2,...) custom-call(s32[1,3136]{1,0:T(1,128)S(1)} %broadcast_in_dim.6.list_ref, ...), custom_call_target="tpu_custom_call" | custom-call | tf_op jit(solution)/shard_map/one_hot/pallas_call | solution.py:309
  16.6 0.5 collective-permute-start.8
  17.2 1.7 %collective-permute-start.5 = (bf16[1840,128]{1,0:T(8,128)(2,1)S(1)}, bf16[1840,128]{1,0:T(8,128)(2,1)S(1)}, u32[]{:S(2)}, u32[]{:S(2)}) collective-permute-start(bf16[1840,128]{1,0:T(8,128)(2,1)S(1)} %latents.1.refs_6_), channel_id=1, source_target_pairs={{0,2},{1,3},{2,0},{3,1},{4,6},{5,7},{6,4},{7,5},{8,10},{9,11},{10,... | collective-permute-start | bytes 1413128 | tf_op jit(solution)/shard_map/ppermute | solution.py:323
  18.9 1.5 %collective-permute-start.7 = (bf16[1792,128]{1,0:T(8,128)(2,1)S(1)}, bf16[1792,128]{1,0:T(8,128)(2,1)S(1)}, u32[]{:S(2)}, u32[]{:S(2)}) collective-permute-start(bf16[1792,128]{1,0:T(8,128)(2,1)S(1)} %collective-permute-done.3.refs_2_), channel_id=1, source_target_pairs={{0,16},{16,0},{1,17},{17,1},{2,18},{18,2},{3,19},{19,3},{4,20},{20... | collective-permute-start | bytes 1376264 | tf_op jit(solution)/shard_map/ppermute | solution.py:422
  20.4 0.6 %collective-permute-done.8.refs_7_ = bf16[1840,128]{1,0:T(8,128)(2,1)S(1)} collective-permute-done((bf16[1840,128]{1,0:T(8,128)(2,1)S(1)}, bf16[1840,128]{1,0:T(8,128)(2,1)S(1)}, u32[]{:S(2)}, u32[]{:S(2)}) %collective-permute-start.8) | collective-permute-done | bytes 471072 | tf_op jit(solution)/shard_map/ppermute | solution.py:323
  21.2 1.7 %collective-permute-start.16 = (bf16[2048,128]{1,0:T(8,128)(2,1)S(1)}, bf16[2048,128]{1,0:T(8,128)(2,1)S(1)}, u32[]{:S(2)}, u32[]{:S(2)}) collective-permute-start(bf16[2048,128]{1,0:T(8,128)(2,1)S(1)} %get-tuple-element.54), channel_id=1, source_target_pairs={{0,2},{1,3},{2,0},{3,1},{4,6},{5,7},{6,4},{7,5},{8,10},{9,11},{10,... | collective-permute-start | bytes 1572872 | tf_op jit(solution)/shard_map/ppermute | solution.py:323
  22.9 8.0 %collective-permute-done.5.refs_8_ = bf16[1840,128]{1,0:T(8,128)(2,1)S(1)} collective-permute-done((bf16[1840,128]{1,0:T(8,128)(2,1)S(1)}, bf16[1840,128]{1,0:T(8,128)(2,1)S(1)}, u32[]{:S(2)}, u32[]{:S(2)}) %collective-permute-start.5) | collective-permute-done | bytes 471072 | tf_op jit(solution)/shard_map/ppermute | solution.py:323
  31.1 0.5 collective-permute-start.10
  31.6 1.5 %collective-permute-start.6 = (bf16[1536,128]{1,0:T(8,128)(2,1)S(1)}, bf16[1536,128]{1,0:T(8,128)(2,1)S(1)}, u32[]{:S(2)}, u32[]{:S(2)}) collective-permute-start(bf16[1536,128]{1,0:T(8,128)(2,1)S(1)} %get-tuple-element.40), channel_id=1, source_target_pairs={{0,2},{1,3},{2,0},{3,1},{4,6},{5,7},{6,4},{7,5},{8,10},{9,11},{10,... | collective-permute-start | bytes 1179656 | tf_op jit(solution)/shard_map/ppermute | solution.py:323
  33.6 5.8 %layer_0.1 = (f32[1536,128]{1,0:T(8,128)S(1)}, bf16[1536,512]{1,0:T(8,128)(2,1)S(1)}, f32[192,128]{1,0:T(8,128)S(1)}, bf16[192,512]{1,0:T(8,128)(2,1)S(1)}, bf16...) custom-call(bf16[7168,128]{1,0:T(8,128)(2,1)S(1)} %get-tuple-element.38.refs_0_, ...), custom_call_target="tpu_custom_call" | custom-call | tf_op jit(solution)/shard_map/layer_0/pallas_call | solution.py:309
  39.4 2.6 %collective-permute-done.16.refs_2_ = bf16[2048,128]{1,0:T(8,128)(2,1)S(1)} collective-permute-done((bf16[2048,128]{1,0:T(8,128)(2,1)S(1)}, bf16[2048,128]{1,0:T(8,128)(2,1)S(1)}, u32[]{:S(2)}, u32[]{:S(2)}) %collective-permute-start.16) | collective-permute-done | bytes 524320 | tf_op jit(solution)/shard_map/ppermute | solution.py:323
  42.1 3.8 %collective-permute-start.13 = (bf16[48,512]{1,0:T(8,128)(2,1)S(1)}, bf16[48,512]{1,0:T(8,128)(2,1)S(1)}, u32[]{:S(2)}, u32[]{:S(2)}) collective-permute-start(bf16[48,512]{1,0:T(8,128)(2,1)S(1)} %get-tuple-element.48), channel_id=1, source_target_pairs={{0,12},{4,0},{8,4},{12,8},{1,13},{5,1},{9,5},{13,9},{2,14},{6,2},{... | collective-permute-start | bytes 147464 | tf_op jit(solution)/shard_map/ppermute | solution.py:328
  45.9 1.0 %collective-permute-start.14 = (bf16[16,512]{1,0:T(8,128)(2,1)S(1)}, bf16[16,512]{1,0:T(8,128)(2,1)S(1)}, u32[]{:S(2)}, u32[]{:S(2)}) collective-permute-start(bf16[16,512]{1,0:T(8,128)(2,1)S(1)} %get-tuple-element.49), channel_id=1, source_target_pairs={{0,8},{4,12},{8,0},{12,4},{1,9},{5,13},{9,1},{13,5},{2,10},{6,14},... | collective-permute-start | bytes 49160 | tf_op jit(solution)/shard_map/ppermute | solution.py:328
  46.9 2.7 %collective-permute-done.6.refs_2_ = bf16[1536,128]{1,0:T(8,128)(2,1)S(1)} collective-permute-done((bf16[1536,128]{1,0:T(8,128)(2,1)S(1)}, bf16[1536,128]{1,0:T(8,128)(2,1)S(1)}, u32[]{:S(2)}, u32[]{:S(2)}) %collective-permute-start.6) | collective-permute-done | bytes 393248 | tf_op jit(solution)/shard_map/ppermute | solution.py:323
  49.6 0.9 %collective-permute-done.14.refs_9_ = bf16[16,512]{1,0:T(8,128)(2,1)S(1)} collective-permute-done((bf16[16,512]{1,0:T(8,128)(2,1)S(1)}, bf16[16,512]{1,0:T(8,128)(2,1)S(1)}, u32[]{:S(2)}, u32[]{:S(2)}) %collective-permute-start.14) | collective-permute-done | bytes 16416 | tf_op jit(solution)/shard_map/ppermute | solution.py:328
  50.5 1.2 %collective-permute-done.12.refs_7_ = bf16[48,512]{1,0:T(8,128)(2,1)S(1)} collective-permute-done((bf16[48,512]{1,0:T(8,128)(2,1)S(1)}, bf16[48,512]{1,0:T(8,128)(2,1)S(1)}, u32[]{:S(2)}, u32[]{:S(2)}) %collective-permute-start.12) | collective-permute-done | bytes 49184 | tf_op jit(solution)/shard_map/ppermute | solution.py:328
  51.8 5.0 %layer_1_edges.1 = (f32[1536,128]{1,0:T(8,128)}, bf16[192,512]{1,0:T(8,128)(2,1)S(1)}) custom-call(bf16[7168,128]{1,0:T(8,128)(2,1)S(1)} %get-tuple-element.38.refs_0_, bf16[7168,128]{1,0:T(8,128)(2,1)S(1)} %collective-permute-done.4.refs_1_, bf16[2048,128]{1,0:T(8,128)(2,1)S(1)} %collective-permute-done.16.refs_2_, ...), custom_call_target="tpu_custom_call" | custom-call | tf_op jit(solution)/shard_map/layer_1_edges/pallas_call | solution.py:309
  56.8 1.5 %layer_1_nodes.1 = f32[192,128]{1,0:T(8,128)} custom-call(bf16[7168,128]{1,0:T(8,128)(2,1)S(1)} %get-tuple-element.38.refs_0_, bf16[7168,128]{1,0:T(8,128)(2,1)S(1)} %collective-permute-done.4.refs_1_, bf16[1536,128]{1,0:T(8,128)(2,1)S(1)} %collective-permute-done.6.refs_2_, bf16[1536,128]{1,0:T(8,128)(2,1)S(1)} %collective-permute-done.15.refs_3_, ...), custom_call_target="tpu_custom_call" | custom-call | tf_op jit(solution)/shard_map/layer_1_nodes/pallas_call | solution.py:309
  (39 shorter events, 1.4 us)
Async XLA Ops:
  0.6 13.6 %copy-start.4 = (bf16[2,128,512]{2,1,0:T(8,128)(2,1)S(1)}, bf16[2,128,512]{2,1,0:T(8,128)(2,1)}, u32[]{:S(2)}) copy-start(bf16[2,128,512]{2,1,0:T(8,128)(2,1)} %ns.3) | copy-start | bytes 786436
  0.6 13.6 %copy-start.2 = (bf16[2,1024,128]{2,1,0:T(8,128)(2,1)S(1)}, bf16[2,1024,128]{2,1,0:T(8,128)(2,1)}, u32[]{:S(2)}) copy-start(bf16[2,1024,128]{2,1,0:T(8,128)(2,1)} %nf.3) | copy-start | bytes 1572868
  0.7 13.6 %copy-start.3 = (bf16[2,128,512]{2,1,0:T(8,128)(2,1)S(1)}, bf16[2,128,512]{2,1,0:T(8,128)(2,1)}, u32[]{:S(2)}) copy-start(bf16[2,128,512]{2,1,0:T(8,128)(2,1)} %es.3) | copy-start | bytes 786436
  0.7 13.6 %copy-start = (bf16[2,1536,128]{2,1,0:T(8,128)(2,1)S(1)}, bf16[2,1536,128]{2,1,0:T(8,128)(2,1)}, u32[]{:S(2)}) copy-start(bf16[2,1536,128]{2,1,0:T(8,128)(2,1)} %ef.3) | copy-start | bytes 2359300
  0.7 11.9 %copy-start.7 = (s32[1536]{0:T(1024)S(1)}, s32[1536]{0:T(1024)}, u32[]{:S(2)}) copy-start(s32[1536]{0:T(1024)} %param.16) | copy-start | bytes 18436
  0.7 15.9 %copy-start.1 = (f32[1536,128]{1,0:T(8,128)S(1)}, f32[1536,128]{1,0:T(8,128)}, u32[]{:S(2)}) copy-start(f32[1536,128]{1,0:T(8,128)} %refs_10_.1) | copy-start | bytes 2359300
  2.8 13.7 %collective-permute-start.3 = (bf16[1792,128]{1,0:T(8,128)(2,1)}, bf16[1792,128]{1,0:T(8,128)(2,1)S(1)}, u32[]{:S(2)}, u32[]{:S(2)}) collective-permute-start(bf16[1792,128]{1,0:T(8,128)(2,1)} %layer_0_half.1), channel_id=1, source_target_pairs={{0,2},{1,3},{2,0},{3,1},{4,6},{5,7},{6,4},{7,5},{8,10},{9,11},{10,... | collective-permute-start | bytes 1376264 | tf_op jit(solution)/shard_map/ppermute | solution.py:323
  6.1 6.5 %collective-permute-start.2 = (bf16[16,128]{1,0:T(8,128)(2,1)S(1)}, bf16[16,128]{1,0:T(8,128)(2,1)S(1)}, u32[]{:S(2)}, u32[]{:S(2)}) collective-permute-start(bf16[16,128]{1,0:T(8,128)(2,1)S(1)} %get-tuple-element.34), channel_id=1, source_target_pairs={{0,8},{4,12},{8,0},{12,4},{1,9},{5,13},{9,1},{13,5},{2,10},{6,14},... | collective-permute-start | bytes 12296 | tf_op jit(solution)/shard_map/ppermute | solution.py:328
  8.7 5.5 %collective-permute-start = (bf16[48,128]{1,0:T(8,128)(2,1)S(1)}, bf16[48,128]{1,0:T(8,128)(2,1)S(1)}, u32[]{:S(2)}, u32[]{:S(2)}) collective-permute-start(bf16[48,128]{1,0:T(8,128)(2,1)S(1)} %get-tuple-element.32), channel_id=1, source_target_pairs={{0,4},{4,8},{8,12},{12,0},{1,5},{5,9},{9,13},{13,1},{2,6},{6,10},{... | collective-permute-start | bytes 36872 | tf_op jit(solution)/shard_map/ppermute | solution.py:328
  10.3 3.9 %collective-permute-start.1 = (bf16[48,128]{1,0:T(8,128)(2,1)S(1)}, bf16[48,128]{1,0:T(8,128)(2,1)S(1)}, u32[]{:S(2)}, u32[]{:S(2)}) collective-permute-start(bf16[48,128]{1,0:T(8,128)(2,1)S(1)} %get-tuple-element.33), channel_id=1, source_target_pairs={{0,12},{4,0},{8,4},{12,8},{1,13},{5,1},{9,5},{13,9},{2,14},{6,2},{... | collective-permute-start | bytes 36872 | tf_op jit(solution)/shard_map/ppermute | solution.py:328
  16.5 14.6 %collective-permute-start.4 = (bf16[7168,128]{1,0:T(8,128)(2,1)S(1)}, bf16[7168,128]{1,0:T(8,128)(2,1)S(1)}, u32[]{:S(2)}, u32[]{:S(2)}) collective-permute-start(bf16[7168,128]{1,0:T(8,128)(2,1)S(1)} %get-tuple-element.38.refs_0_), channel_id=1, source_target_pairs={{0,1},{1,0},{2,3},{3,2},{4,5},{5,4},{6,7},{7,6},{8,9},{9,8},{10,11... | collective-permute-start | bytes 5505032 | tf_op jit(solution)/shard_map/ppermute | solution.py:323
  16.6 4.4 %collective-permute-start.8 = (bf16[1840,128]{1,0:T(8,128)(2,1)S(1)}, bf16[1840,128]{1,0:T(8,128)(2,1)S(1)}, u32[]{:S(2)}, u32[]{:S(2)}) collective-permute-start(bf16[1840,128]{1,0:T(8,128)(2,1)S(1)} %latents.1.refs_6_), channel_id=1, source_target_pairs={{0,1},{1,0},{2,3},{3,2},{4,5},{5,4},{6,7},{7,6},{8,9},{9,8},{10,11... | collective-permute-start | bytes 1413128 | tf_op jit(solution)/shard_map/ppermute | solution.py:323
  17.2 13.6 %collective-permute-start.5 = (bf16[1840,128]{1,0:T(8,128)(2,1)S(1)}, bf16[1840,128]{1,0:T(8,128)(2,1)S(1)}, u32[]{:S(2)}, u32[]{:S(2)}) collective-permute-start(bf16[1840,128]{1,0:T(8,128)(2,1)S(1)} %latents.1.refs_6_), channel_id=1, source_target_pairs={{0,2},{1,3},{2,0},{3,1},{4,6},{5,7},{6,4},{7,5},{8,10},{9,11},{10,... | collective-permute-start | bytes 1413128 | tf_op jit(solution)/shard_map/ppermute | solution.py:323
  18.9 12.2 %collective-permute-start.7 = (bf16[1792,128]{1,0:T(8,128)(2,1)S(1)}, bf16[1792,128]{1,0:T(8,128)(2,1)S(1)}, u32[]{:S(2)}, u32[]{:S(2)}) collective-permute-start(bf16[1792,128]{1,0:T(8,128)(2,1)S(1)} %collective-permute-done.3.refs_2_), channel_id=1, source_target_pairs={{0,16},{16,0},{1,17},{17,1},{2,18},{18,2},{3,19},{19,3},{4,20},{20... | collective-permute-start | bytes 1376264 | tf_op jit(solution)/shard_map/ppermute | solution.py:422
  21.0 10.1 %collective-permute-start.9 = (bf16[1792,128]{1,0:T(8,128)(2,1)S(1)}, bf16[1792,128]{1,0:T(8,128)(2,1)S(1)}, u32[]{:S(2)}, u32[]{:S(2)}) collective-permute-start(bf16[1792,128]{1,0:T(8,128)(2,1)S(1)} %collective-permute-done.3.refs_2_), channel_id=1, source_target_pairs={{0,1},{1,0},{2,3},{3,2},{4,5},{5,4},{6,7},{7,6},{8,9},{9,8},{10,11... | collective-permute-start | bytes 1376264 | tf_op jit(solution)/shard_map/ppermute | solution.py:323
  21.2 20.9 %collective-permute-start.16 = (bf16[2048,128]{1,0:T(8,128)(2,1)S(1)}, bf16[2048,128]{1,0:T(8,128)(2,1)S(1)}, u32[]{:S(2)}, u32[]{:S(2)}) collective-permute-start(bf16[2048,128]{1,0:T(8,128)(2,1)S(1)} %get-tuple-element.54), channel_id=1, source_target_pairs={{0,2},{1,3},{2,0},{3,1},{4,6},{5,7},{6,4},{7,5},{8,10},{9,11},{10,... | collective-permute-start | bytes 1572872 | tf_op jit(solution)/shard_map/ppermute | solution.py:323
  31.1 2.5 %collective-permute-start.11 = (bf16[1840,128]{1,0:T(8,128)(2,1)S(1)}, bf16[1840,128]{1,0:T(8,128)(2,1)S(1)}, u32[]{:S(2)}, u32[]{:S(2)}) collective-permute-start(bf16[1840,128]{1,0:T(8,128)(2,1)S(1)} %collective-permute-done.5.refs_8_), channel_id=1, source_target_pairs={{0,1},{1,0},{2,3},{3,2},{4,5},{5,4},{6,7},{7,6},{8,9},{9,8},{10,11... | collective-permute-start | bytes 1413128 | tf_op jit(solution)/shard_map/ppermute | solution.py:323
  31.1 2.5 %collective-permute-start.10 = (bf16[1792,128]{1,0:T(8,128)(2,1)S(1)}, bf16[1792,128]{1,0:T(8,128)(2,1)S(1)}, u32[]{:S(2)}, u32[]{:S(2)}) collective-permute-start(bf16[1792,128]{1,0:T(8,128)(2,1)S(1)} %collective-permute-done.7.refs_3_), channel_id=1, source_target_pairs={{0,1},{1,0},{2,3},{3,2},{4,5},{5,4},{6,7},{7,6},{8,9},{9,8},{10,11... | collective-permute-start | bytes 1376264 | tf_op jit(solution)/shard_map/ppermute | solution.py:323
  31.6 18.0 %collective-permute-start.6 = (bf16[1536,128]{1,0:T(8,128)(2,1)S(1)}, bf16[1536,128]{1,0:T(8,128)(2,1)S(1)}, u32[]{:S(2)}, u32[]{:S(2)}) collective-permute-start(bf16[1536,128]{1,0:T(8,128)(2,1)S(1)} %get-tuple-element.40), channel_id=1, source_target_pairs={{0,2},{1,3},{2,0},{3,1},{4,6},{5,7},{6,4},{7,5},{8,10},{9,11},{10,... | collective-permute-start | bytes 1179656 | tf_op jit(solution)/shard_map/ppermute | solution.py:323
  42.1 9.7 %collective-permute-start.17 = (bf16[2048,128]{1,0:T(8,128)(2,1)S(1)}, bf16[2048,128]{1,0:T(8,128)(2,1)S(1)}, u32[]{:S(2)}, u32[]{:S(2)}) collective-permute-start(bf16[2048,128]{1,0:T(8,128)(2,1)S(1)} %collective-permute-done.16.refs_2_), channel_id=1, source_target_pairs={{0,1},{1,0},{2,3},{3,2},{4,5},{5,4},{6,7},{7,6},{8,9},{9,8},{10,11... | collective-permute-start | bytes 1572872 | tf_op jit(solution)/shard_map/ppermute | solution.py:323
  42.1 8.5 %collective-permute-start.13 = (bf16[48,512]{1,0:T(8,128)(2,1)S(1)}, bf16[48,512]{1,0:T(8,128)(2,1)S(1)}, u32[]{:S(2)}, u32[]{:S(2)}) collective-permute-start(bf16[48,512]{1,0:T(8,128)(2,1)S(1)} %get-tuple-element.48), channel_id=1, source_target_pairs={{0,12},{4,0},{8,4},{12,8},{1,13},{5,1},{9,5},{13,9},{2,14},{6,2},{... | collective-permute-start | bytes 147464 | tf_op jit(solution)/shard_map/ppermute | solution.py:328
  45.9 5.9 %collective-permute-start.12 = (bf16[48,512]{1,0:T(8,128)(2,1)S(1)}, bf16[48,512]{1,0:T(8,128)(2,1)S(1)}, u32[]{:S(2)}, u32[]{:S(2)}) collective-permute-start(bf16[48,512]{1,0:T(8,128)(2,1)S(1)} %get-tuple-element.47), channel_id=1, source_target_pairs={{0,4},{4,8},{8,12},{12,0},{1,5},{5,9},{9,13},{13,1},{2,6},{6,10},{... | collective-permute-start | bytes 147464 | tf_op jit(solution)/shard_map/ppermute | solution.py:328
  45.9 4.6 %collective-permute-start.14 = (bf16[16,512]{1,0:T(8,128)(2,1)S(1)}, bf16[16,512]{1,0:T(8,128)(2,1)S(1)}, u32[]{:S(2)}, u32[]{:S(2)}) collective-permute-start(bf16[16,512]{1,0:T(8,128)(2,1)S(1)} %get-tuple-element.49), channel_id=1, source_target_pairs={{0,8},{4,12},{8,0},{12,4},{1,9},{5,13},{9,1},{13,5},{2,10},{6,14},... | collective-permute-start | bytes 49160 | tf_op jit(solution)/shard_map/ppermute | solution.py:328
  51.8 5.1 %collective-permute-start.15 = (bf16[1536,128]{1,0:T(8,128)(2,1)S(1)}, bf16[1536,128]{1,0:T(8,128)(2,1)S(1)}, u32[]{:S(2)}, u32[]{:S(2)}) collective-permute-start(bf16[1536,128]{1,0:T(8,128)(2,1)S(1)} %collective-permute-done.6.refs_2_), channel_id=1, source_target_pairs={{0,1},{1,0},{2,3},{3,2},{4,5},{5,4},{6,7},{7,6},{8,9},{9,8},{10,11... | collective-permute-start | bytes 1179656 | tf_op jit(solution)/shard_map/ppermute | solution.py:323
  (3 other events, 22.1 us)

commit v14 on v13

--- a/solution.py
+++ b/solution.py
@@ -10,7 +10,7 @@
 COARSE_DEV = 12
 COARSE_PAD = 16
 EPS = 1e-05
-TILE = 512
+TILE = 768
 HOT_TILE = 256
 F32 = jnp.float32
 BF16 = jnp.bfloat16
@@ -137,10 +137,8 @@
         pick_out[at : at + COARSE_PAD, :] = coarse
 
 
-def prepare_kernel(blocks, halo, table_rows, list_ref, ef, es, nf, ns, hot_out, incidence_out, pick_out, pack_out, edge_late, node_late, sems):
+def pack_kernel(ef, es, nf, ns, pack_out, edge_late, node_late, sems):
     part, features = es.shape[1:]
-    edge_count, lanes_all = hot_out.shape
-    node_count = incidence_out.shape[0]
     copies = Copies(sems)
 
     def pack(first, second, layer, out, at):
@@ -157,6 +155,12 @@
         end = pack(nf, ns, layer, pack_out, pack(ef, es, layer, pack_out, end))
     pack(ef, es, 1, edge_late, 0)
     pack(nf, ns, 1, node_late, 0)
+    copies.wait()
+
+
+def prepare_kernel(blocks, halo, table_rows, list_ref, hot_out, incidence_out, pick_out):
+    edge_count, lanes_all = hot_out.shape
+    node_count = incidence_out.shape[0]
     for at in range(0, edge_count, HOT_TILE):
         senders = table_index(list_ref[:, at : at + HOT_TILE], blocks, node_count, halo)
         receivers = list_ref[:, edge_count + at : edge_count + at + HOT_TILE]
@@ -166,7 +170,6 @@
         node_ids = lax.broadcasted_iota(jnp.int32, (node_count, HOT_TILE), 0)
         incidence_out[:, at : at + HOT_TILE] = one_hot(node_ids == receivers)
     make_pick(list_ref[:, 2 * edge_count : 2 * edge_count + 2 * halo], pick_out)
-    copies.wait()
 
 
 def pick_rows(pick_ref, node_bf, outs):
@@ -177,8 +180,8 @@
         start += out.shape[0]
 
 
-def start_kernel(node_ref, boundary_ref, right, left, coarse, pick_ref):
-    make_pick(boundary_ref[...], pick_ref)
+def start_kernel(at, node_ref, list_ref, right, left, coarse, pick_ref):
+    make_pick(list_ref[:, at:], pick_ref)
     pick_rows(pick_ref, node_ref[...].astype(BF16), (right, left, coarse))
 
 
@@ -400,10 +403,11 @@
     far_rows = 2 * wide + COARSE_PAD if blocks == 4 else 2 * halo + blocks * COARSE_PAD
     table_rows = node_count + far_rows
     lanes = -(-(table_rows + node_count) // 128) * 128
+    lists = jnp.concatenate([senders, receivers, boundary_rows])[None, :]
     right, left, coarse = call(
-        start_kernel,
+        functools.partial(start_kernel, 2 * edge_count),
         sent(part),
-        [(VMEM, after(node_state, ride)), (VMEM, boundary_rows[None, :])],
+        [(VMEM, after(node_state, ride)), (VMEM, lists)],
         [pltpu.VMEM((2 * wide + COARSE_PAD, node_count), BF16)],
         0,
         "boundary_rows",
@@ -421,26 +425,30 @@
     far_latents = swap(latents, 2)
     far = lax.ppermute(near, "groups", [(0, 1), (1, 0)])
     core_latents = swap(latents, 1)
-    lists = jnp.concatenate([senders, receivers, boundary_rows])[None, :]
-    hot, incidence, pick, packs, edge_late, node_late = call(
+    packs, edge_late, node_late = call(
+        pack_kernel,
+        [shape((n, part), BF16) for n in (2 * late_pack, edge_pack, node_pack)],
+        [(ANY, after(weights[0], *rows))] + [(ANY, w) for w in weights[1:]],
+        [dma((32,))],
+        0,
+        "packed_weights",
+    )
+    core_packs = swap(after(packs, near), 1)
+    hot, incidence, pick = call(
         functools.partial(prepare_kernel, blocks, halo, table_rows),
         [
             shape((edge_count, lanes), BF16),
             shape((node_count, edge_count), BF16),
             shape((2 * wide + COARSE_PAD, node_count), BF16),
-            shape((2 * late_pack, part), BF16),
-            shape((edge_pack, part), BF16),
-            shape((node_pack, part), BF16),
         ],
-        [(VMEM, after(lists, *rows))] + [(ANY, w) for w in weights],
-        [dma((32,))],
+        [(VMEM, after(lists, core_latents))],
+        [],
         0,
         "one_hot",
     )
-    core_packs = swap(after(packs, near), 1)
     core_near = swap(after(near, core_latents), 1)
     core_far = swap(after(far, core_packs), 1)
-    edge_late_x = swap(after(edge_late, core_latents), 2)
+    edge_late_x = swap(after(edge_late, core_latents, hot), 2)
     node_late_x = swap(after(node_late, far_latents), 2)
     shards = [latents, core_latents, far_latents, swap(after(far_latents, far, core_packs, core_near), 1)]
     pairs = [near, far, core_near, core_far]

time: 58.5 us -> 58.4 us (level)
  waiting for transfers between devices: 18.6 us -> 20.3 us
  starting transfers between devices: 21.9 us -> 20.3 us
    ppermute x6, waiting for transfers between devices: 3.78 us -> 5.91 us  [shift(): return lax.ppermute(x, 'graph', [(i, (i + by) % size) for i in range(size)])]
    ppermute x6, starting transfers between devices: 11.3 us -> 9.53 us  [shift(): return lax.ppermute(x, 'graph', [(i, (i + by) % size) for i in range(size)])]
    pallas_call x7 -> x8, Pallas kernels: 16.9 us -> 16.7 us  [call(): pl.pallas_call(kernel, out_shape=out_shape, in_specs=[pl.BlockSpec(memory...]
  transfers between devices with their start and end apart: 18 -> 18, of which waited for: 9 -> 10; matrix products, arithmetic and copies ran while one was open for 0% -> 0% of each run, Pallas kernels for 23% -> 23%
where the time goes in v14:
time: 58.4 us; the launch traced here: 58.2 us
  starting transfers between devices  20.3 us (35%)
  waiting for transfers between devices  20.3 us (35%)
  Pallas kernels  16.7 us (29%)
  between operations  0.82 us (1%)
    pallas_call x8, Pallas kernels, call(): pl.pallas_call(kernel, out_shape=out_shape, in_specs=[pl.BlockSpec(memory...  16.7 us
    ppermute x11, waiting for transfers between devices, swap(): return lax.ppermute(x, 'mp', [(i, i ^ mask) for i in range(size)])  14 us
    ppermute x6, starting transfers between devices, shift(): return lax.ppermute(x, 'graph', [(i, (i + by) % size) for i in range(size)])  9.53 us
    ppermute x11, starting transfers between devices, swap(): return lax.ppermute(x, 'mp', [(i, i ^ mask) for i in range(size)])  9.27 us
    ppermute x6, waiting for transfers between devices, shift(): return lax.ppermute(x, 'graph', [(i, (i + by) % size) for i in range(size)])  5.91 us
    ppermute x1, starting transfers between devices, on_device(): far = lax.ppermute(near, 'groups', [(0, 1), (1, 0)])  1.52 us
  transfers between devices with their start and end apart: 18, of which 10 were waited for; matrix products, arithmetic and copies ran while one was open for 0% of the time, Pallas kernels for 23%

profile of v14, /device:TPU:0, one launch (start us, length us, event | category | flops | bytes accessed | tf_op | source)
XLA Modules:
  0.0 58.2 jit_solution(12392083642519653819)
XLA Ops:
  0.7 2.0 %layer_0_half.1 = bf16[1792,128]{1,0:T(8,128)(2,1)} custom-call(bf16[2,1536,128]{2,1,0:T(8,128)(2,1)} %ef.2, bf16[2,128,512]{2,1,0:T(8,128)(2,1)} %es.3, bf16[2,1024,128]{2,1,0:T(8,128)(2,1)} %nf.3, bf16[2,128,512]{2,1,0:T(8,128)(2,1)} %ns.3), custom_call_target="tpu_custom_call" | custom-call | tf_op jit(solution)/shard_map/layer_0_half/pallas_call | solution.py:312
  2.8 3.0 %collective-permute-start.3 = (bf16[1792,128]{1,0:T(8,128)(2,1)}, bf16[1792,128]{1,0:T(8,128)(2,1)S(1)}, u32[]{:S(2)}, u32[]{:S(2)}) collective-permute-start(bf16[1792,128]{1,0:T(8,128)(2,1)} %layer_0_half.1), channel_id=1, source_target_pairs={{0,2},{1,3},{2,0},{3,1},{4,6},{5,7},{6,4},{7,5},{8,10},{9,11},{10,... | collective-permute-start | bytes 1376264 | tf_op jit(solution)/shard_map/ppermute | solution.py:326
  6.1 1.6 %collective-permute-start = (bf16[48,128]{1,0:T(8,128)(2,1)S(1)}, bf16[48,128]{1,0:T(8,128)(2,1)S(1)}, u32[]{:S(2)}, u32[]{:S(2)}) collective-permute-start(bf16[48,128]{1,0:T(8,128)(2,1)S(1)} %get-tuple-element.33), channel_id=1, source_target_pairs={{0,4},{4,8},{8,12},{12,0},{1,5},{5,9},{9,13},{13,1},{2,6},{6,10},{... | collective-permute-start | bytes 36872 | tf_op jit(solution)/shard_map/ppermute | solution.py:331
  7.7 2.2 %collective-permute-start.1 = (bf16[48,128]{1,0:T(8,128)(2,1)S(1)}, bf16[48,128]{1,0:T(8,128)(2,1)S(1)}, u32[]{:S(2)}, u32[]{:S(2)}) collective-permute-start(bf16[48,128]{1,0:T(8,128)(2,1)S(1)} %get-tuple-element.34), channel_id=1, source_target_pairs={{0,12},{4,0},{8,4},{12,8},{1,13},{5,1},{9,5},{13,9},{2,14},{6,2},{... | collective-permute-start | bytes 36872 | tf_op jit(solution)/shard_map/ppermute | solution.py:331
  10.0 0.8 %collective-permute-start.2 = (bf16[16,128]{1,0:T(8,128)(2,1)S(1)}, bf16[16,128]{1,0:T(8,128)(2,1)S(1)}, u32[]{:S(2)}, u32[]{:S(2)}) collective-permute-start(bf16[16,128]{1,0:T(8,128)(2,1)S(1)} %get-tuple-element.35), channel_id=1, source_target_pairs={{0,8},{4,12},{8,0},{12,4},{1,9},{5,13},{9,1},{13,5},{2,10},{6,14},... | collective-permute-start | bytes 12296 | tf_op jit(solution)/shard_map/ppermute | solution.py:331
  10.8 3.7 %collective-permute-done.2.refs_4_ = bf16[16,128]{1,0:T(8,128)(2,1)S(1)} collective-permute-done((bf16[16,128]{1,0:T(8,128)(2,1)S(1)}, bf16[16,128]{1,0:T(8,128)(2,1)S(1)}, u32[]{:S(2)}, u32[]{:S(2)}) %collective-permute-start.2) | collective-permute-done | bytes 4128 | tf_op jit(solution)/shard_map/ppermute | solution.py:331
  14.5 1.1 %packed_weights.1 = (bf16[7168,128]{1,0:T(8,128)(2,1)S(1)}, bf16[2048,128]{1,0:T(8,128)(2,1)S(1)}, bf16[1536,128]{1,0:T(8,128)(2,1)S(1)}) custom-call(bf16[2,1536,128]{2,1,0:T(8,128)(2,1)S(1)} %copy-done, bf16[2,128,512]{2,1,0:T(8,128)(2,1)S(1)} %copy-done.3, bf16[2,1024,128]{2,1,0:T(8,128)(2,1)S(1)} %copy-done.2, bf16[2,128,512]{2,1,0:T(8,128)(2,1)S(1)} %copy-done.4), custom_call_target="tpu_custom_call" | custom-call | tf_op jit(solution)/shard_map/packed_weights/pallas_call | solution.py:312
  15.7 0.9 %collective-permute-done.3.refs_2_ = bf16[1792,128]{1,0:T(8,128)(2,1)S(1)} collective-permute-done((bf16[1792,128]{1,0:T(8,128)(2,1)}, bf16[1792,128]{1,0:T(8,128)(2,1)S(1)}, u32[]{:S(2)}, u32[]{:S(2)}) %collective-permute-start.3) | collective-permute-done | bytes 458784 | tf_op jit(solution)/shard_map/ppermute | solution.py:326
  16.6 0.6 collective-permute-start.8
  17.1 1.7 %collective-permute-start.5 = (bf16[1840,128]{1,0:T(8,128)(2,1)S(1)}, bf16[1840,128]{1,0:T(8,128)(2,1)S(1)}, u32[]{:S(2)}, u32[]{:S(2)}) collective-permute-start(bf16[1840,128]{1,0:T(8,128)(2,1)S(1)} %latents.1.refs_6_), channel_id=1, source_target_pairs={{0,2},{1,3},{2,0},{3,1},{4,6},{5,7},{6,4},{7,5},{8,10},{9,11},{10,... | collective-permute-start | bytes 1413128 | tf_op jit(solution)/shard_map/ppermute | solution.py:326
  18.9 1.5 %collective-permute-start.7 = (bf16[1792,128]{1,0:T(8,128)(2,1)S(1)}, bf16[1792,128]{1,0:T(8,128)(2,1)S(1)}, u32[]{:S(2)}, u32[]{:S(2)}) collective-permute-start(bf16[1792,128]{1,0:T(8,128)(2,1)S(1)} %collective-permute-done.3.refs_2_), channel_id=1, source_target_pairs={{0,16},{16,0},{1,17},{17,1},{2,18},{18,2},{3,19},{19,3},{4,20},{20... | collective-permute-start | bytes 1376264 | tf_op jit(solution)/shard_map/ppermute | solution.py:426
  21.1 1.1 %one_hot.1 = (bf16[1536,512]{1,0:T(8,128)(2,1)S(1)}, bf16[192,1536]{1,0:T(8,128)(2,1)S(1)}, bf16[112,192]{1,0:T(8,128)(2,1)S(1)}) custom-call(s32[1,3136]{1,0:T(1,128)S(1)} %broadcast_in_dim.3.list_ref), custom_call_target="tpu_custom_call" | custom-call | tf_op jit(solution)/shard_map/one_hot/pallas_call | solution.py:312
  22.2 1.8 %collective-permute-start.16 = (bf16[2048,128]{1,0:T(8,128)(2,1)S(1)}, bf16[2048,128]{1,0:T(8,128)(2,1)S(1)}, u32[]{:S(2)}, u32[]{:S(2)}) collective-permute-start(bf16[2048,128]{1,0:T(8,128)(2,1)S(1)} %get-tuple-element.56), channel_id=1, source_target_pairs={{0,2},{1,3},{2,0},{3,1},{4,6},{5,7},{6,4},{7,5},{8,10},{9,11},{10,... | collective-permute-start | bytes 1572872 | tf_op jit(solution)/shard_map/ppermute | solution.py:326
  24.1 6.7 %collective-permute-done.5.refs_8_ = bf16[1840,128]{1,0:T(8,128)(2,1)S(1)} collective-permute-done((bf16[1840,128]{1,0:T(8,128)(2,1)S(1)}, bf16[1840,128]{1,0:T(8,128)(2,1)S(1)}, u32[]{:S(2)}, u32[]{:S(2)}) %collective-permute-start.5) | collective-permute-done | bytes 471072 | tf_op jit(solution)/shard_map/ppermute | solution.py:326
  31.6 1.5 %collective-permute-start.6 = (bf16[1536,128]{1,0:T(8,128)(2,1)S(1)}, bf16[1536,128]{1,0:T(8,128)(2,1)S(1)}, u32[]{:S(2)}, u32[]{:S(2)}) collective-permute-start(bf16[1536,128]{1,0:T(8,128)(2,1)S(1)} %get-tuple-element.41), channel_id=1, source_target_pairs={{0,2},{1,3},{2,0},{3,1},{4,6},{5,7},{6,4},{7,5},{8,10},{9,11},{10,... | collective-permute-start | bytes 1179656 | tf_op jit(solution)/shard_map/ppermute | solution.py:326
  33.6 5.7 %layer_0.1 = (f32[1536,128]{1,0:T(8,128)S(1)}, bf16[1536,512]{1,0:T(8,128)(2,1)S(1)}, f32[192,128]{1,0:T(8,128)S(1)}, bf16[192,512]{1,0:T(8,128)(2,1)S(1)}, bf16...) custom-call(bf16[7168,128]{1,0:T(8,128)(2,1)S(1)} %get-tuple-element.39.refs_0_, ...), custom_call_target="tpu_custom_call" | custom-call | tf_op jit(solution)/shard_map/layer_0/pallas_call | solution.py:312
  39.3 2.7 %collective-permute-done.16.refs_2_ = bf16[2048,128]{1,0:T(8,128)(2,1)S(1)} collective-permute-done((bf16[2048,128]{1,0:T(8,128)(2,1)S(1)}, bf16[2048,128]{1,0:T(8,128)(2,1)S(1)}, u32[]{:S(2)}, u32[]{:S(2)}) %collective-permute-start.16) | collective-permute-done | bytes 524320 | tf_op jit(solution)/shard_map/ppermute | solution.py:326
  42.0 3.9 %collective-permute-start.13 = (bf16[48,512]{1,0:T(8,128)(2,1)S(1)}, bf16[48,512]{1,0:T(8,128)(2,1)S(1)}, u32[]{:S(2)}, u32[]{:S(2)}) collective-permute-start(bf16[48,512]{1,0:T(8,128)(2,1)S(1)} %get-tuple-element.50), channel_id=1, source_target_pairs={{0,12},{4,0},{8,4},{12,8},{1,13},{5,1},{9,5},{13,9},{2,14},{6,2},{... | collective-permute-start | bytes 147464 | tf_op jit(solution)/shard_map/ppermute | solution.py:331
  45.9 1.0 %collective-permute-start.14 = (bf16[16,512]{1,0:T(8,128)(2,1)S(1)}, bf16[16,512]{1,0:T(8,128)(2,1)S(1)}, u32[]{:S(2)}, u32[]{:S(2)}) collective-permute-start(bf16[16,512]{1,0:T(8,128)(2,1)S(1)} %get-tuple-element.51), channel_id=1, source_target_pairs={{0,8},{4,12},{8,0},{12,4},{1,9},{5,13},{9,1},{13,5},{2,10},{6,14},... | collective-permute-start | bytes 49160 | tf_op jit(solution)/shard_map/ppermute | solution.py:331
  46.9 2.7 %collective-permute-done.6.refs_2_ = bf16[1536,128]{1,0:T(8,128)(2,1)S(1)} collective-permute-done((bf16[1536,128]{1,0:T(8,128)(2,1)S(1)}, bf16[1536,128]{1,0:T(8,128)(2,1)S(1)}, u32[]{:S(2)}, u32[]{:S(2)}) %collective-permute-start.6) | collective-permute-done | bytes 393248 | tf_op jit(solution)/shard_map/ppermute | solution.py:326
  49.6 1.0 %collective-permute-done.14.refs_9_ = bf16[16,512]{1,0:T(8,128)(2,1)S(1)} collective-permute-done((bf16[16,512]{1,0:T(8,128)(2,1)S(1)}, bf16[16,512]{1,0:T(8,128)(2,1)S(1)}, u32[]{:S(2)}, u32[]{:S(2)}) %collective-permute-start.14) | collective-permute-done | bytes 16416 | tf_op jit(solution)/shard_map/ppermute | solution.py:331
  50.5 1.2 %collective-permute-done.12.refs_7_ = bf16[48,512]{1,0:T(8,128)(2,1)S(1)} collective-permute-done((bf16[48,512]{1,0:T(8,128)(2,1)S(1)}, bf16[48,512]{1,0:T(8,128)(2,1)S(1)}, u32[]{:S(2)}, u32[]{:S(2)}) %collective-permute-start.12) | collective-permute-done | bytes 49184 | tf_op jit(solution)/shard_map/ppermute | solution.py:331
  51.8 5.0 %layer_1_edges.1 = (f32[1536,128]{1,0:T(8,128)}, bf16[192,512]{1,0:T(8,128)(2,1)S(1)}) custom-call(bf16[7168,128]{1,0:T(8,128)(2,1)S(1)} %get-tuple-element.39.refs_0_, bf16[7168,128]{1,0:T(8,128)(2,1)S(1)} %collective-permute-done.4.refs_1_, bf16[2048,128]{1,0:T(8,128)(2,1)S(1)} %collective-permute-done.16.refs_2_, ...), custom_call_target="tpu_custom_call" | custom-call | tf_op jit(solution)/shard_map/layer_1_edges/pallas_call | solution.py:312
  56.8 1.5 %layer_1_nodes.1 = f32[192,128]{1,0:T(8,128)} custom-call(bf16[7168,128]{1,0:T(8,128)(2,1)S(1)} %get-tuple-element.39.refs_0_, bf16[7168,128]{1,0:T(8,128)(2,1)S(1)} %collective-permute-done.4.refs_1_, bf16[1536,128]{1,0:T(8,128)(2,1)S(1)} %collective-permute-done.6.refs_2_, bf16[1536,128]{1,0:T(8,128)(2,1)S(1)} %collective-permute-done.15.refs_3_, ...), custom_call_target="tpu_custom_call" | custom-call | tf_op jit(solution)/shard_map/layer_1_nodes/pallas_call | solution.py:312
  (40 shorter events, 2.4 us)
Async XLA Ops:
  0.6 13.9 %copy-start.4 = (bf16[2,128,512]{2,1,0:T(8,128)(2,1)S(1)}, bf16[2,128,512]{2,1,0:T(8,128)(2,1)}, u32[]{:S(2)}) copy-start(bf16[2,128,512]{2,1,0:T(8,128)(2,1)} %ns.3) | copy-start | bytes 786436
  0.6 13.9 %copy-start.2 = (bf16[2,1024,128]{2,1,0:T(8,128)(2,1)S(1)}, bf16[2,1024,128]{2,1,0:T(8,128)(2,1)}, u32[]{:S(2)}) copy-start(bf16[2,1024,128]{2,1,0:T(8,128)(2,1)} %nf.3) | copy-start | bytes 1572868
  0.7 13.9 %copy-start.3 = (bf16[2,128,512]{2,1,0:T(8,128)(2,1)S(1)}, bf16[2,128,512]{2,1,0:T(8,128)(2,1)}, u32[]{:S(2)}) copy-start(bf16[2,128,512]{2,1,0:T(8,128)(2,1)} %es.3) | copy-start | bytes 786436
  0.7 13.9 %copy-start = (bf16[2,1536,128]{2,1,0:T(8,128)(2,1)S(1)}, bf16[2,1536,128]{2,1,0:T(8,128)(2,1)}, u32[]{:S(2)}) copy-start(bf16[2,1536,128]{2,1,0:T(8,128)(2,1)} %ef.2) | copy-start | bytes 2359300
  0.7 5.1 %copy-start.5 = (f32[192,128]{1,0:T(8,128)S(1)}, f32[192,128]{1,0:T(8,128)}, u32[]{:S(2)}) copy-start(f32[192,128]{1,0:T(8,128)} %refs_11_.1) | copy-start | bytes 294916
  0.7 15.8 %copy-start.1 = (f32[1536,128]{1,0:T(8,128)S(1)}, f32[1536,128]{1,0:T(8,128)}, u32[]{:S(2)}) copy-start(f32[1536,128]{1,0:T(8,128)} %refs_10_.1) | copy-start | bytes 2359300
  2.8 13.7 %collective-permute-start.3 = (bf16[1792,128]{1,0:T(8,128)(2,1)}, bf16[1792,128]{1,0:T(8,128)(2,1)S(1)}, u32[]{:S(2)}, u32[]{:S(2)}) collective-permute-start(bf16[1792,128]{1,0:T(8,128)(2,1)} %layer_0_half.1), channel_id=1, source_target_pairs={{0,2},{1,3},{2,0},{3,1},{4,6},{5,7},{6,4},{7,5},{8,10},{9,11},{10,... | collective-permute-start | bytes 1376264 | tf_op jit(solution)/shard_map/ppermute | solution.py:326
  6.1 8.4 %collective-permute-start = (bf16[48,128]{1,0:T(8,128)(2,1)S(1)}, bf16[48,128]{1,0:T(8,128)(2,1)S(1)}, u32[]{:S(2)}, u32[]{:S(2)}) collective-permute-start(bf16[48,128]{1,0:T(8,128)(2,1)S(1)} %get-tuple-element.33), channel_id=1, source_target_pairs={{0,4},{4,8},{8,12},{12,0},{1,5},{5,9},{9,13},{13,1},{2,6},{6,10},{... | collective-permute-start | bytes 36872 | tf_op jit(solution)/shard_map/ppermute | solution.py:331
  7.7 6.8 %collective-permute-start.1 = (bf16[48,128]{1,0:T(8,128)(2,1)S(1)}, bf16[48,128]{1,0:T(8,128)(2,1)S(1)}, u32[]{:S(2)}, u32[]{:S(2)}) collective-permute-start(bf16[48,128]{1,0:T(8,128)(2,1)S(1)} %get-tuple-element.34), channel_id=1, source_target_pairs={{0,12},{4,0},{8,4},{12,8},{1,13},{5,1},{9,5},{13,9},{2,14},{6,2},{... | collective-permute-start | bytes 36872 | tf_op jit(solution)/shard_map/ppermute | solution.py:331
  10.0 4.5 %collective-permute-start.2 = (bf16[16,128]{1,0:T(8,128)(2,1)S(1)}, bf16[16,128]{1,0:T(8,128)(2,1)S(1)}, u32[]{:S(2)}, u32[]{:S(2)}) collective-permute-start(bf16[16,128]{1,0:T(8,128)(2,1)S(1)} %get-tuple-element.35), channel_id=1, source_target_pairs={{0,8},{4,12},{8,0},{12,4},{1,9},{5,13},{9,1},{13,5},{2,10},{6,14},... | collective-permute-start | bytes 12296 | tf_op jit(solution)/shard_map/ppermute | solution.py:331
  16.5 14.6 %collective-permute-start.4 = (bf16[7168,128]{1,0:T(8,128)(2,1)S(1)}, bf16[7168,128]{1,0:T(8,128)(2,1)S(1)}, u32[]{:S(2)}, u32[]{:S(2)}) collective-permute-start(bf16[7168,128]{1,0:T(8,128)(2,1)S(1)} %get-tuple-element.39.refs_0_), channel_id=1, source_target_pairs={{0,1},{1,0},{2,3},{3,2},{4,5},{5,4},{6,7},{7,6},{8,9},{9,8},{10,11... | collective-permute-start | bytes 5505032 | tf_op jit(solution)/shard_map/ppermute | solution.py:326
  16.6 4.4 %collective-permute-start.8 = (bf16[1840,128]{1,0:T(8,128)(2,1)S(1)}, bf16[1840,128]{1,0:T(8,128)(2,1)S(1)}, u32[]{:S(2)}, u32[]{:S(2)}) collective-permute-start(bf16[1840,128]{1,0:T(8,128)(2,1)S(1)} %latents.1.refs_6_), channel_id=1, source_target_pairs={{0,1},{1,0},{2,3},{3,2},{4,5},{5,4},{6,7},{7,6},{8,9},{9,8},{10,11... | collective-permute-start | bytes 1413128 | tf_op jit(solution)/shard_map/ppermute | solution.py:326
  17.1 13.6 %collective-permute-start.5 = (bf16[1840,128]{1,0:T(8,128)(2,1)S(1)}, bf16[1840,128]{1,0:T(8,128)(2,1)S(1)}, u32[]{:S(2)}, u32[]{:S(2)}) collective-permute-start(bf16[1840,128]{1,0:T(8,128)(2,1)S(1)} %latents.1.refs_6_), channel_id=1, source_target_pairs={{0,2},{1,3},{2,0},{3,1},{4,6},{5,7},{6,4},{7,5},{8,10},{9,11},{10,... | collective-permute-start | bytes 1413128 | tf_op jit(solution)/shard_map/ppermute | solution.py:326
  18.9 12.2 %collective-permute-start.7 = (bf16[1792,128]{1,0:T(8,128)(2,1)S(1)}, bf16[1792,128]{1,0:T(8,128)(2,1)S(1)}, u32[]{:S(2)}, u32[]{:S(2)}) collective-permute-start(bf16[1792,128]{1,0:T(8,128)(2,1)S(1)} %collective-permute-done.3.refs_2_), channel_id=1, source_target_pairs={{0,16},{16,0},{1,17},{17,1},{2,18},{18,2},{3,19},{19,3},{4,20},{20... | collective-permute-start | bytes 1376264 | tf_op jit(solution)/shard_map/ppermute | solution.py:426
  21.0 10.1 %collective-permute-start.9 = (bf16[1792,128]{1,0:T(8,128)(2,1)S(1)}, bf16[1792,128]{1,0:T(8,128)(2,1)S(1)}, u32[]{:S(2)}, u32[]{:S(2)}) collective-permute-start(bf16[1792,128]{1,0:T(8,128)(2,1)S(1)} %collective-permute-done.3.refs_2_), channel_id=1, source_target_pairs={{0,1},{1,0},{2,3},{3,2},{4,5},{5,4},{6,7},{7,6},{8,9},{9,8},{10,11... | collective-permute-start | bytes 1376264 | tf_op jit(solution)/shard_map/ppermute | solution.py:326
  22.2 19.8 %collective-permute-start.16 = (bf16[2048,128]{1,0:T(8,128)(2,1)S(1)}, bf16[2048,128]{1,0:T(8,128)(2,1)S(1)}, u32[]{:S(2)}, u32[]{:S(2)}) collective-permute-start(bf16[2048,128]{1,0:T(8,128)(2,1)S(1)} %get-tuple-element.56), channel_id=1, source_target_pairs={{0,2},{1,3},{2,0},{3,1},{4,6},{5,7},{6,4},{7,5},{8,10},{9,11},{10,... | collective-permute-start | bytes 1572872 | tf_op jit(solution)/shard_map/ppermute | solution.py:326
  31.1 2.5 %collective-permute-start.11 = (bf16[1840,128]{1,0:T(8,128)(2,1)S(1)}, bf16[1840,128]{1,0:T(8,128)(2,1)S(1)}, u32[]{:S(2)}, u32[]{:S(2)}) collective-permute-start(bf16[1840,128]{1,0:T(8,128)(2,1)S(1)} %collective-permute-done.5.refs_8_), channel_id=1, source_target_pairs={{0,1},{1,0},{2,3},{3,2},{4,5},{5,4},{6,7},{7,6},{8,9},{9,8},{10,11... | collective-permute-start | bytes 1413128 | tf_op jit(solution)/shard_map/ppermute | solution.py:326
  31.1 2.5 %collective-permute-start.10 = (bf16[1792,128]{1,0:T(8,128)(2,1)S(1)}, bf16[1792,128]{1,0:T(8,128)(2,1)S(1)}, u32[]{:S(2)}, u32[]{:S(2)}) collective-permute-start(bf16[1792,128]{1,0:T(8,128)(2,1)S(1)} %collective-permute-done.7.refs_3_), channel_id=1, source_target_pairs={{0,1},{1,0},{2,3},{3,2},{4,5},{5,4},{6,7},{7,6},{8,9},{9,8},{10,11... | collective-permute-start | bytes 1376264 | tf_op jit(solution)/shard_map/ppermute | solution.py:326
  31.6 17.9 %collective-permute-start.6 = (bf16[1536,128]{1,0:T(8,128)(2,1)S(1)}, bf16[1536,128]{1,0:T(8,128)(2,1)S(1)}, u32[]{:S(2)}, u32[]{:S(2)}) collective-permute-start(bf16[1536,128]{1,0:T(8,128)(2,1)S(1)} %get-tuple-element.41), channel_id=1, source_target_pairs={{0,2},{1,3},{2,0},{3,1},{4,6},{5,7},{6,4},{7,5},{8,10},{9,11},{10,... | collective-permute-start | bytes 1179656 | tf_op jit(solution)/shard_map/ppermute | solution.py:326
  42.0 9.7 %collective-permute-start.17 = (bf16[2048,128]{1,0:T(8,128)(2,1)S(1)}, bf16[2048,128]{1,0:T(8,128)(2,1)S(1)}, u32[]{:S(2)}, u32[]{:S(2)}) collective-permute-start(bf16[2048,128]{1,0:T(8,128)(2,1)S(1)} %collective-permute-done.16.refs_2_), channel_id=1, source_target_pairs={{0,1},{1,0},{2,3},{3,2},{4,5},{5,4},{6,7},{7,6},{8,9},{9,8},{10,11... | collective-permute-start | bytes 1572872 | tf_op jit(solution)/shard_map/ppermute | solution.py:326
  42.0 8.5 %collective-permute-start.13 = (bf16[48,512]{1,0:T(8,128)(2,1)S(1)}, bf16[48,512]{1,0:T(8,128)(2,1)S(1)}, u32[]{:S(2)}, u32[]{:S(2)}) collective-permute-start(bf16[48,512]{1,0:T(8,128)(2,1)S(1)} %get-tuple-element.50), channel_id=1, source_target_pairs={{0,12},{4,0},{8,4},{12,8},{1,13},{5,1},{9,5},{13,9},{2,14},{6,2},{... | collective-permute-start | bytes 147464 | tf_op jit(solution)/shard_map/ppermute | solution.py:331
  45.9 5.9 %collective-permute-start.12 = (bf16[48,512]{1,0:T(8,128)(2,1)S(1)}, bf16[48,512]{1,0:T(8,128)(2,1)S(1)}, u32[]{:S(2)}, u32[]{:S(2)}) collective-permute-start(bf16[48,512]{1,0:T(8,128)(2,1)S(1)} %get-tuple-element.49), channel_id=1, source_target_pairs={{0,4},{4,8},{8,12},{12,0},{1,5},{5,9},{9,13},{13,1},{2,6},{6,10},{... | collective-permute-start | bytes 147464 | tf_op jit(solution)/shard_map/ppermute | solution.py:331
  45.9 4.6 %collective-permute-start.14 = (bf16[16,512]{1,0:T(8,128)(2,1)S(1)}, bf16[16,512]{1,0:T(8,128)(2,1)S(1)}, u32[]{:S(2)}, u32[]{:S(2)}) collective-permute-start(bf16[16,512]{1,0:T(8,128)(2,1)S(1)} %get-tuple-element.51), channel_id=1, source_target_pairs={{0,8},{4,12},{8,0},{12,4},{1,9},{5,13},{9,1},{13,5},{2,10},{6,14},... | collective-permute-start | bytes 49160 | tf_op jit(solution)/shard_map/ppermute | solution.py:331
  51.8 5.0 %collective-permute-start.15 = (bf16[1536,128]{1,0:T(8,128)(2,1)S(1)}, bf16[1536,128]{1,0:T(8,128)(2,1)S(1)}, u32[]{:S(2)}, u32[]{:S(2)}) collective-permute-start(bf16[1536,128]{1,0:T(8,128)(2,1)S(1)} %collective-permute-done.6.refs_2_), channel_id=1, source_target_pairs={{0,1},{1,0},{2,3},{3,2},{4,5},{5,4},{6,7},{7,6},{8,9},{9,8},{10,11... | collective-permute-start | bytes 1179656 | tf_op jit(solution)/shard_map/ppermute | solution.py:326
  (3 other events, 15.3 us)

commit v15 on v14

--- a/solution.py
+++ b/solution.py
@@ -17,7 +17,7 @@
 
 
 def silu(x):
-    half = 0.5 * x
+    half = x.astype(BF16) * jnp.asarray(0.5, BF16)
     return half + half * jnp.tanh(half)
 
 
@@ -211,7 +211,7 @@
         rows = slice(at, at + TILE)
         edge_bf = edge_ref[rows, :]
         pre = dot(edge_bf, first_ref[0:features, :]) + dot(hot_ref[rows, :], product_ref[...])
-        norm = normalize(dot(silu(pre).astype(BF16), second_ref[...]))
+        norm = normalize(dot(silu(pre), second_ref[...]))
         edge_new = (edge_bf.astype(F32) + norm).astype(BF16)
         if full_out is not None:
             full_out[rows, :] = edge_new
@@ -223,7 +223,7 @@
 def node_rows(node_bf, incoming, own_ref, first_ref, second_ref, own_out):
     features = second_ref.shape[1]
     pre = dot(node_bf, first_ref[0:features, :]) + dot(incoming, first_ref[features:, :])
-    norm = normalize(dot(silu(pre).astype(BF16), second_ref[...]))
+    norm = normalize(dot(silu(pre), second_ref[...]))
     own_out[...] = own_ref[...] + own_columns(norm, own_ref.shape[1])
     return (node_bf.astype(F32) + norm).astype(BF16)
 

time: 58.4 us -> 58.1 us (level)
  transfers between devices with their start and end apart: 18 -> 18, of which waited for: 10 -> 10; matrix products, arithmetic and copies ran while one was open for 0% -> 0% of each run, Pallas kernels for 23% -> 22%
where the time goes in v15:
time: 58.1 us; the launch traced here: 57.9 us
  waiting for transfers between devices  20.5 us (35%)
  starting transfers between devices  20.3 us (35%)
  Pallas kernels  16.2 us (28%)
  between operations  0.82 us (1%)
    pallas_call x8, Pallas kernels, call(): pl.pallas_call(kernel, out_shape=out_shape, in_specs=[pl.BlockSpec(memory...  16.2 us
    ppermute x11, waiting for transfers between devices, swap(): return lax.ppermute(x, 'mp', [(i, i ^ mask) for i in range(size)])  14.3 us
    ppermute x6, starting transfers between devices, shift(): return lax.ppermute(x, 'graph', [(i, (i + by) % size) for i in range(size)])  9.53 us
    ppermute x11, starting transfers between devices, swap(): return lax.ppermute(x, 'mp', [(i, i ^ mask) for i in range(size)])  9.27 us
    ppermute x6, waiting for transfers between devices, shift(): return lax.ppermute(x, 'graph', [(i, (i + by) % size) for i in range(size)])  5.91 us
    ppermute x1, starting transfers between devices, on_device(): far = lax.ppermute(near, 'groups', [(0, 1), (1, 0)])  1.52 us
  transfers between devices with their start and end apart: 18, of which 10 were waited for; matrix products, arithmetic and copies ran while one was open for 0% of the time, Pallas kernels for 22%

profile of v15, /device:TPU:0, one launch (start us, length us, event | category | flops | bytes accessed | tf_op | source)
XLA Modules:
  0.0 57.9 jit_solution(8021212947623171363)
XLA Ops:
  0.7 2.0 %layer_0_half.1 = bf16[1792,128]{1,0:T(8,128)(2,1)} custom-call(bf16[2,1536,128]{2,1,0:T(8,128)(2,1)} %ef.2, bf16[2,128,512]{2,1,0:T(8,128)(2,1)} %es.3, bf16[2,1024,128]{2,1,0:T(8,128)(2,1)} %nf.3, bf16[2,128,512]{2,1,0:T(8,128)(2,1)} %ns.3), custom_call_target="tpu_custom_call" | custom-call | tf_op jit(solution)/shard_map/layer_0_half/pallas_call | solution.py:312
  2.8 3.0 %collective-permute-start.3 = (bf16[1792,128]{1,0:T(8,128)(2,1)}, bf16[1792,128]{1,0:T(8,128)(2,1)S(1)}, u32[]{:S(2)}, u32[]{:S(2)}) collective-permute-start(bf16[1792,128]{1,0:T(8,128)(2,1)} %layer_0_half.1), channel_id=1, source_target_pairs={{0,2},{1,3},{2,0},{3,1},{4,6},{5,7},{6,4},{7,5},{8,10},{9,11},{10,... | collective-permute-start | bytes 1376264 | tf_op jit(solution)/shard_map/ppermute | solution.py:326
  6.1 1.6 %collective-permute-start = (bf16[48,128]{1,0:T(8,128)(2,1)S(1)}, bf16[48,128]{1,0:T(8,128)(2,1)S(1)}, u32[]{:S(2)}, u32[]{:S(2)}) collective-permute-start(bf16[48,128]{1,0:T(8,128)(2,1)S(1)} %get-tuple-element.33), channel_id=1, source_target_pairs={{0,4},{4,8},{8,12},{12,0},{1,5},{5,9},{9,13},{13,1},{2,6},{6,10},{... | collective-permute-start | bytes 36872 | tf_op jit(solution)/shard_map/ppermute | solution.py:331
  7.7 2.2 %collective-permute-start.1 = (bf16[48,128]{1,0:T(8,128)(2,1)S(1)}, bf16[48,128]{1,0:T(8,128)(2,1)S(1)}, u32[]{:S(2)}, u32[]{:S(2)}) collective-permute-start(bf16[48,128]{1,0:T(8,128)(2,1)S(1)} %get-tuple-element.34), channel_id=1, source_target_pairs={{0,12},{4,0},{8,4},{12,8},{1,13},{5,1},{9,5},{13,9},{2,14},{6,2},{... | collective-permute-start | bytes 36872 | tf_op jit(solution)/shard_map/ppermute | solution.py:331
  10.0 0.8 %collective-permute-start.2 = (bf16[16,128]{1,0:T(8,128)(2,1)S(1)}, bf16[16,128]{1,0:T(8,128)(2,1)S(1)}, u32[]{:S(2)}, u32[]{:S(2)}) collective-permute-start(bf16[16,128]{1,0:T(8,128)(2,1)S(1)} %get-tuple-element.35), channel_id=1, source_target_pairs={{0,8},{4,12},{8,0},{12,4},{1,9},{5,13},{9,1},{13,5},{2,10},{6,14},... | collective-permute-start | bytes 12296 | tf_op jit(solution)/shard_map/ppermute | solution.py:331
  10.8 3.7 %collective-permute-done.2.refs_4_ = bf16[16,128]{1,0:T(8,128)(2,1)S(1)} collective-permute-done((bf16[16,128]{1,0:T(8,128)(2,1)S(1)}, bf16[16,128]{1,0:T(8,128)(2,1)S(1)}, u32[]{:S(2)}, u32[]{:S(2)}) %collective-permute-start.2) | collective-permute-done | bytes 4128 | tf_op jit(solution)/shard_map/ppermute | solution.py:331
  14.5 1.1 %packed_weights.1 = (bf16[7168,128]{1,0:T(8,128)(2,1)S(1)}, bf16[2048,128]{1,0:T(8,128)(2,1)S(1)}, bf16[1536,128]{1,0:T(8,128)(2,1)S(1)}) custom-call(bf16[2,1536,128]{2,1,0:T(8,128)(2,1)S(1)} %copy-done, bf16[2,128,512]{2,1,0:T(8,128)(2,1)S(1)} %copy-done.3, bf16[2,1024,128]{2,1,0:T(8,128)(2,1)S(1)} %copy-done.2, bf16[2,128,512]{2,1,0:T(8,128)(2,1)S(1)} %copy-done.4), custom_call_target="tpu_custom_call" | custom-call | tf_op jit(solution)/shard_map/packed_weights/pallas_call | solution.py:312
  15.7 0.9 %collective-permute-done.3.refs_2_ = bf16[1792,128]{1,0:T(8,128)(2,1)S(1)} collective-permute-done((bf16[1792,128]{1,0:T(8,128)(2,1)}, bf16[1792,128]{1,0:T(8,128)(2,1)S(1)}, u32[]{:S(2)}, u32[]{:S(2)}) %collective-permute-start.3) | collective-permute-done | bytes 458784 | tf_op jit(solution)/shard_map/ppermute | solution.py:326
  16.6 0.6 collective-permute-start.8
  17.1 1.7 %collective-permute-start.5 = (bf16[1840,128]{1,0:T(8,128)(2,1)S(1)}, bf16[1840,128]{1,0:T(8,128)(2,1)S(1)}, u32[]{:S(2)}, u32[]{:S(2)}) collective-permute-start(bf16[1840,128]{1,0:T(8,128)(2,1)S(1)} %latents.1.refs_6_), channel_id=1, source_target_pairs={{0,2},{1,3},{2,0},{3,1},{4,6},{5,7},{6,4},{7,5},{8,10},{9,11},{10,... | collective-permute-start | bytes 1413128 | tf_op jit(solution)/shard_map/ppermute | solution.py:326
  18.9 1.5 %collective-permute-start.7 = (bf16[1792,128]{1,0:T(8,128)(2,1)S(1)}, bf16[1792,128]{1,0:T(8,128)(2,1)S(1)}, u32[]{:S(2)}, u32[]{:S(2)}) collective-permute-start(bf16[1792,128]{1,0:T(8,128)(2,1)S(1)} %collective-permute-done.3.refs_2_), channel_id=1, source_target_pairs={{0,16},{16,0},{1,17},{17,1},{2,18},{18,2},{3,19},{19,3},{4,20},{20... | collective-permute-start | bytes 1376264 | tf_op jit(solution)/shard_map/ppermute | solution.py:426
  21.1 1.1 %one_hot.1 = (bf16[1536,512]{1,0:T(8,128)(2,1)S(1)}, bf16[192,1536]{1,0:T(8,128)(2,1)S(1)}, bf16[112,192]{1,0:T(8,128)(2,1)S(1)}) custom-call(s32[1,3136]{1,0:T(1,128)S(1)} %broadcast_in_dim.3.list_ref), custom_call_target="tpu_custom_call" | custom-call | tf_op jit(solution)/shard_map/one_hot/pallas_call | solution.py:312
  22.2 1.8 %collective-permute-start.16 = (bf16[2048,128]{1,0:T(8,128)(2,1)S(1)}, bf16[2048,128]{1,0:T(8,128)(2,1)S(1)}, u32[]{:S(2)}, u32[]{:S(2)}) collective-permute-start(bf16[2048,128]{1,0:T(8,128)(2,1)S(1)} %get-tuple-element.56), channel_id=1, source_target_pairs={{0,2},{1,3},{2,0},{3,1},{4,6},{5,7},{6,4},{7,5},{8,10},{9,11},{10,... | collective-permute-start | bytes 1572872 | tf_op jit(solution)/shard_map/ppermute | solution.py:326
  24.1 6.7 %collective-permute-done.5.refs_8_ = bf16[1840,128]{1,0:T(8,128)(2,1)S(1)} collective-permute-done((bf16[1840,128]{1,0:T(8,128)(2,1)S(1)}, bf16[1840,128]{1,0:T(8,128)(2,1)S(1)}, u32[]{:S(2)}, u32[]{:S(2)}) %collective-permute-start.5) | collective-permute-done | bytes 471072 | tf_op jit(solution)/shard_map/ppermute | solution.py:326
  31.6 1.5 %collective-permute-start.6 = (bf16[1536,128]{1,0:T(8,128)(2,1)S(1)}, bf16[1536,128]{1,0:T(8,128)(2,1)S(1)}, u32[]{:S(2)}, u32[]{:S(2)}) collective-permute-start(bf16[1536,128]{1,0:T(8,128)(2,1)S(1)} %get-tuple-element.41), channel_id=1, source_target_pairs={{0,2},{1,3},{2,0},{3,1},{4,6},{5,7},{6,4},{7,5},{8,10},{9,11},{10,... | collective-permute-start | bytes 1179656 | tf_op jit(solution)/shard_map/ppermute | solution.py:326
  33.6 5.4 %layer_0.1 = (f32[1536,128]{1,0:T(8,128)S(1)}, bf16[1536,512]{1,0:T(8,128)(2,1)S(1)}, f32[192,128]{1,0:T(8,128)S(1)}, bf16[192,512]{1,0:T(8,128)(2,1)S(1)}, bf16...) custom-call(bf16[7168,128]{1,0:T(8,128)(2,1)S(1)} %get-tuple-element.39.refs_0_, ...), custom_call_target="tpu_custom_call" | custom-call | tf_op jit(solution)/shard_map/layer_0/pallas_call | solution.py:312
  39.0 3.0 %collective-permute-done.16.refs_2_ = bf16[2048,128]{1,0:T(8,128)(2,1)S(1)} collective-permute-done((bf16[2048,128]{1,0:T(8,128)(2,1)S(1)}, bf16[2048,128]{1,0:T(8,128)(2,1)S(1)}, u32[]{:S(2)}, u32[]{:S(2)}) %collective-permute-start.16) | collective-permute-done | bytes 524320 | tf_op jit(solution)/shard_map/ppermute | solution.py:326
  42.0 3.9 %collective-permute-start.13 = (bf16[48,512]{1,0:T(8,128)(2,1)S(1)}, bf16[48,512]{1,0:T(8,128)(2,1)S(1)}, u32[]{:S(2)}, u32[]{:S(2)}) collective-permute-start(bf16[48,512]{1,0:T(8,128)(2,1)S(1)} %get-tuple-element.50), channel_id=1, source_target_pairs={{0,12},{4,0},{8,4},{12,8},{1,13},{5,1},{9,5},{13,9},{2,14},{6,2},{... | collective-permute-start | bytes 147464 | tf_op jit(solution)/shard_map/ppermute | solution.py:331
  45.9 1.0 %collective-permute-start.14 = (bf16[16,512]{1,0:T(8,128)(2,1)S(1)}, bf16[16,512]{1,0:T(8,128)(2,1)S(1)}, u32[]{:S(2)}, u32[]{:S(2)}) collective-permute-start(bf16[16,512]{1,0:T(8,128)(2,1)S(1)} %get-tuple-element.51), channel_id=1, source_target_pairs={{0,8},{4,12},{8,0},{12,4},{1,9},{5,13},{9,1},{13,5},{2,10},{6,14},... | collective-permute-start | bytes 49160 | tf_op jit(solution)/shard_map/ppermute | solution.py:331
  46.9 2.7 %collective-permute-done.6.refs_2_ = bf16[1536,128]{1,0:T(8,128)(2,1)S(1)} collective-permute-done((bf16[1536,128]{1,0:T(8,128)(2,1)S(1)}, bf16[1536,128]{1,0:T(8,128)(2,1)S(1)}, u32[]{:S(2)}, u32[]{:S(2)}) %collective-permute-start.6) | collective-permute-done | bytes 393248 | tf_op jit(solution)/shard_map/ppermute | solution.py:326
  49.6 1.0 %collective-permute-done.14.refs_9_ = bf16[16,512]{1,0:T(8,128)(2,1)S(1)} collective-permute-done((bf16[16,512]{1,0:T(8,128)(2,1)S(1)}, bf16[16,512]{1,0:T(8,128)(2,1)S(1)}, u32[]{:S(2)}, u32[]{:S(2)}) %collective-permute-start.14) | collective-permute-done | bytes 16416 | tf_op jit(solution)/shard_map/ppermute | solution.py:331
  50.5 1.2 %collective-permute-done.12.refs_7_ = bf16[48,512]{1,0:T(8,128)(2,1)S(1)} collective-permute-done((bf16[48,512]{1,0:T(8,128)(2,1)S(1)}, bf16[48,512]{1,0:T(8,128)(2,1)S(1)}, u32[]{:S(2)}, u32[]{:S(2)}) %collective-permute-start.12) | collective-permute-done | bytes 49184 | tf_op jit(solution)/shard_map/ppermute | solution.py:331
  51.8 4.7 %layer_1_edges.1 = (f32[1536,128]{1,0:T(8,128)}, bf16[192,512]{1,0:T(8,128)(2,1)S(1)}) custom-call(bf16[7168,128]{1,0:T(8,128)(2,1)S(1)} %get-tuple-element.39.refs_0_, bf16[7168,128]{1,0:T(8,128)(2,1)S(1)} %collective-permute-done.4.refs_1_, bf16[2048,128]{1,0:T(8,128)(2,1)S(1)} %collective-permute-done.16.refs_2_, ...), custom_call_target="tpu_custom_call" | custom-call | tf_op jit(solution)/shard_map/layer_1_edges/pallas_call | solution.py:312
  56.5 1.4 %layer_1_nodes.1 = f32[192,128]{1,0:T(8,128)} custom-call(bf16[7168,128]{1,0:T(8,128)(2,1)S(1)} %get-tuple-element.39.refs_0_, bf16[7168,128]{1,0:T(8,128)(2,1)S(1)} %collective-permute-done.4.refs_1_, bf16[1536,128]{1,0:T(8,128)(2,1)S(1)} %collective-permute-done.6.refs_2_, bf16[1536,128]{1,0:T(8,128)(2,1)S(1)} %collective-permute-done.15.refs_3_, ...), custom_call_target="tpu_custom_call" | custom-call | tf_op jit(solution)/shard_map/layer_1_nodes/pallas_call | solution.py:312
  (40 shorter events, 2.4 us)
Async XLA Ops:
  0.6 13.9 %copy-start.4 = (bf16[2,128,512]{2,1,0:T(8,128)(2,1)S(1)}, bf16[2,128,512]{2,1,0:T(8,128)(2,1)}, u32[]{:S(2)}) copy-start(bf16[2,128,512]{2,1,0:T(8,128)(2,1)} %ns.3) | copy-start | bytes 786436
  0.6 13.9 %copy-start.2 = (bf16[2,1024,128]{2,1,0:T(8,128)(2,1)S(1)}, bf16[2,1024,128]{2,1,0:T(8,128)(2,1)}, u32[]{:S(2)}) copy-start(bf16[2,1024,128]{2,1,0:T(8,128)(2,1)} %nf.3) | copy-start | bytes 1572868
  0.7 13.9 %copy-start.3 = (bf16[2,128,512]{2,1,0:T(8,128)(2,1)S(1)}, bf16[2,128,512]{2,1,0:T(8,128)(2,1)}, u32[]{:S(2)}) copy-start(bf16[2,128,512]{2,1,0:T(8,128)(2,1)} %es.3) | copy-start | bytes 786436
  0.7 13.9 %copy-start = (bf16[2,1536,128]{2,1,0:T(8,128)(2,1)S(1)}, bf16[2,1536,128]{2,1,0:T(8,128)(2,1)}, u32[]{:S(2)}) copy-start(bf16[2,1536,128]{2,1,0:T(8,128)(2,1)} %ef.2) | copy-start | bytes 2359300
  0.7 5.1 %copy-start.5 = (f32[192,128]{1,0:T(8,128)S(1)}, f32[192,128]{1,0:T(8,128)}, u32[]{:S(2)}) copy-start(f32[192,128]{1,0:T(8,128)} %refs_11_.1) | copy-start | bytes 294916
  0.7 15.8 %copy-start.1 = (f32[1536,128]{1,0:T(8,128)S(1)}, f32[1536,128]{1,0:T(8,128)}, u32[]{:S(2)}) copy-start(f32[1536,128]{1,0:T(8,128)} %refs_10_.1) | copy-start | bytes 2359300
  2.8 13.7 %collective-permute-start.3 = (bf16[1792,128]{1,0:T(8,128)(2,1)}, bf16[1792,128]{1,0:T(8,128)(2,1)S(1)}, u32[]{:S(2)}, u32[]{:S(2)}) collective-permute-start(bf16[1792,128]{1,0:T(8,128)(2,1)} %layer_0_half.1), channel_id=1, source_target_pairs={{0,2},{1,3},{2,0},{3,1},{4,6},{5,7},{6,4},{7,5},{8,10},{9,11},{10,... | collective-permute-start | bytes 1376264 | tf_op jit(solution)/shard_map/ppermute | solution.py:326
  6.1 8.4 %collective-permute-start = (bf16[48,128]{1,0:T(8,128)(2,1)S(1)}, bf16[48,128]{1,0:T(8,128)(2,1)S(1)}, u32[]{:S(2)}, u32[]{:S(2)}) collective-permute-start(bf16[48,128]{1,0:T(8,128)(2,1)S(1)} %get-tuple-element.33), channel_id=1, source_target_pairs={{0,4},{4,8},{8,12},{12,0},{1,5},{5,9},{9,13},{13,1},{2,6},{6,10},{... | collective-permute-start | bytes 36872 | tf_op jit(solution)/shard_map/ppermute | solution.py:331
  7.7 6.8 %collective-permute-start.1 = (bf16[48,128]{1,0:T(8,128)(2,1)S(1)}, bf16[48,128]{1,0:T(8,128)(2,1)S(1)}, u32[]{:S(2)}, u32[]{:S(2)}) collective-permute-start(bf16[48,128]{1,0:T(8,128)(2,1)S(1)} %get-tuple-element.34), channel_id=1, source_target_pairs={{0,12},{4,0},{8,4},{12,8},{1,13},{5,1},{9,5},{13,9},{2,14},{6,2},{... | collective-permute-start | bytes 36872 | tf_op jit(solution)/shard_map/ppermute | solution.py:331
  10.0 4.5 %collective-permute-start.2 = (bf16[16,128]{1,0:T(8,128)(2,1)S(1)}, bf16[16,128]{1,0:T(8,128)(2,1)S(1)}, u32[]{:S(2)}, u32[]{:S(2)}) collective-permute-start(bf16[16,128]{1,0:T(8,128)(2,1)S(1)} %get-tuple-element.35), channel_id=1, source_target_pairs={{0,8},{4,12},{8,0},{12,4},{1,9},{5,13},{9,1},{13,5},{2,10},{6,14},... | collective-permute-start | bytes 12296 | tf_op jit(solution)/shard_map/ppermute | solution.py:331
  16.5 14.6 %collective-permute-start.4 = (bf16[7168,128]{1,0:T(8,128)(2,1)S(1)}, bf16[7168,128]{1,0:T(8,128)(2,1)S(1)}, u32[]{:S(2)}, u32[]{:S(2)}) collective-permute-start(bf16[7168,128]{1,0:T(8,128)(2,1)S(1)} %get-tuple-element.39.refs_0_), channel_id=1, source_target_pairs={{0,1},{1,0},{2,3},{3,2},{4,5},{5,4},{6,7},{7,6},{8,9},{9,8},{10,11... | collective-permute-start | bytes 5505032 | tf_op jit(solution)/shard_map/ppermute | solution.py:326
  16.6 4.4 %collective-permute-start.8 = (bf16[1840,128]{1,0:T(8,128)(2,1)S(1)}, bf16[1840,128]{1,0:T(8,128)(2,1)S(1)}, u32[]{:S(2)}, u32[]{:S(2)}) collective-permute-start(bf16[1840,128]{1,0:T(8,128)(2,1)S(1)} %latents.1.refs_6_), channel_id=1, source_target_pairs={{0,1},{1,0},{2,3},{3,2},{4,5},{5,4},{6,7},{7,6},{8,9},{9,8},{10,11... | collective-permute-start | bytes 1413128 | tf_op jit(solution)/shard_map/ppermute | solution.py:326
  17.1 13.6 %collective-permute-start.5 = (bf16[1840,128]{1,0:T(8,128)(2,1)S(1)}, bf16[1840,128]{1,0:T(8,128)(2,1)S(1)}, u32[]{:S(2)}, u32[]{:S(2)}) collective-permute-start(bf16[1840,128]{1,0:T(8,128)(2,1)S(1)} %latents.1.refs_6_), channel_id=1, source_target_pairs={{0,2},{1,3},{2,0},{3,1},{4,6},{5,7},{6,4},{7,5},{8,10},{9,11},{10,... | collective-permute-start | bytes 1413128 | tf_op jit(solution)/shard_map/ppermute | solution.py:326
  18.9 12.2 %collective-permute-start.7 = (bf16[1792,128]{1,0:T(8,128)(2,1)S(1)}, bf16[1792,128]{1,0:T(8,128)(2,1)S(1)}, u32[]{:S(2)}, u32[]{:S(2)}) collective-permute-start(bf16[1792,128]{1,0:T(8,128)(2,1)S(1)} %collective-permute-done.3.refs_2_), channel_id=1, source_target_pairs={{0,16},{16,0},{1,17},{17,1},{2,18},{18,2},{3,19},{19,3},{4,20},{20... | collective-permute-start | bytes 1376264 | tf_op jit(solution)/shard_map/ppermute | solution.py:426
  21.0 10.1 %collective-permute-start.9 = (bf16[1792,128]{1,0:T(8,128)(2,1)S(1)}, bf16[1792,128]{1,0:T(8,128)(2,1)S(1)}, u32[]{:S(2)}, u32[]{:S(2)}) collective-permute-start(bf16[1792,128]{1,0:T(8,128)(2,1)S(1)} %collective-permute-done.3.refs_2_), channel_id=1, source_target_pairs={{0,1},{1,0},{2,3},{3,2},{4,5},{5,4},{6,7},{7,6},{8,9},{9,8},{10,11... | collective-permute-start | bytes 1376264 | tf_op jit(solution)/shard_map/ppermute | solution.py:326
  22.2 19.8 %collective-permute-start.16 = (bf16[2048,128]{1,0:T(8,128)(2,1)S(1)}, bf16[2048,128]{1,0:T(8,128)(2,1)S(1)}, u32[]{:S(2)}, u32[]{:S(2)}) collective-permute-start(bf16[2048,128]{1,0:T(8,128)(2,1)S(1)} %get-tuple-element.56), channel_id=1, source_target_pairs={{0,2},{1,3},{2,0},{3,1},{4,6},{5,7},{6,4},{7,5},{8,10},{9,11},{10,... | collective-permute-start | bytes 1572872 | tf_op jit(solution)/shard_map/ppermute | solution.py:326
  31.1 2.5 %collective-permute-start.11 = (bf16[1840,128]{1,0:T(8,128)(2,1)S(1)}, bf16[1840,128]{1,0:T(8,128)(2,1)S(1)}, u32[]{:S(2)}, u32[]{:S(2)}) collective-permute-start(bf16[1840,128]{1,0:T(8,128)(2,1)S(1)} %collective-permute-done.5.refs_8_), channel_id=1, source_target_pairs={{0,1},{1,0},{2,3},{3,2},{4,5},{5,4},{6,7},{7,6},{8,9},{9,8},{10,11... | collective-permute-start | bytes 1413128 | tf_op jit(solution)/shard_map/ppermute | solution.py:326
  31.1 2.5 %collective-permute-start.10 = (bf16[1792,128]{1,0:T(8,128)(2,1)S(1)}, bf16[1792,128]{1,0:T(8,128)(2,1)S(1)}, u32[]{:S(2)}, u32[]{:S(2)}) collective-permute-start(bf16[1792,128]{1,0:T(8,128)(2,1)S(1)} %collective-permute-done.7.refs_3_), channel_id=1, source_target_pairs={{0,1},{1,0},{2,3},{3,2},{4,5},{5,4},{6,7},{7,6},{8,9},{9,8},{10,11... | collective-permute-start | bytes 1376264 | tf_op jit(solution)/shard_map/ppermute | solution.py:326
  31.6 17.9 %collective-permute-start.6 = (bf16[1536,128]{1,0:T(8,128)(2,1)S(1)}, bf16[1536,128]{1,0:T(8,128)(2,1)S(1)}, u32[]{:S(2)}, u32[]{:S(2)}) collective-permute-start(bf16[1536,128]{1,0:T(8,128)(2,1)S(1)} %get-tuple-element.41), channel_id=1, source_target_pairs={{0,2},{1,3},{2,0},{3,1},{4,6},{5,7},{6,4},{7,5},{8,10},{9,11},{10,... | collective-permute-start | bytes 1179656 | tf_op jit(solution)/shard_map/ppermute | solution.py:326
  42.0 9.7 %collective-permute-start.17 = (bf16[2048,128]{1,0:T(8,128)(2,1)S(1)}, bf16[2048,128]{1,0:T(8,128)(2,1)S(1)}, u32[]{:S(2)}, u32[]{:S(2)}) collective-permute-start(bf16[2048,128]{1,0:T(8,128)(2,1)S(1)} %collective-permute-done.16.refs_2_), channel_id=1, source_target_pairs={{0,1},{1,0},{2,3},{3,2},{4,5},{5,4},{6,7},{7,6},{8,9},{9,8},{10,11... | collective-permute-start | bytes 1572872 | tf_op jit(solution)/shard_map/ppermute | solution.py:326
  42.0 8.5 %collective-permute-start.13 = (bf16[48,512]{1,0:T(8,128)(2,1)S(1)}, bf16[48,512]{1,0:T(8,128)(2,1)S(1)}, u32[]{:S(2)}, u32[]{:S(2)}) collective-permute-start(bf16[48,512]{1,0:T(8,128)(2,1)S(1)} %get-tuple-element.50), channel_id=1, source_target_pairs={{0,12},{4,0},{8,4},{12,8},{1,13},{5,1},{9,5},{13,9},{2,14},{6,2},{... | collective-permute-start | bytes 147464 | tf_op jit(solution)/shard_map/ppermute | solution.py:331
  45.9 5.9 %collective-permute-start.12 = (bf16[48,512]{1,0:T(8,128)(2,1)S(1)}, bf16[48,512]{1,0:T(8,128)(2,1)S(1)}, u32[]{:S(2)}, u32[]{:S(2)}) collective-permute-start(bf16[48,512]{1,0:T(8,128)(2,1)S(1)} %get-tuple-element.49), channel_id=1, source_target_pairs={{0,4},{4,8},{8,12},{12,0},{1,5},{5,9},{9,13},{13,1},{2,6},{6,10},{... | collective-permute-start | bytes 147464 | tf_op jit(solution)/shard_map/ppermute | solution.py:331
  45.9 4.6 %collective-permute-start.14 = (bf16[16,512]{1,0:T(8,128)(2,1)S(1)}, bf16[16,512]{1,0:T(8,128)(2,1)S(1)}, u32[]{:S(2)}, u32[]{:S(2)}) collective-permute-start(bf16[16,512]{1,0:T(8,128)(2,1)S(1)} %get-tuple-element.51), channel_id=1, source_target_pairs={{0,8},{4,12},{8,0},{12,4},{1,9},{5,13},{9,1},{13,5},{2,10},{6,14},... | collective-permute-start | bytes 49160 | tf_op jit(solution)/shard_map/ppermute | solution.py:331
  51.8 4.7 %collective-permute-start.15 = (bf16[1536,128]{1,0:T(8,128)(2,1)S(1)}, bf16[1536,128]{1,0:T(8,128)(2,1)S(1)}, u32[]{:S(2)}, u32[]{:S(2)}) collective-permute-start(bf16[1536,128]{1,0:T(8,128)(2,1)S(1)} %collective-permute-done.6.refs_2_), channel_id=1, source_target_pairs={{0,1},{1,0},{2,3},{3,2},{4,5},{5,4},{6,7},{7,6},{8,9},{9,8},{10,11... | collective-permute-start | bytes 1179656 | tf_op jit(solution)/shard_map/ppermute | solution.py:326
  (3 other events, 15.3 us)

commit v16 on v15

--- a/solution.py
+++ b/solution.py
@@ -441,14 +441,14 @@
             shape((node_count, edge_count), BF16),
             shape((2 * wide + COARSE_PAD, node_count), BF16),
         ],
-        [(VMEM, after(lists, core_latents))],
+        [(VMEM, after(lists, near))],
         [],
         0,
         "one_hot",
     )
-    core_near = swap(after(near, core_latents), 1)
+    core_near = swap(near, 1)
     core_far = swap(after(far, core_packs), 1)
-    edge_late_x = swap(after(edge_late, core_latents, hot), 2)
+    edge_late_x = swap(after(edge_late, near, hot), 2)
     node_late_x = swap(after(node_late, far_latents), 2)
     shards = [latents, core_latents, far_latents, swap(after(far_latents, far, core_packs, core_near), 1)]
     pairs = [near, far, core_near, core_far]

time: 58.1 us -> 57.5 us (0.990)
  starting transfers between devices: 20.3 us -> 18 us
  waiting for transfers between devices: 20.5 us -> 22.3 us
    ppermute x11, starting transfers between devices: 9.27 us -> 6.95 us  [swap(): return lax.ppermute(x, 'mp', [(i, i ^ mask) for i in range(size)])]
    ppermute x11, waiting for transfers between devices: 14.3 us -> 15.8 us  [swap(): return lax.ppermute(x, 'mp', [(i, i ^ mask) for i in range(size)])]
    ppermute x1, waiting for transfers between devices: 0.32 us -> 1.09 us  [on_device(): far = lax.ppermute(near, 'groups', [(0, 1), (1, 0)])]
  transfers between devices with their start and end apart: 18 -> 18, of which waited for: 10 -> 9; matrix products, arithmetic and copies ran while one was open for 0% -> 0% of each run, Pallas kernels for 22% -> 22%
where the time goes in v16:
time: 57.5 us; the launch traced here: 57.3 us
  waiting for transfers between devices  22.3 us (39%)
  starting transfers between devices  18 us (31%)
  Pallas kernels  16.2 us (28%)
  between operations  0.82 us (1%)
    pallas_call x8, Pallas kernels, call(): pl.pallas_call(kernel, out_shape=out_shape, in_specs=[pl.BlockSpec(memory...  16.2 us
    ppermute x11, waiting for transfers between devices, swap(): return lax.ppermute(x, 'mp', [(i, i ^ mask) for i in range(size)])  15.8 us
    ppermute x6, starting transfers between devices, shift(): return lax.ppermute(x, 'graph', [(i, (i + by) % size) for i in range(size)])  9.53 us
    ppermute x11, starting transfers between devices, swap(): return lax.ppermute(x, 'mp', [(i, i ^ mask) for i in range(size)])  6.95 us
    ppermute x6, waiting for transfers between devices, shift(): return lax.ppermute(x, 'graph', [(i, (i + by) % size) for i in range(size)])  5.42 us
    ppermute x1, starting transfers between devices, on_device(): far = lax.ppermute(near, 'groups', [(0, 1), (1, 0)])  1.52 us
  transfers between devices with their start and end apart: 18, of which 9 were waited for; matrix products, arithmetic and copies ran while one was open for 0% of the time, Pallas kernels for 22%

profile of v16, /device:TPU:0, one launch (start us, length us, event | category | flops | bytes accessed | tf_op | source)
XLA Modules:
  0.0 57.3 jit_solution(14301532369596389517)
XLA Ops:
  0.7 2.0 %layer_0_half.1 = bf16[1792,128]{1,0:T(8,128)(2,1)} custom-call(bf16[2,1536,128]{2,1,0:T(8,128)(2,1)} %ef.2, bf16[2,128,512]{2,1,0:T(8,128)(2,1)} %es.3, bf16[2,1024,128]{2,1,0:T(8,128)(2,1)} %nf.3, bf16[2,128,512]{2,1,0:T(8,128)(2,1)} %ns.3), custom_call_target="tpu_custom_call" | custom-call | tf_op jit(solution)/shard_map/layer_0_half/pallas_call | solution.py:312
  2.8 3.0 %collective-permute-start.3 = (bf16[1792,128]{1,0:T(8,128)(2,1)}, bf16[1792,128]{1,0:T(8,128)(2,1)S(1)}, u32[]{:S(2)}, u32[]{:S(2)}) collective-permute-start(bf16[1792,128]{1,0:T(8,128)(2,1)} %layer_0_half.1), channel_id=1, source_target_pairs={{0,2},{1,3},{2,0},{3,1},{4,6},{5,7},{6,4},{7,5},{8,10},{9,11},{10,... | collective-permute-start | bytes 1376264 | tf_op jit(solution)/shard_map/ppermute | solution.py:326
  6.1 1.6 %collective-permute-start = (bf16[48,128]{1,0:T(8,128)(2,1)S(1)}, bf16[48,128]{1,0:T(8,128)(2,1)S(1)}, u32[]{:S(2)}, u32[]{:S(2)}) collective-permute-start(bf16[48,128]{1,0:T(8,128)(2,1)S(1)} %get-tuple-element.32), channel_id=1, source_target_pairs={{0,4},{4,8},{8,12},{12,0},{1,5},{5,9},{9,13},{13,1},{2,6},{6,10},{... | collective-permute-start | bytes 36872 | tf_op jit(solution)/shard_map/ppermute | solution.py:331
  7.7 2.2 %collective-permute-start.1 = (bf16[48,128]{1,0:T(8,128)(2,1)S(1)}, bf16[48,128]{1,0:T(8,128)(2,1)S(1)}, u32[]{:S(2)}, u32[]{:S(2)}) collective-permute-start(bf16[48,128]{1,0:T(8,128)(2,1)S(1)} %get-tuple-element.33), channel_id=1, source_target_pairs={{0,12},{4,0},{8,4},{12,8},{1,13},{5,1},{9,5},{13,9},{2,14},{6,2},{... | collective-permute-start | bytes 36872 | tf_op jit(solution)/shard_map/ppermute | solution.py:331
  10.0 0.8 %collective-permute-start.2 = (bf16[16,128]{1,0:T(8,128)(2,1)S(1)}, bf16[16,128]{1,0:T(8,128)(2,1)S(1)}, u32[]{:S(2)}, u32[]{:S(2)}) collective-permute-start(bf16[16,128]{1,0:T(8,128)(2,1)S(1)} %get-tuple-element.34), channel_id=1, source_target_pairs={{0,8},{4,12},{8,0},{12,4},{1,9},{5,13},{9,1},{13,5},{2,10},{6,14},... | collective-permute-start | bytes 12296 | tf_op jit(solution)/shard_map/ppermute | solution.py:331
  10.8 3.7 %collective-permute-done.2.refs_4_ = bf16[16,128]{1,0:T(8,128)(2,1)S(1)} collective-permute-done((bf16[16,128]{1,0:T(8,128)(2,1)S(1)}, bf16[16,128]{1,0:T(8,128)(2,1)S(1)}, u32[]{:S(2)}, u32[]{:S(2)}) %collective-permute-start.2) | collective-permute-done | bytes 4128 | tf_op jit(solution)/shard_map/ppermute | solution.py:331
  14.5 1.1 %packed_weights.1 = (bf16[7168,128]{1,0:T(8,128)(2,1)S(1)}, bf16[2048,128]{1,0:T(8,128)(2,1)S(1)}, bf16[1536,128]{1,0:T(8,128)(2,1)S(1)}) custom-call(bf16[2,1536,128]{2,1,0:T(8,128)(2,1)S(1)} %copy-done, bf16[2,128,512]{2,1,0:T(8,128)(2,1)S(1)} %copy-done.3, bf16[2,1024,128]{2,1,0:T(8,128)(2,1)S(1)} %copy-done.2, bf16[2,128,512]{2,1,0:T(8,128)(2,1)S(1)} %copy-done.4), custom_call_target="tpu_custom_call" | custom-call | tf_op jit(solution)/shard_map/packed_weights/pallas_call | solution.py:312
  15.7 0.9 %collective-permute-done.3.refs_2_ = bf16[1792,128]{1,0:T(8,128)(2,1)S(1)} collective-permute-done((bf16[1792,128]{1,0:T(8,128)(2,1)}, bf16[1792,128]{1,0:T(8,128)(2,1)S(1)}, u32[]{:S(2)}, u32[]{:S(2)}) %collective-permute-start.3) | collective-permute-done | bytes 458784 | tf_op jit(solution)/shard_map/ppermute | solution.py:326
  16.6 1.8 %collective-permute-start.5 = (bf16[1840,128]{1,0:T(8,128)(2,1)S(1)}, bf16[1840,128]{1,0:T(8,128)(2,1)S(1)}, u32[]{:S(2)}, u32[]{:S(2)}) collective-permute-start(bf16[1840,128]{1,0:T(8,128)(2,1)S(1)} %latents.1.refs_6_), channel_id=1, source_target_pairs={{0,2},{1,3},{2,0},{3,1},{4,6},{5,7},{6,4},{7,5},{8,10},{9,11},{10,... | collective-permute-start | bytes 1413128 | tf_op jit(solution)/shard_map/ppermute | solution.py:326
  18.6 1.5 %collective-permute-start.7 = (bf16[1792,128]{1,0:T(8,128)(2,1)S(1)}, bf16[1792,128]{1,0:T(8,128)(2,1)S(1)}, u32[]{:S(2)}, u32[]{:S(2)}) collective-permute-start(bf16[1792,128]{1,0:T(8,128)(2,1)S(1)} %collective-permute-done.3.refs_2_), channel_id=1, source_target_pairs={{0,16},{16,0},{1,17},{17,1},{2,18},{18,2},{3,19},{19,3},{4,20},{20... | collective-permute-start | bytes 1376264 | tf_op jit(solution)/shard_map/ppermute | solution.py:426
  20.1 1.1 %one_hot.1 = (bf16[1536,512]{1,0:T(8,128)(2,1)S(1)}, bf16[192,1536]{1,0:T(8,128)(2,1)S(1)}, bf16[112,192]{1,0:T(8,128)(2,1)S(1)}) custom-call(s32[1,3136]{1,0:T(1,128)S(1)} %broadcast_in_dim.3.list_ref), custom_call_target="tpu_custom_call" | custom-call | tf_op jit(solution)/shard_map/one_hot/pallas_call | solution.py:312
  21.2 0.6 %collective-permute-start.16 = (bf16[2048,128]{1,0:T(8,128)(2,1)S(1)}, bf16[2048,128]{1,0:T(8,128)(2,1)S(1)}, u32[]{:S(2)}, u32[]{:S(2)}) collective-permute-start(bf16[2048,128]{1,0:T(8,128)(2,1)S(1)} %get-tuple-element.54), channel_id=1, source_target_pairs={{0,2},{1,3},{2,0},{3,1},{4,6},{5,7},{6,4},{7,5},{8,10},{9,11},{10,... | collective-permute-start | bytes 1572872 | tf_op jit(solution)/shard_map/ppermute | solution.py:326
  21.8 8.4 %collective-permute-done.5.refs_8_ = bf16[1840,128]{1,0:T(8,128)(2,1)S(1)} collective-permute-done((bf16[1840,128]{1,0:T(8,128)(2,1)S(1)}, bf16[1840,128]{1,0:T(8,128)(2,1)S(1)}, u32[]{:S(2)}, u32[]{:S(2)}) %collective-permute-start.5) | collective-permute-done | bytes 471072 | tf_op jit(solution)/shard_map/ppermute | solution.py:326
  30.2 1.1 %collective-permute-done.7.refs_3_ = bf16[1792,128]{1,0:T(8,128)(2,1)S(1)} collective-permute-done((bf16[1792,128]{1,0:T(8,128)(2,1)S(1)}, bf16[1792,128]{1,0:T(8,128)(2,1)S(1)}, u32[]{:S(2)}, u32[]{:S(2)}) %collective-permute-start.7) | collective-permute-done | bytes 458784 | tf_op jit(solution)/shard_map/ppermute | solution.py:426
  31.8 0.8 %collective-permute-start.6 = (bf16[1536,128]{1,0:T(8,128)(2,1)S(1)}, bf16[1536,128]{1,0:T(8,128)(2,1)S(1)}, u32[]{:S(2)}, u32[]{:S(2)}) collective-permute-start(bf16[1536,128]{1,0:T(8,128)(2,1)S(1)} %get-tuple-element.40), channel_id=1, source_target_pairs={{0,2},{1,3},{2,0},{3,1},{4,6},{5,7},{6,4},{7,5},{8,10},{9,11},{10,... | collective-permute-start | bytes 1179656 | tf_op jit(solution)/shard_map/ppermute | solution.py:326
  32.6 1.2 %collective-permute-done.9.refs_5_ = bf16[1792,128]{1,0:T(8,128)(2,1)S(1)} collective-permute-done((bf16[1792,128]{1,0:T(8,128)(2,1)S(1)}, bf16[1792,128]{1,0:T(8,128)(2,1)S(1)}, u32[]{:S(2)}, u32[]{:S(2)}) %collective-permute-start.9) | collective-permute-done | bytes 458784 | tf_op jit(solution)/shard_map/ppermute | solution.py:326
  33.8 5.4 %layer_0.1 = (f32[1536,128]{1,0:T(8,128)S(1)}, bf16[1536,512]{1,0:T(8,128)(2,1)S(1)}, f32[192,128]{1,0:T(8,128)S(1)}, bf16[192,512]{1,0:T(8,128)(2,1)S(1)}, bf16...) custom-call(bf16[7168,128]{1,0:T(8,128)(2,1)S(1)} %get-tuple-element.38.refs_0_, ...), custom_call_target="tpu_custom_call" | custom-call | tf_op jit(solution)/shard_map/layer_0/pallas_call | solution.py:312
  39.2 2.2 %collective-permute-done.16.refs_2_ = bf16[2048,128]{1,0:T(8,128)(2,1)S(1)} collective-permute-done((bf16[2048,128]{1,0:T(8,128)(2,1)S(1)}, bf16[2048,128]{1,0:T(8,128)(2,1)S(1)}, u32[]{:S(2)}, u32[]{:S(2)}) %collective-permute-start.16) | collective-permute-done | bytes 524320 | tf_op jit(solution)/shard_map/ppermute | solution.py:326
  41.4 3.9 %collective-permute-start.13 = (bf16[48,512]{1,0:T(8,128)(2,1)S(1)}, bf16[48,512]{1,0:T(8,128)(2,1)S(1)}, u32[]{:S(2)}, u32[]{:S(2)}) collective-permute-start(bf16[48,512]{1,0:T(8,128)(2,1)S(1)} %get-tuple-element.48), channel_id=1, source_target_pairs={{0,12},{4,0},{8,4},{12,8},{1,13},{5,1},{9,5},{13,9},{2,14},{6,2},{... | collective-permute-start | bytes 147464 | tf_op jit(solution)/shard_map/ppermute | solution.py:331
  45.3 1.0 %collective-permute-start.14 = (bf16[16,512]{1,0:T(8,128)(2,1)S(1)}, bf16[16,512]{1,0:T(8,128)(2,1)S(1)}, u32[]{:S(2)}, u32[]{:S(2)}) collective-permute-start(bf16[16,512]{1,0:T(8,128)(2,1)S(1)} %get-tuple-element.49), channel_id=1, source_target_pairs={{0,8},{4,12},{8,0},{12,4},{1,9},{5,13},{9,1},{13,5},{2,10},{6,14},... | collective-permute-start | bytes 49160 | tf_op jit(solution)/shard_map/ppermute | solution.py:331
  46.3 3.2 %collective-permute-done.6.refs_2_ = bf16[1536,128]{1,0:T(8,128)(2,1)S(1)} collective-permute-done((bf16[1536,128]{1,0:T(8,128)(2,1)S(1)}, bf16[1536,128]{1,0:T(8,128)(2,1)S(1)}, u32[]{:S(2)}, u32[]{:S(2)}) %collective-permute-start.6) | collective-permute-done | bytes 393248 | tf_op jit(solution)/shard_map/ppermute | solution.py:326
  50.0 1.2 %collective-permute-done.12.refs_7_ = bf16[48,512]{1,0:T(8,128)(2,1)S(1)} collective-permute-done((bf16[48,512]{1,0:T(8,128)(2,1)S(1)}, bf16[48,512]{1,0:T(8,128)(2,1)S(1)}, u32[]{:S(2)}, u32[]{:S(2)}) %collective-permute-start.12) | collective-permute-done | bytes 49184 | tf_op jit(solution)/shard_map/ppermute | solution.py:331
  51.2 4.7 %layer_1_edges.1 = (f32[1536,128]{1,0:T(8,128)}, bf16[192,512]{1,0:T(8,128)(2,1)S(1)}) custom-call(bf16[7168,128]{1,0:T(8,128)(2,1)S(1)} %get-tuple-element.38.refs_0_, bf16[7168,128]{1,0:T(8,128)(2,1)S(1)} %collective-permute-done.4.refs_1_, bf16[2048,128]{1,0:T(8,128)(2,1)S(1)} %collective-permute-done.16.refs_2_, ...), custom_call_target="tpu_custom_call" | custom-call | tf_op jit(solution)/shard_map/layer_1_edges/pallas_call | solution.py:312
  55.9 1.4 %layer_1_nodes.1 = f32[192,128]{1,0:T(8,128)} custom-call(bf16[7168,128]{1,0:T(8,128)(2,1)S(1)} %get-tuple-element.38.refs_0_, bf16[7168,128]{1,0:T(8,128)(2,1)S(1)} %collective-permute-done.4.refs_1_, bf16[1536,128]{1,0:T(8,128)(2,1)S(1)} %collective-permute-done.6.refs_2_, bf16[1536,128]{1,0:T(8,128)(2,1)S(1)} %collective-permute-done.15.refs_3_, ...), custom_call_target="tpu_custom_call" | custom-call | tf_op jit(solution)/shard_map/layer_1_nodes/pallas_call | solution.py:312
  (40 shorter events, 1.6 us)
Async XLA Ops:
  0.6 13.9 %copy-start.4 = (bf16[2,128,512]{2,1,0:T(8,128)(2,1)S(1)}, bf16[2,128,512]{2,1,0:T(8,128)(2,1)}, u32[]{:S(2)}) copy-start(bf16[2,128,512]{2,1,0:T(8,128)(2,1)} %ns.3) | copy-start | bytes 786436
  0.6 13.9 %copy-start.2 = (bf16[2,1024,128]{2,1,0:T(8,128)(2,1)S(1)}, bf16[2,1024,128]{2,1,0:T(8,128)(2,1)}, u32[]{:S(2)}) copy-start(bf16[2,1024,128]{2,1,0:T(8,128)(2,1)} %nf.3) | copy-start | bytes 1572868
  0.7 13.9 %copy-start.3 = (bf16[2,128,512]{2,1,0:T(8,128)(2,1)S(1)}, bf16[2,128,512]{2,1,0:T(8,128)(2,1)}, u32[]{:S(2)}) copy-start(bf16[2,128,512]{2,1,0:T(8,128)(2,1)} %es.3) | copy-start | bytes 786436
  0.7 13.9 %copy-start = (bf16[2,1536,128]{2,1,0:T(8,128)(2,1)S(1)}, bf16[2,1536,128]{2,1,0:T(8,128)(2,1)}, u32[]{:S(2)}) copy-start(bf16[2,1536,128]{2,1,0:T(8,128)(2,1)} %ef.2) | copy-start | bytes 2359300
  0.7 5.1 %copy-start.5 = (f32[192,128]{1,0:T(8,128)S(1)}, f32[192,128]{1,0:T(8,128)}, u32[]{:S(2)}) copy-start(f32[192,128]{1,0:T(8,128)} %refs_11_.1) | copy-start | bytes 294916
  0.7 15.8 %copy-start.1 = (f32[1536,128]{1,0:T(8,128)S(1)}, f32[1536,128]{1,0:T(8,128)}, u32[]{:S(2)}) copy-start(f32[1536,128]{1,0:T(8,128)} %refs_10_.1) | copy-start | bytes 2359300
  2.8 13.7 %collective-permute-start.3 = (bf16[1792,128]{1,0:T(8,128)(2,1)}, bf16[1792,128]{1,0:T(8,128)(2,1)S(1)}, u32[]{:S(2)}, u32[]{:S(2)}) collective-permute-start(bf16[1792,128]{1,0:T(8,128)(2,1)} %layer_0_half.1), channel_id=1, source_target_pairs={{0,2},{1,3},{2,0},{3,1},{4,6},{5,7},{6,4},{7,5},{8,10},{9,11},{10,... | collective-permute-start | bytes 1376264 | tf_op jit(solution)/shard_map/ppermute | solution.py:326
  6.1 8.4 %collective-permute-start = (bf16[48,128]{1,0:T(8,128)(2,1)S(1)}, bf16[48,128]{1,0:T(8,128)(2,1)S(1)}, u32[]{:S(2)}, u32[]{:S(2)}) collective-permute-start(bf16[48,128]{1,0:T(8,128)(2,1)S(1)} %get-tuple-element.32), channel_id=1, source_target_pairs={{0,4},{4,8},{8,12},{12,0},{1,5},{5,9},{9,13},{13,1},{2,6},{6,10},{... | collective-permute-start | bytes 36872 | tf_op jit(solution)/shard_map/ppermute | solution.py:331
  7.7 6.8 %collective-permute-start.1 = (bf16[48,128]{1,0:T(8,128)(2,1)S(1)}, bf16[48,128]{1,0:T(8,128)(2,1)S(1)}, u32[]{:S(2)}, u32[]{:S(2)}) collective-permute-start(bf16[48,128]{1,0:T(8,128)(2,1)S(1)} %get-tuple-element.33), channel_id=1, source_target_pairs={{0,12},{4,0},{8,4},{12,8},{1,13},{5,1},{9,5},{13,9},{2,14},{6,2},{... | collective-permute-start | bytes 36872 | tf_op jit(solution)/shard_map/ppermute | solution.py:331
  10.0 4.5 %collective-permute-start.2 = (bf16[16,128]{1,0:T(8,128)(2,1)S(1)}, bf16[16,128]{1,0:T(8,128)(2,1)S(1)}, u32[]{:S(2)}, u32[]{:S(2)}) collective-permute-start(bf16[16,128]{1,0:T(8,128)(2,1)S(1)} %get-tuple-element.34), channel_id=1, source_target_pairs={{0,8},{4,12},{8,0},{12,4},{1,9},{5,13},{9,1},{13,5},{2,10},{6,14},... | collective-permute-start | bytes 12296 | tf_op jit(solution)/shard_map/ppermute | solution.py:331
  16.5 14.8 %collective-permute-start.4 = (bf16[7168,128]{1,0:T(8,128)(2,1)S(1)}, bf16[7168,128]{1,0:T(8,128)(2,1)S(1)}, u32[]{:S(2)}, u32[]{:S(2)}) collective-permute-start(bf16[7168,128]{1,0:T(8,128)(2,1)S(1)} %get-tuple-element.38.refs_0_), channel_id=1, source_target_pairs={{0,1},{1,0},{2,3},{3,2},{4,5},{5,4},{6,7},{7,6},{8,9},{9,8},{10,11... | collective-permute-start | bytes 5505032 | tf_op jit(solution)/shard_map/ppermute | solution.py:326
  16.6 13.6 %collective-permute-start.5 = (bf16[1840,128]{1,0:T(8,128)(2,1)S(1)}, bf16[1840,128]{1,0:T(8,128)(2,1)S(1)}, u32[]{:S(2)}, u32[]{:S(2)}) collective-permute-start(bf16[1840,128]{1,0:T(8,128)(2,1)S(1)} %latents.1.refs_6_), channel_id=1, source_target_pairs={{0,2},{1,3},{2,0},{3,1},{4,6},{5,7},{6,4},{7,5},{8,10},{9,11},{10,... | collective-permute-start | bytes 1413128 | tf_op jit(solution)/shard_map/ppermute | solution.py:326
  18.4 11.8 %collective-permute-start.8 = (bf16[1792,128]{1,0:T(8,128)(2,1)S(1)}, bf16[1792,128]{1,0:T(8,128)(2,1)S(1)}, u32[]{:S(2)}, u32[]{:S(2)}) collective-permute-start(bf16[1792,128]{1,0:T(8,128)(2,1)S(1)} %collective-permute-done.3.refs_2_), channel_id=1, source_target_pairs={{0,1},{1,0},{2,3},{3,2},{4,5},{5,4},{6,7},{7,6},{8,9},{9,8},{10,11... | collective-permute-start | bytes 1376264 | tf_op jit(solution)/shard_map/ppermute | solution.py:326
  18.6 12.7 %collective-permute-start.7 = (bf16[1792,128]{1,0:T(8,128)(2,1)S(1)}, bf16[1792,128]{1,0:T(8,128)(2,1)S(1)}, u32[]{:S(2)}, u32[]{:S(2)}) collective-permute-start(bf16[1792,128]{1,0:T(8,128)(2,1)S(1)} %collective-permute-done.3.refs_2_), channel_id=1, source_target_pairs={{0,16},{16,0},{1,17},{17,1},{2,18},{18,2},{3,19},{19,3},{4,20},{20... | collective-permute-start | bytes 1376264 | tf_op jit(solution)/shard_map/ppermute | solution.py:426
  21.2 20.2 %collective-permute-start.16 = (bf16[2048,128]{1,0:T(8,128)(2,1)S(1)}, bf16[2048,128]{1,0:T(8,128)(2,1)S(1)}, u32[]{:S(2)}, u32[]{:S(2)}) collective-permute-start(bf16[2048,128]{1,0:T(8,128)(2,1)S(1)} %get-tuple-element.54), channel_id=1, source_target_pairs={{0,2},{1,3},{2,0},{3,1},{4,6},{5,7},{6,4},{7,5},{8,10},{9,11},{10,... | collective-permute-start | bytes 1572872 | tf_op jit(solution)/shard_map/ppermute | solution.py:326
  30.2 2.4 %collective-permute-start.10 = (bf16[1840,128]{1,0:T(8,128)(2,1)S(1)}, bf16[1840,128]{1,0:T(8,128)(2,1)S(1)}, u32[]{:S(2)}, u32[]{:S(2)}) collective-permute-start(bf16[1840,128]{1,0:T(8,128)(2,1)S(1)} %latents.1.refs_6_), channel_id=1, source_target_pairs={{0,1},{1,0},{2,3},{3,2},{4,5},{5,4},{6,7},{7,6},{8,9},{9,8},{10,11... | collective-permute-start | bytes 1413128 | tf_op jit(solution)/shard_map/ppermute | solution.py:326
  31.3 2.5 %collective-permute-start.11 = (bf16[1840,128]{1,0:T(8,128)(2,1)S(1)}, bf16[1840,128]{1,0:T(8,128)(2,1)S(1)}, u32[]{:S(2)}, u32[]{:S(2)}) collective-permute-start(bf16[1840,128]{1,0:T(8,128)(2,1)S(1)} %collective-permute-done.5.refs_8_), channel_id=1, source_target_pairs={{0,1},{1,0},{2,3},{3,2},{4,5},{5,4},{6,7},{7,6},{8,9},{9,8},{10,11... | collective-permute-start | bytes 1413128 | tf_op jit(solution)/shard_map/ppermute | solution.py:326
  31.3 2.5 %collective-permute-start.9 = (bf16[1792,128]{1,0:T(8,128)(2,1)S(1)}, bf16[1792,128]{1,0:T(8,128)(2,1)S(1)}, u32[]{:S(2)}, u32[]{:S(2)}) collective-permute-start(bf16[1792,128]{1,0:T(8,128)(2,1)S(1)} %collective-permute-done.7.refs_3_), channel_id=1, source_target_pairs={{0,1},{1,0},{2,3},{3,2},{4,5},{5,4},{6,7},{7,6},{8,9},{9,8},{10,11... | collective-permute-start | bytes 1376264 | tf_op jit(solution)/shard_map/ppermute | solution.py:326
  31.8 17.7 %collective-permute-start.6 = (bf16[1536,128]{1,0:T(8,128)(2,1)S(1)}, bf16[1536,128]{1,0:T(8,128)(2,1)S(1)}, u32[]{:S(2)}, u32[]{:S(2)}) collective-permute-start(bf16[1536,128]{1,0:T(8,128)(2,1)S(1)} %get-tuple-element.40), channel_id=1, source_target_pairs={{0,2},{1,3},{2,0},{3,1},{4,6},{5,7},{6,4},{7,5},{8,10},{9,11},{10,... | collective-permute-start | bytes 1179656 | tf_op jit(solution)/shard_map/ppermute | solution.py:326
  41.4 9.7 %collective-permute-start.17 = (bf16[2048,128]{1,0:T(8,128)(2,1)S(1)}, bf16[2048,128]{1,0:T(8,128)(2,1)S(1)}, u32[]{:S(2)}, u32[]{:S(2)}) collective-permute-start(bf16[2048,128]{1,0:T(8,128)(2,1)S(1)} %collective-permute-done.16.refs_2_), channel_id=1, source_target_pairs={{0,1},{1,0},{2,3},{3,2},{4,5},{5,4},{6,7},{7,6},{8,9},{9,8},{10,11... | collective-permute-start | bytes 1572872 | tf_op jit(solution)/shard_map/ppermute | solution.py:326
  41.4 8.5 %collective-permute-start.13 = (bf16[48,512]{1,0:T(8,128)(2,1)S(1)}, bf16[48,512]{1,0:T(8,128)(2,1)S(1)}, u32[]{:S(2)}, u32[]{:S(2)}) collective-permute-start(bf16[48,512]{1,0:T(8,128)(2,1)S(1)} %get-tuple-element.48), channel_id=1, source_target_pairs={{0,12},{4,0},{8,4},{12,8},{1,13},{5,1},{9,5},{13,9},{2,14},{6,2},{... | collective-permute-start | bytes 147464 | tf_op jit(solution)/shard_map/ppermute | solution.py:331
  45.3 5.9 %collective-permute-start.12 = (bf16[48,512]{1,0:T(8,128)(2,1)S(1)}, bf16[48,512]{1,0:T(8,128)(2,1)S(1)}, u32[]{:S(2)}, u32[]{:S(2)}) collective-permute-start(bf16[48,512]{1,0:T(8,128)(2,1)S(1)} %get-tuple-element.47), channel_id=1, source_target_pairs={{0,4},{4,8},{8,12},{12,0},{1,5},{5,9},{9,13},{13,1},{2,6},{6,10},{... | collective-permute-start | bytes 147464 | tf_op jit(solution)/shard_map/ppermute | solution.py:331
  45.3 4.6 %collective-permute-start.14 = (bf16[16,512]{1,0:T(8,128)(2,1)S(1)}, bf16[16,512]{1,0:T(8,128)(2,1)S(1)}, u32[]{:S(2)}, u32[]{:S(2)}) collective-permute-start(bf16[16,512]{1,0:T(8,128)(2,1)S(1)} %get-tuple-element.49), channel_id=1, source_target_pairs={{0,8},{4,12},{8,0},{12,4},{1,9},{5,13},{9,1},{13,5},{2,10},{6,14},... | collective-permute-start | bytes 49160 | tf_op jit(solution)/shard_map/ppermute | solution.py:331
  51.2 4.7 %collective-permute-start.15 = (bf16[1536,128]{1,0:T(8,128)(2,1)S(1)}, bf16[1536,128]{1,0:T(8,128)(2,1)S(1)}, u32[]{:S(2)}, u32[]{:S(2)}) collective-permute-start(bf16[1536,128]{1,0:T(8,128)(2,1)S(1)} %collective-permute-done.6.refs_2_), channel_id=1, source_target_pairs={{0,1},{1,0},{2,3},{3,2},{4,5},{5,4},{6,7},{7,6},{8,9},{9,8},{10,11... | collective-permute-start | bytes 1179656 | tf_op jit(solution)/shard_map/ppermute | solution.py:326
  (3 other events, 15.3 us)

commit v17 on v16

--- a/solution.py
+++ b/solution.py
@@ -499,7 +499,7 @@
         "layer_1_edges",
         16,
     )
-    node_late_d = swap(after(node_late_x, *tables[1:]), 1)
+    node_late_d = swap(after(node_late_x, incoming), 1)
     (node_own,) = call(
         functools.partial(late_node_kernel, late_pack + edge_pack),
         [own_node],

time: 57.5 us -> 60.3 us (1.049)
  waiting for transfers between devices: 22.3 us -> 24.4 us
  starting transfers between devices: 18 us -> 18.7 us
    ppermute x6, waiting for transfers between devices: 5.42 us -> 8.59 us  [shift(): return lax.ppermute(x, 'graph', [(i, (i + by) % size) for i in range(size)])]
    ppermute x11, waiting for transfers between devices: 15.8 us -> 14.7 us  [swap(): return lax.ppermute(x, 'mp', [(i, i ^ mask) for i in range(size)])]
    ppermute x11, starting transfers between devices: 6.95 us -> 7.9 us  [swap(): return lax.ppermute(x, 'mp', [(i, i ^ mask) for i in range(size)])]
  transfers between devices with their start and end apart: 18 -> 18, of which waited for: 9 -> 10; matrix products, arithmetic and copies ran while one was open for 0% -> 0% of each run, Pallas kernels for 22% -> 21%
where the time goes in v17:
time: 60.3 us; the launch traced here: 60.2 us
  waiting for transfers between devices  24.4 us (40%)
  starting transfers between devices  18.7 us (31%)
  Pallas kernels  16.2 us (27%)
  between operations  0.82 us (1%)
    pallas_call x8, Pallas kernels, call(): pl.pallas_call(kernel, out_shape=out_shape, in_specs=[pl.BlockSpec(memory...  16.2 us
    ppermute x11, waiting for transfers between devices, swap(): return lax.ppermute(x, 'mp', [(i, i ^ mask) for i in range(size)])  14.7 us
    ppermute x6, starting transfers between devices, shift(): return lax.ppermute(x, 'graph', [(i, (i + by) % size) for i in range(size)])  9.28 us
    ppermute x6, waiting for transfers between devices, shift(): return lax.ppermute(x, 'graph', [(i, (i + by) % size) for i in range(size)])  8.59 us
    ppermute x11, starting transfers between devices, swap(): return lax.ppermute(x, 'mp', [(i, i ^ mask) for i in range(size)])  7.9 us
    ppermute x1, starting transfers between devices, on_device(): far = lax.ppermute(near, 'groups', [(0, 1), (1, 0)])  1.52 us
  transfers between devices with their start and end apart: 18, of which 10 were waited for; matrix products, arithmetic and copies ran while one was open for 0% of the time, Pallas kernels for 21%

profile of v17, /device:TPU:0, one launch (start us, length us, event | category | flops | bytes accessed | tf_op | source)
XLA Modules:
  0.0 60.2 jit_solution(18144197447853719812)
XLA Ops:
  0.7 2.0 %layer_0_half.1 = bf16[1792,128]{1,0:T(8,128)(2,1)} custom-call(bf16[2,1536,128]{2,1,0:T(8,128)(2,1)} %ef.2, bf16[2,128,512]{2,1,0:T(8,128)(2,1)} %es.3, bf16[2,1024,128]{2,1,0:T(8,128)(2,1)} %nf.3, bf16[2,128,512]{2,1,0:T(8,128)(2,1)} %ns.3), custom_call_target="tpu_custom_call" | custom-call | tf_op jit(solution)/shard_map/layer_0_half/pallas_call | solution.py:312
  2.8 3.0 %collective-permute-start.3 = (bf16[1792,128]{1,0:T(8,128)(2,1)}, bf16[1792,128]{1,0:T(8,128)(2,1)S(1)}, u32[]{:S(2)}, u32[]{:S(2)}) collective-permute-start(bf16[1792,128]{1,0:T(8,128)(2,1)} %layer_0_half.1), channel_id=1, source_target_pairs={{0,2},{1,3},{2,0},{3,1},{4,6},{5,7},{6,4},{7,5},{8,10},{9,11},{10,... | collective-permute-start | bytes 1376264 | tf_op jit(solution)/shard_map/ppermute | solution.py:326
  6.1 1.6 %collective-permute-start = (bf16[48,128]{1,0:T(8,128)(2,1)S(1)}, bf16[48,128]{1,0:T(8,128)(2,1)S(1)}, u32[]{:S(2)}, u32[]{:S(2)}) collective-permute-start(bf16[48,128]{1,0:T(8,128)(2,1)S(1)} %get-tuple-element.32), channel_id=1, source_target_pairs={{0,4},{4,8},{8,12},{12,0},{1,5},{5,9},{9,13},{13,1},{2,6},{6,10},{... | collective-permute-start | bytes 36872 | tf_op jit(solution)/shard_map/ppermute | solution.py:331
  7.7 2.2 %collective-permute-start.1 = (bf16[48,128]{1,0:T(8,128)(2,1)S(1)}, bf16[48,128]{1,0:T(8,128)(2,1)S(1)}, u32[]{:S(2)}, u32[]{:S(2)}) collective-permute-start(bf16[48,128]{1,0:T(8,128)(2,1)S(1)} %get-tuple-element.33), channel_id=1, source_target_pairs={{0,12},{4,0},{8,4},{12,8},{1,13},{5,1},{9,5},{13,9},{2,14},{6,2},{... | collective-permute-start | bytes 36872 | tf_op jit(solution)/shard_map/ppermute | solution.py:331
  10.0 0.8 %collective-permute-start.2 = (bf16[16,128]{1,0:T(8,128)(2,1)S(1)}, bf16[16,128]{1,0:T(8,128)(2,1)S(1)}, u32[]{:S(2)}, u32[]{:S(2)}) collective-permute-start(bf16[16,128]{1,0:T(8,128)(2,1)S(1)} %get-tuple-element.34), channel_id=1, source_target_pairs={{0,8},{4,12},{8,0},{12,4},{1,9},{5,13},{9,1},{13,5},{2,10},{6,14},... | collective-permute-start | bytes 12296 | tf_op jit(solution)/shard_map/ppermute | solution.py:331
  10.8 3.7 %collective-permute-done.2.refs_4_ = bf16[16,128]{1,0:T(8,128)(2,1)S(1)} collective-permute-done((bf16[16,128]{1,0:T(8,128)(2,1)S(1)}, bf16[16,128]{1,0:T(8,128)(2,1)S(1)}, u32[]{:S(2)}, u32[]{:S(2)}) %collective-permute-start.2) | collective-permute-done | bytes 4128 | tf_op jit(solution)/shard_map/ppermute | solution.py:331
  14.5 1.1 %packed_weights.1 = (bf16[7168,128]{1,0:T(8,128)(2,1)S(1)}, bf16[2048,128]{1,0:T(8,128)(2,1)S(1)}, bf16[1536,128]{1,0:T(8,128)(2,1)S(1)}) custom-call(bf16[2,1536,128]{2,1,0:T(8,128)(2,1)S(1)} %copy-done, bf16[2,128,512]{2,1,0:T(8,128)(2,1)S(1)} %copy-done.3, bf16[2,1024,128]{2,1,0:T(8,128)(2,1)S(1)} %copy-done.2, bf16[2,128,512]{2,1,0:T(8,128)(2,1)S(1)} %copy-done.4), custom_call_target="tpu_custom_call" | custom-call | tf_op jit(solution)/shard_map/packed_weights/pallas_call | solution.py:312
  15.7 0.9 %collective-permute-done.3.refs_2_ = bf16[1792,128]{1,0:T(8,128)(2,1)S(1)} collective-permute-done((bf16[1792,128]{1,0:T(8,128)(2,1)}, bf16[1792,128]{1,0:T(8,128)(2,1)S(1)}, u32[]{:S(2)}, u32[]{:S(2)}) %collective-permute-start.3) | collective-permute-done | bytes 458784 | tf_op jit(solution)/shard_map/ppermute | solution.py:326
  16.6 1.8 %collective-permute-start.5 = (bf16[1840,128]{1,0:T(8,128)(2,1)S(1)}, bf16[1840,128]{1,0:T(8,128)(2,1)S(1)}, u32[]{:S(2)}, u32[]{:S(2)}) collective-permute-start(bf16[1840,128]{1,0:T(8,128)(2,1)S(1)} %latents.1.refs_6_), channel_id=1, source_target_pairs={{0,2},{1,3},{2,0},{3,1},{4,6},{5,7},{6,4},{7,5},{8,10},{9,11},{10,... | collective-permute-start | bytes 1413128 | tf_op jit(solution)/shard_map/ppermute | solution.py:326
  18.6 1.5 %collective-permute-start.8 = (bf16[1792,128]{1,0:T(8,128)(2,1)S(1)}, bf16[1792,128]{1,0:T(8,128)(2,1)S(1)}, u32[]{:S(2)}, u32[]{:S(2)}) collective-permute-start(bf16[1792,128]{1,0:T(8,128)(2,1)S(1)} %collective-permute-done.3.refs_2_), channel_id=1, source_target_pairs={{0,16},{16,0},{1,17},{17,1},{2,18},{18,2},{3,19},{19,3},{4,20},{20... | collective-permute-start | bytes 1376264 | tf_op jit(solution)/shard_map/ppermute | solution.py:426
  20.1 1.1 %one_hot.1 = (bf16[1536,512]{1,0:T(8,128)(2,1)S(1)}, bf16[192,1536]{1,0:T(8,128)(2,1)S(1)}, bf16[112,192]{1,0:T(8,128)(2,1)S(1)}) custom-call(s32[1,3136]{1,0:T(1,128)S(1)} %broadcast_in_dim.3.list_ref), custom_call_target="tpu_custom_call" | custom-call | tf_op jit(solution)/shard_map/one_hot/pallas_call | solution.py:312
  21.8 8.4 %collective-permute-done.5.refs_8_ = bf16[1840,128]{1,0:T(8,128)(2,1)S(1)} collective-permute-done((bf16[1840,128]{1,0:T(8,128)(2,1)S(1)}, bf16[1840,128]{1,0:T(8,128)(2,1)S(1)}, u32[]{:S(2)}, u32[]{:S(2)}) %collective-permute-start.5) | collective-permute-done | bytes 471072 | tf_op jit(solution)/shard_map/ppermute | solution.py:326
  30.2 1.1 %collective-permute-done.8.refs_3_ = bf16[1792,128]{1,0:T(8,128)(2,1)S(1)} collective-permute-done((bf16[1792,128]{1,0:T(8,128)(2,1)S(1)}, bf16[1792,128]{1,0:T(8,128)(2,1)S(1)}, u32[]{:S(2)}, u32[]{:S(2)}) %collective-permute-start.8) | collective-permute-done | bytes 458784 | tf_op jit(solution)/shard_map/ppermute | solution.py:426
  32.0 1.8 %collective-permute-done.10.refs_5_ = bf16[1792,128]{1,0:T(8,128)(2,1)S(1)} collective-permute-done((bf16[1792,128]{1,0:T(8,128)(2,1)S(1)}, bf16[1792,128]{1,0:T(8,128)(2,1)S(1)}, u32[]{:S(2)}, u32[]{:S(2)}) %collective-permute-start.10) | collective-permute-done | bytes 458784 | tf_op jit(solution)/shard_map/ppermute | solution.py:326
  33.8 5.4 %layer_0.1 = (f32[1536,128]{1,0:T(8,128)S(1)}, bf16[1536,512]{1,0:T(8,128)(2,1)S(1)}, f32[192,128]{1,0:T(8,128)S(1)}, bf16[192,512]{1,0:T(8,128)(2,1)S(1)}, bf16...) custom-call(bf16[7168,128]{1,0:T(8,128)(2,1)S(1)} %get-tuple-element.38.refs_0_, ...), custom_call_target="tpu_custom_call" | custom-call | tf_op jit(solution)/shard_map/layer_0/pallas_call | solution.py:312
  39.2 1.8 %collective-permute-done.7.refs_2_ = bf16[2048,128]{1,0:T(8,128)(2,1)S(1)} collective-permute-done((bf16[2048,128]{1,0:T(8,128)(2,1)S(1)}, bf16[2048,128]{1,0:T(8,128)(2,1)S(1)}, u32[]{:S(2)}, u32[]{:S(2)}) %collective-permute-start.7) | collective-permute-done | bytes 524320 | tf_op jit(solution)/shard_map/ppermute | solution.py:326
  41.1 1.7 %collective-permute-start.6 = (bf16[1536,128]{1,0:T(8,128)(2,1)S(1)}, bf16[1536,128]{1,0:T(8,128)(2,1)S(1)}, u32[]{:S(2)}, u32[]{:S(2)}) collective-permute-start(bf16[1536,128]{1,0:T(8,128)(2,1)S(1)} %get-tuple-element.40), channel_id=1, source_target_pairs={{0,2},{1,3},{2,0},{3,1},{4,6},{5,7},{6,4},{7,5},{8,10},{9,11},{10,... | collective-permute-start | bytes 1179656 | tf_op jit(solution)/shard_map/ppermute | solution.py:326
  42.8 3.6 %collective-permute-start.15 = (bf16[48,512]{1,0:T(8,128)(2,1)S(1)}, bf16[48,512]{1,0:T(8,128)(2,1)S(1)}, u32[]{:S(2)}, u32[]{:S(2)}) collective-permute-start(bf16[48,512]{1,0:T(8,128)(2,1)S(1)} %get-tuple-element.54), channel_id=1, source_target_pairs={{0,12},{4,0},{8,4},{12,8},{1,13},{5,1},{9,5},{13,9},{2,14},{6,2},{... | collective-permute-start | bytes 147464 | tf_op jit(solution)/shard_map/ppermute | solution.py:331
  46.4 1.0 %collective-permute-start.16 = (bf16[16,512]{1,0:T(8,128)(2,1)S(1)}, bf16[16,512]{1,0:T(8,128)(2,1)S(1)}, u32[]{:S(2)}, u32[]{:S(2)}) collective-permute-start(bf16[16,512]{1,0:T(8,128)(2,1)S(1)} %get-tuple-element.55), channel_id=1, source_target_pairs={{0,8},{4,12},{8,0},{12,4},{1,9},{5,13},{9,1},{13,5},{2,10},{6,14},... | collective-permute-start | bytes 49160 | tf_op jit(solution)/shard_map/ppermute | solution.py:331
  47.4 4.2 %collective-permute-done.16.refs_9_ = bf16[16,512]{1,0:T(8,128)(2,1)S(1)} collective-permute-done((bf16[16,512]{1,0:T(8,128)(2,1)S(1)}, bf16[16,512]{1,0:T(8,128)(2,1)S(1)}, u32[]{:S(2)}, u32[]{:S(2)}) %collective-permute-start.16) | collective-permute-done | bytes 16416 | tf_op jit(solution)/shard_map/ppermute | solution.py:331
  51.6 0.7 %collective-permute-done.14.refs_7_ = bf16[48,512]{1,0:T(8,128)(2,1)S(1)} collective-permute-done((bf16[48,512]{1,0:T(8,128)(2,1)S(1)}, bf16[48,512]{1,0:T(8,128)(2,1)S(1)}, u32[]{:S(2)}, u32[]{:S(2)}) %collective-permute-start.14) | collective-permute-done | bytes 49184 | tf_op jit(solution)/shard_map/ppermute | solution.py:331
  52.3 4.7 %layer_1_edges.1 = (f32[1536,128]{1,0:T(8,128)}, bf16[192,512]{1,0:T(8,128)(2,1)S(1)}) custom-call(bf16[7168,128]{1,0:T(8,128)(2,1)S(1)} %get-tuple-element.38.refs_0_, bf16[7168,128]{1,0:T(8,128)(2,1)S(1)} %collective-permute-done.4.refs_1_, bf16[2048,128]{1,0:T(8,128)(2,1)S(1)} %collective-permute-done.7.refs_2_, ...), custom_call_target="tpu_custom_call" | custom-call | tf_op jit(solution)/shard_map/layer_1_edges/pallas_call | solution.py:312
  57.0 1.7 %collective-permute-done.17.refs_3_ = bf16[1536,128]{1,0:T(8,128)(2,1)S(1)} collective-permute-done((bf16[1536,128]{1,0:T(8,128)(2,1)S(1)}, bf16[1536,128]{1,0:T(8,128)(2,1)S(1)}, u32[]{:S(2)}, u32[]{:S(2)}) %collective-permute-start.17) | collective-permute-done | bytes 393248 | tf_op jit(solution)/shard_map/ppermute | solution.py:326
  58.7 1.4 %layer_1_nodes.1 = f32[192,128]{1,0:T(8,128)} custom-call(bf16[7168,128]{1,0:T(8,128)(2,1)S(1)} %get-tuple-element.38.refs_0_, bf16[7168,128]{1,0:T(8,128)(2,1)S(1)} %collective-permute-done.4.refs_1_, bf16[1536,128]{1,0:T(8,128)(2,1)S(1)} %collective-permute-done.6.refs_2_, bf16[1536,128]{1,0:T(8,128)(2,1)S(1)} %collective-permute-done.17.refs_3_, ...), custom_call_target="tpu_custom_call" | custom-call | tf_op jit(solution)/shard_map/layer_1_nodes/pallas_call | solution.py:312
  (40 shorter events, 2.0 us)
Async XLA Ops:
  0.6 13.9 %copy-start.4 = (bf16[2,128,512]{2,1,0:T(8,128)(2,1)S(1)}, bf16[2,128,512]{2,1,0:T(8,128)(2,1)}, u32[]{:S(2)}) copy-start(bf16[2,128,512]{2,1,0:T(8,128)(2,1)} %ns.3) | copy-start | bytes 786436
  0.6 13.9 %copy-start.2 = (bf16[2,1024,128]{2,1,0:T(8,128)(2,1)S(1)}, bf16[2,1024,128]{2,1,0:T(8,128)(2,1)}, u32[]{:S(2)}) copy-start(bf16[2,1024,128]{2,1,0:T(8,128)(2,1)} %nf.3) | copy-start | bytes 1572868
  0.7 13.9 %copy-start.3 = (bf16[2,128,512]{2,1,0:T(8,128)(2,1)S(1)}, bf16[2,128,512]{2,1,0:T(8,128)(2,1)}, u32[]{:S(2)}) copy-start(bf16[2,128,512]{2,1,0:T(8,128)(2,1)} %es.3) | copy-start | bytes 786436
  0.7 13.9 %copy-start = (bf16[2,1536,128]{2,1,0:T(8,128)(2,1)S(1)}, bf16[2,1536,128]{2,1,0:T(8,128)(2,1)}, u32[]{:S(2)}) copy-start(bf16[2,1536,128]{2,1,0:T(8,128)(2,1)} %ef.2) | copy-start | bytes 2359300
  0.7 5.1 %copy-start.5 = (f32[192,128]{1,0:T(8,128)S(1)}, f32[192,128]{1,0:T(8,128)}, u32[]{:S(2)}) copy-start(f32[192,128]{1,0:T(8,128)} %refs_11_.1) | copy-start | bytes 294916
  0.7 15.8 %copy-start.1 = (f32[1536,128]{1,0:T(8,128)S(1)}, f32[1536,128]{1,0:T(8,128)}, u32[]{:S(2)}) copy-start(f32[1536,128]{1,0:T(8,128)} %refs_10_.1) | copy-start | bytes 2359300
  2.8 13.7 %collective-permute-start.3 = (bf16[1792,128]{1,0:T(8,128)(2,1)}, bf16[1792,128]{1,0:T(8,128)(2,1)S(1)}, u32[]{:S(2)}, u32[]{:S(2)}) collective-permute-start(bf16[1792,128]{1,0:T(8,128)(2,1)} %layer_0_half.1), channel_id=1, source_target_pairs={{0,2},{1,3},{2,0},{3,1},{4,6},{5,7},{6,4},{7,5},{8,10},{9,11},{10,... | collective-permute-start | bytes 1376264 | tf_op jit(solution)/shard_map/ppermute | solution.py:326
  6.1 8.4 %collective-permute-start = (bf16[48,128]{1,0:T(8,128)(2,1)S(1)}, bf16[48,128]{1,0:T(8,128)(2,1)S(1)}, u32[]{:S(2)}, u32[]{:S(2)}) collective-permute-start(bf16[48,128]{1,0:T(8,128)(2,1)S(1)} %get-tuple-element.32), channel_id=1, source_target_pairs={{0,4},{4,8},{8,12},{12,0},{1,5},{5,9},{9,13},{13,1},{2,6},{6,10},{... | collective-permute-start | bytes 36872 | tf_op jit(solution)/shard_map/ppermute | solution.py:331
  7.7 6.8 %collective-permute-start.1 = (bf16[48,128]{1,0:T(8,128)(2,1)S(1)}, bf16[48,128]{1,0:T(8,128)(2,1)S(1)}, u32[]{:S(2)}, u32[]{:S(2)}) collective-permute-start(bf16[48,128]{1,0:T(8,128)(2,1)S(1)} %get-tuple-element.33), channel_id=1, source_target_pairs={{0,12},{4,0},{8,4},{12,8},{1,13},{5,1},{9,5},{13,9},{2,14},{6,2},{... | collective-permute-start | bytes 36872 | tf_op jit(solution)/shard_map/ppermute | solution.py:331
  10.0 4.5 %collective-permute-start.2 = (bf16[16,128]{1,0:T(8,128)(2,1)S(1)}, bf16[16,128]{1,0:T(8,128)(2,1)S(1)}, u32[]{:S(2)}, u32[]{:S(2)}) collective-permute-start(bf16[16,128]{1,0:T(8,128)(2,1)S(1)} %get-tuple-element.34), channel_id=1, source_target_pairs={{0,8},{4,12},{8,0},{12,4},{1,9},{5,13},{9,1},{13,5},{2,10},{6,14},... | collective-permute-start | bytes 12296 | tf_op jit(solution)/shard_map/ppermute | solution.py:331
  16.5 14.8 %collective-permute-start.4 = (bf16[7168,128]{1,0:T(8,128)(2,1)S(1)}, bf16[7168,128]{1,0:T(8,128)(2,1)S(1)}, u32[]{:S(2)}, u32[]{:S(2)}) collective-permute-start(bf16[7168,128]{1,0:T(8,128)(2,1)S(1)} %get-tuple-element.38.refs_0_), channel_id=1, source_target_pairs={{0,1},{1,0},{2,3},{3,2},{4,5},{5,4},{6,7},{7,6},{8,9},{9,8},{10,11... | collective-permute-start | bytes 5505032 | tf_op jit(solution)/shard_map/ppermute | solution.py:326
  16.6 13.6 %collective-permute-start.5 = (bf16[1840,128]{1,0:T(8,128)(2,1)S(1)}, bf16[1840,128]{1,0:T(8,128)(2,1)S(1)}, u32[]{:S(2)}, u32[]{:S(2)}) collective-permute-start(bf16[1840,128]{1,0:T(8,128)(2,1)S(1)} %latents.1.refs_6_), channel_id=1, source_target_pairs={{0,2},{1,3},{2,0},{3,1},{4,6},{5,7},{6,4},{7,5},{8,10},{9,11},{10,... | collective-permute-start | bytes 1413128 | tf_op jit(solution)/shard_map/ppermute | solution.py:326
  18.4 11.8 %collective-permute-start.9 = (bf16[1792,128]{1,0:T(8,128)(2,1)S(1)}, bf16[1792,128]{1,0:T(8,128)(2,1)S(1)}, u32[]{:S(2)}, u32[]{:S(2)}) collective-permute-start(bf16[1792,128]{1,0:T(8,128)(2,1)S(1)} %collective-permute-done.3.refs_2_), channel_id=1, source_target_pairs={{0,1},{1,0},{2,3},{3,2},{4,5},{5,4},{6,7},{7,6},{8,9},{9,8},{10,11... | collective-permute-start | bytes 1376264 | tf_op jit(solution)/shard_map/ppermute | solution.py:326
  18.6 12.7 %collective-permute-start.8 = (bf16[1792,128]{1,0:T(8,128)(2,1)S(1)}, bf16[1792,128]{1,0:T(8,128)(2,1)S(1)}, u32[]{:S(2)}, u32[]{:S(2)}) collective-permute-start(bf16[1792,128]{1,0:T(8,128)(2,1)S(1)} %collective-permute-done.3.refs_2_), channel_id=1, source_target_pairs={{0,16},{16,0},{1,17},{17,1},{2,18},{18,2},{3,19},{19,3},{4,20},{20... | collective-permute-start | bytes 1376264 | tf_op jit(solution)/shard_map/ppermute | solution.py:426
  21.2 19.8 %collective-permute-start.7 = (bf16[2048,128]{1,0:T(8,128)(2,1)S(1)}, bf16[2048,128]{1,0:T(8,128)(2,1)S(1)}, u32[]{:S(2)}, u32[]{:S(2)}) collective-permute-start(bf16[2048,128]{1,0:T(8,128)(2,1)S(1)} %get-tuple-element.44), channel_id=1, source_target_pairs={{0,2},{1,3},{2,0},{3,1},{4,6},{5,7},{6,4},{7,5},{8,10},{9,11},{10,... | collective-permute-start | bytes 1572872 | tf_op jit(solution)/shard_map/ppermute | solution.py:326
  30.2 1.8 %collective-permute-start.11 = (bf16[1840,128]{1,0:T(8,128)(2,1)S(1)}, bf16[1840,128]{1,0:T(8,128)(2,1)S(1)}, u32[]{:S(2)}, u32[]{:S(2)}) collective-permute-start(bf16[1840,128]{1,0:T(8,128)(2,1)S(1)} %latents.1.refs_6_), channel_id=1, source_target_pairs={{0,1},{1,0},{2,3},{3,2},{4,5},{5,4},{6,7},{7,6},{8,9},{9,8},{10,11... | collective-permute-start | bytes 1413128 | tf_op jit(solution)/shard_map/ppermute | solution.py:326
  31.3 2.5 %collective-permute-start.12 = (bf16[1840,128]{1,0:T(8,128)(2,1)S(1)}, bf16[1840,128]{1,0:T(8,128)(2,1)S(1)}, u32[]{:S(2)}, u32[]{:S(2)}) collective-permute-start(bf16[1840,128]{1,0:T(8,128)(2,1)S(1)} %collective-permute-done.5.refs_8_), channel_id=1, source_target_pairs={{0,1},{1,0},{2,3},{3,2},{4,5},{5,4},{6,7},{7,6},{8,9},{9,8},{10,11... | collective-permute-start | bytes 1413128 | tf_op jit(solution)/shard_map/ppermute | solution.py:326
  31.3 2.5 %collective-permute-start.10 = (bf16[1792,128]{1,0:T(8,128)(2,1)S(1)}, bf16[1792,128]{1,0:T(8,128)(2,1)S(1)}, u32[]{:S(2)}, u32[]{:S(2)}) collective-permute-start(bf16[1792,128]{1,0:T(8,128)(2,1)S(1)} %collective-permute-done.8.refs_3_), channel_id=1, source_target_pairs={{0,1},{1,0},{2,3},{3,2},{4,5},{5,4},{6,7},{7,6},{8,9},{9,8},{10,11... | collective-permute-start | bytes 1376264 | tf_op jit(solution)/shard_map/ppermute | solution.py:326
  41.1 11.2 %collective-permute-start.13 = (bf16[2048,128]{1,0:T(8,128)(2,1)S(1)}, bf16[2048,128]{1,0:T(8,128)(2,1)S(1)}, u32[]{:S(2)}, u32[]{:S(2)}) collective-permute-start(bf16[2048,128]{1,0:T(8,128)(2,1)S(1)} %collective-permute-done.7.refs_2_), channel_id=1, source_target_pairs={{0,1},{1,0},{2,3},{3,2},{4,5},{5,4},{6,7},{7,6},{8,9},{9,8},{10,11... | collective-permute-start | bytes 1572872 | tf_op jit(solution)/shard_map/ppermute | solution.py:326
  41.1 15.9 %collective-permute-start.6 = (bf16[1536,128]{1,0:T(8,128)(2,1)S(1)}, bf16[1536,128]{1,0:T(8,128)(2,1)S(1)}, u32[]{:S(2)}, u32[]{:S(2)}) collective-permute-start(bf16[1536,128]{1,0:T(8,128)(2,1)S(1)} %get-tuple-element.40), channel_id=1, source_target_pairs={{0,2},{1,3},{2,0},{3,1},{4,6},{5,7},{6,4},{7,5},{8,10},{9,11},{10,... | collective-permute-start | bytes 1179656 | tf_op jit(solution)/shard_map/ppermute | solution.py:326
  42.8 8.8 %collective-permute-start.15 = (bf16[48,512]{1,0:T(8,128)(2,1)S(1)}, bf16[48,512]{1,0:T(8,128)(2,1)S(1)}, u32[]{:S(2)}, u32[]{:S(2)}) collective-permute-start(bf16[48,512]{1,0:T(8,128)(2,1)S(1)} %get-tuple-element.54), channel_id=1, source_target_pairs={{0,12},{4,0},{8,4},{12,8},{1,13},{5,1},{9,5},{13,9},{2,14},{6,2},{... | collective-permute-start | bytes 147464 | tf_op jit(solution)/shard_map/ppermute | solution.py:331
  46.4 5.9 %collective-permute-start.14 = (bf16[48,512]{1,0:T(8,128)(2,1)S(1)}, bf16[48,512]{1,0:T(8,128)(2,1)S(1)}, u32[]{:S(2)}, u32[]{:S(2)}) collective-permute-start(bf16[48,512]{1,0:T(8,128)(2,1)S(1)} %get-tuple-element.49), channel_id=1, source_target_pairs={{0,4},{4,8},{8,12},{12,0},{1,5},{5,9},{9,13},{13,1},{2,6},{6,10},{... | collective-permute-start | bytes 147464 | tf_op jit(solution)/shard_map/ppermute | solution.py:331
  46.4 5.2 %collective-permute-start.16 = (bf16[16,512]{1,0:T(8,128)(2,1)S(1)}, bf16[16,512]{1,0:T(8,128)(2,1)S(1)}, u32[]{:S(2)}, u32[]{:S(2)}) collective-permute-start(bf16[16,512]{1,0:T(8,128)(2,1)S(1)} %get-tuple-element.55), channel_id=1, source_target_pairs={{0,8},{4,12},{8,0},{12,4},{1,9},{5,13},{9,1},{13,5},{2,10},{6,14},... | collective-permute-start | bytes 49160 | tf_op jit(solution)/shard_map/ppermute | solution.py:331
  57.0 1.7 %collective-permute-start.17 = (bf16[1536,128]{1,0:T(8,128)(2,1)S(1)}, bf16[1536,128]{1,0:T(8,128)(2,1)S(1)}, u32[]{:S(2)}, u32[]{:S(2)}) collective-permute-start(bf16[1536,128]{1,0:T(8,128)(2,1)S(1)} %collective-permute-done.6.refs_2_), channel_id=1, source_target_pairs={{0,1},{1,0},{2,3},{3,2},{4,5},{5,4},{6,7},{7,6},{8,9},{9,8},{10,11... | collective-permute-start | bytes 1179656 | tf_op jit(solution)/shard_map/ppermute | solution.py:326
  (3 other events, 15.3 us)

commit v18 on v16

--- a/solution.py
+++ b/solution.py
@@ -212,7 +212,7 @@
         edge_bf = edge_ref[rows, :]
         pre = dot(edge_bf, first_ref[0:features, :]) + dot(hot_ref[rows, :], product_ref[...])
         norm = normalize(dot(silu(pre), second_ref[...]))
-        edge_new = (edge_bf.astype(F32) + norm).astype(BF16)
+        edge_new = edge_bf + norm.astype(BF16)
         if full_out is not None:
             full_out[rows, :] = edge_new
         own_out[rows, :] = own_ref[rows, :] + own_columns(norm, part)

time: 57.5 us -> 57.5 us (level)
  no operation moved by 1% of the time
where the time goes in v18:
time: 57.5 us; the launch traced here: 57.3 us
  waiting for transfers between devices  22.5 us (39%)
  starting transfers between devices  18 us (31%)
  Pallas kernels  15.9 us (28%)
  between operations  0.82 us (1%)
    ppermute x11, waiting for transfers between devices, swap(): return lax.ppermute(x, 'mp', [(i, i ^ mask) for i in range(size)])  16 us
    pallas_call x8, Pallas kernels, call(): pl.pallas_call(kernel, out_shape=out_shape, in_specs=[pl.BlockSpec(memory...  15.9 us
    ppermute x6, starting transfers between devices, shift(): return lax.ppermute(x, 'graph', [(i, (i + by) % size) for i in range(size)])  9.53 us
    ppermute x11, starting transfers between devices, swap(): return lax.ppermute(x, 'mp', [(i, i ^ mask) for i in range(size)])  6.95 us
    ppermute x6, waiting for transfers between devices, shift(): return lax.ppermute(x, 'graph', [(i, (i + by) % size) for i in range(size)])  5.42 us
    ppermute x1, starting transfers between devices, on_device(): far = lax.ppermute(near, 'groups', [(0, 1), (1, 0)])  1.52 us
  transfers between devices with their start and end apart: 18, of which 9 were waited for; matrix products, arithmetic and copies ran while one was open for 0% of the time, Pallas kernels for 22%

profile of v18, /device:TPU:0, one launch (start us, length us, event | category | flops | bytes accessed | tf_op | source)
XLA Modules:
  0.0 57.3 jit_solution(14548667586637624882)
XLA Ops:
  0.7 2.0 %layer_0_half.1 = bf16[1792,128]{1,0:T(8,128)(2,1)} custom-call(bf16[2,1536,128]{2,1,0:T(8,128)(2,1)} %ef.2, bf16[2,128,512]{2,1,0:T(8,128)(2,1)} %es.3, bf16[2,1024,128]{2,1,0:T(8,128)(2,1)} %nf.3, bf16[2,128,512]{2,1,0:T(8,128)(2,1)} %ns.3), custom_call_target="tpu_custom_call" | custom-call | tf_op jit(solution)/shard_map/layer_0_half/pallas_call | solution.py:312
  2.8 3.0 %collective-permute-start.3 = (bf16[1792,128]{1,0:T(8,128)(2,1)}, bf16[1792,128]{1,0:T(8,128)(2,1)S(1)}, u32[]{:S(2)}, u32[]{:S(2)}) collective-permute-start(bf16[1792,128]{1,0:T(8,128)(2,1)} %layer_0_half.1), channel_id=1, source_target_pairs={{0,2},{1,3},{2,0},{3,1},{4,6},{5,7},{6,4},{7,5},{8,10},{9,11},{10,... | collective-permute-start | bytes 1376264 | tf_op jit(solution)/shard_map/ppermute | solution.py:326
  6.1 1.6 %collective-permute-start = (bf16[48,128]{1,0:T(8,128)(2,1)S(1)}, bf16[48,128]{1,0:T(8,128)(2,1)S(1)}, u32[]{:S(2)}, u32[]{:S(2)}) collective-permute-start(bf16[48,128]{1,0:T(8,128)(2,1)S(1)} %get-tuple-element.32), channel_id=1, source_target_pairs={{0,4},{4,8},{8,12},{12,0},{1,5},{5,9},{9,13},{13,1},{2,6},{6,10},{... | collective-permute-start | bytes 36872 | tf_op jit(solution)/shard_map/ppermute | solution.py:331
  7.7 2.2 %collective-permute-start.1 = (bf16[48,128]{1,0:T(8,128)(2,1)S(1)}, bf16[48,128]{1,0:T(8,128)(2,1)S(1)}, u32[]{:S(2)}, u32[]{:S(2)}) collective-permute-start(bf16[48,128]{1,0:T(8,128)(2,1)S(1)} %get-tuple-element.33), channel_id=1, source_target_pairs={{0,12},{4,0},{8,4},{12,8},{1,13},{5,1},{9,5},{13,9},{2,14},{6,2},{... | collective-permute-start | bytes 36872 | tf_op jit(solution)/shard_map/ppermute | solution.py:331
  10.0 0.8 %collective-permute-start.2 = (bf16[16,128]{1,0:T(8,128)(2,1)S(1)}, bf16[16,128]{1,0:T(8,128)(2,1)S(1)}, u32[]{:S(2)}, u32[]{:S(2)}) collective-permute-start(bf16[16,128]{1,0:T(8,128)(2,1)S(1)} %get-tuple-element.34), channel_id=1, source_target_pairs={{0,8},{4,12},{8,0},{12,4},{1,9},{5,13},{9,1},{13,5},{2,10},{6,14},... | collective-permute-start | bytes 12296 | tf_op jit(solution)/shard_map/ppermute | solution.py:331
  10.8 3.7 %collective-permute-done.2.refs_4_ = bf16[16,128]{1,0:T(8,128)(2,1)S(1)} collective-permute-done((bf16[16,128]{1,0:T(8,128)(2,1)S(1)}, bf16[16,128]{1,0:T(8,128)(2,1)S(1)}, u32[]{:S(2)}, u32[]{:S(2)}) %collective-permute-start.2) | collective-permute-done | bytes 4128 | tf_op jit(solution)/shard_map/ppermute | solution.py:331
  14.5 1.1 %packed_weights.1 = (bf16[7168,128]{1,0:T(8,128)(2,1)S(1)}, bf16[2048,128]{1,0:T(8,128)(2,1)S(1)}, bf16[1536,128]{1,0:T(8,128)(2,1)S(1)}) custom-call(bf16[2,1536,128]{2,1,0:T(8,128)(2,1)S(1)} %copy-done, bf16[2,128,512]{2,1,0:T(8,128)(2,1)S(1)} %copy-done.3, bf16[2,1024,128]{2,1,0:T(8,128)(2,1)S(1)} %copy-done.2, bf16[2,128,512]{2,1,0:T(8,128)(2,1)S(1)} %copy-done.4), custom_call_target="tpu_custom_call" | custom-call | tf_op jit(solution)/shard_map/packed_weights/pallas_call | solution.py:312
  15.7 0.9 %collective-permute-done.3.refs_2_ = bf16[1792,128]{1,0:T(8,128)(2,1)S(1)} collective-permute-done((bf16[1792,128]{1,0:T(8,128)(2,1)}, bf16[1792,128]{1,0:T(8,128)(2,1)S(1)}, u32[]{:S(2)}, u32[]{:S(2)}) %collective-permute-start.3) | collective-permute-done | bytes 458784 | tf_op jit(solution)/shard_map/ppermute | solution.py:326
  16.6 1.8 %collective-permute-start.5 = (bf16[1840,128]{1,0:T(8,128)(2,1)S(1)}, bf16[1840,128]{1,0:T(8,128)(2,1)S(1)}, u32[]{:S(2)}, u32[]{:S(2)}) collective-permute-start(bf16[1840,128]{1,0:T(8,128)(2,1)S(1)} %latents.1.refs_6_), channel_id=1, source_target_pairs={{0,2},{1,3},{2,0},{3,1},{4,6},{5,7},{6,4},{7,5},{8,10},{9,11},{10,... | collective-permute-start | bytes 1413128 | tf_op jit(solution)/shard_map/ppermute | solution.py:326
  18.6 1.5 %collective-permute-start.7 = (bf16[1792,128]{1,0:T(8,128)(2,1)S(1)}, bf16[1792,128]{1,0:T(8,128)(2,1)S(1)}, u32[]{:S(2)}, u32[]{:S(2)}) collective-permute-start(bf16[1792,128]{1,0:T(8,128)(2,1)S(1)} %collective-permute-done.3.refs_2_), channel_id=1, source_target_pairs={{0,16},{16,0},{1,17},{17,1},{2,18},{18,2},{3,19},{19,3},{4,20},{20... | collective-permute-start | bytes 1376264 | tf_op jit(solution)/shard_map/ppermute | solution.py:426
  20.1 1.1 %one_hot.1 = (bf16[1536,512]{1,0:T(8,128)(2,1)S(1)}, bf16[192,1536]{1,0:T(8,128)(2,1)S(1)}, bf16[112,192]{1,0:T(8,128)(2,1)S(1)}) custom-call(s32[1,3136]{1,0:T(1,128)S(1)} %broadcast_in_dim.3.list_ref), custom_call_target="tpu_custom_call" | custom-call | tf_op jit(solution)/shard_map/one_hot/pallas_call | solution.py:312
  21.2 0.6 %collective-permute-start.16 = (bf16[2048,128]{1,0:T(8,128)(2,1)S(1)}, bf16[2048,128]{1,0:T(8,128)(2,1)S(1)}, u32[]{:S(2)}, u32[]{:S(2)}) collective-permute-start(bf16[2048,128]{1,0:T(8,128)(2,1)S(1)} %get-tuple-element.54), channel_id=1, source_target_pairs={{0,2},{1,3},{2,0},{3,1},{4,6},{5,7},{6,4},{7,5},{8,10},{9,11},{10,... | collective-permute-start | bytes 1572872 | tf_op jit(solution)/shard_map/ppermute | solution.py:326
  21.8 8.4 %collective-permute-done.5.refs_8_ = bf16[1840,128]{1,0:T(8,128)(2,1)S(1)} collective-permute-done((bf16[1840,128]{1,0:T(8,128)(2,1)S(1)}, bf16[1840,128]{1,0:T(8,128)(2,1)S(1)}, u32[]{:S(2)}, u32[]{:S(2)}) %collective-permute-start.5) | collective-permute-done | bytes 471072 | tf_op jit(solution)/shard_map/ppermute | solution.py:326
  30.2 1.1 %collective-permute-done.7.refs_3_ = bf16[1792,128]{1,0:T(8,128)(2,1)S(1)} collective-permute-done((bf16[1792,128]{1,0:T(8,128)(2,1)S(1)}, bf16[1792,128]{1,0:T(8,128)(2,1)S(1)}, u32[]{:S(2)}, u32[]{:S(2)}) %collective-permute-start.7) | collective-permute-done | bytes 458784 | tf_op jit(solution)/shard_map/ppermute | solution.py:426
  31.8 0.8 %collective-permute-start.6 = (bf16[1536,128]{1,0:T(8,128)(2,1)S(1)}, bf16[1536,128]{1,0:T(8,128)(2,1)S(1)}, u32[]{:S(2)}, u32[]{:S(2)}) collective-permute-start(bf16[1536,128]{1,0:T(8,128)(2,1)S(1)} %get-tuple-element.40), channel_id=1, source_target_pairs={{0,2},{1,3},{2,0},{3,1},{4,6},{5,7},{6,4},{7,5},{8,10},{9,11},{10,... | collective-permute-start | bytes 1179656 | tf_op jit(solution)/shard_map/ppermute | solution.py:326
  32.6 1.2 %collective-permute-done.9.refs_5_ = bf16[1792,128]{1,0:T(8,128)(2,1)S(1)} collective-permute-done((bf16[1792,128]{1,0:T(8,128)(2,1)S(1)}, bf16[1792,128]{1,0:T(8,128)(2,1)S(1)}, u32[]{:S(2)}, u32[]{:S(2)}) %collective-permute-start.9) | collective-permute-done | bytes 458784 | tf_op jit(solution)/shard_map/ppermute | solution.py:326
  33.8 5.2 %layer_0.1 = (f32[1536,128]{1,0:T(8,128)S(1)}, bf16[1536,512]{1,0:T(8,128)(2,1)S(1)}, f32[192,128]{1,0:T(8,128)S(1)}, bf16[192,512]{1,0:T(8,128)(2,1)S(1)}, bf16...) custom-call(bf16[7168,128]{1,0:T(8,128)(2,1)S(1)} %get-tuple-element.38.refs_0_, ...), custom_call_target="tpu_custom_call" | custom-call | tf_op jit(solution)/shard_map/layer_0/pallas_call | solution.py:312
  39.0 2.4 %collective-permute-done.16.refs_2_ = bf16[2048,128]{1,0:T(8,128)(2,1)S(1)} collective-permute-done((bf16[2048,128]{1,0:T(8,128)(2,1)S(1)}, bf16[2048,128]{1,0:T(8,128)(2,1)S(1)}, u32[]{:S(2)}, u32[]{:S(2)}) %collective-permute-start.16) | collective-permute-done | bytes 524320 | tf_op jit(solution)/shard_map/ppermute | solution.py:326
  41.4 3.9 %collective-permute-start.13 = (bf16[48,512]{1,0:T(8,128)(2,1)S(1)}, bf16[48,512]{1,0:T(8,128)(2,1)S(1)}, u32[]{:S(2)}, u32[]{:S(2)}) collective-permute-start(bf16[48,512]{1,0:T(8,128)(2,1)S(1)} %get-tuple-element.48), channel_id=1, source_target_pairs={{0,12},{4,0},{8,4},{12,8},{1,13},{5,1},{9,5},{13,9},{2,14},{6,2},{... | collective-permute-start | bytes 147464 | tf_op jit(solution)/shard_map/ppermute | solution.py:331
  45.3 1.0 %collective-permute-start.14 = (bf16[16,512]{1,0:T(8,128)(2,1)S(1)}, bf16[16,512]{1,0:T(8,128)(2,1)S(1)}, u32[]{:S(2)}, u32[]{:S(2)}) collective-permute-start(bf16[16,512]{1,0:T(8,128)(2,1)S(1)} %get-tuple-element.49), channel_id=1, source_target_pairs={{0,8},{4,12},{8,0},{12,4},{1,9},{5,13},{9,1},{13,5},{2,10},{6,14},... | collective-permute-start | bytes 49160 | tf_op jit(solution)/shard_map/ppermute | solution.py:331
  46.3 3.2 %collective-permute-done.6.refs_2_ = bf16[1536,128]{1,0:T(8,128)(2,1)S(1)} collective-permute-done((bf16[1536,128]{1,0:T(8,128)(2,1)S(1)}, bf16[1536,128]{1,0:T(8,128)(2,1)S(1)}, u32[]{:S(2)}, u32[]{:S(2)}) %collective-permute-start.6) | collective-permute-done | bytes 393248 | tf_op jit(solution)/shard_map/ppermute | solution.py:326
  50.0 1.2 %collective-permute-done.12.refs_7_ = bf16[48,512]{1,0:T(8,128)(2,1)S(1)} collective-permute-done((bf16[48,512]{1,0:T(8,128)(2,1)S(1)}, bf16[48,512]{1,0:T(8,128)(2,1)S(1)}, u32[]{:S(2)}, u32[]{:S(2)}) %collective-permute-start.12) | collective-permute-done | bytes 49184 | tf_op jit(solution)/shard_map/ppermute | solution.py:331
  51.2 4.6 %layer_1_edges.1 = (f32[1536,128]{1,0:T(8,128)}, bf16[192,512]{1,0:T(8,128)(2,1)S(1)}) custom-call(bf16[7168,128]{1,0:T(8,128)(2,1)S(1)} %get-tuple-element.38.refs_0_, bf16[7168,128]{1,0:T(8,128)(2,1)S(1)} %collective-permute-done.4.refs_1_, bf16[2048,128]{1,0:T(8,128)(2,1)S(1)} %collective-permute-done.16.refs_2_, ...), custom_call_target="tpu_custom_call" | custom-call | tf_op jit(solution)/shard_map/layer_1_edges/pallas_call | solution.py:312
  55.8 1.4 %layer_1_nodes.1 = f32[192,128]{1,0:T(8,128)} custom-call(bf16[7168,128]{1,0:T(8,128)(2,1)S(1)} %get-tuple-element.38.refs_0_, bf16[7168,128]{1,0:T(8,128)(2,1)S(1)} %collective-permute-done.4.refs_1_, bf16[1536,128]{1,0:T(8,128)(2,1)S(1)} %collective-permute-done.6.refs_2_, bf16[1536,128]{1,0:T(8,128)(2,1)S(1)} %collective-permute-done.15.refs_3_, ...), custom_call_target="tpu_custom_call" | custom-call | tf_op jit(solution)/shard_map/layer_1_nodes/pallas_call | solution.py:312
  (40 shorter events, 1.6 us)
Async XLA Ops:
  0.6 13.9 %copy-start.4 = (bf16[2,128,512]{2,1,0:T(8,128)(2,1)S(1)}, bf16[2,128,512]{2,1,0:T(8,128)(2,1)}, u32[]{:S(2)}) copy-start(bf16[2,128,512]{2,1,0:T(8,128)(2,1)} %ns.3) | copy-start | bytes 786436
  0.6 13.9 %copy-start.2 = (bf16[2,1024,128]{2,1,0:T(8,128)(2,1)S(1)}, bf16[2,1024,128]{2,1,0:T(8,128)(2,1)}, u32[]{:S(2)}) copy-start(bf16[2,1024,128]{2,1,0:T(8,128)(2,1)} %nf.3) | copy-start | bytes 1572868
  0.7 13.9 %copy-start.3 = (bf16[2,128,512]{2,1,0:T(8,128)(2,1)S(1)}, bf16[2,128,512]{2,1,0:T(8,128)(2,1)}, u32[]{:S(2)}) copy-start(bf16[2,128,512]{2,1,0:T(8,128)(2,1)} %es.3) | copy-start | bytes 786436
  0.7 13.9 %copy-start = (bf16[2,1536,128]{2,1,0:T(8,128)(2,1)S(1)}, bf16[2,1536,128]{2,1,0:T(8,128)(2,1)}, u32[]{:S(2)}) copy-start(bf16[2,1536,128]{2,1,0:T(8,128)(2,1)} %ef.2) | copy-start | bytes 2359300
  0.7 5.1 %copy-start.5 = (f32[192,128]{1,0:T(8,128)S(1)}, f32[192,128]{1,0:T(8,128)}, u32[]{:S(2)}) copy-start(f32[192,128]{1,0:T(8,128)} %refs_11_.1) | copy-start | bytes 294916
  0.7 15.8 %copy-start.1 = (f32[1536,128]{1,0:T(8,128)S(1)}, f32[1536,128]{1,0:T(8,128)}, u32[]{:S(2)}) copy-start(f32[1536,128]{1,0:T(8,128)} %refs_10_.1) | copy-start | bytes 2359300
  2.8 13.7 %collective-permute-start.3 = (bf16[1792,128]{1,0:T(8,128)(2,1)}, bf16[1792,128]{1,0:T(8,128)(2,1)S(1)}, u32[]{:S(2)}, u32[]{:S(2)}) collective-permute-start(bf16[1792,128]{1,0:T(8,128)(2,1)} %layer_0_half.1), channel_id=1, source_target_pairs={{0,2},{1,3},{2,0},{3,1},{4,6},{5,7},{6,4},{7,5},{8,10},{9,11},{10,... | collective-permute-start | bytes 1376264 | tf_op jit(solution)/shard_map/ppermute | solution.py:326
  6.1 8.4 %collective-permute-start = (bf16[48,128]{1,0:T(8,128)(2,1)S(1)}, bf16[48,128]{1,0:T(8,128)(2,1)S(1)}, u32[]{:S(2)}, u32[]{:S(2)}) collective-permute-start(bf16[48,128]{1,0:T(8,128)(2,1)S(1)} %get-tuple-element.32), channel_id=1, source_target_pairs={{0,4},{4,8},{8,12},{12,0},{1,5},{5,9},{9,13},{13,1},{2,6},{6,10},{... | collective-permute-start | bytes 36872 | tf_op jit(solution)/shard_map/ppermute | solution.py:331
  7.7 6.8 %collective-permute-start.1 = (bf16[48,128]{1,0:T(8,128)(2,1)S(1)}, bf16[48,128]{1,0:T(8,128)(2,1)S(1)}, u32[]{:S(2)}, u32[]{:S(2)}) collective-permute-start(bf16[48,128]{1,0:T(8,128)(2,1)S(1)} %get-tuple-element.33), channel_id=1, source_target_pairs={{0,12},{4,0},{8,4},{12,8},{1,13},{5,1},{9,5},{13,9},{2,14},{6,2},{... | collective-permute-start | bytes 36872 | tf_op jit(solution)/shard_map/ppermute | solution.py:331
  10.0 4.5 %collective-permute-start.2 = (bf16[16,128]{1,0:T(8,128)(2,1)S(1)}, bf16[16,128]{1,0:T(8,128)(2,1)S(1)}, u32[]{:S(2)}, u32[]{:S(2)}) collective-permute-start(bf16[16,128]{1,0:T(8,128)(2,1)S(1)} %get-tuple-element.34), channel_id=1, source_target_pairs={{0,8},{4,12},{8,0},{12,4},{1,9},{5,13},{9,1},{13,5},{2,10},{6,14},... | collective-permute-start | bytes 12296 | tf_op jit(solution)/shard_map/ppermute | solution.py:331
  16.5 14.8 %collective-permute-start.4 = (bf16[7168,128]{1,0:T(8,128)(2,1)S(1)}, bf16[7168,128]{1,0:T(8,128)(2,1)S(1)}, u32[]{:S(2)}, u32[]{:S(2)}) collective-permute-start(bf16[7168,128]{1,0:T(8,128)(2,1)S(1)} %get-tuple-element.38.refs_0_), channel_id=1, source_target_pairs={{0,1},{1,0},{2,3},{3,2},{4,5},{5,4},{6,7},{7,6},{8,9},{9,8},{10,11... | collective-permute-start | bytes 5505032 | tf_op jit(solution)/shard_map/ppermute | solution.py:326
  16.6 13.6 %collective-permute-start.5 = (bf16[1840,128]{1,0:T(8,128)(2,1)S(1)}, bf16[1840,128]{1,0:T(8,128)(2,1)S(1)}, u32[]{:S(2)}, u32[]{:S(2)}) collective-permute-start(bf16[1840,128]{1,0:T(8,128)(2,1)S(1)} %latents.1.refs_6_), channel_id=1, source_target_pairs={{0,2},{1,3},{2,0},{3,1},{4,6},{5,7},{6,4},{7,5},{8,10},{9,11},{10,... | collective-permute-start | bytes 1413128 | tf_op jit(solution)/shard_map/ppermute | solution.py:326
  18.4 11.8 %collective-permute-start.8 = (bf16[1792,128]{1,0:T(8,128)(2,1)S(1)}, bf16[1792,128]{1,0:T(8,128)(2,1)S(1)}, u32[]{:S(2)}, u32[]{:S(2)}) collective-permute-start(bf16[1792,128]{1,0:T(8,128)(2,1)S(1)} %collective-permute-done.3.refs_2_), channel_id=1, source_target_pairs={{0,1},{1,0},{2,3},{3,2},{4,5},{5,4},{6,7},{7,6},{8,9},{9,8},{10,11... | collective-permute-start | bytes 1376264 | tf_op jit(solution)/shard_map/ppermute | solution.py:326
  18.6 12.7 %collective-permute-start.7 = (bf16[1792,128]{1,0:T(8,128)(2,1)S(1)}, bf16[1792,128]{1,0:T(8,128)(2,1)S(1)}, u32[]{:S(2)}, u32[]{:S(2)}) collective-permute-start(bf16[1792,128]{1,0:T(8,128)(2,1)S(1)} %collective-permute-done.3.refs_2_), channel_id=1, source_target_pairs={{0,16},{16,0},{1,17},{17,1},{2,18},{18,2},{3,19},{19,3},{4,20},{20... | collective-permute-start | bytes 1376264 | tf_op jit(solution)/shard_map/ppermute | solution.py:426
  21.2 20.2 %collective-permute-start.16 = (bf16[2048,128]{1,0:T(8,128)(2,1)S(1)}, bf16[2048,128]{1,0:T(8,128)(2,1)S(1)}, u32[]{:S(2)}, u32[]{:S(2)}) collective-permute-start(bf16[2048,128]{1,0:T(8,128)(2,1)S(1)} %get-tuple-element.54), channel_id=1, source_target_pairs={{0,2},{1,3},{2,0},{3,1},{4,6},{5,7},{6,4},{7,5},{8,10},{9,11},{10,... | collective-permute-start | bytes 1572872 | tf_op jit(solution)/shard_map/ppermute | solution.py:326
  30.2 2.4 %collective-permute-start.10 = (bf16[1840,128]{1,0:T(8,128)(2,1)S(1)}, bf16[1840,128]{1,0:T(8,128)(2,1)S(1)}, u32[]{:S(2)}, u32[]{:S(2)}) collective-permute-start(bf16[1840,128]{1,0:T(8,128)(2,1)S(1)} %latents.1.refs_6_), channel_id=1, source_target_pairs={{0,1},{1,0},{2,3},{3,2},{4,5},{5,4},{6,7},{7,6},{8,9},{9,8},{10,11... | collective-permute-start | bytes 1413128 | tf_op jit(solution)/shard_map/ppermute | solution.py:326
  31.3 2.5 %collective-permute-start.11 = (bf16[1840,128]{1,0:T(8,128)(2,1)S(1)}, bf16[1840,128]{1,0:T(8,128)(2,1)S(1)}, u32[]{:S(2)}, u32[]{:S(2)}) collective-permute-start(bf16[1840,128]{1,0:T(8,128)(2,1)S(1)} %collective-permute-done.5.refs_8_), channel_id=1, source_target_pairs={{0,1},{1,0},{2,3},{3,2},{4,5},{5,4},{6,7},{7,6},{8,9},{9,8},{10,11... | collective-permute-start | bytes 1413128 | tf_op jit(solution)/shard_map/ppermute | solution.py:326
  31.3 2.5 %collective-permute-start.9 = (bf16[1792,128]{1,0:T(8,128)(2,1)S(1)}, bf16[1792,128]{1,0:T(8,128)(2,1)S(1)}, u32[]{:S(2)}, u32[]{:S(2)}) collective-permute-start(bf16[1792,128]{1,0:T(8,128)(2,1)S(1)} %collective-permute-done.7.refs_3_), channel_id=1, source_target_pairs={{0,1},{1,0},{2,3},{3,2},{4,5},{5,4},{6,7},{7,6},{8,9},{9,8},{10,11... | collective-permute-start | bytes 1376264 | tf_op jit(solution)/shard_map/ppermute | solution.py:326
  31.8 17.7 %collective-permute-start.6 = (bf16[1536,128]{1,0:T(8,128)(2,1)S(1)}, bf16[1536,128]{1,0:T(8,128)(2,1)S(1)}, u32[]{:S(2)}, u32[]{:S(2)}) collective-permute-start(bf16[1536,128]{1,0:T(8,128)(2,1)S(1)} %get-tuple-element.40), channel_id=1, source_target_pairs={{0,2},{1,3},{2,0},{3,1},{4,6},{5,7},{6,4},{7,5},{8,10},{9,11},{10,... | collective-permute-start | bytes 1179656 | tf_op jit(solution)/shard_map/ppermute | solution.py:326
  41.4 9.7 %collective-permute-start.17 = (bf16[2048,128]{1,0:T(8,128)(2,1)S(1)}, bf16[2048,128]{1,0:T(8,128)(2,1)S(1)}, u32[]{:S(2)}, u32[]{:S(2)}) collective-permute-start(bf16[2048,128]{1,0:T(8,128)(2,1)S(1)} %collective-permute-done.16.refs_2_), channel_id=1, source_target_pairs={{0,1},{1,0},{2,3},{3,2},{4,5},{5,4},{6,7},{7,6},{8,9},{9,8},{10,11... | collective-permute-start | bytes 1572872 | tf_op jit(solution)/shard_map/ppermute | solution.py:326
  41.4 8.5 %collective-permute-start.13 = (bf16[48,512]{1,0:T(8,128)(2,1)S(1)}, bf16[48,512]{1,0:T(8,128)(2,1)S(1)}, u32[]{:S(2)}, u32[]{:S(2)}) collective-permute-start(bf16[48,512]{1,0:T(8,128)(2,1)S(1)} %get-tuple-element.48), channel_id=1, source_target_pairs={{0,12},{4,0},{8,4},{12,8},{1,13},{5,1},{9,5},{13,9},{2,14},{6,2},{... | collective-permute-start | bytes 147464 | tf_op jit(solution)/shard_map/ppermute | solution.py:331
  45.3 5.9 %collective-permute-start.12 = (bf16[48,512]{1,0:T(8,128)(2,1)S(1)}, bf16[48,512]{1,0:T(8,128)(2,1)S(1)}, u32[]{:S(2)}, u32[]{:S(2)}) collective-permute-start(bf16[48,512]{1,0:T(8,128)(2,1)S(1)} %get-tuple-element.47), channel_id=1, source_target_pairs={{0,4},{4,8},{8,12},{12,0},{1,5},{5,9},{9,13},{13,1},{2,6},{6,10},{... | collective-permute-start | bytes 147464 | tf_op jit(solution)/shard_map/ppermute | solution.py:331
  45.3 4.6 %collective-permute-start.14 = (bf16[16,512]{1,0:T(8,128)(2,1)S(1)}, bf16[16,512]{1,0:T(8,128)(2,1)S(1)}, u32[]{:S(2)}, u32[]{:S(2)}) collective-permute-start(bf16[16,512]{1,0:T(8,128)(2,1)S(1)} %get-tuple-element.49), channel_id=1, source_target_pairs={{0,8},{4,12},{8,0},{12,4},{1,9},{5,13},{9,1},{13,5},{2,10},{6,14},... | collective-permute-start | bytes 49160 | tf_op jit(solution)/shard_map/ppermute | solution.py:331
  51.2 4.6 %collective-permute-start.15 = (bf16[1536,128]{1,0:T(8,128)(2,1)S(1)}, bf16[1536,128]{1,0:T(8,128)(2,1)S(1)}, u32[]{:S(2)}, u32[]{:S(2)}) collective-permute-start(bf16[1536,128]{1,0:T(8,128)(2,1)S(1)} %collective-permute-done.6.refs_2_), channel_id=1, source_target_pairs={{0,1},{1,0},{2,3},{3,2},{4,5},{5,4},{6,7},{7,6},{8,9},{9,8},{10,11... | collective-permute-start | bytes 1179656 | tf_op jit(solution)/shard_map/ppermute | solution.py:326
  (3 other events, 15.3 us)
